TPU v7x, 256 devices: a whole 4x4x8 slice. The times are simulated.
256 devices in a mesh: twist: 8 (over z_lo, y), walker: 16 (over z_hi, x), mp: 2 (over core).
Axes of the slice: x: 4, y: 4, z: 8 (z_hi: 4, z_lo: 2; z = z_hi * 2 + z_lo), core: 2. Of those that a mesh axis runs over, the one named last changes fastest.
Arguments:
- features: bfloat16 [8, 256, 64, 256], P('twist', 'walker', 'mp'), may hold values from -6 to 6
- psi_grad: bfloat16 [8, 256, 64, 256], P('twist', 'walker', 'mp'), may hold values from -6 to 6
- pair_means: bfloat16 [8, 2, 256, 64, 128], P('twist', None, 'walker', 'mp'), may hold values from -6 to 6
- energies: float32 [8, 256], P('twist', 'walker'), may hold values from -8 to -6
- multiplicity: int32 [8], P('twist'), may hold values from 1 to 48
- weights: bfloat16 [2, 896, 256], replicated, may hold values from -0.1875 to 0.1875
- a_inverse: float32 [2, 896, 896], P('mp'), as said below
- s_inverse: float32 [2, 256, 256], P('mp'), as said below
Outputs:
- a_batch: float32 [2, 896, 896], P('mp')
- s_batch: float32 [2, 256, 256], P('mp')
- direction: float32 [2, 896, 256], P('mp')
Inputs may be any that keep to these rules, and one draw needn't show every extreme that they name: `multiplicity`: the number of symmetry-equivalent twists that each irreducible twist stands for. `a_inverse`: each layer's matrix is symmetric with a positive diagonal that exceeds the sum of the magnitudes of its row's other entries. `s_inverse`: each layer's matrix is symmetric with a positive diagonal that exceeds the sum of the magnitudes of its row's other entries.
All inputs are finite; a program needn't handle non-finite values.
Results may differ from a plain program's by a relative error of at most 0.0047.
Values sent between devices are 32-bit elements; how exact they have to be, the bound alone decides.
No kernel may reach another device: no remote copies, remote signals or barrier semaphores. Data moves between devices by JAX's collectives and lax.ppermute only.
A program may use at most 64 MiB of HBM per device.

v0:
```python
import jax
import jax.numpy as jnp
from jax import lax
from jax.sharding import PartitionSpec as P


def body(features, psi_grad, pair_means, energies, multiplicity, weights, a_inverse, s_inverse):
    walker_total = energies.shape[1] * lax.axis_size("walker")
    local_electrons = features.shape[2]
    electron_total = local_electrons * lax.axis_size("mp")
    half_count = electron_total // 2
    hidden_width = features.shape[3]
    layer_count = weights.shape[0]
    input_width = weights.shape[1]
    electron_index = lax.axis_index("mp") * local_electrons + jnp.arange(local_electrons)
    is_up = electron_index < half_count
    spin_table = jnp.stack([is_up, jnp.logical_not(is_up)], 1).astype(jnp.bfloat16)
    hidden = features[0]
    inputs_seen = []
    tanh_list = []
    for layer in range(layer_count):
        local_sums = jnp.einsum(
            "wed,es->wsd", hidden, spin_table, preferred_element_type=jnp.float32
        )
        spin_sums = lax.psum(local_sums, "mp")
        means = (spin_sums / half_count).astype(jnp.bfloat16)
        shape_full = hidden.shape
        wide = jnp.concatenate(
            [
                hidden,
                jnp.broadcast_to(means[:, None, 0], shape_full),
                jnp.broadcast_to(means[:, None, 1], shape_full),
                pair_means[0, layer],
            ],
            -1,
        )
        inputs_seen.append(wide)
        z_value = jnp.einsum(
            "wei,if->wef", wide, weights[layer], preferred_element_type=jnp.float32
        )
        tanh_value = jnp.tanh(z_value)
        tanh_list.append(tanh_value)
        if layer + 1 < layer_count:
            hidden = (hidden.astype(jnp.float32) + tanh_value).astype(jnp.bfloat16)
    local_energy = jnp.sum(energies)
    mult_value = multiplicity.astype(jnp.float32)[0]
    energy_sum = lax.psum(local_energy, "walker")
    mult_total = lax.psum(mult_value, "twist")
    mean_energy = energy_sum / walker_total
    centered = (energies[0] - mean_energy)[:, None, None]
    row_scale = mult_value / mult_total / (walker_total * electron_total)
    upstream = psi_grad[0].astype(jnp.float32)
    blocks_a = [None] * layer_count
    blocks_s = [None] * layer_count
    blocks_g = [None] * layer_count
    for layer in reversed(range(layer_count)):
        slope = (upstream * (1.0 - tanh_list[layer] ** 2)).astype(jnp.bfloat16)
        weighted = (centered * slope.astype(jnp.float32)).astype(jnp.bfloat16)
        left = inputs_seen[layer]
        blocks_a[layer] = (
            jnp.einsum("wei,wej->ij", left, left, preferred_element_type=jnp.float32) * row_scale
        )
        blocks_s[layer] = (
            jnp.einsum("wei,wej->ij", slope, slope, preferred_element_type=jnp.float32) * row_scale
        )
        blocks_g[layer] = (
            jnp.einsum("wei,wej->ij", left, weighted, preferred_element_type=jnp.float32)
            * row_scale
        )
        if layer > 0:
            layer_weight = weights[layer]
            direct = jnp.einsum(
                "wef,df->wed",
                slope,
                layer_weight[:hidden_width],
                preferred_element_type=jnp.float32,
            )
            local_total = jnp.sum(slope, axis=1, dtype=jnp.float32)
            slope_total = lax.psum(local_total, "mp")
            up_part = (
                jnp.dot(
                    slope_total,
                    layer_weight[hidden_width : 2 * hidden_width].astype(jnp.float32).T,
                    precision=lax.Precision.HIGHEST,
                )
                / half_count
            )
            down_part = (
                jnp.dot(
                    slope_total,
                    layer_weight[2 * hidden_width : 3 * hidden_width].astype(jnp.float32).T,
                    precision=lax.Precision.HIGHEST,
                )
                / half_count
            )
            spin_part = jnp.where(is_up[None, :, None], up_part[:, None, :], down_part[:, None, :])
            upstream = upstream + direct + spin_part
    owned_a, owned_s, owned_g = (
        lax.psum_scatter(jnp.stack(blocks_a), "mp", scatter_dimension=0, tiled=True),
        lax.psum_scatter(jnp.stack(blocks_s), "mp", scatter_dimension=0, tiled=True),
        lax.psum_scatter(jnp.stack(blocks_g), "mp", scatter_dimension=0, tiled=True),
    )
    entry_count = layer_count * input_width * hidden_width
    a_sum, s_sum, g_sum = lax.psum((owned_a, owned_s, owned_g), ("twist", "walker"))
    half_all = jnp.einsum("lij,ljk->lik", g_sum, s_inverse, precision=lax.Precision.HIGHEST)
    natural = jnp.einsum("lij,ljk->lik", a_inverse, half_all, precision=lax.Precision.HIGHEST)
    curvature = lax.psum(jnp.sum(natural * g_sum), "mp")
    direction = natural * lax.rsqrt(curvature / entry_count)
    return (a_sum, s_sum, direction)


def solution(mesh):
    placed = (
        P("twist", "walker", "mp", None),
        P("twist", "walker", "mp", None),
        P("twist", None, "walker", "mp", None),
        P("twist", "walker"),
        P("twist"),
        P(),
        P("mp", None, None),
        P("mp", None, None),
    )
    return jax.shard_map(
        body,
        mesh=mesh,
        in_specs=placed,
        out_specs=(P("mp", None, None), P("mp", None, None), P("mp", None, None)),
        check_vma=False,
    )
```

profile of v0, /device:TPU:1, one launch (start us, length us, event | category | flops | bytes accessed | tf_op | source)
XLA Modules:
  0.0 407.3 jit_solution(216285517571525768)
XLA Ops:
  7.2 0.0 copy-start
  7.2 0.0 reduce-scatter.6.cloned.1.call-start
  7.3 1.2 convolution_bitcast_fusion.5
  8.5 6.5 %psum.63 = f32[16,2,256]{2,1,0:T(2,128)S(1)} all-reduce(f32[16,2,256]{2,1,0:T(2,128)S(1)} %convolution_bitcast_fusion.5), channel_id=1, replica_groups=mesh['twist'=8,'walker'=16,'mp'=2] {'mp'}, use_global_device_ids=true, to_apply=%region_0.0 | all-reduce | flops 8192 | bytes 65536 | tf_op jit(solution)/shard_map/psum | solution.py:25
  15.1 1.6 slice_bitcast_fusion.1
  16.7 0.0 copy-start.4
  16.8 0.0 copy-start.7
  16.8 2.6 add_convert_fusion
  19.4 0.0 copy-done.14
  19.4 0.0 copy-done.4
  19.4 0.0 copy-done.7
  19.4 0.0 copy-start.3
  19.4 0.1 convolution_bitcast_fusion.4
  19.5 3.4 psum.65
  23.1 0.0 copy-start.10
  23.1 0.0 copy-start.11
  23.1 2.5 convert_reduce_fusion
  25.6 0.0 copy-done.3
  25.6 0.0 copy-done.10
  25.6 0.0 copy-done.11
  25.6 3.5 psum.67
  29.1 1.1 convolution_multiply_fusion
  30.3 1.2 convolution_multiply_fusion.1
  32.1 16.0 %psum.64 = f32[]{:T(128)} all-reduce(f32[]{:T(128)} %bitcast.5), channel_id=1, replica_groups=mesh['twist'=8,'walker'=16,'mp'=2] {'twist'}, use_global_device_ids=true, to_apply=%region_1.0 | all-reduce | flops 1 | bytes 8 | tf_op jit(solution)/shard_map/psum | solution.py:48
  48.8 0.0 copy-start.18
  48.8 1.4 fusion.16
  50.2 0.0 copy-done.19
  50.2 0.0 copy-done.18
  50.2 1.3 fusion.13
  51.6 0.7 copy-done.20
  52.2 0.3 fusion.18
  52.5 0.8 pad_maximum_fusion.4
  53.4 0.0 reduce-scatter.6.cloned.1.call-update
  53.4 0.0 reduce-scatter.8.cloned.1.call-start
  53.4 0.7 reduce_sum.28
  54.1 40.6 %psum.69 = f32[]{:T(128)} all-reduce(f32[]{:T(128)} %reduce_sum.28), channel_id=1, replica_groups=mesh['twist'=8,'walker'=16,'mp'=2] {'walker'}, use_global_device_ids=true, to_apply=%region_10.11 | all-reduce | flops 1 | bytes 8 | tf_op jit(solution)/shard_map/psum | solution.py:47
  95.4 0.0 copy-start.2
  95.4 0.0 copy-start.5
  95.4 0.0 copy-start.8
  95.5 0.0 copy-start.15
  95.5 0.0 copy-start.21
  95.5 1.8 fusion.5
  97.4 0.5 fusion.7
  97.9 1.3 pad_maximum_fusion.1
  99.2 0.0 reduce-scatter.8.cloned.1.call-update
  99.2 0.0 reduce-scatter.4.cloned.1.call-start
  99.3 2.8 fusion.2
  102.1 1.1 fusion.3
  103.3 3.1 pad_maximum_fusion
  106.4 0.0 reduce-scatter.4.cloned.1.call-update
  106.4 0.0 all-reduce.3.cloned.1.call-start
  106.5 0.0 reduce-scatter.6.cloned.1.call-done
  106.5 10.3 %reduce-scatter.8.cloned.1.call-done = f32[1,896,256]{2,1,0:T(8,128)} async-done(((f32[2,896,256]{2,1,0:T(8,128)}), f32[1,896,256]{2,1,0:T(8,128)}) %reduce-scatter.8.cloned.1.call-update) | async-done | bytes 917520 | tf_op jit(solution)/shard_map/reduce_scatter | solution.py:101
  116.8 23.8 %reduce-scatter.4.cloned.1.call-done = f32[1,896,896]{2,1,0:T(8,128)} async-done(((f32[2,896,896]{2,1,0:T(8,128)}), f32[1,896,896]{2,1,0:T(8,128)}) %reduce-scatter.4.cloned.1.call-update) | async-done | bytes 3211280 | tf_op jit(solution)/shard_map/reduce_scatter | solution.py:99
  140.6 0.0 all-reduce.3.cloned.1.call-update
  140.6 238.2 %all-reduce.3.cloned.1.call-done = (f32[1,896,896]{2,1,0:T(8,128)}, f32[1,256,256]{2,1,0:T(8,128)}, f32[1,896,256]{2,1,0:T(8,128)}) async-done(((f32[1,896,896]{2,1,0:T(8,128)}, f32[1,256,256]{2,1,0:T(8,128)}, f32[1,896,256]{2,1,0:T(8,128)}), (f32[1,896,896]{2,1,0:T(8,128)}, f32[1,256,256]{2,1,0:T(8,128)}, f32[1,896,256]{2,1,0:T(8,128)})) %all-reduce.3.cloned.1.call-update) | async-done | bytes 4390928 | tf_op jit(solution)/shard_map/psum | solution.py:104
  378.8 2.1 fusion.21
  381.0 0.0 copy-done
  381.0 0.0 copy-done.1
  381.0 4.6 %fusion.19 = (f32[]{:T(128)}, f32[256,896]{0,1:T(8,128)}) fusion(f32[1,896,256]{2,1,0:T(8,128)S(1)} %copy-done.1, f32[896,256]{1,0:T(8,128)S(1)} %fusion.21, f32[1,896,896]{2,1,0:T(8,128)S(1)} %copy-done), kind=kOutput, calls=%fused_computation.37 | convolution fusion | flops 2466709504 | bytes 5963780 | tf_op jit(solution)/shard_map/lij,ljk->lik/dot_general | solution.py:106
  385.6 7.8 %psum.71 = f32[]{:T(128)} all-reduce(f32[]{:T(128)} %get-tuple-element.16), channel_id=1, replica_groups=mesh['twist'=8,'walker'=16,'mp'=2] {'mp'}, use_global_device_ids=true, to_apply=%region_14.15 | all-reduce | flops 1 | bytes 8 | tf_op jit(solution)/shard_map/psum | solution.py:107
  394.1 2.2 fusion.20
  396.2 3.8 copy.30
  400.1 0.7 copy.31
  (36 shorter events, 0.3 us)
Async XLA Ops:
  7.2 373.8 %copy-start = (f32[1,896,896]{2,1,0:T(8,128)S(1)}, f32[1,896,896]{2,1,0:T(8,128)}, u32[]{:S(2)}) copy-start(f32[1,896,896]{2,1,0:T(8,128)} %param.14) | copy-start | bytes 9633796
  7.2 99.3 %reduce-scatter.6.cloned.1.call-start = ((), (), s32[]{:S(2)}) async-start(), calls=%async_computation.4 | async-start | bytes 786432 | tf_op jit(solution)/shard_map/reduce_scatter | solution.py:100
  16.7 2.7 copy-start.14
  16.7 2.6 copy-start.4
  16.8 2.6 copy-start.7
  19.4 6.2 %copy-start.3 = (bf16[16,32,256]{2,1,0:T(8,128)(2,1)}, bf16[16,32,256]{2,1,0:T(8,128)(2,1)S(1)}, u32[]{:S(2)}) copy-start(bf16[16,32,256]{2,1,0:T(8,128)(2,1)S(1)} %get-tuple-element.12) | copy-start | bytes 786436
  23.1 2.5 copy-start.10
  23.1 2.5 copy-start.11
  29.1 21.1 %copy-start.19 = (bf16[16,32,256]{2,1,0:T(8,128)(2,1)S(1)}, bf16[16,32,256]{2,1,0:T(8,128)(2,1)}, u32[]{:S(2)}) copy-start(bf16[16,32,256]{2,1,0:T(8,128)(2,1)} %get-tuple-element.15) | copy-start | bytes 786436
  48.8 1.4 copy-start.18
  51.5 0.7 copy-start.20
  52.2 1.2 copy-start.17
  53.4 63.4 %reduce-scatter.8.cloned.1.call-start = ((), (), s32[]{:S(2)}) async-start(), calls=%async_computation.5 | async-start | bytes 2752512 | tf_op jit(solution)/shard_map/reduce_scatter | solution.py:101
  95.4 1.9 copy-start.2
  95.4 1.9 copy-start.5
  95.4 1.9 copy-start.8
  95.5 1.9 copy-start.15
  95.5 1.9 copy-start.21
  99.2 41.4 %reduce-scatter.4.cloned.1.call-start = ((), (), s32[]{:S(2)}) async-start(), calls=%async_computation.3 | async-start | bytes 9633792 | tf_op jit(solution)/shard_map/reduce_scatter | solution.py:99
  99.3 2.8 copy-start.6
  99.3 2.8 copy-start.9
  99.3 2.8 copy-start.16
  106.4 272.4 %all-reduce.3.cloned.1.call-start = ((), (), s32[]{:S(2)}) async-start(), calls=%async_computation.6 | async-start | bytes 8781824 | tf_op jit(solution)/shard_map/psum | solution.py:104
  140.6 238.2 %copy-start.13 = (f32[1,256,256]{2,1,0:T(8,128)S(1)}, f32[1,256,256]{2,1,0:T(8,128)}, u32[]{:S(2)}) copy-start(f32[1,256,256]{2,1,0:T(8,128)} %param.15) | copy-start | bytes 786436
  378.8 2.2 copy-start.1
  396.2 3.8 copy-start.12
Sparse Core Ops, SparseCore 0:
  53.5 16.7 reduce-scatter.5
  99.4 17.4 reduce-scatter.7
  119.4 21.1 reduce-scatter.3
  147.3 231.4 all-reduce.2
where the time goes:
time: 408 us; the launch traced here: 407 us
  waiting for transfers between devices  272 us (67%)
  blocking collectives  77.8 us (19%)
  matrix products  24.7 us (6%)
  between operations  17 us (4%)
  other arithmetic  8.19 us (2%)
  local copies, waits for them, and re-layouts  7.13 us (2%)
    psum x1, waiting for transfers between devices, body(): lax.psum((owned_a, owned_s, owned_g), ('twist', 'walker'))  238 us
    psum x1, blocking collectives, body(): energy_sum = lax.psum(local_energy, 'walker')  40.6 us
    reduce_scatter x1, waiting for transfers between devices, body(): lax.psum_scatter(jnp.stack(blocks_a), 'mp', scatter_dimension=0, tiled=True)  23.8 us
    psum x1, blocking collectives, body(): mult_total = lax.psum(mult_value, 'twist')  16 us
    reduce_scatter x1, waiting for transfers between devices, body(): lax.psum_scatter(jnp.stack(blocks_g), 'mp', scatter_dimension=0, tiled=True)  10.3 us
    psum x2, blocking collectives, body(): spin_sums = lax.psum(local_sums, 'mp')  9.88 us
  transfers between devices with their start and end apart: 4, of which 3 were waited for; matrix products, arithmetic and copies ran while one was open for 3% of the time, Pallas kernels for 0%

commit v1 on v0

v1 whole, which is shorter than its diff:
```python
import functools

import jax
import jax.numpy as jnp
from jax import lax
from jax.experimental import pallas as pl
from jax.experimental.pallas import tpu as pltpu
from jax.sharding import Mesh, PartitionSpec as P

F32, BF16 = jnp.float32, jnp.bfloat16
D, PAIR, DIN = 256, 128, 896
WALK, HALF, ROWS = 16, 512, 1024
B = 128
GROUP = 32
PACKED = 4352
EXTRA = 33 * B
CHUNK = PACKED // GROUP
ENTRIES = 2 * DIN * D
VMEM_LIMIT = 56 * 1024 * 1024


def dot_t(a, b):
    return lax.dot_general(a, b, (((0,), (0,)), ((), ())), preferred_element_type=F32)


def dot_nt(a, b):
    return lax.dot_general(a, b, (((1,), (1,)), ((), ())), preferred_element_type=F32)


def dot(a, b):
    return jnp.dot(a, b, preferred_element_type=F32)


def split(a):
    high = a.astype(BF16)
    return high, (a - high.astype(F32)).astype(BF16)


def per_walker(a):
    n = a.shape[1]
    return jnp.broadcast_to(a[:, None, :], (WALK, HALF // WALK, n)).reshape(HALF, n)


def square_iotas():
    return lax.broadcasted_iota(jnp.int32, (B, B), 0), lax.broadcasted_iota(jnp.int32, (B, B), 1)


def factors_kernel(
    feat, pair, psi, other, weights, energy, mean, scale, mult, out, x_s, s_s, d_s, m_s
):
    mp = lax.axis_index("c")
    own_row = pl.multiple_of(D + D * mp, D)
    oth_row = pl.multiple_of(2 * D - D * mp, D)
    x_s[0, :HALF, :D] = feat[...]
    x_s[0, HALF:, :D] = other[:, :D].astype(BF16)
    for l in range(2):
        x_s[l, :HALF, D:] = pair[l]
        x_s[l, HALF:, D:] = other[:, 2 * D + l * PAIR : 2 * D + (l + 1) * PAIR].astype(BF16)
    group = lax.broadcasted_iota(jnp.int32, (2 * WALK, ROWS), 1) // (HALF // WALK)
    pick = (group == lax.broadcasted_iota(jnp.int32, (2 * WALK, ROWS), 0)).astype(BF16)

    for l in range(2):
        means = (dot(pick, x_s[l, :, :D]) * (1.0 / 32.0)).astype(BF16)
        m_s[l] = means
        z_walk = dot(means[:WALK], weights[l, pl.ds(own_row, D), :]) + dot(
            means[WALK:], weights[l, pl.ds(oth_row, D), :]
        )
        z_wide = per_walker(z_walk)
        for half in range(2):
            rows = slice(half * HALF, (half + 1) * HALF)
            z = dot(x_s[l, rows, :D], weights[l, :D, :]) + dot(
                x_s[l, rows, D:], weights[l, 3 * D :, :]
            )
            t = jnp.tanh(z + z_wide)
            d_s[l, rows, :] = 1.0 - t * t
            if l == 0:
                x_s[1, rows, :D] = (x_s[0, rows, :D].astype(F32) + t).astype(BF16)

    s_s[1, :HALF, :] = (psi[...].astype(F32) * d_s[1, :HALF, :]).astype(BF16)
    s_s[1, HALF:, :] = (other[:, D : 2 * D] * d_s[1, HALF:, :]).astype(BF16)
    q_both = dot(pick, s_s[1])
    q_high, q_low = split(q_both[:WALK] + q_both[WALK:])
    for half in range(2):
        rows = slice(half * HALF, (half + 1) * HALF)
        w_spin = weights[1, pl.ds(own_row if half == 0 else oth_row, D), :]
        spin = (dot_nt(q_high, w_spin) + dot_nt(q_low, w_spin)) * (1.0 / 32.0)
        up = psi[...].astype(F32) if half == 0 else other[:, D : 2 * D]
        u = up + dot_nt(s_s[1, rows, :], weights[1, :D, :]) + per_walker(spin)
        s_s[0, rows, :] = (u * d_s[0, rows, :]).astype(BF16)

    l = mp
    row_scale = scale[0, 0]
    x = x_s[l]
    s = s_s[l]
    centered = energy[...] - mean[0, 0]
    c_wide = jnp.broadcast_to(centered, (WALK, HALF // WALK, D)).reshape(HALF, D)
    c = jnp.concatenate(
        [(c_wide * s[:HALF].astype(F32)).astype(BF16), (c_wide * s[HALF:].astype(F32)).astype(BF16)], 0
    )
    h, p = x[:, :D], x[:, D:]
    row, col = square_iotas()

    def put(slot, value):
        out[slot * B : (slot + 1) * B, :] = value * row_scale

    def put_symmetric(slot, line, full):
        low = full[B:, B:]
        put(slot, jnp.where(col >= row, full[:B, :B], low))
        put(slot + 1, full[:B, B:])
        out[EXTRA + line : EXTRA + line + 1, :] = (
            jnp.sum(jnp.where(col == row, low, 0.0), axis=0, keepdims=True) * row_scale
        )

    out[EXTRA:, :] = jnp.zeros((PACKED - EXTRA, B), F32)
    put_symmetric(0, 0, dot_t(h, h))
    hp = dot_t(h, p)
    put(11, hp[:B])
    put(12, hp[B:])
    put(10, dot_t(p, p))
    hc = dot_t(h, c)
    pc = dot_t(p, c)
    for j in range(2):
        cols = slice(j * B, (j + 1) * B)
        put(19 + j, hc[:B, cols])
        put(21 + j, hc[B:, cols])
        put(31 + j, pc[:, cols])
    put_symmetric(17, 3, dot_t(s, s))

    means = m_s[l]
    up_first = mp == 0
    up = jnp.where(up_first, means[:WALK].astype(F32), means[WALK:].astype(F32)).astype(BF16)
    down = jnp.where(up_first, means[WALK:].astype(F32), means[:WALK].astype(F32)).astype(BF16)
    both = jnp.concatenate([up, down], 1)
    mm = dot_t(both, both) * 64.0
    put_symmetric(2, 1, mm[:D, :D])
    put_symmetric(4, 2, mm[D:, D:])
    for i in range(2):
        for j in range(2):
            put(6 + 2 * i + j, mm[i * B : (i + 1) * B, D + j * B : D + (j + 1) * B])
    totals = dot(pick, jnp.concatenate([p, c], 1))
    t_high, t_low = split(totals[:WALK] + totals[WALK:])
    side = dot_t(jnp.concatenate([both, both], 0), jnp.concatenate([t_high, t_low], 0))
    for i in range(4):
        rows = slice(i * B, (i + 1) * B)
        put(13 + i, side[rows, :B])
        put(23 + 2 * i, side[rows, B : 2 * B])
        put(24 + 2 * i, side[rows, 2 * B :])
    out[EXTRA + 4 : EXTRA + 5, :] = jnp.full((1, B), mult[0, 0], F32)


def finish_kernel(packed, a_inverse, s_inverse, a_out, s_out, natural, curvature):
    row, col = square_iotas()
    inverse = 1.0 / packed[EXTRA + 4 : EXTRA + 5, :]

    def get(slot):
        return packed[slot * B : (slot + 1) * B, :] * inverse

    def symmetric(slot, line):
        tri = get(slot)
        off = get(slot + 1)
        flipped = tri.T
        diag = packed[EXTRA + line : EXTRA + line + 1, :] * inverse
        first = jnp.where(col >= row, tri, flipped)
        second = jnp.where(col < row, tri, flipped)
        second = jnp.where(col == row, jnp.broadcast_to(diag, (B, B)), second)
        return [[first, off], [off.T, second]]

    def place(target, i, j, value):
        target[i * B : (i + 1) * B, j * B : (j + 1) * B] = value

    ss = symmetric(17, 3)
    hh = symmetric(0, 0)
    for i in range(2):
        for j in range(2):
            place(s_out, i, j, ss[i][j])
            place(a_out, i, j, hh[i][j])
    uu = symmetric(2, 1)
    dd = symmetric(4, 2)
    ud = [[get(6 + 2 * i + j) for j in range(2)] for i in range(2)]
    du = [[ud[j][i].T for j in range(2)] for i in range(2)]
    for i in range(2):
        for j in range(2):
            place(a_out, 2 + i, 2 + j, uu[i][j])
            place(a_out, 4 + i, 4 + j, dd[i][j])
            place(a_out, 2 + i, 4 + j, ud[i][j])
            place(a_out, 4 + i, 2 + j, du[i][j])
            place(a_out, i, 2 + j, (uu[i][j] + du[i][j]) * 0.5)
            place(a_out, i, 4 + j, (ud[i][j] + dd[i][j]) * 0.5)
            place(a_out, 2 + i, j, (uu[i][j] + ud[i][j]) * 0.5)
            place(a_out, 4 + i, j, (du[i][j] + dd[i][j]) * 0.5)
    place(a_out, 6, 6, get(10))
    for i in range(6):
        block = get(11 + i)
        place(a_out, i, 6, block)
        place(a_out, 6, i, block.T)

    grad = jnp.concatenate(
        [jnp.concatenate([get(19 + 2 * i), get(20 + 2 * i)], 1) for i in range(7)], 0
    )
    g_high, g_low = split(grad)
    s_high, s_low = split(s_inverse[...])
    half = dot(g_high, s_high) + (dot(g_high, s_low) + dot(g_low, s_high))
    h_high, h_low = split(half)
    total = jnp.zeros((1, D), F32)
    for i in range(7):
        rows = slice(i * B, (i + 1) * B)
        a_high, a_low = split(a_inverse[rows, :])
        part = dot(a_high, h_high) + (dot(a_high, h_low) + dot(a_low, h_high))
        natural[rows, :] = part
        total = total + jnp.sum(part * grad[rows, :], axis=0, keepdims=True)
    curvature[...] = jnp.broadcast_to(jnp.sum(total, axis=1, keepdims=True), (1, B))


def vmem(count):
    return [pl.BlockSpec(memory_space=pltpu.VMEM)] * count


def body(features, psi_grad, pair_means, energies, multiplicity, weights, a_inverse, s_inverse):
    feat = features.reshape(HALF, D)
    psi = psi_grad.reshape(HALF, D)
    pair = pair_means.reshape(2, HALF, PAIR)
    swap = [(0, 1), (1, 0)]
    sent = jnp.concatenate([feat, psi, pair[0], pair[1]], 1).astype(F32)
    other = lax.ppermute(sent, "c", swap)

    total = jnp.broadcast_to(jnp.sum(energies), (1, B))
    for axis in ("x", "zh"):
        total = total + sum(
            lax.ppermute(total, axis, [(i, (i + k) % 4) for i in range(4)]) for k in (1, 2, 3)
        )
    mean = total / 256.0
    energy = jnp.broadcast_to(energies.reshape(WALK, 1, 1), (WALK, 1, D))
    mult = jnp.broadcast_to(multiplicity.astype(F32).reshape(1, 1), (1, B))

    packed = pl.pallas_call(
        factors_kernel,
        out_shape=jax.ShapeDtypeStruct((PACKED, B), F32),
        in_specs=vmem(6) + [pl.BlockSpec(memory_space=pltpu.SMEM)] * 3,
        out_specs=pl.BlockSpec(memory_space=pltpu.VMEM),
        scratch_shapes=[
            pltpu.VMEM((2, ROWS, D + PAIR), BF16),
            pltpu.VMEM((2, ROWS, D), BF16),
            pltpu.VMEM((2, ROWS, D), F32),
            pltpu.VMEM((2, 2 * WALK, D), BF16),
        ],
        compiler_params=pltpu.CompilerParams(vmem_limit_bytes=VMEM_LIMIT),
        name="factors",
    )(feat, pair, psi, other, weights, energy, mean, mult / 16384.0, mult / 16.0)

    ring = ("zl", "y", "x")
    parts = lax.all_to_all(packed, ring, 0, 0, tiled=True)
    mine = jnp.sum(parts.reshape(GROUP, CHUNK, B), axis=0)
    one, two, three = (
        lax.ppermute(mine, "zh", [(i, (i + k) % 4) for i in range(4)]) for k in (1, 2, 3)
    )
    mine = (mine + two) + (one + three)
    copies = jnp.broadcast_to(mine[None], (GROUP, CHUNK, B)).reshape(PACKED, B)
    summed = lax.all_to_all(copies, ring, 0, 0, tiled=True)

    a_sum, s_sum, natural, curvature = pl.pallas_call(
        finish_kernel,
        out_shape=(
            jax.ShapeDtypeStruct((DIN, DIN), F32),
            jax.ShapeDtypeStruct((D, D), F32),
            jax.ShapeDtypeStruct((DIN, D), F32),
            jax.ShapeDtypeStruct((1, B), F32),
        ),
        in_specs=vmem(3),
        out_specs=tuple(vmem(4)),
        compiler_params=pltpu.CompilerParams(vmem_limit_bytes=VMEM_LIMIT),
        name="finish",
    )(summed, a_inverse[0], s_inverse[0])
    curvature = curvature + lax.ppermute(curvature, "c", swap)
    direction = natural * lax.rsqrt(curvature[:, :1] / ENTRIES)
    return a_sum[None], s_sum[None], direction[None]


def solution(mesh):
    fine = Mesh(mesh.devices.reshape(2, 4, 4, 4, 2), ("zl", "y", "zh", "x", "c"))
    twist, walker = ("zl", "y"), ("zh", "x")
    return jax.shard_map(
        body,
        mesh=fine,
        in_specs=(
            P(twist, walker, "c", None),
            P(twist, walker, "c", None),
            P(twist, None, walker, "c", None),
            P(twist, walker),
            P(twist),
            P(),
            P("c", None, None),
            P("c", None, None),
        ),
        out_specs=(P("c", None, None),) * 3,
        check_vma=False,
    )
```

time: 408 us -> 125 us (0.31)
  waiting for transfers between devices: 272 us -> 10.5 us
  starting transfers between devices: 0.16 us -> 25.9 us
  matrix products: 24.7 us -> 0 us
  between operations: 17 us -> 1.44 us
  blocking collectives: 77.8 us -> 63.8 us
  Pallas kernels: 0 us -> 13.7 us
    psum x1 -> x0, waiting for transfers between devices: 238 us -> none  [body(): lax.psum((owned_a, owned_s, owned_g), ('twist', 'walker'))]
    psum x6 -> x0, blocking collectives: 77.8 us -> none  [the longest x1 40.6 us: body(): energy_sum = lax.psum(local_energy, 'walker')]
    all_to_all x0 -> x2, blocking collectives: none -> 63.8 us  [the longest x1 32.5 us: body(): parts = lax.all_to_all(packed, ring, 0, 0, tiled=True)]
    reduce_scatter x3 -> x0, waiting for transfers between devices: 34.1 us -> none  [the longest x1 23.8 us: body(): lax.psum_scatter(jnp.stack(blocks_a), 'mp', scatter_dimension=0, tiled=True)]
    ppermute x0 -> x11, starting transfers between devices: none -> 25.9 us  [the longest x6 11.3 us: body(): lax.ppermute(total, axis, [(i, (i + k) % 4) for i in range(4)])]
    dot_general x15 -> x0, matrix products: 24.7 us -> none  [the longest x2 5.05 us: body(): jnp.einsum('wei,if->wef', wide, weights[layer], preferred_element_type=jn...]
    pallas_call x0 -> x2, Pallas kernels: none -> 13.7 us  [the longest x1 6.99 us: body(): pl.pallas_call(finish_kernel, out_shape=(jax.ShapeDtypeStruct((DIN, DIN),...]
    ppermute x0 -> x11, waiting for transfers between devices: none -> 10.5 us  [the longest x6 5.38 us: body(): lax.ppermute(total, axis, [(i, (i + k) % 4) for i in range(4)])]
  transfers between devices with their start and end apart: 4 -> 11, of which waited for: 3 -> 7; matrix products, arithmetic and copies ran while one was open for 3% -> 2% of each run, Pallas kernels for 0% -> 0%
where the time goes in v1:
time: 125 us
  blocking collectives  63.8 us (51%)
  starting transfers between devices  25.9 us (21%)
  Pallas kernels  13.7 us (11%)
  waiting for transfers between devices  10.5 us (8%)
  other arithmetic  5.88 us (5%)
  local copies, waits for them, and re-layouts  3.57 us (3%)
  between operations  1.44 us (1%)
    all_to_all x1, blocking collectives, body(): parts = lax.all_to_all(packed, ring, 0, 0, tiled=True)  32.5 us
    all_to_all x1, blocking collectives, body(): summed = lax.all_to_all(copies, ring, 0, 0, tiled=True)  31.3 us
    ppermute x6, starting transfers between devices, body(): lax.ppermute(total, axis, [(i, (i + k) % 4) for i in range(4)])  11.3 us
    pallas_call x1, Pallas kernels, body(): pl.pallas_call(finish_kernel, out_shape=(jax.ShapeDtypeStruct((DIN, DIN),...  6.99 us
    pallas_call x1, Pallas kernels, body(): pl.pallas_call(factors_kernel, out_shape=jax.ShapeDtypeStruct((PACKED, B)...  6.7 us
    ppermute x3, starting transfers between devices, body(): lax.ppermute(mine, 'zh', [(i, (i + k) % 4) for i in range(4)])  5.92 us
    ppermute x6, waiting for transfers between devices, body(): lax.ppermute(total, axis, [(i, (i + k) % 4) for i in range(4)])  5.38 us
    ppermute x1, starting transfers between devices, body(): curvature = curvature + lax.ppermute(curvature, 'c', swap)  5.35 us
  transfers between devices with their start and end apart: 11, of which 7 were waited for; matrix products, arithmetic and copies ran while one was open for 2% of the time, Pallas kernels for 0%

profile of v1, /device:TPU:1, one launch (start us, length us, event | category | flops | bytes accessed | tf_op | source)
XLA Modules:
  0.0 124.7 jit_solution(3093854490929773621)
XLA Ops:
  0.6 0.0 copy-start.1
  0.6 1.0 fusion
  1.6 1.1 maximum_convert_fusion
  2.8 3.3 %collective-permute-start = (f32[512,768]{1,0:T(8,128)S(1)}, f32[512,768]{1,0:T(8,128)S(1)}, u32[]{:S(2)}, u32[]{:S(2)}) collective-permute-start(f32[512,768]{1,0:T(8,128)S(1)} %maximum_convert_fusion), channel_id=1, source_target_pairs={{0,1},{1,0},{2,3},{3,2},{4,5},{5,4},{6,7},{7,6},{8,9},{9,8},{10,11... | collective-permute-start | bytes 4718600 | tf_op jit(solution)/shard_map/ppermute | solution.py:224
  6.1 0.0 copy-done.1
  6.1 0.6 reduce_sum.18
  6.7 0.6 broadcast_in_dim.34
  7.4 0.8 collective-permute-start.3
  8.2 0.5 collective-permute-start.2
  8.7 0.6 collective-permute-start.1
  9.3 0.5 collective-permute-done.3
  9.8 2.2 %collective-permute-done.2 = f32[1,128]{1,0:T(1,128)S(1)} collective-permute-done((f32[1,128]{1,0:T(1,128)S(1)}, f32[1,128]{1,0:T(1,128)S(1)}, u32[]{:S(2)}, u32[]{:S(2)}) %collective-permute-start.2) | collective-permute-done | bytes 544 | tf_op jit(solution)/shard_map/ppermute | solution.py:229
  12.1 0.2 collective-permute-done.1
  12.3 0.7 add_add_fusion.1
  13.0 6.1 %collective-permute-start.6 = (f32[1,128]{1,0:T(1,128)S(1)}, f32[1,128]{1,0:T(1,128)S(1)}, u32[]{:S(2)}, u32[]{:S(2)}) collective-permute-start(f32[1,128]{1,0:T(1,128)S(1)} %add_add_fusion.1), channel_id=1, source_target_pairs={{0,24},{8,0},{16,8},{24,16},{1,25},{9,1},{17,9},{25,17},{2,26},{10... | collective-permute-start | bytes 1544 | tf_op jit(solution)/shard_map/ppermute | solution.py:229
  19.1 1.0 collective-permute-start.5
  20.1 2.3 %collective-permute-start.4 = (f32[1,128]{1,0:T(1,128)S(1)}, f32[1,128]{1,0:T(1,128)S(1)}, u32[]{:S(2)}, u32[]{:S(2)}) collective-permute-start(f32[1,128]{1,0:T(1,128)S(1)} %add_add_fusion.1), channel_id=1, source_target_pairs={{0,8},{8,16},{16,24},{24,0},{1,9},{9,17},{17,25},{25,1},{2,10},{10... | collective-permute-start | bytes 1544 | tf_op jit(solution)/shard_map/ppermute | solution.py:229
  23.0 0.0 collective-permute-done.6
  23.0 2.4 %collective-permute-done.5 = f32[1,128]{1,0:T(1,128)S(1)} collective-permute-done((f32[1,128]{1,0:T(1,128)S(1)}, f32[1,128]{1,0:T(1,128)S(1)}, u32[]{:S(2)}, u32[]{:S(2)}) %collective-permute-start.5) | collective-permute-done | bytes 544 | tf_op jit(solution)/shard_map/ppermute | solution.py:229
  25.4 0.0 collective-permute-done.4
  25.4 0.5 add_multiply_fusion.mean
  25.9 0.0 collective-permute-done.other
  25.9 0.0 copy-start
  25.9 0.6 broadcast_in_dim.35.scale
  26.5 0.5 broadcast_in_dim.36.mult
  27.0 0.7 broadcast_in_dim.33.energy
  27.7 0.0 copy-done
  27.7 6.7 %factors.1 = f32[4352,128]{1,0:T(8,128)} custom-call(bf16[512,256]{1,0:T(8,128)(2,1)} %bitcast.22, bf16[2,512,128]{2,1,0:T(8,128)(2,1)} %bitcast.25, bf16[512,256]{1,0:T(8,128)(2,1)} %bitcast.24, f32[512,768]{1,0:T(8,128)} %copy-done, bf16[2,896,256]{2,1,0:T(8,128)(2,1)} %weights.1, f32[16,1,256]{2,1,0:T(1,128)} %broadcast_in_dim.33.energy, ...), custom_call_target="tpu_custom_call" | custom-call | tf_op jit(solution)/shard_map/factors/pallas_call | solution.py:235
  34.4 32.5 %all_to_all.17 = f32[32,136,128]{2,1,0:T(8,128)S(1)} all-to-all(f32[32,136,128]{2,1,0:T(8,128)} %bitcast.18), channel_id=1, replica_groups=mesh['zl'=2,'y'=4,'zh'=4,'x'=4,'c'=2] {'zl','y','x'}, dimensions={0} | all-to-all | bytes 4456448 | tf_op jit(solution)/shard_map/all_to_all | solution.py:251
  66.9 0.1 reduce_sum.19
  67.0 1.2 %collective-permute-start.9 = (f32[136,128]{1,0:T(8,128)S(1)}, f32[136,128]{1,0:T(8,128)S(1)}, u32[]{:S(2)}, u32[]{:S(2)}) collective-permute-start(f32[136,128]{1,0:T(8,128)S(1)} %reduce_sum.19), channel_id=1, source_target_pairs={{0,24},{8,0},{16,8},{24,16},{1,25},{9,1},{17,9},{25,17},{2,26},{10... | collective-permute-start | bytes 208904 | tf_op jit(solution)/shard_map/ppermute | solution.py:254
  68.2 1.2 collective-permute-start.8
  69.4 3.5 %collective-permute-start.7 = (f32[136,128]{1,0:T(8,128)S(1)}, f32[136,128]{1,0:T(8,128)S(1)}, u32[]{:S(2)}, u32[]{:S(2)}) collective-permute-start(f32[136,128]{1,0:T(8,128)S(1)} %reduce_sum.19), channel_id=1, source_target_pairs={{0,16},{8,24},{16,0},{24,8},{1,17},{9,25},{17,1},{25,9},{2,18},{10... | collective-permute-start | bytes 208904 | tf_op jit(solution)/shard_map/ppermute | solution.py:254
  72.9 0.0 collective-permute-done.9
  72.9 0.6 collective-permute-done.8
  73.6 3.6 %collective-permute-done.7 = f32[136,128]{1,0:T(8,128)S(1)} collective-permute-done((f32[136,128]{1,0:T(8,128)S(1)}, f32[136,128]{1,0:T(8,128)S(1)}, u32[]{:S(2)}, u32[]{:S(2)}) %collective-permute-start.7) | collective-permute-done | bytes 69664 | tf_op jit(solution)/shard_map/ppermute | solution.py:254
  77.1 0.1 broadcast_in_dim.37
  77.3 31.3 %all_to_all.18 = f32[32,136,128]{2,1,0:T(8,128)} all-to-all(f32[32,136,128]{2,1,0:T(8,128)S(1)} %broadcast_in_dim.37), channel_id=1, replica_groups=mesh['zl'=2,'y'=4,'zh'=4,'x'=4,'c'=2] {'zl','y','x'}, dimensions={0} | all-to-all | bytes 4456448 | tf_op jit(solution)/shard_map/all_to_all | solution.py:258
  108.6 7.0 %finish.1 = (f32[896,896]{1,0:T(8,128)}, f32[256,256]{1,0:T(8,128)}, f32[896,256]{1,0:T(8,128)}, f32[1,128]{1,0:T(1,128)}) custom-call(f32[4352,128]{1,0:T(8,128)} %bitcast.19, f32[896,896]{1,0:T(8,128)} %bitcast.20, f32[256,256]{1,0:T(8,128)} %bitcast.28), custom_call_target="tpu_custom_call" | custom-call | tf_op jit(solution)/shard_map/finish/pallas_call | solution.py:260
  115.6 5.4 %collective-permute-start.10 = (f32[1,128]{1,0:T(1,128)}, f32[1,128]{1,0:T(1,128)S(1)}, u32[]{:S(2)}, u32[]{:S(2)}) collective-permute-start(f32[1,128]{1,0:T(1,128)} %get-tuple-element.10), channel_id=1, source_target_pairs={{0,1},{1,0},{2,3},{3,2},{4,5},{5,4},{6,7},{7,6},{8,9},{9,8},{10,11... | collective-permute-start | bytes 1544 | tf_op jit(solution)/shard_map/ppermute | solution.py:273
  120.9 0.9 collective-permute-done.10
  121.8 0.7 add.39
  122.6 2.2 %multiply_bitcast_fusion = f32[1,896,256]{2,1,0:T(8,128)} fusion(f32[896,256]{1,0:T(8,128)} %get-tuple-element.9, f32[]{:T(128)} %bitcast.14), kind=kLoop, calls=%fused_computation | loop fusion | flops 229376 | bytes 1835012 | tf_op jit(solution)/shard_map/broadcast_in_dim | solution.py:275
  (1 shorter events, 0.0 us)
Async XLA Ops:
  0.6 5.5 %copy-start.1 = (f32[1,16]{1,0:T(1,128)S(1)}, f32[1,16]{1,0:T(1,128)}, u32[]{:S(2)}) copy-start(f32[1,16]{1,0:T(1,128)} %param.11) | copy-start | bytes 196
  2.8 23.1 %collective-permute-start = (f32[512,768]{1,0:T(8,128)S(1)}, f32[512,768]{1,0:T(8,128)S(1)}, u32[]{:S(2)}, u32[]{:S(2)}) collective-permute-start(f32[512,768]{1,0:T(8,128)S(1)} %maximum_convert_fusion), channel_id=1, source_target_pairs={{0,1},{1,0},{2,3},{3,2},{4,5},{5,4},{6,7},{7,6},{8,9},{9,8},{10,11... | collective-permute-start | bytes 4718600 | tf_op jit(solution)/shard_map/ppermute | solution.py:224
  7.4 2.5 %collective-permute-start.3 = (f32[1,128]{1,0:T(1,128)S(1)}, f32[1,128]{1,0:T(1,128)S(1)}, u32[]{:S(2)}, u32[]{:S(2)}) collective-permute-start(f32[1,128]{1,0:T(1,128)S(1)} %broadcast_in_dim.34), channel_id=1, source_target_pairs={{0,6},{2,0},{4,2},{6,4},{1,7},{3,1},{5,3},{7,5},{8,14},{10,8},{12,... | collective-permute-start | bytes 1544 | tf_op jit(solution)/shard_map/ppermute | solution.py:229
  8.2 3.9 %collective-permute-start.2 = (f32[1,128]{1,0:T(1,128)S(1)}, f32[1,128]{1,0:T(1,128)S(1)}, u32[]{:S(2)}, u32[]{:S(2)}) collective-permute-start(f32[1,128]{1,0:T(1,128)S(1)} %broadcast_in_dim.34), channel_id=1, source_target_pairs={{0,4},{2,6},{4,0},{6,2},{1,5},{3,7},{5,1},{7,3},{8,12},{10,14},{12... | collective-permute-start | bytes 1544 | tf_op jit(solution)/shard_map/ppermute | solution.py:229
  8.7 3.6 %collective-permute-start.1 = (f32[1,128]{1,0:T(1,128)S(1)}, f32[1,128]{1,0:T(1,128)S(1)}, u32[]{:S(2)}, u32[]{:S(2)}) collective-permute-start(f32[1,128]{1,0:T(1,128)S(1)} %broadcast_in_dim.34), channel_id=1, source_target_pairs={{0,2},{2,4},{4,6},{6,0},{1,3},{3,5},{5,7},{7,1},{8,10},{10,12},{12... | collective-permute-start | bytes 1544 | tf_op jit(solution)/shard_map/ppermute | solution.py:229
  13.0 10.0 %collective-permute-start.6 = (f32[1,128]{1,0:T(1,128)S(1)}, f32[1,128]{1,0:T(1,128)S(1)}, u32[]{:S(2)}, u32[]{:S(2)}) collective-permute-start(f32[1,128]{1,0:T(1,128)S(1)} %add_add_fusion.1), channel_id=1, source_target_pairs={{0,24},{8,0},{16,8},{24,16},{1,25},{9,1},{17,9},{25,17},{2,26},{10... | collective-permute-start | bytes 1544 | tf_op jit(solution)/shard_map/ppermute | solution.py:229
  19.1 6.3 %collective-permute-start.5 = (f32[1,128]{1,0:T(1,128)S(1)}, f32[1,128]{1,0:T(1,128)S(1)}, u32[]{:S(2)}, u32[]{:S(2)}) collective-permute-start(f32[1,128]{1,0:T(1,128)S(1)} %add_add_fusion.1), channel_id=1, source_target_pairs={{0,16},{8,24},{16,0},{24,8},{1,17},{9,25},{17,1},{25,9},{2,18},{10... | collective-permute-start | bytes 1544 | tf_op jit(solution)/shard_map/ppermute | solution.py:229
  20.1 5.3 %collective-permute-start.4 = (f32[1,128]{1,0:T(1,128)S(1)}, f32[1,128]{1,0:T(1,128)S(1)}, u32[]{:S(2)}, u32[]{:S(2)}) collective-permute-start(f32[1,128]{1,0:T(1,128)S(1)} %add_add_fusion.1), channel_id=1, source_target_pairs={{0,8},{8,16},{16,24},{24,0},{1,9},{9,17},{17,25},{25,1},{2,10},{10... | collective-permute-start | bytes 1544 | tf_op jit(solution)/shard_map/ppermute | solution.py:229
  25.9 1.8 %copy-start = (f32[512,768]{1,0:T(8,128)}, f32[512,768]{1,0:T(8,128)S(1)}, u32[]{:S(2)}) copy-start(f32[512,768]{1,0:T(8,128)S(1)} %collective-permute-done.other) | copy-start | bytes 4718596
  67.0 5.9 %collective-permute-start.9 = (f32[136,128]{1,0:T(8,128)S(1)}, f32[136,128]{1,0:T(8,128)S(1)}, u32[]{:S(2)}, u32[]{:S(2)}) collective-permute-start(f32[136,128]{1,0:T(8,128)S(1)} %reduce_sum.19), channel_id=1, source_target_pairs={{0,24},{8,0},{16,8},{24,16},{1,25},{9,1},{17,9},{25,17},{2,26},{10... | collective-permute-start | bytes 208904 | tf_op jit(solution)/shard_map/ppermute | solution.py:254
  68.2 5.3 %collective-permute-start.8 = (f32[136,128]{1,0:T(8,128)S(1)}, f32[136,128]{1,0:T(8,128)S(1)}, u32[]{:S(2)}, u32[]{:S(2)}) collective-permute-start(f32[136,128]{1,0:T(8,128)S(1)} %reduce_sum.19), channel_id=1, source_target_pairs={{0,8},{8,16},{16,24},{24,0},{1,9},{9,17},{17,25},{25,1},{2,10},{10... | collective-permute-start | bytes 208904 | tf_op jit(solution)/shard_map/ppermute | solution.py:254
  69.4 7.7 %collective-permute-start.7 = (f32[136,128]{1,0:T(8,128)S(1)}, f32[136,128]{1,0:T(8,128)S(1)}, u32[]{:S(2)}, u32[]{:S(2)}) collective-permute-start(f32[136,128]{1,0:T(8,128)S(1)} %reduce_sum.19), channel_id=1, source_target_pairs={{0,16},{8,24},{16,0},{24,8},{1,17},{9,25},{17,1},{25,9},{2,18},{10... | collective-permute-start | bytes 208904 | tf_op jit(solution)/shard_map/ppermute | solution.py:254
  115.6 6.2 %collective-permute-start.10 = (f32[1,128]{1,0:T(1,128)}, f32[1,128]{1,0:T(1,128)S(1)}, u32[]{:S(2)}, u32[]{:S(2)}) collective-permute-start(f32[1,128]{1,0:T(1,128)} %get-tuple-element.10), channel_id=1, source_target_pairs={{0,1},{1,0},{2,3},{3,2},{4,5},{5,4},{6,7},{7,6},{8,9},{9,8},{10,11... | collective-permute-start | bytes 1544 | tf_op jit(solution)/shard_map/ppermute | solution.py:273

commit v2 on v1

--- a/solution.py
+++ b/solution.py
@@ -1,5 +1,3 @@
-import functools
-
 import jax
 import jax.numpy as jnp
 from jax import lax
@@ -16,7 +14,6 @@
 EXTRA = 33 * B
 CHUNK = PACKED // GROUP
 ENTRIES = 2 * DIN * D
-VMEM_LIMIT = 56 * 1024 * 1024
 
 
 def dot_t(a, b):
@@ -45,20 +42,21 @@
     return lax.broadcasted_iota(jnp.int32, (B, B), 0), lax.broadcasted_iota(jnp.int32, (B, B), 1)
 
 
-def factors_kernel(
-    feat, pair, psi, other, weights, energy, mean, scale, mult, out, x_s, s_s, d_s, m_s
-):
+def walker_table():
+    group = lax.broadcasted_iota(jnp.int32, (2 * WALK, ROWS), 1) // (HALF // WALK)
+    return (group == lax.broadcasted_iota(jnp.int32, (2 * WALK, ROWS), 0)).astype(BF16)
+
+
+def forward_kernel(feat, pair, oth_feat, oth_pair, weights, x_s, d_s, m_s):
     mp = lax.axis_index("c")
     own_row = pl.multiple_of(D + D * mp, D)
     oth_row = pl.multiple_of(2 * D - D * mp, D)
     x_s[0, :HALF, :D] = feat[...]
-    x_s[0, HALF:, :D] = other[:, :D].astype(BF16)
+    x_s[0, HALF:, :D] = oth_feat[...].astype(BF16)
     for l in range(2):
         x_s[l, :HALF, D:] = pair[l]
-        x_s[l, HALF:, D:] = other[:, 2 * D + l * PAIR : 2 * D + (l + 1) * PAIR].astype(BF16)
-    group = lax.broadcasted_iota(jnp.int32, (2 * WALK, ROWS), 1) // (HALF // WALK)
-    pick = (group == lax.broadcasted_iota(jnp.int32, (2 * WALK, ROWS), 0)).astype(BF16)
-
+        x_s[l, HALF:, D:] = oth_pair[l].astype(BF16)
+    pick = walker_table()
     for l in range(2):
         means = (dot(pick, x_s[l, :, :D]) * (1.0 / 32.0)).astype(BF16)
         m_s[l] = means
@@ -76,27 +74,40 @@
             if l == 0:
                 x_s[1, rows, :D] = (x_s[0, rows, :D].astype(F32) + t).astype(BF16)
 
+
+def factors_kernel(
+    x_s, d_s, m_s, psi, oth_psi, weights, sum_0, sum_1, sum_2, sum_3, energy, multiplicity, out, s_s, c_s
+):
+    mp = lax.axis_index("c")
+    own_row = pl.multiple_of(D + D * mp, D)
+    oth_row = pl.multiple_of(2 * D - D * mp, D)
+    pick = walker_table()
     s_s[1, :HALF, :] = (psi[...].astype(F32) * d_s[1, :HALF, :]).astype(BF16)
-    s_s[1, HALF:, :] = (other[:, D : 2 * D] * d_s[1, HALF:, :]).astype(BF16)
+    s_s[1, HALF:, :] = (oth_psi[...] * d_s[1, HALF:, :]).astype(BF16)
     q_both = dot(pick, s_s[1])
     q_high, q_low = split(q_both[:WALK] + q_both[WALK:])
     for half in range(2):
         rows = slice(half * HALF, (half + 1) * HALF)
         w_spin = weights[1, pl.ds(own_row if half == 0 else oth_row, D), :]
         spin = (dot_nt(q_high, w_spin) + dot_nt(q_low, w_spin)) * (1.0 / 32.0)
-        up = psi[...].astype(F32) if half == 0 else other[:, D : 2 * D]
+        up = psi[...].astype(F32) if half == 0 else oth_psi[...]
         u = up + dot_nt(s_s[1, rows, :], weights[1, :D, :]) + per_walker(spin)
         s_s[0, rows, :] = (u * d_s[0, rows, :]).astype(BF16)
 
     l = mp
-    row_scale = scale[0, 0]
+    mult = multiplicity[0].astype(F32)
+    row_scale = mult * (1.0 / 16384.0)
     x = x_s[l]
     s = s_s[l]
-    centered = energy[...] - mean[0, 0]
-    c_wide = jnp.broadcast_to(centered, (WALK, HALF // WALK, D)).reshape(HALF, D)
-    c = jnp.concatenate(
-        [(c_wide * s[:HALF].astype(F32)).astype(BF16), (c_wide * s[HALF:].astype(F32)).astype(BF16)], 0
-    )
+    mean = jnp.sum((sum_0[...] + sum_2[...]) + (sum_1[...] + sum_3[...]), axis=1, keepdims=True)
+    mean = mean * (1.0 / 256.0)
+    step = HALF // WALK
+    for w in range(WALK):
+        centered = energy[0, w] - mean
+        for first in (w * step, HALF + w * step):
+            rows = slice(first, first + step)
+            c_s[rows, :] = (centered * s_s[l, rows, :].astype(F32)).astype(BF16)
+    c = c_s[...]
     h, p = x[:, :D], x[:, D:]
     row, col = square_iotas()
 
@@ -145,10 +156,10 @@
         put(13 + i, side[rows, :B])
         put(23 + 2 * i, side[rows, B : 2 * B])
         put(24 + 2 * i, side[rows, 2 * B :])
-    out[EXTRA + 4 : EXTRA + 5, :] = jnp.full((1, B), mult[0, 0], F32)
-
-
-def finish_kernel(packed, a_inverse, s_inverse, a_out, s_out, natural, curvature):
+    out[EXTRA + 4 : EXTRA + 5, :] = jnp.full((1, B), mult * (1.0 / 16.0), F32)
+
+
+def unpack_kernel(packed, a_out, s_out):
     row, col = square_iotas()
     inverse = 1.0 / packed[EXTRA + 4 : EXTRA + 5, :]
 
@@ -194,6 +205,11 @@
         place(a_out, i, 6, block)
         place(a_out, 6, i, block.T)
 
+
+def natural_kernel(packed, a_inverse, s_inverse, natural, curvature):
+    def get(slot):
+        return packed[slot * B : (slot + 1) * B, :]
+
     grad = jnp.concatenate(
         [jnp.concatenate([get(19 + 2 * i), get(20 + 2 * i)], 1) for i in range(7)], 0
     )
@@ -211,8 +227,25 @@
     curvature[...] = jnp.broadcast_to(jnp.sum(total, axis=1, keepdims=True), (1, B))
 
 
-def vmem(count):
-    return [pl.BlockSpec(memory_space=pltpu.VMEM)] * count
+def scale_kernel(natural, curvature, other, direction):
+    total = curvature[:, :1] + other[:, :1]
+    direction[...] = natural[...] * lax.rsqrt(total * (1.0 / ENTRIES))
+
+
+def call(kernel, out_shapes, in_spaces, limit_mib, name, scratch=(), flops=0, moved=0):
+    return pl.pallas_call(
+        kernel,
+        out_shape=tuple(jax.ShapeDtypeStruct(shape, dtype) for shape, dtype in out_shapes),
+        in_specs=[pl.BlockSpec(memory_space=space) for space in in_spaces],
+        out_specs=tuple(pl.BlockSpec(memory_space=pltpu.VMEM) for _ in out_shapes),
+        scratch_shapes=scratch,
+        compiler_params=pltpu.CompilerParams(vmem_limit_bytes=limit_mib * 1024 * 1024),
+        cost_estimate=pl.CostEstimate(flops=flops, bytes_accessed=moved, transcendentals=0),
+        name=name,
+    )
+
+
+V, S = pltpu.VMEM, pltpu.SMEM
 
 
 def body(features, psi_grad, pair_means, energies, multiplicity, weights, a_inverse, s_inverse):
@@ -220,58 +253,67 @@
     psi = psi_grad.reshape(HALF, D)
     pair = pair_means.reshape(2, HALF, PAIR)
     swap = [(0, 1), (1, 0)]
-    sent = jnp.concatenate([feat, psi, pair[0], pair[1]], 1).astype(F32)
-    other = lax.ppermute(sent, "c", swap)
-
-    total = jnp.broadcast_to(jnp.sum(energies), (1, B))
-    for axis in ("x", "zh"):
-        total = total + sum(
-            lax.ppermute(total, axis, [(i, (i + k) % 4) for i in range(4)]) for k in (1, 2, 3)
-        )
-    mean = total / 256.0
-    energy = jnp.broadcast_to(energies.reshape(WALK, 1, 1), (WALK, 1, D))
-    mult = jnp.broadcast_to(multiplicity.astype(F32).reshape(1, 1), (1, B))
-
-    packed = pl.pallas_call(
+
+    def turned(value, axis):
+        return [lax.ppermute(value, axis, [(i, (i + k) % 4) for i in range(4)]) for k in (1, 2, 3)]
+
+    one, two, three = turned(energies, "x")
+    row_sum = (energies + two) + (one + three)
+    oth_feat = lax.ppermute(feat.astype(F32), "c", swap)
+    oth_pair = lax.ppermute(pair.astype(F32), "c", swap)
+    oth_psi = lax.ppermute(psi.astype(F32), "c", swap)
+    one, two, three = turned(row_sum, "zh")
+
+    x_s, d_s, m_s = call(
+        forward_kernel,
+        [((2, ROWS, D + PAIR), BF16), ((2, ROWS, D), F32), ((2, 2 * WALK, D), BF16)],
+        [V] * 5,
+        16,
+        "forward",
+        flops=1_000_000_000,
+        moved=6_000_000,
+    )(feat, pair, oth_feat, oth_pair, weights)
+    (packed,) = call(
         factors_kernel,
-        out_shape=jax.ShapeDtypeStruct((PACKED, B), F32),
-        in_specs=vmem(6) + [pl.BlockSpec(memory_space=pltpu.SMEM)] * 3,
-        out_specs=pl.BlockSpec(memory_space=pltpu.VMEM),
-        scratch_shapes=[
-            pltpu.VMEM((2, ROWS, D + PAIR), BF16),
-            pltpu.VMEM((2, ROWS, D), BF16),
-            pltpu.VMEM((2, ROWS, D), F32),
-            pltpu.VMEM((2, 2 * WALK, D), BF16),
-        ],
-        compiler_params=pltpu.CompilerParams(vmem_limit_bytes=VMEM_LIMIT),
-        name="factors",
-    )(feat, pair, psi, other, weights, energy, mean, mult / 16384.0, mult / 16.0)
+        [((PACKED, B), F32)],
+        [V] * 10 + [S] * 2,
+        20,
+        "factors",
+        scratch=[pltpu.VMEM((2, ROWS, D), BF16), pltpu.VMEM((ROWS, D), BF16)],
+        flops=1_500_000_000,
+        moved=8_000_000,
+    )(x_s, d_s, m_s, psi, oth_psi, weights, row_sum, one, two, three, energies, multiplicity)
 
     ring = ("zl", "y", "x")
     parts = lax.all_to_all(packed, ring, 0, 0, tiled=True)
     mine = jnp.sum(parts.reshape(GROUP, CHUNK, B), axis=0)
-    one, two, three = (
-        lax.ppermute(mine, "zh", [(i, (i + k) % 4) for i in range(4)]) for k in (1, 2, 3)
-    )
+    one, two, three = turned(mine, "zh")
     mine = (mine + two) + (one + three)
     copies = jnp.broadcast_to(mine[None], (GROUP, CHUNK, B)).reshape(PACKED, B)
     summed = lax.all_to_all(copies, ring, 0, 0, tiled=True)
 
-    a_sum, s_sum, natural, curvature = pl.pallas_call(
-        finish_kernel,
-        out_shape=(
-            jax.ShapeDtypeStruct((DIN, DIN), F32),
-            jax.ShapeDtypeStruct((D, D), F32),
-            jax.ShapeDtypeStruct((DIN, D), F32),
-            jax.ShapeDtypeStruct((1, B), F32),
-        ),
-        in_specs=vmem(3),
-        out_specs=tuple(vmem(4)),
-        compiler_params=pltpu.CompilerParams(vmem_limit_bytes=VMEM_LIMIT),
-        name="finish",
+    natural, curvature = call(
+        natural_kernel,
+        [((DIN, D), F32), ((1, B), F32)],
+        [V] * 3,
+        18,
+        "natural",
+        flops=1_500_000_000,
+        moved=5_000_000,
     )(summed, a_inverse[0], s_inverse[0])
-    curvature = curvature + lax.ppermute(curvature, "c", swap)
-    direction = natural * lax.rsqrt(curvature[:, :1] / ENTRIES)
+    other = lax.ppermute(curvature, "c", swap)
+    a_sum, s_sum = call(
+        unpack_kernel,
+        [((DIN, DIN), F32), ((D, D), F32)],
+        [V],
+        14,
+        "unpack",
+        flops=10_000_000,
+        moved=6_000_000,
+    )(summed)
+    (direction,) = call(
+        scale_kernel, [((DIN, D), F32)], [V] * 3, 6, "scale", flops=1_000_000, moved=2_000_000
+    )(natural, curvature, other)
     return a_sum[None], s_sum[None], direction[None]
 
 

time: 125 us -> 114 us (0.912)
  Pallas kernels: 13.7 us -> 9.48 us
  local copies, waits for them, and re-layouts: 3.57 us -> 0.18 us
  other arithmetic: 5.88 us -> 3.2 us
    pallas_call x2 -> x5, Pallas kernels: 13.7 us -> 9.48 us  [the longest x1 2.51 us: body(): call(factors_kernel, [((PACKED, B), F32)], [V] * 10 + [S] * 2, 20, 'facto...]
    broadcast_in_dim x4 -> x0, local copies, waits for them, and re-layouts: 2.42 us -> none  [the longest x2 1.09 us: body(): mult = jnp.broadcast_to(multiplicity.astype(F32).reshape(1, 1), (1, B))]
    broadcast_in_dim x1 -> x0, other arithmetic: 2.17 us -> none  [body(): return (a_sum[None], s_sum[None], direction[None])]
    convert_element_type x1 -> x3, other arithmetic: 1.14 us -> 3.06 us  [the longest x1 1.09 us: body(): oth_feat = lax.ppermute(feat.astype(F32), 'c', swap)]
    add x2 -> x1, other arithmetic: 1.33 us -> 0.01 us  [body(): row_sum = energies + two + (one + three)]
    ppermute x11 -> x13, waiting for transfers between devices: 10.5 us -> 9.39 us  [the longest x9 9.38 us: turned(): lax.ppermute(value, axis, [(i, (i + k) % 4) for i in range(4)])]
    ppermute x11 -> x13, starting transfers between devices: 25.9 us -> 25.9 us  [the longest x9 16.2 us: turned(): lax.ppermute(value, axis, [(i, (i + k) % 4) for i in range(4)])]
  transfers between devices with their start and end apart: 11 -> 13, of which waited for: 7 -> 6; matrix products, arithmetic and copies ran while one was open for 2% -> 2% of each run, Pallas kernels for 0% -> 3%
where the time goes in v2:
time: 114 us
  blocking collectives  64.2 us (56%)
  starting transfers between devices  25.9 us (23%)
  Pallas kernels  9.48 us (8%)
  waiting for transfers between devices  9.39 us (8%)
  other arithmetic  3.2 us (3%)
  between operations  1.41 us (1%)
    all_to_all x1, blocking collectives, body(): parts = lax.all_to_all(packed, ring, 0, 0, tiled=True)  33.5 us
    all_to_all x1, blocking collectives, body(): summed = lax.all_to_all(copies, ring, 0, 0, tiled=True)  30.6 us
    ppermute x9, starting transfers between devices, turned(): lax.ppermute(value, axis, [(i, (i + k) % 4) for i in range(4)])  16.2 us
    ppermute x9, waiting for transfers between devices, turned(): lax.ppermute(value, axis, [(i, (i + k) % 4) for i in range(4)])  9.38 us
    ppermute x1, starting transfers between devices, body(): other = lax.ppermute(curvature, 'c', swap)  5.66 us
    ppermute x1, starting transfers between devices, body(): oth_feat = lax.ppermute(feat.astype(F32), 'c', swap)  3.33 us
    pallas_call x1, Pallas kernels, body(): call(factors_kernel, [((PACKED, B), F32)], [V] * 10 + [S] * 2, 20, 'facto...  2.51 us
    pallas_call x1, Pallas kernels, body(): call(natural_kernel, [((DIN, D), F32), ((1, B), F32)], [V] * 3, 18, 'natu...  2.47 us
  transfers between devices with their start and end apart: 13, of which 6 were waited for; matrix products, arithmetic and copies ran while one was open for 2% of the time, Pallas kernels for 3%

profile of v2, /device:TPU:1, one launch (start us, length us, event | category | flops | bytes accessed | tf_op | source)
XLA Modules:
  0.0 113.8 jit_solution(770109835861943246)
XLA Ops:
  0.6 0.0 copy-start.3
  0.6 0.0 copy-start.4
  0.7 0.0 copy-start.6
  0.7 0.0 copy-start.2
  0.7 1.1 bitcast_convert_fusion.1
  1.8 3.3 %collective-permute-start = (f32[512,256]{1,0:T(8,128)S(1)}, f32[512,256]{1,0:T(8,128)S(1)}, u32[]{:S(2)}, u32[]{:S(2)}) collective-permute-start(f32[512,256]{1,0:T(8,128)S(1)} %bitcast_convert_fusion.1), channel_id=1, source_target_pairs={{0,1},{1,0},{2,3},{3,2},{4,5},{5,4},{6,7},{7,6},{8,9},{9,8},{10,11... | collective-permute-start | bytes 1572872 | tf_op jit(solution)/shard_map/ppermute | solution.py:262
  5.1 1.0 convert_element_type.10
  6.1 0.0 copy-start.1
  6.1 0.1 collective-permute-start.1
  6.2 1.0 bitcast_convert_fusion
  7.2 0.6 collective-permute-start.2
  7.8 0.0 copy-done.6
  7.8 0.0 collective-permute-start.4
  7.8 1.9 %collective-permute-start.3 = (f32[1,16]{1,0:T(1,128)S(1)}, f32[1,16]{1,0:T(1,128)S(1)}, u32[]{:S(2)}, u32[]{:S(2)}) collective-permute-start(f32[1,16]{1,0:T(1,128)S(1)} %copy-done.6), channel_id=1, source_target_pairs={{0,4},{2,6},{4,0},{6,2},{1,5},{3,7},{5,1},{7,3},{8,12},{10,14},{12... | collective-permute-start | bytes 200 | tf_op jit(solution)/shard_map/ppermute | solution.py:258
  10.4 1.0 collective-permute-done.4
  11.4 0.2 collective-permute-start.5
  11.6 0.1 collective-permute-done.3
  11.7 2.1 %collective-permute-done.5 = f32[1,16]{1,0:T(1,128)S(1)} collective-permute-done((f32[1,16]{1,0:T(1,128)S(1)}, f32[1,16]{1,0:T(1,128)S(1)}, u32[]{:S(2)}, u32[]{:S(2)}) %collective-permute-start.5) | collective-permute-done | bytes 96 | tf_op jit(solution)/shard_map/ppermute | solution.py:258
  13.8 5.1 %collective-permute-start.8 = (f32[1,16]{1,0:T(1,128)S(1)}, f32[1,16]{1,0:T(1,128)S(1)}, u32[]{:S(2)}, u32[]{:S(2)}) collective-permute-start(f32[1,16]{1,0:T(1,128)S(1)} %add_add_fusion.1.sum_0), channel_id=1, source_target_pairs={{0,24},{8,0},{16,8},{24,16},{1,25},{9,1},{17,9},{25,17},{2,26},{10... | collective-permute-start | bytes 200 | tf_op jit(solution)/shard_map/ppermute | solution.py:258
  18.9 1.0 collective-permute-start.7
  19.9 0.0 collective-permute-done.oth_feat
  19.9 2.3 %collective-permute-start.6 = (f32[1,16]{1,0:T(1,128)S(1)}, f32[1,16]{1,0:T(1,128)S(1)}, u32[]{:S(2)}, u32[]{:S(2)}) collective-permute-start(f32[1,16]{1,0:T(1,128)S(1)} %add_add_fusion.1.sum_0), channel_id=1, source_target_pairs={{0,8},{8,16},{16,24},{24,0},{1,9},{9,17},{17,25},{25,1},{2,10},{10... | collective-permute-start | bytes 200 | tf_op jit(solution)/shard_map/ppermute | solution.py:258
  22.1 0.0 collective-permute-done.1.oth_pair
  22.1 0.0 copy-done.3
  22.1 0.0 copy-done.4
  22.1 0.0 copy-done.2
  22.2 1.4 %forward.1 = (bf16[2,1024,384]{2,1,0:T(8,128)(2,1)S(1)}, f32[2,1024,256]{2,1,0:T(8,128)S(1)}, bf16[2,32,256]{2,1,0:T(8,128)(2,1)S(1)}) custom-call(bf16[512,256]{1,0:T(8,128)(2,1)S(1)} %bitcast.17, bf16[2,512,128]{2,1,0:T(8,128)(2,1)S(1)} %bitcast.19, f32[512,256]{1,0:T(8,128)S(1)} %collective-permute-done.oth_feat, ...), custom_call_target="tpu_custom_call" | custom-call | flops 1000000000 | bytes 6000000 | tf_op jit(solution)/shard_map/forward/pallas_call | solution.py:267
  23.5 0.0 collective-permute-done.8.sum_3
  23.5 1.6 %collective-permute-done.7.sum_2 = f32[1,16]{1,0:T(1,128)S(1)} collective-permute-done((f32[1,16]{1,0:T(1,128)S(1)}, f32[1,16]{1,0:T(1,128)S(1)}, u32[]{:S(2)}, u32[]{:S(2)}) %collective-permute-start.7) | collective-permute-done | bytes 96 | tf_op jit(solution)/shard_map/ppermute | solution.py:258
  25.2 0.0 collective-permute-done.6.sum_1
  25.2 0.0 collective-permute-done.2.oth_psi
  25.2 0.0 copy-done.1
  25.2 2.5 %factors.1 = f32[4352,128]{1,0:T(8,128)S(1)} custom-call(bf16[2,1024,384]{2,1,0:T(8,128)(2,1)S(1)} %get-tuple-element.10.x_s, f32[2,1024,256]{2,1,0:T(8,128)S(1)} %get-tuple-element.11.d_s, bf16[2,32,256]{2,1,0:T(8,128)(2,1)S(1)} %get-tuple-element.12.m_s, bf16[512,256]{1,0:T(8,128)(2,1)S(1)} %bitcast.16, f32[512,256]{1,0:T(8,128)S(1)} %collective-permute-done.2.oth_psi, ...), custom_call_target="tpu_custom_call" | custom-call | flops 1500000000 | bytes 8000000 | tf_op jit(solution)/shard_map/factors/pallas_call | solution.py:276
  27.7 33.5 %all_to_all.17 = f32[32,136,128]{2,1,0:T(8,128)S(1)} all-to-all(f32[32,136,128]{2,1,0:T(8,128)S(1)} %bitcast.14), channel_id=1, replica_groups=mesh['zl'=2,'y'=4,'zh'=4,'x'=4,'c'=2] {'zl','y','x'}, dimensions={0} | all-to-all | bytes 4456448 | tf_op jit(solution)/shard_map/all_to_all | solution.py:288
  61.2 0.1 reduce_sum.9
  61.3 1.2 %collective-permute-start.11 = (f32[136,128]{1,0:T(8,128)S(1)}, f32[136,128]{1,0:T(8,128)S(1)}, u32[]{:S(2)}, u32[]{:S(2)}) collective-permute-start(f32[136,128]{1,0:T(8,128)S(1)} %reduce_sum.9), channel_id=1, source_target_pairs={{0,24},{8,0},{16,8},{24,16},{1,25},{9,1},{17,9},{25,17},{2,26},{10... | collective-permute-start | bytes 208904 | tf_op jit(solution)/shard_map/ppermute | solution.py:258
  62.6 1.2 %collective-permute-start.10 = (f32[136,128]{1,0:T(8,128)S(1)}, f32[136,128]{1,0:T(8,128)S(1)}, u32[]{:S(2)}, u32[]{:S(2)}) collective-permute-start(f32[136,128]{1,0:T(8,128)S(1)} %reduce_sum.9), channel_id=1, source_target_pairs={{0,8},{8,16},{16,24},{24,0},{1,9},{9,17},{17,25},{25,1},{2,10},{10... | collective-permute-start | bytes 208904 | tf_op jit(solution)/shard_map/ppermute | solution.py:258
  63.8 3.3 %collective-permute-start.9 = (f32[136,128]{1,0:T(8,128)S(1)}, f32[136,128]{1,0:T(8,128)S(1)}, u32[]{:S(2)}, u32[]{:S(2)}) collective-permute-start(f32[136,128]{1,0:T(8,128)S(1)} %reduce_sum.9), channel_id=1, source_target_pairs={{0,16},{8,24},{16,0},{24,8},{1,17},{9,25},{17,1},{25,9},{2,18},{10... | collective-permute-start | bytes 208904 | tf_op jit(solution)/shard_map/ppermute | solution.py:258
  67.1 0.0 collective-permute-done.11
  67.1 0.8 collective-permute-done.10
  67.9 3.7 %collective-permute-done.9 = f32[136,128]{1,0:T(8,128)S(1)} collective-permute-done((f32[136,128]{1,0:T(8,128)S(1)}, f32[136,128]{1,0:T(8,128)S(1)}, u32[]{:S(2)}, u32[]{:S(2)}) %collective-permute-start.9) | collective-permute-done | bytes 69664 | tf_op jit(solution)/shard_map/ppermute | solution.py:258
  71.6 0.1 broadcast_in_dim.15
  71.8 0.0 copy-start
  71.8 0.0 copy-start.5
  71.8 30.6 %all_to_all.18 = f32[32,136,128]{2,1,0:T(8,128)S(1)} all-to-all(f32[32,136,128]{2,1,0:T(8,128)S(1)} %broadcast_in_dim.15), channel_id=1, replica_groups=mesh['zl'=2,'y'=4,'zh'=4,'x'=4,'c'=2] {'zl','y','x'}, dimensions={0} | all-to-all | bytes 4456448 | tf_op jit(solution)/shard_map/all_to_all | solution.py:293
  102.5 0.0 copy-done
  102.5 0.0 copy-done.5
  102.5 2.5 %natural.1 = (f32[896,256]{1,0:T(8,128)S(1)}, f32[1,128]{1,0:T(1,128)S(1)}) custom-call(f32[4352,128]{1,0:T(8,128)S(1)} %bitcast.12, f32[896,896]{1,0:T(8,128)S(1)} %bitcast.15, f32[256,256]{1,0:T(8,128)S(1)} %bitcast.20), custom_call_target="tpu_custom_call" | custom-call | flops 1500000000 | bytes 5000000 | tf_op jit(solution)/shard_map/natural/pallas_call | solution.py:295
  104.9 5.7 %collective-permute-start.12 = (f32[1,128]{1,0:T(1,128)S(1)}, f32[1,128]{1,0:T(1,128)S(1)}, u32[]{:S(2)}, u32[]{:S(2)}) collective-permute-start(f32[1,128]{1,0:T(1,128)S(1)} %get-tuple-element.16.curvature), channel_id=1, source_target_pairs={{0,1},{1,0},{2,3},{3,2},{4,5},{5,4},{6,7},{7,6},{8,9},{9,8},{10,11... | collective-permute-start | bytes 1544 | tf_op jit(solution)/shard_map/ppermute | solution.py:304
  110.6 2.1 %unpack.1 = (f32[896,896]{1,0:T(8,128)}, f32[256,256]{1,0:T(8,128)}) custom-call(f32[4352,128]{1,0:T(8,128)S(1)} %bitcast.13), custom_call_target="tpu_custom_call" | custom-call | flops 10000000 | bytes 6000000 | tf_op jit(solution)/shard_map/unpack/pallas_call | solution.py:305
  112.7 0.0 collective-permute-done.12.other
  112.7 1.1 scale.1
  (2 shorter events, 0.0 us)
Async XLA Ops:
  0.6 21.5 %copy-start.3 = (bf16[1,16,32,256]{3,2,1,0:T(8,128)(2,1)S(1)}, bf16[1,16,32,256]{3,2,1,0:T(8,128)(2,1)}, u32[]{:S(2)}) copy-start(bf16[1,16,32,256]{3,2,1,0:T(8,128)(2,1)} %param.8) | copy-start | bytes 786436
  0.6 21.5 %copy-start.4 = (bf16[1,2,16,32,128]{4,3,2,1,0:T(8,128)(2,1)S(1)}, bf16[1,2,16,32,128]{4,3,2,1,0:T(8,128)(2,1)}, u32[]{:S(2)}) copy-start(bf16[1,2,16,32,128]{4,3,2,1,0:T(8,128)(2,1)} %param.10) | copy-start | bytes 786436
  0.7 7.1 %copy-start.6 = (f32[1,16]{1,0:T(1,128)S(1)}, f32[1,16]{1,0:T(1,128)}, u32[]{:S(2)}) copy-start(f32[1,16]{1,0:T(1,128)} %energy.1) | copy-start | bytes 196
  0.7 21.5 %copy-start.2 = (bf16[2,896,256]{2,1,0:T(8,128)(2,1)S(1)}, bf16[2,896,256]{2,1,0:T(8,128)(2,1)}, u32[]{:S(2)}) copy-start(bf16[2,896,256]{2,1,0:T(8,128)(2,1)} %weights.3) | copy-start | bytes 2752516
  1.8 18.1 %collective-permute-start = (f32[512,256]{1,0:T(8,128)S(1)}, f32[512,256]{1,0:T(8,128)S(1)}, u32[]{:S(2)}, u32[]{:S(2)}) collective-permute-start(f32[512,256]{1,0:T(8,128)S(1)} %bitcast_convert_fusion.1), channel_id=1, source_target_pairs={{0,1},{1,0},{2,3},{3,2},{4,5},{5,4},{6,7},{7,6},{8,9},{9,8},{10,11... | collective-permute-start | bytes 1572872 | tf_op jit(solution)/shard_map/ppermute | solution.py:262
  6.1 19.1 %copy-start.1 = (bf16[1,16,32,256]{3,2,1,0:T(8,128)(2,1)S(1)}, bf16[1,16,32,256]{3,2,1,0:T(8,128)(2,1)}, u32[]{:S(2)}) copy-start(bf16[1,16,32,256]{3,2,1,0:T(8,128)(2,1)} %param.9) | copy-start | bytes 786436
  6.1 16.0 %collective-permute-start.1 = (f32[2,512,128]{2,1,0:T(8,128)S(1)}, f32[2,512,128]{2,1,0:T(8,128)S(1)}, u32[]{:S(2)}, u32[]{:S(2)}) collective-permute-start(f32[2,512,128]{2,1,0:T(8,128)S(1)} %convert_element_type.10), channel_id=1, source_target_pairs={{0,1},{1,0},{2,3},{3,2},{4,5},{5,4},{6,7},{7,6},{8,9},{9,8},{10,11... | collective-permute-start | bytes 1572872 | tf_op jit(solution)/shard_map/ppermute | solution.py:263
  7.2 18.0 %collective-permute-start.2 = (f32[512,256]{1,0:T(8,128)S(1)}, f32[512,256]{1,0:T(8,128)S(1)}, u32[]{:S(2)}, u32[]{:S(2)}) collective-permute-start(f32[512,256]{1,0:T(8,128)S(1)} %bitcast_convert_fusion), channel_id=1, source_target_pairs={{0,1},{1,0},{2,3},{3,2},{4,5},{5,4},{6,7},{7,6},{8,9},{9,8},{10,11... | collective-permute-start | bytes 1572872 | tf_op jit(solution)/shard_map/ppermute | solution.py:264
  7.8 3.6 %collective-permute-start.4 = (f32[1,16]{1,0:T(1,128)S(1)}, f32[1,16]{1,0:T(1,128)S(1)}, u32[]{:S(2)}, u32[]{:S(2)}) collective-permute-start(f32[1,16]{1,0:T(1,128)S(1)} %copy-done.6), channel_id=1, source_target_pairs={{0,2},{2,4},{4,6},{6,0},{1,3},{3,5},{5,7},{7,1},{8,10},{10,12},{12... | collective-permute-start | bytes 200 | tf_op jit(solution)/shard_map/ppermute | solution.py:258
  7.8 3.9 %collective-permute-start.3 = (f32[1,16]{1,0:T(1,128)S(1)}, f32[1,16]{1,0:T(1,128)S(1)}, u32[]{:S(2)}, u32[]{:S(2)}) collective-permute-start(f32[1,16]{1,0:T(1,128)S(1)} %copy-done.6), channel_id=1, source_target_pairs={{0,4},{2,6},{4,0},{6,2},{1,5},{3,7},{5,1},{7,3},{8,12},{10,14},{12... | collective-permute-start | bytes 200 | tf_op jit(solution)/shard_map/ppermute | solution.py:258
  11.4 2.4 %collective-permute-start.5 = (f32[1,16]{1,0:T(1,128)S(1)}, f32[1,16]{1,0:T(1,128)S(1)}, u32[]{:S(2)}, u32[]{:S(2)}) collective-permute-start(f32[1,16]{1,0:T(1,128)S(1)} %copy-done.6), channel_id=1, source_target_pairs={{0,6},{2,0},{4,2},{6,4},{1,7},{3,1},{5,3},{7,5},{8,14},{10,8},{12,... | collective-permute-start | bytes 200 | tf_op jit(solution)/shard_map/ppermute | solution.py:258
  13.8 9.7 %collective-permute-start.8 = (f32[1,16]{1,0:T(1,128)S(1)}, f32[1,16]{1,0:T(1,128)S(1)}, u32[]{:S(2)}, u32[]{:S(2)}) collective-permute-start(f32[1,16]{1,0:T(1,128)S(1)} %add_add_fusion.1.sum_0), channel_id=1, source_target_pairs={{0,24},{8,0},{16,8},{24,16},{1,25},{9,1},{17,9},{25,17},{2,26},{10... | collective-permute-start | bytes 200 | tf_op jit(solution)/shard_map/ppermute | solution.py:258
  18.9 6.3 %collective-permute-start.7 = (f32[1,16]{1,0:T(1,128)S(1)}, f32[1,16]{1,0:T(1,128)S(1)}, u32[]{:S(2)}, u32[]{:S(2)}) collective-permute-start(f32[1,16]{1,0:T(1,128)S(1)} %add_add_fusion.1.sum_0), channel_id=1, source_target_pairs={{0,16},{8,24},{16,0},{24,8},{1,17},{9,25},{17,1},{25,9},{2,18},{10... | collective-permute-start | bytes 200 | tf_op jit(solution)/shard_map/ppermute | solution.py:258
  19.9 5.3 %collective-permute-start.6 = (f32[1,16]{1,0:T(1,128)S(1)}, f32[1,16]{1,0:T(1,128)S(1)}, u32[]{:S(2)}, u32[]{:S(2)}) collective-permute-start(f32[1,16]{1,0:T(1,128)S(1)} %add_add_fusion.1.sum_0), channel_id=1, source_target_pairs={{0,8},{8,16},{16,24},{24,0},{1,9},{9,17},{17,25},{25,1},{2,10},{10... | collective-permute-start | bytes 200 | tf_op jit(solution)/shard_map/ppermute | solution.py:258
  61.3 5.7 %collective-permute-start.11 = (f32[136,128]{1,0:T(8,128)S(1)}, f32[136,128]{1,0:T(8,128)S(1)}, u32[]{:S(2)}, u32[]{:S(2)}) collective-permute-start(f32[136,128]{1,0:T(8,128)S(1)} %reduce_sum.9), channel_id=1, source_target_pairs={{0,24},{8,0},{16,8},{24,16},{1,25},{9,1},{17,9},{25,17},{2,26},{10... | collective-permute-start | bytes 208904 | tf_op jit(solution)/shard_map/ppermute | solution.py:258
  62.6 5.3 %collective-permute-start.10 = (f32[136,128]{1,0:T(8,128)S(1)}, f32[136,128]{1,0:T(8,128)S(1)}, u32[]{:S(2)}, u32[]{:S(2)}) collective-permute-start(f32[136,128]{1,0:T(8,128)S(1)} %reduce_sum.9), channel_id=1, source_target_pairs={{0,8},{8,16},{16,24},{24,0},{1,9},{9,17},{17,25},{25,1},{2,10},{10... | collective-permute-start | bytes 208904 | tf_op jit(solution)/shard_map/ppermute | solution.py:258
  63.8 7.8 %collective-permute-start.9 = (f32[136,128]{1,0:T(8,128)S(1)}, f32[136,128]{1,0:T(8,128)S(1)}, u32[]{:S(2)}, u32[]{:S(2)}) collective-permute-start(f32[136,128]{1,0:T(8,128)S(1)} %reduce_sum.9), channel_id=1, source_target_pairs={{0,16},{8,24},{16,0},{24,8},{1,17},{9,25},{17,1},{25,9},{2,18},{10... | collective-permute-start | bytes 208904 | tf_op jit(solution)/shard_map/ppermute | solution.py:258
  71.8 30.7 %copy-start = (f32[1,896,896]{2,1,0:T(8,128)S(1)}, f32[1,896,896]{2,1,0:T(8,128)}, u32[]{:S(2)}) copy-start(f32[1,896,896]{2,1,0:T(8,128)} %param.14) | copy-start | bytes 9633796
  71.8 30.7 %copy-start.5 = (f32[1,256,256]{2,1,0:T(8,128)S(1)}, f32[1,256,256]{2,1,0:T(8,128)}, u32[]{:S(2)}) copy-start(f32[1,256,256]{2,1,0:T(8,128)} %param.15) | copy-start | bytes 786436
  104.9 7.7 %collective-permute-start.12 = (f32[1,128]{1,0:T(1,128)S(1)}, f32[1,128]{1,0:T(1,128)S(1)}, u32[]{:S(2)}, u32[]{:S(2)}) collective-permute-start(f32[1,128]{1,0:T(1,128)S(1)} %get-tuple-element.16.curvature), channel_id=1, source_target_pairs={{0,1},{1,0},{2,3},{3,2},{4,5},{5,4},{6,7},{7,6},{8,9},{9,8},{10,11... | collective-permute-start | bytes 1544 | tf_op jit(solution)/shard_map/ppermute | solution.py:304

commit v3 on v2

--- a/solution.py
+++ b/solution.py
@@ -9,10 +9,11 @@
 D, PAIR, DIN = 256, 128, 896
 WALK, HALF, ROWS = 16, 512, 1024
 B = 128
-GROUP = 32
-PACKED = 4352
-EXTRA = 33 * B
-CHUNK = PACKED // GROUP
+GROUP = 16
+SLOTS = 17
+KEPT = SLOTS * B
+CHUNK = KEPT // GROUP
+STREAMS = ((0, 6), (6, 12), (12, 17))
 ENTRIES = 2 * DIN * D
 
 
@@ -42,20 +43,32 @@
     return lax.broadcasted_iota(jnp.int32, (B, B), 0), lax.broadcasted_iota(jnp.int32, (B, B), 1)
 
 
+def own_parity():
+    return lax.rem(lax.axis_index("x") + lax.axis_index("y") + lax.axis_index("zl"), 2)
+
+
 def walker_table():
     group = lax.broadcasted_iota(jnp.int32, (2 * WALK, ROWS), 1) // (HALF // WALK)
     return (group == lax.broadcasted_iota(jnp.int32, (2 * WALK, ROWS), 0)).astype(BF16)
 
 
-def forward_kernel(feat, pair, oth_feat, oth_pair, weights, x_s, d_s, m_s):
+def widen_kernel(feat, psi, pair, energies, sent, spread):
+    sent[:, :D] = feat[...].astype(F32)
+    sent[:, D : 2 * D] = psi[...].astype(F32)
+    for l in range(2):
+        sent[:, 2 * D + l * PAIR : 2 * D + (l + 1) * PAIR] = pair[l].astype(F32)
+    spread[...] = jnp.broadcast_to(energies[...], (WALK, WALK))
+
+
+def forward_kernel(feat, pair, other, weights, x_s, d_s, m_s):
     mp = lax.axis_index("c")
     own_row = pl.multiple_of(D + D * mp, D)
     oth_row = pl.multiple_of(2 * D - D * mp, D)
     x_s[0, :HALF, :D] = feat[...]
-    x_s[0, HALF:, :D] = oth_feat[...].astype(BF16)
+    x_s[0, HALF:, :D] = other[:, :D].astype(BF16)
     for l in range(2):
         x_s[l, :HALF, D:] = pair[l]
-        x_s[l, HALF:, D:] = oth_pair[l].astype(BF16)
+        x_s[l, HALF:, D:] = other[:, 2 * D + l * PAIR : 2 * D + (l + 1) * PAIR].astype(BF16)
     pick = walker_table()
     for l in range(2):
         means = (dot(pick, x_s[l, :, :D]) * (1.0 / 32.0)).astype(BF16)
@@ -76,21 +89,21 @@
 
 
 def factors_kernel(
-    x_s, d_s, m_s, psi, oth_psi, weights, sum_0, sum_1, sum_2, sum_3, energy, multiplicity, out, s_s, c_s
+    x_s, d_s, m_s, psi, other, weights, gathered, energy, multiplicity, keep, to_x, to_y, to_z, s_s, c_s, out
 ):
     mp = lax.axis_index("c")
     own_row = pl.multiple_of(D + D * mp, D)
     oth_row = pl.multiple_of(2 * D - D * mp, D)
     pick = walker_table()
     s_s[1, :HALF, :] = (psi[...].astype(F32) * d_s[1, :HALF, :]).astype(BF16)
-    s_s[1, HALF:, :] = (oth_psi[...] * d_s[1, HALF:, :]).astype(BF16)
+    s_s[1, HALF:, :] = (other[:, D : 2 * D] * d_s[1, HALF:, :]).astype(BF16)
     q_both = dot(pick, s_s[1])
     q_high, q_low = split(q_both[:WALK] + q_both[WALK:])
     for half in range(2):
         rows = slice(half * HALF, (half + 1) * HALF)
         w_spin = weights[1, pl.ds(own_row if half == 0 else oth_row, D), :]
         spin = (dot_nt(q_high, w_spin) + dot_nt(q_low, w_spin)) * (1.0 / 32.0)
-        up = psi[...].astype(F32) if half == 0 else oth_psi[...]
+        up = psi[...].astype(F32) if half == 0 else other[:, D : 2 * D]
         u = up + dot_nt(s_s[1, rows, :], weights[1, :D, :]) + per_walker(spin)
         s_s[0, rows, :] = (u * d_s[0, rows, :]).astype(BF16)
 
@@ -99,8 +112,7 @@
     row_scale = mult * (1.0 / 16384.0)
     x = x_s[l]
     s = s_s[l]
-    mean = jnp.sum((sum_0[...] + sum_2[...]) + (sum_1[...] + sum_3[...]), axis=1, keepdims=True)
-    mean = mean * (1.0 / 256.0)
+    mean = jnp.sum(jnp.sum(gathered[...], axis=0, keepdims=True), axis=1, keepdims=True) * (1.0 / 256.0)
     step = HALF // WALK
     for w in range(WALK):
         centered = energy[0, w] - mean
@@ -111,18 +123,20 @@
     h, p = x[:, :D], x[:, D:]
     row, col = square_iotas()
 
+    parity = own_parity()
+
     def put(slot, value):
-        out[slot * B : (slot + 1) * B, :] = value * row_scale
+        first = slot % SLOTS * B
+        out[parity ^ (slot // SLOTS), first : first + B, :] = value * row_scale
+
+    lines = {}
 
     def put_symmetric(slot, line, full):
         low = full[B:, B:]
         put(slot, jnp.where(col >= row, full[:B, :B], low))
         put(slot + 1, full[:B, B:])
-        out[EXTRA + line : EXTRA + line + 1, :] = (
-            jnp.sum(jnp.where(col == row, low, 0.0), axis=0, keepdims=True) * row_scale
-        )
-
-    out[EXTRA:, :] = jnp.zeros((PACKED - EXTRA, B), F32)
+        lines[line] = jnp.sum(jnp.where(col == row, low, 0.0), axis=0, keepdims=True) * row_scale
+
     put_symmetric(0, 0, dot_t(h, h))
     hp = dot_t(h, p)
     put(11, hp[:B])
@@ -156,21 +170,55 @@
         put(13 + i, side[rows, :B])
         put(23 + 2 * i, side[rows, B : 2 * B])
         put(24 + 2 * i, side[rows, 2 * B :])
-    out[EXTRA + 4 : EXTRA + 5, :] = jnp.full((1, B), mult * (1.0 / 16.0), F32)
-
-
-def unpack_kernel(packed, a_out, s_out):
+    lines[4] = jnp.full((1, B), mult * (1.0 / 16.0), F32)
+    last = KEPT - B
+    out[parity ^ 1, last:, :] = jnp.zeros((B, B), F32)
+    for line, value in lines.items():
+        out[parity ^ 1, last + line : last + line + 1, :] = value
+    keep[...] = out[0]
+    for target, (first, end) in zip((to_x, to_y, to_z), STREAMS):
+        target[...] = out[1, first * B : end * B, :]
+
+
+def add_kernel(keep, from_x, from_y, from_z, total):
+    for part, (first, end) in zip((from_x, from_y, from_z), STREAMS):
+        rows = slice(first * B, end * B)
+        total[rows, :] = keep[rows, :] + part[...]
+
+
+def cut_kernel(kept, to_x, to_y, to_z):
+    for target, (first, end) in zip((to_x, to_y, to_z), STREAMS):
+        target[...] = kept[first * B : end * B, :]
+
+
+def reader(kept, parts):
+    parity = own_parity()
+
+    def read(slot, first=0, size=B):
+        place = slot % SLOTS
+        for part, (begin, end) in zip(parts, STREAMS):
+            if begin <= place < end:
+                other = part[(place - begin) * B + first : (place - begin) * B + first + size, :]
+        own = kept[place * B + first : place * B + first + size, :]
+        return jnp.where(parity == slot // SLOTS, own, other)
+
+    return read
+
+
+def unpack_kernel(kept, from_x, from_y, from_z, a_out, s_out):
     row, col = square_iotas()
-    inverse = 1.0 / packed[EXTRA + 4 : EXTRA + 5, :]
+    read = reader(kept, (from_x, from_y, from_z))
+    lines = read(33, 0, 8)
+    inverse = 1.0 / lines[4:5, :]
 
     def get(slot):
-        return packed[slot * B : (slot + 1) * B, :] * inverse
+        return read(slot) * inverse
 
     def symmetric(slot, line):
         tri = get(slot)
         off = get(slot + 1)
         flipped = tri.T
-        diag = packed[EXTRA + line : EXTRA + line + 1, :] * inverse
+        diag = lines[line : line + 1, :] * inverse
         first = jnp.where(col >= row, tri, flipped)
         second = jnp.where(col < row, tri, flipped)
         second = jnp.where(col == row, jnp.broadcast_to(diag, (B, B)), second)
@@ -206,9 +254,8 @@
         place(a_out, 6, i, block.T)
 
 
-def natural_kernel(packed, a_inverse, s_inverse, natural, curvature):
-    def get(slot):
-        return packed[slot * B : (slot + 1) * B, :]
+def natural_kernel(kept, from_x, from_y, from_z, a_inverse, s_inverse, natural, curvature):
+    get = reader(kept, (from_x, from_y, from_z))
 
     grad = jnp.concatenate(
         [jnp.concatenate([get(19 + 2 * i), get(20 + 2 * i)], 1) for i in range(7)], 0
@@ -248,69 +295,95 @@
 V, S = pltpu.VMEM, pltpu.SMEM
 
 
+def parity_groups():
+    groups = {}
+    for place in range(256):
+        rest, c = divmod(place, 2)
+        rest, x = divmod(rest, 4)
+        rest, zh = divmod(rest, 4)
+        zl, y = divmod(rest, 4)
+        groups.setdefault((zh, c, (x + y + zl) % 2), []).append(place)
+    return [groups[key] for key in sorted(groups)]
+
+
+def same_parity(value):
+    axes = ("zl", "y", "zh", "x", "c")
+    return lax.all_to_all(value, axes, 0, 0, axis_index_groups=parity_groups(), tiled=True)
+
+
+def to_neighbours(parts):
+    pairs = {"x": [(0, 1), (1, 0), (2, 3), (3, 2)], "zl": [(0, 1), (1, 0)]}
+    pairs["y"] = pairs["x"]
+    return [lax.ppermute(part, axis, pairs[axis]) for part, axis in zip(parts, ("x", "y", "zl"))]
+
+
 def body(features, psi_grad, pair_means, energies, multiplicity, weights, a_inverse, s_inverse):
     feat = features.reshape(HALF, D)
     psi = psi_grad.reshape(HALF, D)
     pair = pair_means.reshape(2, HALF, PAIR)
     swap = [(0, 1), (1, 0)]
-
-    def turned(value, axis):
-        return [lax.ppermute(value, axis, [(i, (i + k) % 4) for i in range(4)]) for k in (1, 2, 3)]
-
-    one, two, three = turned(energies, "x")
-    row_sum = (energies + two) + (one + three)
-    oth_feat = lax.ppermute(feat.astype(F32), "c", swap)
-    oth_pair = lax.ppermute(pair.astype(F32), "c", swap)
-    oth_psi = lax.ppermute(psi.astype(F32), "c", swap)
-    one, two, three = turned(row_sum, "zh")
+    streams = [(((end - first) * B, B), F32) for first, end in STREAMS]
+
+    sent, spread = call(
+        widen_kernel, [((HALF, 3 * D), F32), ((WALK, WALK), F32)], [V] * 4, 6, "widen", moved=2_400_000
+    )(feat, psi, pair, energies)
+    other = lax.ppermute(sent, "c", swap)
+    gathered = lax.all_to_all(spread, ("zh", "x"), 0, 0, tiled=True)
 
     x_s, d_s, m_s = call(
         forward_kernel,
         [((2, ROWS, D + PAIR), BF16), ((2, ROWS, D), F32), ((2, 2 * WALK, D), BF16)],
-        [V] * 5,
+        [V] * 4,
         16,
         "forward",
         flops=1_000_000_000,
         moved=6_000_000,
-    )(feat, pair, oth_feat, oth_pair, weights)
-    (packed,) = call(
+    )(feat, pair, other, weights)
+    keep, *parts = call(
         factors_kernel,
-        [((PACKED, B), F32)],
-        [V] * 10 + [S] * 2,
-        20,
+        [((KEPT, B), F32)] + streams,
+        [V] * 7 + [S] * 2,
+        22,
         "factors",
-        scratch=[pltpu.VMEM((2, ROWS, D), BF16), pltpu.VMEM((ROWS, D), BF16)],
+        scratch=[
+            pltpu.VMEM((2, ROWS, D), BF16),
+            pltpu.VMEM((ROWS, D), BF16),
+            pltpu.VMEM((2, KEPT, B), F32),
+        ],
         flops=1_500_000_000,
         moved=8_000_000,
-    )(x_s, d_s, m_s, psi, oth_psi, weights, row_sum, one, two, three, energies, multiplicity)
-
-    ring = ("zl", "y", "x")
-    parts = lax.all_to_all(packed, ring, 0, 0, tiled=True)
-    mine = jnp.sum(parts.reshape(GROUP, CHUNK, B), axis=0)
-    one, two, three = turned(mine, "zh")
+    )(x_s, d_s, m_s, psi, other, weights, gathered, energies, multiplicity)
+
+    parts = to_neighbours(parts)
+    (total,) = call(add_kernel, [((KEPT, B), F32)], [V] * 4, 6, "add", moved=3_000_000)(keep, *parts)
+    mine = jnp.sum(same_parity(total).reshape(GROUP, CHUNK, B), axis=0)
+    one, two, three = (
+        lax.ppermute(mine, "zh", [(i, (i + k) % 4) for i in range(4)]) for k in (1, 2, 3)
+    )
     mine = (mine + two) + (one + three)
-    copies = jnp.broadcast_to(mine[None], (GROUP, CHUNK, B)).reshape(PACKED, B)
-    summed = lax.all_to_all(copies, ring, 0, 0, tiled=True)
+    kept = same_parity(jnp.broadcast_to(mine[None], (GROUP, CHUNK, B)).reshape(KEPT, B))
+    parts = call(cut_kernel, streams, [V], 6, "cut", moved=2_200_000)(kept)
+    parts = to_neighbours(parts)
 
     natural, curvature = call(
         natural_kernel,
         [((DIN, D), F32), ((1, B), F32)],
-        [V] * 3,
+        [V] * 6,
         18,
         "natural",
         flops=1_500_000_000,
         moved=5_000_000,
-    )(summed, a_inverse[0], s_inverse[0])
+    )(kept, *parts, a_inverse[0], s_inverse[0])
     other = lax.ppermute(curvature, "c", swap)
     a_sum, s_sum = call(
         unpack_kernel,
         [((DIN, DIN), F32), ((D, D), F32)],
-        [V],
+        [V] * 4,
         14,
         "unpack",
         flops=10_000_000,
         moved=6_000_000,
-    )(summed)
+    )(kept, *parts)
     (direction,) = call(
         scale_kernel, [((DIN, D), F32)], [V] * 3, 6, "scale", flops=1_000_000, moved=2_000_000
     )(natural, curvature, other)

time: 114 us -> 115 us (level)
  blocking collectives: 64.2 us -> 42.6 us
  local copies, waits for them, and re-layouts: 0.18 us -> 13.2 us
  waiting for transfers between devices: 9.39 us -> 16.8 us
  starting transfers between devices: 25.9 us -> 30.1 us
  other arithmetic: 3.2 us -> 0.08 us
    all_to_all x2, blocking collectives: 64.2 us -> 42.6 us  [same_parity(): lax.all_to_all(value, axes, 0, 0, axis_index_groups=parity_groups(), tile...]
    unnamed x14 -> x34, local copies, waits for them, and re-layouts: 0.04 us -> 13.1 us
    all_to_all x0 -> x1, starting transfers between devices: none -> 9.01 us  [body(): gathered = lax.all_to_all(spread, ('zh', 'x'), 0, 0, tiled=True)]
    ppermute x12 -> x10, waiting for transfers between devices: 9.39 us -> 16.8 us  [the longest x6 13.5 us: to_neighbours(): lax.ppermute(part, axis, pairs[axis])]
    ppermute x12 -> x10, starting transfers between devices: 20.2 us -> 15.3 us  [the longest x3 7.53 us: body(): lax.ppermute(mine, 'zh', [(i, (i + k) % 4) for i in range(4)])]
    convert_element_type x3 -> x0, other arithmetic: 3.06 us -> none  [the longest x1 1.09 us: body(): oth_feat = lax.ppermute(feat.astype(F32), 'c', swap)]
    pallas_call x3 -> x6, Pallas kernels: 7.05 us -> 8.21 us  [the longest x1 2.69 us: body(): call(factors_kernel, [((KEPT, B), F32)] + streams, [V] * 7 + [S] * 2, 22,...]
  transfers between devices with their start and end apart: 13 -> 12, of which waited for: 6 -> 7; matrix products, arithmetic and copies ran while one was open for 2% -> 0% of each run, Pallas kernels for 3% -> 3%
where the time goes in v3:
time: 115 us
  blocking collectives  42.6 us (37%)
  starting transfers between devices  30.1 us (26%)
  waiting for transfers between devices  16.8 us (15%)
  local copies, waits for them, and re-layouts  13.2 us (11%)
  Pallas kernels  10.6 us (9%)
  between operations  1.42 us (1%)
    all_to_all x2, blocking collectives, same_parity(): lax.all_to_all(value, axes, 0, 0, axis_index_groups=parity_groups(), tile...  42.6 us
    ppermute x6, waiting for transfers between devices, to_neighbours(): lax.ppermute(part, axis, pairs[axis])  13.5 us
    unnamed x34, local copies, waits for them, and re-layouts  13.1 us
    all_to_all x1, starting transfers between devices, body(): gathered = lax.all_to_all(spread, ('zh', 'x'), 0, 0, tiled=True)  9.01 us
    ppermute x3, starting transfers between devices, body(): lax.ppermute(mine, 'zh', [(i, (i + k) % 4) for i in range(4)])  7.53 us
    ppermute x1, starting transfers between devices, body(): other = lax.ppermute(curvature, 'c', swap)  5.8 us
    ppermute x6, starting transfers between devices, to_neighbours(): lax.ppermute(part, axis, pairs[axis])  4.55 us
    ppermute x3, waiting for transfers between devices, body(): lax.ppermute(mine, 'zh', [(i, (i + k) % 4) for i in range(4)])  3.29 us
  transfers between devices with their start and end apart: 12, of which 7 were waited for; matrix products, arithmetic and copies ran while one was open for 0% of the time, Pallas kernels for 3%

profile of v3, /device:TPU:1, one launch (start us, length us, event | category | flops | bytes accessed | tf_op | source)
XLA Modules:
  0.0 114.8 jit_solution(14327478482831246958)
XLA Ops:
  0.6 0.0 copy-start.6
  0.6 0.9 copy-done.6
  1.6 0.0 copy-start.11
  1.6 0.9 copy-done.11
  2.5 0.0 copy-start.13
  2.5 0.9 copy-done.13
  3.5 0.0 copy-start.15
  3.5 0.7 copy-done.15
  4.1 0.7 widen.1
  4.8 3.2 %collective-permute-start = (f32[512,768]{1,0:T(8,128)S(1)}, f32[512,768]{1,0:T(8,128)S(1)}, u32[]{:S(2)}, u32[]{:S(2)}) collective-permute-start(f32[512,768]{1,0:T(8,128)S(1)} %get-tuple-element.19), channel_id=1, source_target_pairs={{0,1},{1,0},{2,3},{3,2},{4,5},{5,4},{6,7},{7,6},{8,9},{9,8},{10,11... | collective-permute-start | bytes 4718600 | tf_op jit(solution)/shard_map/ppermute | solution.py:330
  8.0 9.0 %all-to-all-start = ((f32[16,1,16]{2,1,0:T(1,128)}), f32[16,1,16]{2,1,0:T(1,128)S(1)}, u32[]{:S(2)}, u32[]{:S(2)}) async-start(f32[16,1,16]{2,1,0:T(1,128)} %bitcast.4), calls=%async_computation | async-start | bytes 16384 | tf_op jit(solution)/shard_map/all_to_all | solution.py:331
  17.7 0.0 collective-permute-done.other
  17.7 0.0 copy-start.1
  17.7 1.1 copy-done.1
  18.9 0.0 copy-start.2
  18.9 1.4 %copy-done.2 = f32[512,768]{1,0:T(8,128)S(1)} copy-done((f32[512,768]{1,0:T(8,128)S(1)}, f32[512,768]{1,0:T(8,128)}, u32[]{:S(2)}) %copy-start.2) | copy-done | bytes 1572888
  20.3 0.0 copy-start.8
  20.3 1.2 %copy-done.8 = bf16[2,896,256]{2,1,0:T(8,128)(2,1)S(1)} copy-done((bf16[2,896,256]{2,1,0:T(8,128)(2,1)S(1)}, bf16[2,896,256]{2,1,0:T(8,128)(2,1)}, u32[]{:S(2)}) %copy-start.8) | copy-done | bytes 917528
  21.5 0.9 copy-done.12
  22.4 0.9 copy-done.14
  23.4 1.3 %forward.1 = (bf16[2,1024,384]{2,1,0:T(8,128)(2,1)S(1)}, f32[2,1024,256]{2,1,0:T(8,128)S(1)}, bf16[2,32,256]{2,1,0:T(8,128)(2,1)S(1)}) custom-call(bf16[512,256]{1,0:T(8,128)(2,1)S(1)} %bitcast.23, bf16[2,512,128]{2,1,0:T(8,128)(2,1)S(1)} %bitcast.25, f32[512,768]{1,0:T(8,128)S(1)} %copy-done.2, bf16[2,896,256]{2,1,0:T(8,128)(2,1)S(1)} %copy-done.8), custom_call_target="tpu_custom_call" | custom-call | flops 1000000000 | bytes 6000000 | tf_op jit(solution)/shard_map/forward/pallas_call | solution.py:333
  24.7 0.0 copy-start.4
  24.7 1.2 %copy-done.4 = bf16[2,1024,384]{2,1,0:T(8,128)(2,1)} copy-done((bf16[2,1024,384]{2,1,0:T(8,128)(2,1)}, bf16[2,1024,384]{2,1,0:T(8,128)(2,1)S(1)}, u32[]{:S(2)}) %copy-start.4) | copy-done | bytes 1572888
  25.9 0.0 all-to-all-done
  25.9 0.0 copy-done.7
  25.9 0.0 copy-done.9
  25.9 0.0 copy-done.16
  25.9 0.0 copy-start.3
  25.9 1.4 %copy-done.3 = f32[512,768]{1,0:T(8,128)S(1)} copy-done((f32[512,768]{1,0:T(8,128)S(1)}, f32[512,768]{1,0:T(8,128)}, u32[]{:S(2)}) %copy-start.3) | copy-done | bytes 1572888
  27.3 1.4 %copy-done.5 = bf16[2,1024,384]{2,1,0:T(8,128)(2,1)S(1)} copy-done((bf16[2,1024,384]{2,1,0:T(8,128)(2,1)S(1)}, bf16[2,1024,384]{2,1,0:T(8,128)(2,1)}, u32[]{:S(2)}) %copy-start.5) | copy-done | bytes 1572888
  28.7 2.7 %factors.1 = (f32[2176,128]{1,0:T(8,128)S(1)}, f32[768,128]{1,0:T(8,128)S(1)}, f32[768,128]{1,0:T(8,128)S(1)}, f32[640,128]{1,0:T(8,128)S(1)}) custom-call(bf16[2,1024,384]{2,1,0:T(8,128)(2,1)S(1)} %copy-done.5, f32[2,1024,256]{2,1,0:T(8,128)S(1)} %get-tuple-element.21.d_s, bf16[2,32,256]{2,1,0:T(8,128)(2,1)S(1)} %get-tuple-element.22.m_s, ...), custom_call_target="tpu_custom_call" | custom-call | flops 1500000000 | bytes 8000000 | tf_op jit(solution)/shard_map/factors/pallas_call | solution.py:342
  31.5 1.5 %collective-permute-start.1 = (f32[768,128]{1,0:T(8,128)S(1)}, f32[768,128]{1,0:T(8,128)S(1)}, u32[]{:S(2)}, u32[]{:S(2)}) collective-permute-start(f32[768,128]{1,0:T(8,128)S(1)} %get-tuple-element.25), channel_id=1, source_target_pairs={{0,2},{2,0},{4,6},{6,4},{1,3},{3,1},{5,7},{7,5},{8,10},{10,8},{12,... | collective-permute-start | bytes 1179656 | tf_op jit(solution)/shard_map/ppermute | solution.py:317
  32.9 1.3 %collective-permute-start.2 = (f32[768,128]{1,0:T(8,128)S(1)}, f32[768,128]{1,0:T(8,128)S(1)}, u32[]{:S(2)}, u32[]{:S(2)}) collective-permute-start(f32[768,128]{1,0:T(8,128)S(1)} %get-tuple-element.26), channel_id=1, source_target_pairs={{0,32},{32,0},{64,96},{96,64},{1,33},{33,1},{65,97},{97,65},{2,34}... | collective-permute-start | bytes 1179656 | tf_op jit(solution)/shard_map/ppermute | solution.py:317
  34.2 0.7 collective-permute-start.3
  34.9 7.3 %collective-permute-done.3.from_z = f32[640,128]{1,0:T(8,128)S(1)} collective-permute-done((f32[640,128]{1,0:T(8,128)S(1)}, f32[640,128]{1,0:T(8,128)S(1)}, u32[]{:S(2)}, u32[]{:S(2)}) %collective-permute-start.3) | collective-permute-done | bytes 327712 | tf_op jit(solution)/shard_map/ppermute | solution.py:317
  42.3 0.0 collective-permute-done.1.from_x
  42.3 0.4 collective-permute-done.2.from_y
  42.7 0.2 add.16
  42.9 23.0 %all_to_all.28 = f32[16,136,128]{2,1,0:T(8,128)S(1)} all-to-all(f32[16,136,128]{2,1,0:T(8,128)S(1)} %bitcast.17), channel_id=1, replica_groups={{0,4,34,38,64,68,98,102,130,134,160,164,194,198,224,228},{2,6,32,36,66,..., dimensions={0} | all-to-all | bytes 2228224 | tf_op jit(solution)/shard_map/all_to_all | solution.py:311
  65.8 0.1 reduce_sum.9
  65.9 3.4 %collective-permute-start.6 = (f32[136,128]{1,0:T(8,128)S(1)}, f32[136,128]{1,0:T(8,128)S(1)}, u32[]{:S(2)}, u32[]{:S(2)}) collective-permute-start(f32[136,128]{1,0:T(8,128)S(1)} %reduce_sum.9), channel_id=1, source_target_pairs={{0,24},{8,0},{16,8},{24,16},{1,25},{9,1},{17,9},{25,17},{2,26},{10... | collective-permute-start | bytes 208904 | tf_op jit(solution)/shard_map/ppermute | solution.py:361
  69.3 0.0 collective-permute-start.5
  69.3 4.2 %collective-permute-start.4 = (f32[136,128]{1,0:T(8,128)S(1)}, f32[136,128]{1,0:T(8,128)S(1)}, u32[]{:S(2)}, u32[]{:S(2)}) collective-permute-start(f32[136,128]{1,0:T(8,128)S(1)} %reduce_sum.9), channel_id=1, source_target_pairs={{0,16},{8,24},{16,0},{24,8},{1,17},{9,25},{17,1},{25,9},{2,18},{10... | collective-permute-start | bytes 208904 | tf_op jit(solution)/shard_map/ppermute | solution.py:361
  73.4 0.0 collective-permute-done.6
  73.4 1.4 %collective-permute-done.5 = f32[136,128]{1,0:T(8,128)S(1)} collective-permute-done((f32[136,128]{1,0:T(8,128)S(1)}, f32[136,128]{1,0:T(8,128)S(1)}, u32[]{:S(2)}, u32[]{:S(2)}) %collective-permute-start.5) | collective-permute-done | bytes 69664 | tf_op jit(solution)/shard_map/ppermute | solution.py:361
  74.8 1.9 %collective-permute-done.4 = f32[136,128]{1,0:T(8,128)S(1)} collective-permute-done((f32[136,128]{1,0:T(8,128)S(1)}, f32[136,128]{1,0:T(8,128)S(1)}, u32[]{:S(2)}, u32[]{:S(2)}) %collective-permute-start.4) | collective-permute-done | bytes 69664 | tf_op jit(solution)/shard_map/ppermute | solution.py:361
  76.7 0.0 copy-start.10
  76.8 0.1 broadcast_in_dim.15
  76.8 0.0 copy-start
  76.8 19.6 %all_to_all.29 = f32[16,136,128]{2,1,0:T(8,128)S(1)} all-to-all(f32[16,136,128]{2,1,0:T(8,128)S(1)} %broadcast_in_dim.15), channel_id=1, replica_groups={{0,4,34,38,64,68,98,102,130,134,160,164,194,198,224,228},{2,6,32,36,66,..., dimensions={0} | all-to-all | bytes 2228224 | tf_op jit(solution)/shard_map/all_to_all | solution.py:311
  96.4 0.1 cut.1
  96.5 0.1 collective-permute-start.7
  96.6 0.6 collective-permute-start.8
  97.2 0.4 collective-permute-start.9
  97.6 5.5 %collective-permute-done.9.from_z = f32[640,128]{1,0:T(8,128)S(1)} collective-permute-done((f32[640,128]{1,0:T(8,128)S(1)}, f32[640,128]{1,0:T(8,128)S(1)}, u32[]{:S(2)}, u32[]{:S(2)}) %collective-permute-start.9) | collective-permute-done | bytes 327712 | tf_op jit(solution)/shard_map/ppermute | solution.py:317
  103.1 0.1 collective-permute-done.7.from_x
  103.2 0.1 collective-permute-done.8.from_y
  103.3 0.0 copy-done.10
  103.3 0.0 copy-done
  103.3 2.5 %natural.1 = (f32[896,256]{1,0:T(8,128)S(1)}, f32[1,128]{1,0:T(1,128)S(1)}) custom-call(f32[2176,128]{1,0:T(8,128)S(1)} %bitcast.15, f32[768,128]{1,0:T(8,128)S(1)} %collective-permute-done.7.from_x, f32[768,128]{1,0:T(8,128)S(1)} %collective-permute-done.8.from_y, f32[640,128]{1,0:T(8,128)S(1)} %collective-permute-done.9.from_z, f32[896,896]{1,0:T(8,128)S(1)} %bitcast.18, ...), custom_call_target="tpu_custom_call" | custom-call | flops 1500000000 | bytes 5000000 | tf_op jit(solution)/shard_map/natural/pallas_call | solution.py:368
  105.8 5.8 %collective-permute-start.10 = (f32[1,128]{1,0:T(1,128)S(1)}, f32[1,128]{1,0:T(1,128)S(1)}, u32[]{:S(2)}, u32[]{:S(2)}) collective-permute-start(f32[1,128]{1,0:T(1,128)S(1)} %get-tuple-element.34.curvature), channel_id=1, source_target_pairs={{0,1},{1,0},{2,3},{3,2},{4,5},{5,4},{6,7},{7,6},{8,9},{9,8},{10,11... | collective-permute-start | bytes 1544 | tf_op jit(solution)/shard_map/ppermute | solution.py:377
  111.6 2.1 %unpack.1 = (f32[896,896]{1,0:T(8,128)}, f32[256,256]{1,0:T(8,128)}) custom-call(f32[2176,128]{1,0:T(8,128)S(1)} %bitcast.16, f32[768,128]{1,0:T(8,128)S(1)} %collective-permute-done.7.from_x, f32[768,128]{1,0:T(8,128)S(1)} %collective-permute-done.8.from_y, f32[640,128]{1,0:T(8,128)S(1)} %collective-permute-done.9.from_z), custom_call_target="tpu_custom_call" | custom-call | flops 10000000 | bytes 6000000 | tf_op jit(solution)/shard_map/unpack/pallas_call | solution.py:378
  113.8 0.0 collective-permute-done.10.other
  113.8 1.1 scale.1
  (7 shorter events, 0.0 us)
Async XLA Ops:
  0.6 1.0 copy-start.6
  1.6 0.9 copy-start.11
  2.5 0.9 copy-start.13
  3.5 0.7 copy-start.15
  4.8 12.9 %collective-permute-start = (f32[512,768]{1,0:T(8,128)S(1)}, f32[512,768]{1,0:T(8,128)S(1)}, u32[]{:S(2)}, u32[]{:S(2)}) collective-permute-start(f32[512,768]{1,0:T(8,128)S(1)} %get-tuple-element.19), channel_id=1, source_target_pairs={{0,1},{1,0},{2,3},{3,2},{4,5},{5,4},{6,7},{7,6},{8,9},{9,8},{10,11... | collective-permute-start | bytes 4718600 | tf_op jit(solution)/shard_map/ppermute | solution.py:330
  8.0 17.9 %all-to-all-start = ((f32[16,1,16]{2,1,0:T(1,128)}), f32[16,1,16]{2,1,0:T(1,128)S(1)}, u32[]{:S(2)}, u32[]{:S(2)}) async-start(f32[16,1,16]{2,1,0:T(1,128)} %bitcast.4), calls=%async_computation | async-start | bytes 16384 | tf_op jit(solution)/shard_map/all_to_all | solution.py:331
  17.7 1.1 copy-start.1
  18.9 1.4 %copy-start.2 = (f32[512,768]{1,0:T(8,128)S(1)}, f32[512,768]{1,0:T(8,128)}, u32[]{:S(2)}) copy-start(f32[512,768]{1,0:T(8,128)} %copy-done.1) | copy-start | bytes 4718596
  20.3 1.2 %copy-start.8 = (bf16[2,896,256]{2,1,0:T(8,128)(2,1)S(1)}, bf16[2,896,256]{2,1,0:T(8,128)(2,1)}, u32[]{:S(2)}) copy-start(bf16[2,896,256]{2,1,0:T(8,128)(2,1)} %weights.3) | copy-start | bytes 2752516
  21.5 0.9 copy-start.12
  22.4 0.9 copy-start.14
  23.4 2.6 %copy-start.7 = (bf16[1,16,32,256]{3,2,1,0:T(8,128)(2,1)S(1)}, bf16[1,16,32,256]{3,2,1,0:T(8,128)(2,1)}, u32[]{:S(2)}) copy-start(bf16[1,16,32,256]{3,2,1,0:T(8,128)(2,1)} %param.9) | copy-start | bytes 786436
  23.4 2.6 %copy-start.9 = (bf16[2,896,256]{2,1,0:T(8,128)(2,1)S(1)}, bf16[2,896,256]{2,1,0:T(8,128)(2,1)}, u32[]{:S(2)}) copy-start(bf16[2,896,256]{2,1,0:T(8,128)(2,1)} %weights.3) | copy-start | bytes 2752516
  23.4 2.6 %copy-start.16 = (f32[1,16]{1,0:T(1,128)S(1)}, f32[1,16]{1,0:T(1,128)}, u32[]{:S(2)}) copy-start(f32[1,16]{1,0:T(1,128)} %energy.1) | copy-start | bytes 196
  24.7 1.2 %copy-start.4 = (bf16[2,1024,384]{2,1,0:T(8,128)(2,1)}, bf16[2,1024,384]{2,1,0:T(8,128)(2,1)S(1)}, u32[]{:S(2)}) copy-start(bf16[2,1024,384]{2,1,0:T(8,128)(2,1)S(1)} %get-tuple-element.20.x_s) | copy-start | bytes 4718596
  25.9 1.4 %copy-start.3 = (f32[512,768]{1,0:T(8,128)S(1)}, f32[512,768]{1,0:T(8,128)}, u32[]{:S(2)}) copy-start(f32[512,768]{1,0:T(8,128)} %copy-done.1) | copy-start | bytes 4718596
  27.3 1.4 %copy-start.5 = (bf16[2,1024,384]{2,1,0:T(8,128)(2,1)S(1)}, bf16[2,1024,384]{2,1,0:T(8,128)(2,1)}, u32[]{:S(2)}) copy-start(bf16[2,1024,384]{2,1,0:T(8,128)(2,1)} %copy-done.4) | copy-start | bytes 4718596
  31.5 10.8 %collective-permute-start.1 = (f32[768,128]{1,0:T(8,128)S(1)}, f32[768,128]{1,0:T(8,128)S(1)}, u32[]{:S(2)}, u32[]{:S(2)}) collective-permute-start(f32[768,128]{1,0:T(8,128)S(1)} %get-tuple-element.25), channel_id=1, source_target_pairs={{0,2},{2,0},{4,6},{6,4},{1,3},{3,1},{5,7},{7,5},{8,10},{10,8},{12,... | collective-permute-start | bytes 1179656 | tf_op jit(solution)/shard_map/ppermute | solution.py:317
  32.9 9.8 %collective-permute-start.2 = (f32[768,128]{1,0:T(8,128)S(1)}, f32[768,128]{1,0:T(8,128)S(1)}, u32[]{:S(2)}, u32[]{:S(2)}) collective-permute-start(f32[768,128]{1,0:T(8,128)S(1)} %get-tuple-element.26), channel_id=1, source_target_pairs={{0,32},{32,0},{64,96},{96,64},{1,33},{33,1},{65,97},{97,65},{2,34}... | collective-permute-start | bytes 1179656 | tf_op jit(solution)/shard_map/ppermute | solution.py:317
  34.2 8.1 %collective-permute-start.3 = (f32[640,128]{1,0:T(8,128)S(1)}, f32[640,128]{1,0:T(8,128)S(1)}, u32[]{:S(2)}, u32[]{:S(2)}) collective-permute-start(f32[640,128]{1,0:T(8,128)S(1)} %get-tuple-element.27), channel_id=1, source_target_pairs={{0,128},{128,0},{1,129},{129,1},{2,130},{130,2},{3,131},{131,3},{4... | collective-permute-start | bytes 983048 | tf_op jit(solution)/shard_map/ppermute | solution.py:317
  65.9 7.5 %collective-permute-start.6 = (f32[136,128]{1,0:T(8,128)S(1)}, f32[136,128]{1,0:T(8,128)S(1)}, u32[]{:S(2)}, u32[]{:S(2)}) collective-permute-start(f32[136,128]{1,0:T(8,128)S(1)} %reduce_sum.9), channel_id=1, source_target_pairs={{0,24},{8,0},{16,8},{24,16},{1,25},{9,1},{17,9},{25,17},{2,26},{10... | collective-permute-start | bytes 208904 | tf_op jit(solution)/shard_map/ppermute | solution.py:361
  69.3 5.5 %collective-permute-start.5 = (f32[136,128]{1,0:T(8,128)S(1)}, f32[136,128]{1,0:T(8,128)S(1)}, u32[]{:S(2)}, u32[]{:S(2)}) collective-permute-start(f32[136,128]{1,0:T(8,128)S(1)} %reduce_sum.9), channel_id=1, source_target_pairs={{0,8},{8,16},{16,24},{24,0},{1,9},{9,17},{17,25},{25,1},{2,10},{10... | collective-permute-start | bytes 208904 | tf_op jit(solution)/shard_map/ppermute | solution.py:361
  69.3 7.5 %collective-permute-start.4 = (f32[136,128]{1,0:T(8,128)S(1)}, f32[136,128]{1,0:T(8,128)S(1)}, u32[]{:S(2)}, u32[]{:S(2)}) collective-permute-start(f32[136,128]{1,0:T(8,128)S(1)} %reduce_sum.9), channel_id=1, source_target_pairs={{0,16},{8,24},{16,0},{24,8},{1,17},{9,25},{17,1},{25,9},{2,18},{10... | collective-permute-start | bytes 208904 | tf_op jit(solution)/shard_map/ppermute | solution.py:361
  76.7 26.6 %copy-start.10 = (f32[1,256,256]{2,1,0:T(8,128)S(1)}, f32[1,256,256]{2,1,0:T(8,128)}, u32[]{:S(2)}) copy-start(f32[1,256,256]{2,1,0:T(8,128)} %param.15) | copy-start | bytes 786436
  76.8 26.5 %copy-start = (f32[1,896,896]{2,1,0:T(8,128)S(1)}, f32[1,896,896]{2,1,0:T(8,128)}, u32[]{:S(2)}) copy-start(f32[1,896,896]{2,1,0:T(8,128)} %param.14) | copy-start | bytes 9633796
  96.5 6.7 %collective-permute-start.7 = (f32[768,128]{1,0:T(8,128)S(1)}, f32[768,128]{1,0:T(8,128)S(1)}, u32[]{:S(2)}, u32[]{:S(2)}) collective-permute-start(f32[768,128]{1,0:T(8,128)S(1)} %get-tuple-element.28), channel_id=1, source_target_pairs={{0,2},{2,0},{4,6},{6,4},{1,3},{3,1},{5,7},{7,5},{8,10},{10,8},{12,... | collective-permute-start | bytes 1179656 | tf_op jit(solution)/shard_map/ppermute | solution.py:317
  96.6 6.7 %collective-permute-start.8 = (f32[768,128]{1,0:T(8,128)S(1)}, f32[768,128]{1,0:T(8,128)S(1)}, u32[]{:S(2)}, u32[]{:S(2)}) collective-permute-start(f32[768,128]{1,0:T(8,128)S(1)} %get-tuple-element.29), channel_id=1, source_target_pairs={{0,32},{32,0},{64,96},{96,64},{1,33},{33,1},{65,97},{97,65},{2,34}... | collective-permute-start | bytes 1179656 | tf_op jit(solution)/shard_map/ppermute | solution.py:317
  97.2 5.9 %collective-permute-start.9 = (f32[640,128]{1,0:T(8,128)S(1)}, f32[640,128]{1,0:T(8,128)S(1)}, u32[]{:S(2)}, u32[]{:S(2)}) collective-permute-start(f32[640,128]{1,0:T(8,128)S(1)} %get-tuple-element.30), channel_id=1, source_target_pairs={{0,128},{128,0},{1,129},{129,1},{2,130},{130,2},{3,131},{131,3},{4... | collective-permute-start | bytes 983048 | tf_op jit(solution)/shard_map/ppermute | solution.py:317
  105.8 7.9 %collective-permute-start.10 = (f32[1,128]{1,0:T(1,128)S(1)}, f32[1,128]{1,0:T(1,128)S(1)}, u32[]{:S(2)}, u32[]{:S(2)}) collective-permute-start(f32[1,128]{1,0:T(1,128)S(1)} %get-tuple-element.34.curvature), channel_id=1, source_target_pairs={{0,1},{1,0},{2,3},{3,2},{4,5},{5,4},{6,7},{7,6},{8,9},{9,8},{10,11... | collective-permute-start | bytes 1544 | tf_op jit(solution)/shard_map/ppermute | solution.py:377

commit v4 on v3

--- a/solution.py
+++ b/solution.py
@@ -13,7 +13,9 @@
 SLOTS = 17
 KEPT = SLOTS * B
 CHUNK = KEPT // GROUP
-STREAMS = ((0, 6), (6, 12), (12, 17))
+GRADS, FACTORS = 7, 10
+OUT_STREAMS = ((0, 5), (5, 9), (9, 12), (12, 15), (15, 17))
+BACK_STREAMS = ((0, 4), (4, 7), (7, 11), (11, 14), (14, 17))
 ENTRIES = 2 * DIN * D
 
 
@@ -52,15 +54,18 @@
     return (group == lax.broadcasted_iota(jnp.int32, (2 * WALK, ROWS), 0)).astype(BF16)
 
 
-def widen_kernel(feat, psi, pair, energies, sent, spread):
-    sent[:, :D] = feat[...].astype(F32)
-    sent[:, D : 2 * D] = psi[...].astype(F32)
-    for l in range(2):
-        sent[:, 2 * D + l * PAIR : 2 * D + (l + 1) * PAIR] = pair[l].astype(F32)
-    spread[...] = jnp.broadcast_to(energies[...], (WALK, WALK))
-
-
-def forward_kernel(feat, pair, other, weights, x_s, d_s, m_s):
+def place_of(slot):
+    if 19 <= slot < 33:
+        half, place = divmod(slot - 19, GRADS)
+        return half, place
+    half, place = divmod(slot if slot < 19 else 19, FACTORS)
+    return half, place + GRADS
+
+
+def factors_kernel(
+    feat, pair, psi, other, oth_pair, weights, gathered, energy, multiplicity,
+    keep, to_0, to_1, to_2, to_3, to_4, x_s, d_s, m_s, s_s, c_s, out
+):
     mp = lax.axis_index("c")
     own_row = pl.multiple_of(D + D * mp, D)
     oth_row = pl.multiple_of(2 * D - D * mp, D)
@@ -68,7 +73,7 @@
     x_s[0, HALF:, :D] = other[:, :D].astype(BF16)
     for l in range(2):
         x_s[l, :HALF, D:] = pair[l]
-        x_s[l, HALF:, D:] = other[:, 2 * D + l * PAIR : 2 * D + (l + 1) * PAIR].astype(BF16)
+        x_s[l, HALF:, D:] = oth_pair[l].astype(BF16)
     pick = walker_table()
     for l in range(2):
         means = (dot(pick, x_s[l, :, :D]) * (1.0 / 32.0)).astype(BF16)
@@ -87,14 +92,6 @@
             if l == 0:
                 x_s[1, rows, :D] = (x_s[0, rows, :D].astype(F32) + t).astype(BF16)
 
-
-def factors_kernel(
-    x_s, d_s, m_s, psi, other, weights, gathered, energy, multiplicity, keep, to_x, to_y, to_z, s_s, c_s, out
-):
-    mp = lax.axis_index("c")
-    own_row = pl.multiple_of(D + D * mp, D)
-    oth_row = pl.multiple_of(2 * D - D * mp, D)
-    pick = walker_table()
     s_s[1, :HALF, :] = (psi[...].astype(F32) * d_s[1, :HALF, :]).astype(BF16)
     s_s[1, HALF:, :] = (other[:, D : 2 * D] * d_s[1, HALF:, :]).astype(BF16)
     q_both = dot(pick, s_s[1])
@@ -126,8 +123,8 @@
     parity = own_parity()
 
     def put(slot, value):
-        first = slot % SLOTS * B
-        out[parity ^ (slot // SLOTS), first : first + B, :] = value * row_scale
+        half, place = place_of(slot)
+        out[parity ^ half, place * B : (place + 1) * B, :] = value * row_scale
 
     lines = {}
 
@@ -176,39 +173,39 @@
     for line, value in lines.items():
         out[parity ^ 1, last + line : last + line + 1, :] = value
     keep[...] = out[0]
-    for target, (first, end) in zip((to_x, to_y, to_z), STREAMS):
+    for target, (first, end) in zip((to_0, to_1, to_2, to_3, to_4), OUT_STREAMS):
         target[...] = out[1, first * B : end * B, :]
 
 
-def add_kernel(keep, from_x, from_y, from_z, total):
-    for part, (first, end) in zip((from_x, from_y, from_z), STREAMS):
+def add_kernel(keep, from_0, from_1, from_2, from_3, from_4, total):
+    for part, (first, end) in zip((from_0, from_1, from_2, from_3, from_4), OUT_STREAMS):
         rows = slice(first * B, end * B)
         total[rows, :] = keep[rows, :] + part[...]
 
 
-def cut_kernel(kept, to_x, to_y, to_z):
-    for target, (first, end) in zip((to_x, to_y, to_z), STREAMS):
+def cut_kernel(kept, to_0, to_1, to_2, to_3, to_4):
+    for target, (first, end) in zip((to_0, to_1, to_2, to_3, to_4), BACK_STREAMS):
         target[...] = kept[first * B : end * B, :]
 
 
-def reader(kept, parts):
+def reader(kept, parts, streams):
     parity = own_parity()
 
-    def read(slot, first=0, size=B):
-        place = slot % SLOTS
-        for part, (begin, end) in zip(parts, STREAMS):
+    def read(slot, size=B):
+        half, place = place_of(slot)
+        for part, (begin, end) in zip(parts, streams):
             if begin <= place < end:
-                other = part[(place - begin) * B + first : (place - begin) * B + first + size, :]
-        own = kept[place * B + first : place * B + first + size, :]
-        return jnp.where(parity == slot // SLOTS, own, other)
+                other = part[(place - begin) * B : (place - begin) * B + size, :]
+        own = kept[place * B : place * B + size, :]
+        return jnp.where(parity == half, own, other)
 
     return read
 
 
-def unpack_kernel(kept, from_x, from_y, from_z, a_out, s_out):
+def unpack_kernel(kept, from_2, from_3, from_4, a_out, s_out):
     row, col = square_iotas()
-    read = reader(kept, (from_x, from_y, from_z))
-    lines = read(33, 0, 8)
+    read = reader(kept, (from_2, from_3, from_4), BACK_STREAMS[2:])
+    lines = read(33, 8)
     inverse = 1.0 / lines[4:5, :]
 
     def get(slot):
@@ -254,8 +251,8 @@
         place(a_out, 6, i, block.T)
 
 
-def natural_kernel(kept, from_x, from_y, from_z, a_inverse, s_inverse, natural, curvature):
-    get = reader(kept, (from_x, from_y, from_z))
+def natural_kernel(kept, from_0, from_1, a_inverse, s_inverse, natural, curvature):
+    get = reader(kept, (from_0, from_1), BACK_STREAMS[:2])
 
     grad = jnp.concatenate(
         [jnp.concatenate([get(19 + 2 * i), get(20 + 2 * i)], 1) for i in range(7)], 0
@@ -312,9 +309,13 @@
 
 
 def to_neighbours(parts):
-    pairs = {"x": [(0, 1), (1, 0), (2, 3), (3, 2)], "zl": [(0, 1), (1, 0)]}
-    pairs["y"] = pairs["x"]
-    return [lax.ppermute(part, axis, pairs[axis]) for part, axis in zip(parts, ("x", "y", "zl"))]
+    low, high = [(0, 1), (1, 0), (2, 3), (3, 2)], [(1, 2), (2, 1), (3, 0), (0, 3)]
+    ways = (("x", low), ("y", low), ("zl", [(0, 1), (1, 0)]), ("x", high), ("y", high))
+    return [lax.ppermute(part, axis, pairs) for part, (axis, pairs) in zip(parts, ways)]
+
+
+def streams_of(streams):
+    return [(((end - first) * B, B), F32) for first, end in streams]
 
 
 def body(features, psi_grad, pair_means, energies, multiplicity, weights, a_inverse, s_inverse):
@@ -322,58 +323,50 @@
     psi = psi_grad.reshape(HALF, D)
     pair = pair_means.reshape(2, HALF, PAIR)
     swap = [(0, 1), (1, 0)]
-    streams = [(((end - first) * B, B), F32) for first, end in STREAMS]
-
-    sent, spread = call(
-        widen_kernel, [((HALF, 3 * D), F32), ((WALK, WALK), F32)], [V] * 4, 6, "widen", moved=2_400_000
-    )(feat, psi, pair, energies)
-    other = lax.ppermute(sent, "c", swap)
+
+    other = lax.ppermute(jnp.concatenate([feat, psi], 1).astype(F32), "c", swap)
+    oth_pair = lax.ppermute(pair.astype(F32), "c", swap)
+    spread = jnp.broadcast_to(energies, (WALK, WALK))
     gathered = lax.all_to_all(spread, ("zh", "x"), 0, 0, tiled=True)
 
-    x_s, d_s, m_s = call(
-        forward_kernel,
-        [((2, ROWS, D + PAIR), BF16), ((2, ROWS, D), F32), ((2, 2 * WALK, D), BF16)],
-        [V] * 4,
-        16,
-        "forward",
-        flops=1_000_000_000,
-        moved=6_000_000,
-    )(feat, pair, other, weights)
     keep, *parts = call(
         factors_kernel,
-        [((KEPT, B), F32)] + streams,
+        [((KEPT, B), F32)] + streams_of(OUT_STREAMS),
         [V] * 7 + [S] * 2,
-        22,
+        24,
         "factors",
         scratch=[
+            pltpu.VMEM((2, ROWS, D + PAIR), BF16),
+            pltpu.VMEM((2, ROWS, D), F32),
+            pltpu.VMEM((2, 2 * WALK, D), BF16),
             pltpu.VMEM((2, ROWS, D), BF16),
             pltpu.VMEM((ROWS, D), BF16),
             pltpu.VMEM((2, KEPT, B), F32),
         ],
-        flops=1_500_000_000,
+        flops=2_500_000_000,
         moved=8_000_000,
-    )(x_s, d_s, m_s, psi, other, weights, gathered, energies, multiplicity)
+    )(feat, pair, psi, other, oth_pair, weights, gathered, energies, multiplicity)
 
     parts = to_neighbours(parts)
-    (total,) = call(add_kernel, [((KEPT, B), F32)], [V] * 4, 6, "add", moved=3_000_000)(keep, *parts)
+    (total,) = call(add_kernel, [((KEPT, B), F32)], [V] * 6, 6, "add", moved=3_000_000)(keep, *parts)
     mine = jnp.sum(same_parity(total).reshape(GROUP, CHUNK, B), axis=0)
     one, two, three = (
         lax.ppermute(mine, "zh", [(i, (i + k) % 4) for i in range(4)]) for k in (1, 2, 3)
     )
     mine = (mine + two) + (one + three)
     kept = same_parity(jnp.broadcast_to(mine[None], (GROUP, CHUNK, B)).reshape(KEPT, B))
-    parts = call(cut_kernel, streams, [V], 6, "cut", moved=2_200_000)(kept)
+    parts = call(cut_kernel, streams_of(BACK_STREAMS), [V], 6, "cut", moved=2_200_000)(kept)
     parts = to_neighbours(parts)
 
     natural, curvature = call(
         natural_kernel,
         [((DIN, D), F32), ((1, B), F32)],
-        [V] * 6,
+        [V] * 5,
         18,
         "natural",
         flops=1_500_000_000,
         moved=5_000_000,
-    )(kept, *parts, a_inverse[0], s_inverse[0])
+    )(kept, *parts[:2], a_inverse[0], s_inverse[0])
     other = lax.ppermute(curvature, "c", swap)
     a_sum, s_sum = call(
         unpack_kernel,
@@ -383,7 +376,7 @@
         "unpack",
         flops=10_000_000,
         moved=6_000_000,
-    )(kept, *parts)
+    )(kept, *parts[2:])
     (direction,) = call(
         scale_kernel, [((DIN, D), F32)], [V] * 3, 6, "scale", flops=1_000_000, moved=2_000_000
     )(natural, curvature, other)

time: 115 us -> 109 us (0.948)
  local copies, waits for them, and re-layouts: 13.2 us -> 0.71 us
  waiting for transfers between devices: 16.8 us -> 22.3 us
  blocking collectives: 42.6 us -> 37.5 us
  starting transfers between devices: 30.1 us -> 34 us
  other arithmetic: 0.08 us -> 3.16 us
    unnamed x34 -> x14, local copies, waits for them, and re-layouts: 13.1 us -> 0.03 us
    all_to_all x1, waiting for transfers between devices: 0.01 us -> 8.09 us  [body(): gathered = lax.all_to_all(spread, ('zh', 'x'), 0, 0, tiled=True)]
    ppermute x7 -> x12, waiting for transfers between devices: 13.5 us -> 6.81 us  [the longest x10 6.81 us: to_neighbours(): lax.ppermute(part, axis, pairs)]
    all_to_all x2, blocking collectives: 42.6 us -> 37.5 us  [same_parity(): lax.all_to_all(value, axes, 0, 0, axis_index_groups=parity_groups(), tile...]
    ppermute x1, starting transfers between devices: 5.8 us -> 10.2 us  [body(): other = lax.ppermute(curvature, 'c', swap)]
    ppermute x3, waiting for transfers between devices: 3.29 us -> 7.35 us  [body(): lax.ppermute(mine, 'zh', [(i, (i + k) % 4) for i in range(4)])]
    ppermute x3, starting transfers between devices: 7.53 us -> 3.97 us  [body(): lax.ppermute(mine, 'zh', [(i, (i + k) % 4) for i in range(4)])]
    ppermute x7 -> x12, starting transfers between devices: 7.79 us -> 10.9 us  [the longest x10 7.65 us: to_neighbours(): lax.ppermute(part, axis, pairs)]
  transfers between devices with their start and end apart: 12 -> 17, of which waited for: 7 -> 7; matrix products, arithmetic and copies ran while one was open for 0% -> 1% of each run, Pallas kernels for 3% -> 4%
where the time goes in v4:
time: 109 us
  blocking collectives  37.5 us (34%)
  starting transfers between devices  34 us (31%)
  waiting for transfers between devices  22.3 us (20%)
  Pallas kernels  10 us (9%)
  other arithmetic  3.16 us (3%)
  between operations  1.43 us (1%)
    all_to_all x2, blocking collectives, same_parity(): lax.all_to_all(value, axes, 0, 0, axis_index_groups=parity_groups(), tile...  37.5 us
    ppermute x1, starting transfers between devices, body(): other = lax.ppermute(curvature, 'c', swap)  10.2 us
    all_to_all x1, starting transfers between devices, body(): gathered = lax.all_to_all(spread, ('zh', 'x'), 0, 0, tiled=True)  9.01 us
    all_to_all x1, waiting for transfers between devices, body(): gathered = lax.all_to_all(spread, ('zh', 'x'), 0, 0, tiled=True)  8.09 us
    ppermute x10, starting transfers between devices, to_neighbours(): lax.ppermute(part, axis, pairs)  7.65 us
    ppermute x3, waiting for transfers between devices, body(): lax.ppermute(mine, 'zh', [(i, (i + k) % 4) for i in range(4)])  7.35 us
    ppermute x10, waiting for transfers between devices, to_neighbours(): lax.ppermute(part, axis, pairs)  6.81 us
    pallas_call x1, Pallas kernels, body(): call(factors_kernel, [((KEPT, B), F32)] + streams_of(OUT_STREAMS), [V] *...  4.1 us
  transfers between devices with their start and end apart: 17, of which 7 were waited for; matrix products, arithmetic and copies ran while one was open for 1% of the time, Pallas kernels for 4%

profile of v4, /device:TPU:1, one launch (start us, length us, event | category | flops | bytes accessed | tf_op | source)
XLA Modules:
  0.0 109.1 jit_solution(11886872790445233196)
XLA Ops:
  0.6 0.0 copy-start
  0.6 0.0 copy-start.3
  0.7 0.0 copy-start.1
  0.7 0.0 copy-start.2
  0.7 0.0 copy-start.5
  0.7 2.2 %maximum_convert_fusion = f32[512,512]{1,0:T(8,128)} fusion(bf16[512,256]{1,0:T(8,128)(2,1)} %bitcast.20, bf16[512,256]{1,0:T(8,128)(2,1)} %bitcast.18), kind=kLoop, calls=%fused_computation | loop fusion | flops 1048576 | bytes 1572864 | tf_op jit(solution)/shard_map/convert_element_type | solution.py:327
  2.9 3.2 %collective-permute-start = (f32[512,512]{1,0:T(8,128)}, f32[512,512]{1,0:T(8,128)S(1)}, u32[]{:S(2)}, u32[]{:S(2)}) collective-permute-start(f32[512,512]{1,0:T(8,128)} %maximum_convert_fusion), channel_id=1, source_target_pairs={{0,1},{1,0},{2,3},{3,2},{4,5},{5,4},{6,7},{7,6},{8,9},{9,8},{10,11... | collective-permute-start | bytes 3145736 | tf_op jit(solution)/shard_map/ppermute | solution.py:327
  6.2 0.0 copy-done
  6.2 0.8 convert_element_type.7
  7.0 0.0 collective-permute-start.1
  7.0 0.0 copy-done.3
  7.0 0.6 broadcast_in_dim.20
  7.6 9.0 %all-to-all-start = ((f32[16,1,16]{2,1,0:T(1,128)}), f32[16,1,16]{2,1,0:T(1,128)S(1)}, u32[]{:S(2)}, u32[]{:S(2)}) async-start(f32[16,1,16]{2,1,0:T(1,128)} %broadcast_in_dim.20), calls=%async_computation | async-start | bytes 16384 | tf_op jit(solution)/shard_map/all_to_all | solution.py:330
  17.3 8.1 %all-to-all-done = f32[16,1,16]{2,1,0:T(1,128)S(1)} async-done(((f32[16,1,16]{2,1,0:T(1,128)}), f32[16,1,16]{2,1,0:T(1,128)S(1)}, u32[]{:S(2)}, u32[]{:S(2)}) %all-to-all-start) | async-done | bytes 1056 | tf_op jit(solution)/shard_map/all_to_all | solution.py:330
  25.4 0.0 collective-permute-done.1.oth_pair
  25.4 0.0 collective-permute-done.other
  25.4 0.0 copy-done.1
  25.4 0.0 copy-done.2
  25.4 0.0 copy-done.5
  25.4 4.1 %factors.1 = (f32[2176,128]{1,0:T(8,128)S(1)}, f32[640,128]{1,0:T(8,128)S(1)}, f32[512,128]{1,0:T(8,128)S(1)}, f32[384,128]{1,0:T(8,128)S(1)}, f32[384,128]{1,0:T(8,128)S(1)}, /*index=5*/f32[256,128]{1,0:T(8,128)S(1)}) custom-call(bf16[512,256]{1,0:T(8,128)(2,1)S(1)} %bitcast.19, bf16[2,512,128]{2,1,0:T(8,128)(2,1)S(1)} %bitcast.17, ...), custom_call_target="tpu_custom_call" | custom-call | flops 2500000000 | bytes 8000000 | tf_op jit(solution)/shard_map/factors/pallas_call | solution.py:332
  29.5 0.4 collective-permute-start.2
  29.9 1.3 %collective-permute-start.3 = (f32[512,128]{1,0:T(8,128)S(1)}, f32[512,128]{1,0:T(8,128)S(1)}, u32[]{:S(2)}, u32[]{:S(2)}) collective-permute-start(f32[512,128]{1,0:T(8,128)S(1)} %get-tuple-element.20), channel_id=1, source_target_pairs={{0,32},{32,0},{64,96},{96,64},{1,33},{33,1},{65,97},{97,65},{2,34}... | collective-permute-start | bytes 786440 | tf_op jit(solution)/shard_map/ppermute | solution.py:314
  31.2 0.7 collective-permute-start.4
  31.9 0.9 collective-permute-start.5
  32.8 1.9 %collective-permute-start.6 = (f32[256,128]{1,0:T(8,128)S(1)}, f32[256,128]{1,0:T(8,128)S(1)}, u32[]{:S(2)}, u32[]{:S(2)}) collective-permute-start(f32[256,128]{1,0:T(8,128)S(1)} %get-tuple-element.23), channel_id=1, source_target_pairs={{32,64},{64,32},{96,0},{0,96},{33,65},{65,33},{97,1},{1,97},{34,66... | collective-permute-start | bytes 393224 | tf_op jit(solution)/shard_map/ppermute | solution.py:314
  34.7 3.1 %collective-permute-done.6.from_4 = f32[256,128]{1,0:T(8,128)S(1)} collective-permute-done((f32[256,128]{1,0:T(8,128)S(1)}, f32[256,128]{1,0:T(8,128)S(1)}, u32[]{:S(2)}, u32[]{:S(2)}) %collective-permute-start.6) | collective-permute-done | bytes 131104 | tf_op jit(solution)/shard_map/ppermute | solution.py:314
  37.9 0.0 collective-permute-done.4.from_2
  37.9 0.0 collective-permute-done.5.from_3
  37.9 0.0 collective-permute-done.3.from_1
  37.9 0.0 collective-permute-done.2.from_0
  37.9 0.2 add.16
  38.1 19.6 %all_to_all.25 = f32[16,136,128]{2,1,0:T(8,128)S(1)} all-to-all(f32[16,136,128]{2,1,0:T(8,128)S(1)} %bitcast.15), channel_id=1, replica_groups={{0,4,34,38,64,68,98,102,130,134,160,164,194,198,224,228},{2,6,32,36,66,..., dimensions={0} | all-to-all | bytes 2228224 | tf_op jit(solution)/shard_map/all_to_all | solution.py:308
  57.6 0.1 reduce_sum.9
  57.7 0.4 collective-permute-start.8
  58.0 3.3 %collective-permute-start.9 = (f32[136,128]{1,0:T(8,128)S(1)}, f32[136,128]{1,0:T(8,128)S(1)}, u32[]{:S(2)}, u32[]{:S(2)}) collective-permute-start(f32[136,128]{1,0:T(8,128)S(1)} %reduce_sum.9), channel_id=1, source_target_pairs={{0,24},{8,0},{16,8},{24,16},{1,25},{9,1},{17,9},{25,17},{2,26},{10... | collective-permute-start | bytes 208904 | tf_op jit(solution)/shard_map/ppermute | solution.py:354
  61.3 0.3 collective-permute-start.7
  61.6 1.6 %collective-permute-done.8 = f32[136,128]{1,0:T(8,128)S(1)} collective-permute-done((f32[136,128]{1,0:T(8,128)S(1)}, f32[136,128]{1,0:T(8,128)S(1)}, u32[]{:S(2)}, u32[]{:S(2)}) %collective-permute-start.8) | collective-permute-done | bytes 69664 | tf_op jit(solution)/shard_map/ppermute | solution.py:354
  63.2 0.8 collective-permute-done.9
  64.1 4.9 %collective-permute-done.7 = f32[136,128]{1,0:T(8,128)S(1)} collective-permute-done((f32[136,128]{1,0:T(8,128)S(1)}, f32[136,128]{1,0:T(8,128)S(1)}, u32[]{:S(2)}, u32[]{:S(2)}) %collective-permute-start.7) | collective-permute-done | bytes 69664 | tf_op jit(solution)/shard_map/ppermute | solution.py:354
  69.0 0.0 copy-start.6
  69.0 0.1 broadcast_in_dim.21
  69.1 0.0 copy-start.4
  69.1 18.0 %all_to_all.26 = f32[16,136,128]{2,1,0:T(8,128)S(1)} all-to-all(f32[16,136,128]{2,1,0:T(8,128)S(1)} %broadcast_in_dim.21), channel_id=1, replica_groups={{0,4,34,38,64,68,98,102,130,134,160,164,194,198,224,228},{2,6,32,36,66,..., dimensions={0} | all-to-all | bytes 2228224 | tf_op jit(solution)/shard_map/all_to_all | solution.py:308
  87.1 0.1 cut.1
  87.2 0.1 collective-permute-start.13
  87.3 0.2 collective-permute-start.14
  87.5 0.2 collective-permute-start.10
  87.7 0.9 collective-permute-start.11
  88.6 1.0 collective-permute-start.12
  89.6 3.4 %collective-permute-done.14.from_1 = f32[384,128]{1,0:T(8,128)S(1)} collective-permute-done((f32[384,128]{1,0:T(8,128)S(1)}, f32[384,128]{1,0:T(8,128)S(1)}, u32[]{:S(2)}, u32[]{:S(2)}) %collective-permute-start.14) | collective-permute-done | bytes 196640 | tf_op jit(solution)/shard_map/ppermute | solution.py:314
  93.0 0.3 collective-permute-done.13.from_0
  93.3 0.0 copy-done.6
  93.3 0.0 copy-done.4
  93.3 2.5 %natural.1 = (f32[896,256]{1,0:T(8,128)S(1)}, f32[1,128]{1,0:T(1,128)S(1)}) custom-call(f32[2176,128]{1,0:T(8,128)S(1)} %bitcast.13, f32[512,128]{1,0:T(8,128)S(1)} %collective-permute-done.13.from_0, f32[384,128]{1,0:T(8,128)S(1)} %collective-permute-done.14.from_1, f32[896,896]{1,0:T(8,128)S(1)} %bitcast.24, f32[256,256]{1,0:T(8,128)S(1)} %bitcast.25), custom_call_target="tpu_custom_call" | custom-call | flops 1500000000 | bytes 5000000 | tf_op jit(solution)/shard_map/natural/pallas_call | solution.py:361
  95.8 10.2 %collective-permute-start.15 = (f32[1,128]{1,0:T(1,128)S(1)}, f32[1,128]{1,0:T(1,128)S(1)}, u32[]{:S(2)}, u32[]{:S(2)}) collective-permute-start(f32[1,128]{1,0:T(1,128)S(1)} %get-tuple-element.32.curvature), channel_id=1, source_target_pairs={{0,1},{1,0},{2,3},{3,2},{4,5},{5,4},{6,7},{7,6},{8,9},{9,8},{10,11... | collective-permute-start | bytes 1544 | tf_op jit(solution)/shard_map/ppermute | solution.py:370
  105.9 0.0 collective-permute-done.11.from_3
  105.9 0.0 collective-permute-done.12.from_4
  105.9 0.0 collective-permute-done.10.from_2
  105.9 2.1 %unpack.1 = (f32[896,896]{1,0:T(8,128)}, f32[256,256]{1,0:T(8,128)}) custom-call(f32[2176,128]{1,0:T(8,128)S(1)} %bitcast.14, f32[512,128]{1,0:T(8,128)S(1)} %collective-permute-done.10.from_2, f32[384,128]{1,0:T(8,128)S(1)} %collective-permute-done.11.from_3, f32[384,128]{1,0:T(8,128)S(1)} %collective-permute-done.12.from_4), custom_call_target="tpu_custom_call" | custom-call | flops 10000000 | bytes 6000000 | tf_op jit(solution)/shard_map/unpack/pallas_call | solution.py:371
  108.1 0.0 collective-permute-done.15.other
  108.1 1.1 scale.1
  (1 shorter events, 0.0 us)
Async XLA Ops:
  0.6 5.5 %copy-start = (bf16[1,2,16,32,128]{4,3,2,1,0:T(8,128)(2,1)S(1)}, bf16[1,2,16,32,128]{4,3,2,1,0:T(8,128)(2,1)}, u32[]{:S(2)}) copy-start(bf16[1,2,16,32,128]{4,3,2,1,0:T(8,128)(2,1)} %param.10) | copy-start | bytes 786436
  0.6 6.4 %copy-start.3 = (f32[1,16]{1,0:T(1,128)S(1)}, f32[1,16]{1,0:T(1,128)}, u32[]{:S(2)}) copy-start(f32[1,16]{1,0:T(1,128)} %energy.1) | copy-start | bytes 196
  0.7 24.7 %copy-start.1 = (bf16[1,16,32,256]{3,2,1,0:T(8,128)(2,1)S(1)}, bf16[1,16,32,256]{3,2,1,0:T(8,128)(2,1)}, u32[]{:S(2)}) copy-start(bf16[1,16,32,256]{3,2,1,0:T(8,128)(2,1)} %param.8) | copy-start | bytes 786436
  0.7 24.7 %copy-start.2 = (bf16[1,16,32,256]{3,2,1,0:T(8,128)(2,1)S(1)}, bf16[1,16,32,256]{3,2,1,0:T(8,128)(2,1)}, u32[]{:S(2)}) copy-start(bf16[1,16,32,256]{3,2,1,0:T(8,128)(2,1)} %param.9) | copy-start | bytes 786436
  0.7 24.7 %copy-start.5 = (bf16[2,896,256]{2,1,0:T(8,128)(2,1)S(1)}, bf16[2,896,256]{2,1,0:T(8,128)(2,1)}, u32[]{:S(2)}) copy-start(bf16[2,896,256]{2,1,0:T(8,128)(2,1)} %weights.1) | copy-start | bytes 2752516
  2.9 22.4 %collective-permute-start = (f32[512,512]{1,0:T(8,128)}, f32[512,512]{1,0:T(8,128)S(1)}, u32[]{:S(2)}, u32[]{:S(2)}) collective-permute-start(f32[512,512]{1,0:T(8,128)} %maximum_convert_fusion), channel_id=1, source_target_pairs={{0,1},{1,0},{2,3},{3,2},{4,5},{5,4},{6,7},{7,6},{8,9},{9,8},{10,11... | collective-permute-start | bytes 3145736 | tf_op jit(solution)/shard_map/ppermute | solution.py:327
  7.0 18.4 %collective-permute-start.1 = (f32[2,512,128]{2,1,0:T(8,128)}, f32[2,512,128]{2,1,0:T(8,128)S(1)}, u32[]{:S(2)}, u32[]{:S(2)}) collective-permute-start(f32[2,512,128]{2,1,0:T(8,128)} %convert_element_type.7), channel_id=1, source_target_pairs={{0,1},{1,0},{2,3},{3,2},{4,5},{5,4},{6,7},{7,6},{8,9},{9,8},{10,11... | collective-permute-start | bytes 1572872 | tf_op jit(solution)/shard_map/ppermute | solution.py:328
  7.6 17.8 %all-to-all-start = ((f32[16,1,16]{2,1,0:T(1,128)}), f32[16,1,16]{2,1,0:T(1,128)S(1)}, u32[]{:S(2)}, u32[]{:S(2)}) async-start(f32[16,1,16]{2,1,0:T(1,128)} %broadcast_in_dim.20), calls=%async_computation | async-start | bytes 16384 | tf_op jit(solution)/shard_map/all_to_all | solution.py:330
  29.5 8.4 %collective-permute-start.2 = (f32[640,128]{1,0:T(8,128)S(1)}, f32[640,128]{1,0:T(8,128)S(1)}, u32[]{:S(2)}, u32[]{:S(2)}) collective-permute-start(f32[640,128]{1,0:T(8,128)S(1)} %get-tuple-element.19), channel_id=1, source_target_pairs={{0,2},{2,0},{4,6},{6,4},{1,3},{3,1},{5,7},{7,5},{8,10},{10,8},{12,... | collective-permute-start | bytes 983048 | tf_op jit(solution)/shard_map/ppermute | solution.py:314
  29.9 8.0 %collective-permute-start.3 = (f32[512,128]{1,0:T(8,128)S(1)}, f32[512,128]{1,0:T(8,128)S(1)}, u32[]{:S(2)}, u32[]{:S(2)}) collective-permute-start(f32[512,128]{1,0:T(8,128)S(1)} %get-tuple-element.20), channel_id=1, source_target_pairs={{0,32},{32,0},{64,96},{96,64},{1,33},{33,1},{65,97},{97,65},{2,34}... | collective-permute-start | bytes 786440 | tf_op jit(solution)/shard_map/ppermute | solution.py:314
  31.2 6.7 %collective-permute-start.4 = (f32[384,128]{1,0:T(8,128)S(1)}, f32[384,128]{1,0:T(8,128)S(1)}, u32[]{:S(2)}, u32[]{:S(2)}) collective-permute-start(f32[384,128]{1,0:T(8,128)S(1)} %get-tuple-element.21), channel_id=1, source_target_pairs={{0,128},{128,0},{1,129},{129,1},{2,130},{130,2},{3,131},{131,3},{4... | collective-permute-start | bytes 589832 | tf_op jit(solution)/shard_map/ppermute | solution.py:314
  31.9 6.0 %collective-permute-start.5 = (f32[384,128]{1,0:T(8,128)S(1)}, f32[384,128]{1,0:T(8,128)S(1)}, u32[]{:S(2)}, u32[]{:S(2)}) collective-permute-start(f32[384,128]{1,0:T(8,128)S(1)} %get-tuple-element.22), channel_id=1, source_target_pairs={{2,4},{4,2},{6,0},{0,6},{3,5},{5,3},{7,1},{1,7},{10,12},{12,10},{1... | collective-permute-start | bytes 589832 | tf_op jit(solution)/shard_map/ppermute | solution.py:314
  32.8 5.0 %collective-permute-start.6 = (f32[256,128]{1,0:T(8,128)S(1)}, f32[256,128]{1,0:T(8,128)S(1)}, u32[]{:S(2)}, u32[]{:S(2)}) collective-permute-start(f32[256,128]{1,0:T(8,128)S(1)} %get-tuple-element.23), channel_id=1, source_target_pairs={{32,64},{64,32},{96,0},{0,96},{33,65},{65,33},{97,1},{1,97},{34,66... | collective-permute-start | bytes 393224 | tf_op jit(solution)/shard_map/ppermute | solution.py:314
  57.7 5.6 %collective-permute-start.8 = (f32[136,128]{1,0:T(8,128)S(1)}, f32[136,128]{1,0:T(8,128)S(1)}, u32[]{:S(2)}, u32[]{:S(2)}) collective-permute-start(f32[136,128]{1,0:T(8,128)S(1)} %reduce_sum.9), channel_id=1, source_target_pairs={{0,8},{8,16},{16,24},{24,0},{1,9},{9,17},{17,25},{25,1},{2,10},{10... | collective-permute-start | bytes 208904 | tf_op jit(solution)/shard_map/ppermute | solution.py:354
  58.0 6.0 %collective-permute-start.9 = (f32[136,128]{1,0:T(8,128)S(1)}, f32[136,128]{1,0:T(8,128)S(1)}, u32[]{:S(2)}, u32[]{:S(2)}) collective-permute-start(f32[136,128]{1,0:T(8,128)S(1)} %reduce_sum.9), channel_id=1, source_target_pairs={{0,24},{8,0},{16,8},{24,16},{1,25},{9,1},{17,9},{25,17},{2,26},{10... | collective-permute-start | bytes 208904 | tf_op jit(solution)/shard_map/ppermute | solution.py:354
  61.3 7.7 %collective-permute-start.7 = (f32[136,128]{1,0:T(8,128)S(1)}, f32[136,128]{1,0:T(8,128)S(1)}, u32[]{:S(2)}, u32[]{:S(2)}) collective-permute-start(f32[136,128]{1,0:T(8,128)S(1)} %reduce_sum.9), channel_id=1, source_target_pairs={{0,16},{8,24},{16,0},{24,8},{1,17},{9,25},{17,1},{25,9},{2,18},{10... | collective-permute-start | bytes 208904 | tf_op jit(solution)/shard_map/ppermute | solution.py:354
  69.0 24.3 %copy-start.6 = (f32[1,256,256]{2,1,0:T(8,128)S(1)}, f32[1,256,256]{2,1,0:T(8,128)}, u32[]{:S(2)}) copy-start(f32[1,256,256]{2,1,0:T(8,128)} %param.15) | copy-start | bytes 786436
  69.1 24.2 %copy-start.4 = (f32[1,896,896]{2,1,0:T(8,128)S(1)}, f32[1,896,896]{2,1,0:T(8,128)}, u32[]{:S(2)}) copy-start(f32[1,896,896]{2,1,0:T(8,128)} %param.14) | copy-start | bytes 9633796
  87.2 6.1 %collective-permute-start.13 = (f32[512,128]{1,0:T(8,128)S(1)}, f32[512,128]{1,0:T(8,128)S(1)}, u32[]{:S(2)}, u32[]{:S(2)}) collective-permute-start(f32[512,128]{1,0:T(8,128)S(1)} %get-tuple-element.29), channel_id=1, source_target_pairs={{0,2},{2,0},{4,6},{6,4},{1,3},{3,1},{5,7},{7,5},{8,10},{10,8},{12,... | collective-permute-start | bytes 786440 | tf_op jit(solution)/shard_map/ppermute | solution.py:314
  87.3 5.7 %collective-permute-start.14 = (f32[384,128]{1,0:T(8,128)S(1)}, f32[384,128]{1,0:T(8,128)S(1)}, u32[]{:S(2)}, u32[]{:S(2)}) collective-permute-start(f32[384,128]{1,0:T(8,128)S(1)} %get-tuple-element.30), channel_id=1, source_target_pairs={{0,32},{32,0},{64,96},{96,64},{1,33},{33,1},{65,97},{97,65},{2,34}... | collective-permute-start | bytes 589832 | tf_op jit(solution)/shard_map/ppermute | solution.py:314
  87.5 18.4 %collective-permute-start.10 = (f32[512,128]{1,0:T(8,128)S(1)}, f32[512,128]{1,0:T(8,128)S(1)}, u32[]{:S(2)}, u32[]{:S(2)}) collective-permute-start(f32[512,128]{1,0:T(8,128)S(1)} %get-tuple-element.24), channel_id=1, source_target_pairs={{0,128},{128,0},{1,129},{129,1},{2,130},{130,2},{3,131},{131,3},{4... | collective-permute-start | bytes 786440 | tf_op jit(solution)/shard_map/ppermute | solution.py:314
  87.7 18.2 %collective-permute-start.11 = (f32[384,128]{1,0:T(8,128)S(1)}, f32[384,128]{1,0:T(8,128)S(1)}, u32[]{:S(2)}, u32[]{:S(2)}) collective-permute-start(f32[384,128]{1,0:T(8,128)S(1)} %get-tuple-element.25), channel_id=1, source_target_pairs={{2,4},{4,2},{6,0},{0,6},{3,5},{5,3},{7,1},{1,7},{10,12},{12,10},{1... | collective-permute-start | bytes 589832 | tf_op jit(solution)/shard_map/ppermute | solution.py:314
  88.6 17.3 %collective-permute-start.12 = (f32[384,128]{1,0:T(8,128)S(1)}, f32[384,128]{1,0:T(8,128)S(1)}, u32[]{:S(2)}, u32[]{:S(2)}) collective-permute-start(f32[384,128]{1,0:T(8,128)S(1)} %get-tuple-element.26), channel_id=1, source_target_pairs={{32,64},{64,32},{96,0},{0,96},{33,65},{65,33},{97,1},{1,97},{34,66... | collective-permute-start | bytes 589832 | tf_op jit(solution)/shard_map/ppermute | solution.py:314
  95.8 12.3 %collective-permute-start.15 = (f32[1,128]{1,0:T(1,128)S(1)}, f32[1,128]{1,0:T(1,128)S(1)}, u32[]{:S(2)}, u32[]{:S(2)}) collective-permute-start(f32[1,128]{1,0:T(1,128)S(1)} %get-tuple-element.32.curvature), channel_id=1, source_target_pairs={{0,1},{1,0},{2,3},{3,2},{4,5},{5,4},{6,7},{7,6},{8,9},{9,8},{10,11... | collective-permute-start | bytes 1544 | tf_op jit(solution)/shard_map/ppermute | solution.py:370

commit v5 on v4

--- a/solution.py
+++ b/solution.py
@@ -14,9 +14,10 @@
 KEPT = SLOTS * B
 CHUNK = KEPT // GROUP
 GRADS, FACTORS = 7, 10
-OUT_STREAMS = ((0, 5), (5, 9), (9, 12), (12, 15), (15, 17))
+OUT_STREAMS = ((7, 12), (12, 17))
 BACK_STREAMS = ((0, 4), (4, 7), (7, 11), (11, 14), (14, 17))
 ENTRIES = 2 * DIN * D
+SHIFT = 7.0
 
 
 def dot_t(a, b):
@@ -63,8 +64,8 @@
 
 
 def factors_kernel(
-    feat, pair, psi, other, oth_pair, weights, gathered, energy, multiplicity,
-    keep, to_0, to_1, to_2, to_3, to_4, x_s, d_s, m_s, s_s, c_s, out
+    feat, pair, psi, other, oth_pair, weights, half_sum, half_other, energies, energy, multiplicity,
+    keep, keep_0, to_a, to_0, to_2, to_3, row_sum, x_s, d_s, m_s, s_s, c_s, out, out_0
 ):
     mp = lax.axis_index("c")
     own_row = pl.multiple_of(D + D * mp, D)
@@ -109,7 +110,10 @@
     row_scale = mult * (1.0 / 16384.0)
     x = x_s[l]
     s = s_s[l]
-    mean = jnp.sum(jnp.sum(gathered[...], axis=0, keepdims=True), axis=1, keepdims=True) * (1.0 / 256.0)
+    mean = jnp.sum(energies[...], axis=1, keepdims=True) * (1.0 / WALK)
+    shifted = mean + SHIFT
+    zh_sum = jnp.sum(half_sum[...] + half_other[...], axis=1, keepdims=True)
+    row_sum[...] = jnp.broadcast_to(zh_sum, (8, B))
     step = HALF // WALK
     for w in range(WALK):
         centered = energy[0, w] - mean
@@ -126,6 +130,12 @@
         half, place = place_of(slot)
         out[parity ^ half, place * B : (place + 1) * B, :] = value * row_scale
 
+    def put_grad(slot, centered, plain):
+        half, place = place_of(slot)
+        rows = slice(place * B, (place + 1) * B)
+        out[parity ^ half, rows, :] = (centered + shifted * plain) * row_scale
+        out_0[parity ^ half, rows, :] = plain * row_scale
+
     lines = {}
 
     def put_symmetric(slot, line, full):
@@ -139,13 +149,13 @@
     put(11, hp[:B])
     put(12, hp[B:])
     put(10, dot_t(p, p))
-    hc = dot_t(h, c)
-    pc = dot_t(p, c)
+    hc, hs = dot_t(h, c), dot_t(h, s)
+    pc, ps = dot_t(p, c), dot_t(p, s)
     for j in range(2):
         cols = slice(j * B, (j + 1) * B)
-        put(19 + j, hc[:B, cols])
-        put(21 + j, hc[B:, cols])
-        put(31 + j, pc[:, cols])
+        put_grad(19 + j, hc[:B, cols], hs[:B, cols])
+        put_grad(21 + j, hc[B:, cols], hs[B:, cols])
+        put_grad(31 + j, pc[:, cols], ps[:, cols])
     put_symmetric(17, 3, dot_t(s, s))
 
     means = m_s[l]
@@ -159,26 +169,38 @@
     for i in range(2):
         for j in range(2):
             put(6 + 2 * i + j, mm[i * B : (i + 1) * B, D + j * B : D + (j + 1) * B])
-    totals = dot(pick, jnp.concatenate([p, c], 1))
+    totals = dot(pick, jnp.concatenate([p, c, s], 1))
     t_high, t_low = split(totals[:WALK] + totals[WALK:])
     side = dot_t(jnp.concatenate([both, both], 0), jnp.concatenate([t_high, t_low], 0))
     for i in range(4):
         rows = slice(i * B, (i + 1) * B)
         put(13 + i, side[rows, :B])
-        put(23 + 2 * i, side[rows, B : 2 * B])
-        put(24 + 2 * i, side[rows, 2 * B :])
+        for j in range(2):
+            at = (1 + j) * B
+            put_grad(23 + 2 * i + j, side[rows, at : at + B], side[rows, at + D : at + D + B])
     lines[4] = jnp.full((1, B), mult * (1.0 / 16.0), F32)
     last = KEPT - B
     out[parity ^ 1, last:, :] = jnp.zeros((B, B), F32)
     for line, value in lines.items():
         out[parity ^ 1, last + line : last + line + 1, :] = value
     keep[...] = out[0]
-    for target, (first, end) in zip((to_0, to_1, to_2, to_3, to_4), OUT_STREAMS):
+    keep_0[...] = out_0[0]
+    grads = GRADS * B
+    to_a[:grads, :] = out[1, :grads, :]
+    to_0[:grads, :] = out_0[1]
+    to_a[grads:, :] = row_sum[...]
+    to_0[grads:, :] = row_sum[...]
+    for target, (first, end) in zip((to_2, to_3), OUT_STREAMS):
         target[...] = out[1, first * B : end * B, :]
 
 
-def add_kernel(keep, from_0, from_1, from_2, from_3, from_4, total):
-    for part, (first, end) in zip((from_0, from_1, from_2, from_3, from_4), OUT_STREAMS):
+def add_kernel(keep, keep_0, from_a, from_0, from_2, from_3, row_sum, row_two, total):
+    grads = GRADS * B
+    energy = (row_sum[...] + row_two[...]) + (from_a[grads:, :] + from_0[grads:, :])
+    shifted = energy[:1, :] * (1.0 / 256.0) + SHIFT
+    plain = keep_0[...] + from_0[:grads, :]
+    total[:grads, :] = (keep[:grads, :] + from_a[:grads, :]) - shifted * plain
+    for part, (first, end) in zip((from_2, from_3), OUT_STREAMS):
         rows = slice(first * B, end * B)
         total[rows, :] = keep[rows, :] + part[...]
 
@@ -308,9 +330,11 @@
     return lax.all_to_all(value, axes, 0, 0, axis_index_groups=parity_groups(), tiled=True)
 
 
+LOW, HIGH = [(0, 1), (1, 0), (2, 3), (3, 2)], [(1, 2), (2, 1), (3, 0), (0, 3)]
+
+
 def to_neighbours(parts):
-    low, high = [(0, 1), (1, 0), (2, 3), (3, 2)], [(1, 2), (2, 1), (3, 0), (0, 3)]
-    ways = (("x", low), ("y", low), ("zl", [(0, 1), (1, 0)]), ("x", high), ("y", high))
+    ways = (("x", LOW), ("y", LOW), ("zl", [(0, 1), (1, 0)]), ("x", HIGH), ("y", HIGH))
     return [lax.ppermute(part, axis, pairs) for part, (axis, pairs) in zip(parts, ways)]
 
 
@@ -324,16 +348,20 @@
     pair = pair_means.reshape(2, HALF, PAIR)
     swap = [(0, 1), (1, 0)]
 
+    half_sum = energies + lax.ppermute(energies, "zh", LOW)
     other = lax.ppermute(jnp.concatenate([feat, psi], 1).astype(F32), "c", swap)
     oth_pair = lax.ppermute(pair.astype(F32), "c", swap)
-    spread = jnp.broadcast_to(energies, (WALK, WALK))
-    gathered = lax.all_to_all(spread, ("zh", "x"), 0, 0, tiled=True)
-
-    keep, *parts = call(
+    half_other = lax.ppermute(half_sum, "zh", HIGH)
+
+    grads = GRADS * B
+    keep, keep_0, to_a, to_0, to_2, to_3, row_sum = call(
         factors_kernel,
-        [((KEPT, B), F32)] + streams_of(OUT_STREAMS),
-        [V] * 7 + [S] * 2,
-        24,
+        [((KEPT, B), F32), ((grads, B), F32)]
+        + [((grads + 8, B), F32)] * 2
+        + streams_of(OUT_STREAMS)
+        + [((8, B), F32)],
+        [V] * 9 + [S] * 2,
+        26,
         "factors",
         scratch=[
             pltpu.VMEM((2, ROWS, D + PAIR), BF16),
@@ -342,13 +370,20 @@
             pltpu.VMEM((2, ROWS, D), BF16),
             pltpu.VMEM((ROWS, D), BF16),
             pltpu.VMEM((2, KEPT, B), F32),
+            pltpu.VMEM((2, grads, B), F32),
         ],
         flops=2_500_000_000,
         moved=8_000_000,
-    )(feat, pair, psi, other, oth_pair, weights, gathered, energies, multiplicity)
-
-    parts = to_neighbours(parts)
-    (total,) = call(add_kernel, [((KEPT, B), F32)], [V] * 6, 6, "add", moved=3_000_000)(keep, *parts)
+    )(feat, pair, psi, other, oth_pair, weights, half_sum, half_other, energies, energies, multiplicity)
+
+    from_a = lax.ppermute(to_a, "x", LOW)
+    from_0 = lax.ppermute(to_0, "x", HIGH)
+    from_2 = lax.ppermute(to_2, "y", LOW)
+    from_3 = lax.ppermute(to_3, "zl", swap)
+    row_two = lax.ppermute(row_sum, "x", [(0, 2), (1, 3), (2, 0), (3, 1)])
+    (total,) = call(add_kernel, [((KEPT, B), F32)], [V] * 8, 8, "add", moved=3_000_000)(
+        keep, keep_0, from_a, from_0, from_2, from_3, row_sum, row_two
+    )
     mine = jnp.sum(same_parity(total).reshape(GROUP, CHUNK, B), axis=0)
     one, two, three = (
         lax.ppermute(mine, "zh", [(i, (i + k) % 4) for i in range(4)]) for k in (1, 2, 3)

time: 109 us -> 100 us (0.917)
  waiting for transfers between devices: 22.3 us -> 13.8 us
  other arithmetic: 3.16 us -> 1.39 us
  blocking collectives: 37.5 us -> 38.8 us
    ppermute x0 -> x7, starting transfers between devices: none -> 11.4 us  [the longest x1 4.28 us: body(): half_other = lax.ppermute(half_sum, 'zh', HIGH)]
    all_to_all x1 -> x0, starting transfers between devices: 9.01 us -> none  [body(): gathered = lax.all_to_all(spread, ('zh', 'x'), 0, 0, tiled=True)]
    ppermute x0 -> x7, waiting for transfers between devices: none -> 8.44 us  [the longest x1 5.97 us: body(): row_two = lax.ppermute(row_sum, 'x', [(0, 2), (1, 3), (2, 0), (3, 1)])]
    all_to_all x1 -> x0, waiting for transfers between devices: 8.09 us -> none  [body(): gathered = lax.all_to_all(spread, ('zh', 'x'), 0, 0, tiled=True)]
    ppermute x10 -> x5, waiting for transfers between devices: 6.81 us -> 1.97 us  [to_neighbours(): lax.ppermute(part, axis, pairs)]
    ppermute x3, waiting for transfers between devices: 7.35 us -> 3.33 us  [body(): lax.ppermute(mine, 'zh', [(i, (i + k) % 4) for i in range(4)])]
    ppermute x3, starting transfers between devices: 3.97 us -> 7.59 us  [body(): lax.ppermute(mine, 'zh', [(i, (i + k) % 4) for i in range(4)])]
    ppermute x1, starting transfers between devices: 10.2 us -> 6.84 us  [body(): other = lax.ppermute(curvature, 'c', swap)]
  transfers between devices with their start and end apart: 17 -> 18, of which waited for: 7 -> 6; matrix products, arithmetic and copies ran while one was open for 1% -> 0% of each run, Pallas kernels for 4% -> 5%
where the time goes in v5:
time: 100 us
  blocking collectives  38.8 us (39%)
  starting transfers between devices  34.4 us (34%)
  waiting for transfers between devices  13.8 us (14%)
  Pallas kernels  10.4 us (10%)
  between operations  1.43 us (1%)
  other arithmetic  1.39 us (1%)
    all_to_all x2, blocking collectives, same_parity(): lax.all_to_all(value, axes, 0, 0, axis_index_groups=parity_groups(), tile...  38.8 us
    ppermute x3, starting transfers between devices, body(): lax.ppermute(mine, 'zh', [(i, (i + k) % 4) for i in range(4)])  7.59 us
    ppermute x1, starting transfers between devices, body(): other = lax.ppermute(curvature, 'c', swap)  6.84 us
    ppermute x1, waiting for transfers between devices, body(): row_two = lax.ppermute(row_sum, 'x', [(0, 2), (1, 3), (2, 0), (3, 1)])  5.97 us
    ppermute x5, starting transfers between devices, to_neighbours(): lax.ppermute(part, axis, pairs)  5.15 us
    pallas_call x1, Pallas kernels, body(): call(factors_kernel, [((KEPT, B), F32), ((grads, B), F32)] + [((grads + 8...  4.49 us
    ppermute x1, starting transfers between devices, body(): half_other = lax.ppermute(half_sum, 'zh', HIGH)  4.28 us
    ppermute x3, waiting for transfers between devices, body(): lax.ppermute(mine, 'zh', [(i, (i + k) % 4) for i in range(4)])  3.33 us
  transfers between devices with their start and end apart: 18, of which 6 were waited for; matrix products, arithmetic and copies ran while one was open for 0% of the time, Pallas kernels for 5%

profile of v5, /device:TPU:1, one launch (start us, length us, event | category | flops | bytes accessed | tf_op | source)
XLA Modules:
  0.0 100.3 jit_solution(1661188766694942239)
XLA Ops:
  0.6 0.0 copy-start
  0.6 0.0 copy-start.6
  0.7 0.0 copy-start.1
  0.7 0.0 copy-start.2
  0.7 0.0 copy-start.4
  0.7 1.3 %maximum_convert_fusion = f32[512,512]{1,0:T(8,128)S(1)} fusion(bf16[512,256]{1,0:T(8,128)(2,1)} %bitcast.18, bf16[512,256]{1,0:T(8,128)(2,1)} %bitcast.16), kind=kLoop, calls=%fused_computation | loop fusion | flops 1048576 | bytes 1572864 | tf_op jit(solution)/shard_map/convert_element_type | solution.py:352
  2.0 3.3 %collective-permute-start = (f32[512,512]{1,0:T(8,128)S(1)}, f32[512,512]{1,0:T(8,128)S(1)}, u32[]{:S(2)}, u32[]{:S(2)}) collective-permute-start(f32[512,512]{1,0:T(8,128)S(1)} %maximum_convert_fusion), channel_id=1, source_target_pairs={{0,1},{1,0},{2,3},{3,2},{4,5},{5,4},{6,7},{7,6},{8,9},{9,8},{10,11... | collective-permute-start | bytes 3145736 | tf_op jit(solution)/shard_map/ppermute | solution.py:352
  5.3 0.0 copy-done
  5.3 0.1 collective-permute-start.1
  5.4 0.0 copy-done.6
  5.4 1.3 %collective-permute-start.2 = (f32[1,16]{1,0:T(1,128)S(1)}, f32[1,16]{1,0:T(1,128)S(1)}, u32[]{:S(2)}, u32[]{:S(2)}) collective-permute-start(f32[1,16]{1,0:T(1,128)S(1)} %copy-done.6), channel_id=1, source_target_pairs={{0,8},{8,0},{16,24},{24,16},{1,9},{9,1},{17,25},{25,17},{2,10},{10... | collective-permute-start | bytes 200 | tf_op jit(solution)/shard_map/ppermute | solution.py:351
  6.8 2.0 %collective-permute-done.2 = f32[1,16]{1,0:T(1,128)S(1)} collective-permute-done((f32[1,16]{1,0:T(1,128)S(1)}, f32[1,16]{1,0:T(1,128)S(1)}, u32[]{:S(2)}, u32[]{:S(2)}) %collective-permute-start.2) | collective-permute-done | bytes 96 | tf_op jit(solution)/shard_map/ppermute | solution.py:351
  8.8 4.3 %collective-permute-start.3 = (f32[1,16]{1,0:T(1,128)S(1)}, f32[1,16]{1,0:T(1,128)S(1)}, u32[]{:S(2)}, u32[]{:S(2)}) collective-permute-start(f32[1,16]{1,0:T(1,128)S(1)} %add.13.half_sum), channel_id=1, source_target_pairs={{8,16},{16,8},{24,0},{0,24},{9,17},{17,9},{25,1},{1,25},{10,18},{1... | collective-permute-start | bytes 200 | tf_op jit(solution)/shard_map/ppermute | solution.py:354
  13.8 0.3 collective-permute-done.3.half_other
  14.0 0.0 collective-permute-done.1.oth_pair
  14.0 0.0 collective-permute-done.other
  14.0 0.0 copy-done.1
  14.0 0.0 copy-done.2
  14.1 0.0 copy-done.4
  14.1 4.5 %factors.1 = (f32[2176,128]{1,0:T(8,128)S(1)}, f32[896,128]{1,0:T(8,128)S(1)}, f32[904,128]{1,0:T(8,128)S(1)}, f32[904,128]{1,0:T(8,128)S(1)}, f32[640,128]{1,0:...) custom-call(bf16[512,256]{1,0:T(8,128)(2,1)S(1)} %bitcast.17, bf16[2,512,128]{2,1,0:T(8,128)(2,1)S(1)} %bitcast.15, ...), custom_call_target="tpu_custom_call" | custom-call | flops 2500000000 | bytes 8000000 | tf_op jit(solution)/shard_map/factors/pallas_call | solution.py:357
  18.6 1.3 %collective-permute-start.4 = (f32[904,128]{1,0:T(8,128)S(1)}, f32[904,128]{1,0:T(8,128)S(1)}, u32[]{:S(2)}, u32[]{:S(2)}) collective-permute-start(f32[904,128]{1,0:T(8,128)S(1)} %get-tuple-element.21), channel_id=1, source_target_pairs={{0,2},{2,0},{4,6},{6,4},{1,3},{3,1},{5,7},{7,5},{8,10},{10,8},{12,... | collective-permute-start | bytes 1388552 | tf_op jit(solution)/shard_map/ppermute | solution.py:379
  19.9 1.8 %collective-permute-start.5 = (f32[904,128]{1,0:T(8,128)S(1)}, f32[904,128]{1,0:T(8,128)S(1)}, u32[]{:S(2)}, u32[]{:S(2)}) collective-permute-start(f32[904,128]{1,0:T(8,128)S(1)} %get-tuple-element.22), channel_id=1, source_target_pairs={{2,4},{4,2},{6,0},{0,6},{3,5},{5,3},{7,1},{1,7},{10,12},{12,10},{1... | collective-permute-start | bytes 1388552 | tf_op jit(solution)/shard_map/ppermute | solution.py:380
  21.7 1.3 %collective-permute-start.6 = (f32[640,128]{1,0:T(8,128)S(1)}, f32[640,128]{1,0:T(8,128)S(1)}, u32[]{:S(2)}, u32[]{:S(2)}) collective-permute-start(f32[640,128]{1,0:T(8,128)S(1)} %get-tuple-element.23), channel_id=1, source_target_pairs={{0,32},{32,0},{64,96},{96,64},{1,33},{33,1},{65,97},{97,65},{2,34}... | collective-permute-start | bytes 983048 | tf_op jit(solution)/shard_map/ppermute | solution.py:381
  23.0 0.7 collective-permute-start.7
  23.7 0.6 collective-permute-start.8
  24.4 6.0 %collective-permute-done.8.row_two = f32[8,128]{1,0:T(8,128)S(1)} collective-permute-done((f32[8,128]{1,0:T(8,128)S(1)}, f32[8,128]{1,0:T(8,128)S(1)}, u32[]{:S(2)}, u32[]{:S(2)}) %collective-permute-start.8) | collective-permute-done | bytes 4128 | tf_op jit(solution)/shard_map/ppermute | solution.py:383
  30.3 0.0 collective-permute-done.6.from_2
  30.3 0.0 collective-permute-done.7.from_3
  30.3 0.0 collective-permute-done.4.from_a
  30.3 0.1 collective-permute-done.5.from_0
  30.5 0.2 add.20
  30.7 20.8 %all_to_all.17 = f32[16,136,128]{2,1,0:T(8,128)S(1)} all-to-all(f32[16,136,128]{2,1,0:T(8,128)S(1)} %bitcast.13), channel_id=1, replica_groups={{0,4,34,38,64,68,98,102,130,134,160,164,194,198,224,228},{2,6,32,36,66,..., dimensions={0} | all-to-all | bytes 2228224 | tf_op jit(solution)/shard_map/all_to_all | solution.py:330
  51.5 0.1 reduce_sum.9
  51.6 1.0 %collective-permute-start.10 = (f32[136,128]{1,0:T(8,128)S(1)}, f32[136,128]{1,0:T(8,128)S(1)}, u32[]{:S(2)}, u32[]{:S(2)}) collective-permute-start(f32[136,128]{1,0:T(8,128)S(1)} %reduce_sum.9), channel_id=1, source_target_pairs={{0,8},{8,16},{16,24},{24,0},{1,9},{9,17},{17,25},{25,1},{2,10},{10... | collective-permute-start | bytes 208904 | tf_op jit(solution)/shard_map/ppermute | solution.py:389
  52.6 2.6 %collective-permute-start.11 = (f32[136,128]{1,0:T(8,128)S(1)}, f32[136,128]{1,0:T(8,128)S(1)}, u32[]{:S(2)}, u32[]{:S(2)}) collective-permute-start(f32[136,128]{1,0:T(8,128)S(1)} %reduce_sum.9), channel_id=1, source_target_pairs={{0,24},{8,0},{16,8},{24,16},{1,25},{9,1},{17,9},{25,17},{2,26},{10... | collective-permute-start | bytes 208904 | tf_op jit(solution)/shard_map/ppermute | solution.py:389
  55.3 3.9 %collective-permute-start.9 = (f32[136,128]{1,0:T(8,128)S(1)}, f32[136,128]{1,0:T(8,128)S(1)}, u32[]{:S(2)}, u32[]{:S(2)}) collective-permute-start(f32[136,128]{1,0:T(8,128)S(1)} %reduce_sum.9), channel_id=1, source_target_pairs={{0,16},{8,24},{16,0},{24,8},{1,17},{9,25},{17,1},{25,9},{2,18},{10... | collective-permute-start | bytes 208904 | tf_op jit(solution)/shard_map/ppermute | solution.py:389
  59.2 0.0 collective-permute-done.10
  59.2 0.0 collective-permute-done.11
  59.2 3.3 %collective-permute-done.9 = f32[136,128]{1,0:T(8,128)S(1)} collective-permute-done((f32[136,128]{1,0:T(8,128)S(1)}, f32[136,128]{1,0:T(8,128)S(1)}, u32[]{:S(2)}, u32[]{:S(2)}) %collective-permute-start.9) | collective-permute-done | bytes 69664 | tf_op jit(solution)/shard_map/ppermute | solution.py:389
  62.5 0.0 copy-start.5
  62.6 0.1 broadcast_in_dim.15
  62.6 0.0 copy-start.3
  62.6 17.9 %all_to_all.18 = f32[16,136,128]{2,1,0:T(8,128)S(1)} all-to-all(f32[16,136,128]{2,1,0:T(8,128)S(1)} %broadcast_in_dim.15), channel_id=1, replica_groups={{0,4,34,38,64,68,98,102,130,134,160,164,194,198,224,228},{2,6,32,36,66,..., dimensions={0} | all-to-all | bytes 2228224 | tf_op jit(solution)/shard_map/all_to_all | solution.py:330
  80.6 0.1 cut.1
  80.7 2.5 %collective-permute-start.15 = (f32[512,128]{1,0:T(8,128)S(1)}, f32[512,128]{1,0:T(8,128)S(1)}, u32[]{:S(2)}, u32[]{:S(2)}) collective-permute-start(f32[512,128]{1,0:T(8,128)S(1)} %get-tuple-element.31), channel_id=1, source_target_pairs={{0,2},{2,0},{4,6},{6,4},{1,3},{3,1},{5,7},{7,5},{8,10},{10,8},{12,... | collective-permute-start | bytes 786440 | tf_op jit(solution)/shard_map/ppermute | solution.py:338
  83.2 0.0 collective-permute-start.16
  83.2 0.7 collective-permute-start.12
  83.9 0.8 collective-permute-start.13
  84.7 1.1 %collective-permute-start.14 = (f32[384,128]{1,0:T(8,128)S(1)}, f32[384,128]{1,0:T(8,128)S(1)}, u32[]{:S(2)}, u32[]{:S(2)}) collective-permute-start(f32[384,128]{1,0:T(8,128)S(1)} %get-tuple-element.28), channel_id=1, source_target_pairs={{32,64},{64,32},{96,0},{0,96},{33,65},{65,33},{97,1},{1,97},{34,66... | collective-permute-start | bytes 589832 | tf_op jit(solution)/shard_map/ppermute | solution.py:338
  85.8 2.0 %collective-permute-done.16.from_1 = f32[384,128]{1,0:T(8,128)S(1)} collective-permute-done((f32[384,128]{1,0:T(8,128)S(1)}, f32[384,128]{1,0:T(8,128)S(1)}, u32[]{:S(2)}, u32[]{:S(2)}) %collective-permute-start.16) | collective-permute-done | bytes 196640 | tf_op jit(solution)/shard_map/ppermute | solution.py:338
  87.8 0.0 collective-permute-done.15.from_0
  87.8 0.0 copy-done.5
  87.8 0.0 copy-done.3
  87.8 2.5 %natural.1 = (f32[896,256]{1,0:T(8,128)S(1)}, f32[1,128]{1,0:T(1,128)S(1)}) custom-call(f32[2176,128]{1,0:T(8,128)S(1)} %bitcast.11, f32[512,128]{1,0:T(8,128)S(1)} %collective-permute-done.15.from_0, f32[384,128]{1,0:T(8,128)S(1)} %collective-permute-done.16.from_1, f32[896,896]{1,0:T(8,128)S(1)} %bitcast.20, f32[256,256]{1,0:T(8,128)S(1)} %bitcast.21), custom_call_target="tpu_custom_call" | custom-call | flops 1500000000 | bytes 5000000 | tf_op jit(solution)/shard_map/natural/pallas_call | solution.py:396
  90.3 6.8 %collective-permute-start.17 = (f32[1,128]{1,0:T(1,128)S(1)}, f32[1,128]{1,0:T(1,128)S(1)}, u32[]{:S(2)}, u32[]{:S(2)}) collective-permute-start(f32[1,128]{1,0:T(1,128)S(1)} %get-tuple-element.34.curvature), channel_id=1, source_target_pairs={{0,1},{1,0},{2,3},{3,2},{4,5},{5,4},{6,7},{7,6},{8,9},{9,8},{10,11... | collective-permute-start | bytes 1544 | tf_op jit(solution)/shard_map/ppermute | solution.py:405
  97.1 0.0 collective-permute-done.13.from_3
  97.1 0.0 collective-permute-done.14.from_4
  97.1 0.0 collective-permute-done.12.from_2
  97.1 2.1 %unpack.1 = (f32[896,896]{1,0:T(8,128)}, f32[256,256]{1,0:T(8,128)}) custom-call(f32[2176,128]{1,0:T(8,128)S(1)} %bitcast.12, f32[512,128]{1,0:T(8,128)S(1)} %collective-permute-done.12.from_2, f32[384,128]{1,0:T(8,128)S(1)} %collective-permute-done.13.from_3, f32[384,128]{1,0:T(8,128)S(1)} %collective-permute-done.14.from_4), custom_call_target="tpu_custom_call" | custom-call | flops 10000000 | bytes 6000000 | tf_op jit(solution)/shard_map/unpack/pallas_call | solution.py:406
  99.3 0.0 collective-permute-done.17.other
  99.3 1.1 %scale.1 = f32[896,256]{1,0:T(8,128)} custom-call(f32[896,256]{1,0:T(8,128)S(1)} %get-tuple-element.33.natural, f32[1,128]{1,0:T(1,128)S(1)} %get-tuple-element.34.curvature, f32[1,128]{1,0:T(1,128)S(1)} %collective-permute-done.17.other), custom_call_target="tpu_custom_call" | custom-call | flops 1000000 | bytes 2000000 | tf_op jit(solution)/shard_map/scale/pallas_call | solution.py:415
  (3 shorter events, 0.1 us)
Async XLA Ops:
  0.6 4.7 %copy-start = (bf16[1,2,16,32,128]{4,3,2,1,0:T(8,128)(2,1)S(1)}, bf16[1,2,16,32,128]{4,3,2,1,0:T(8,128)(2,1)}, u32[]{:S(2)}) copy-start(bf16[1,2,16,32,128]{4,3,2,1,0:T(8,128)(2,1)} %param.10) | copy-start | bytes 786436
  0.6 4.8 %copy-start.6 = (f32[1,16]{1,0:T(1,128)S(1)}, f32[1,16]{1,0:T(1,128)}, u32[]{:S(2)}) copy-start(f32[1,16]{1,0:T(1,128)} %energy.1) | copy-start | bytes 196
  0.7 13.4 %copy-start.1 = (bf16[1,16,32,256]{3,2,1,0:T(8,128)(2,1)S(1)}, bf16[1,16,32,256]{3,2,1,0:T(8,128)(2,1)}, u32[]{:S(2)}) copy-start(bf16[1,16,32,256]{3,2,1,0:T(8,128)(2,1)} %param.8) | copy-start | bytes 786436
  0.7 13.4 %copy-start.2 = (bf16[1,16,32,256]{3,2,1,0:T(8,128)(2,1)S(1)}, bf16[1,16,32,256]{3,2,1,0:T(8,128)(2,1)}, u32[]{:S(2)}) copy-start(bf16[1,16,32,256]{3,2,1,0:T(8,128)(2,1)} %param.9) | copy-start | bytes 786436
  0.7 13.4 %copy-start.4 = (bf16[2,896,256]{2,1,0:T(8,128)(2,1)S(1)}, bf16[2,896,256]{2,1,0:T(8,128)(2,1)}, u32[]{:S(2)}) copy-start(bf16[2,896,256]{2,1,0:T(8,128)(2,1)} %weights.1) | copy-start | bytes 2752516
  2.0 12.1 %collective-permute-start = (f32[512,512]{1,0:T(8,128)S(1)}, f32[512,512]{1,0:T(8,128)S(1)}, u32[]{:S(2)}, u32[]{:S(2)}) collective-permute-start(f32[512,512]{1,0:T(8,128)S(1)} %maximum_convert_fusion), channel_id=1, source_target_pairs={{0,1},{1,0},{2,3},{3,2},{4,5},{5,4},{6,7},{7,6},{8,9},{9,8},{10,11... | collective-permute-start | bytes 3145736 | tf_op jit(solution)/shard_map/ppermute | solution.py:352
  5.3 8.7 %collective-permute-start.1 = (f32[2,512,128]{2,1,0:T(8,128)S(1)}, f32[2,512,128]{2,1,0:T(8,128)S(1)}, u32[]{:S(2)}, u32[]{:S(2)}) collective-permute-start(f32[2,512,128]{2,1,0:T(8,128)S(1)} %convert_element_type.7), channel_id=1, source_target_pairs={{0,1},{1,0},{2,3},{3,2},{4,5},{5,4},{6,7},{7,6},{8,9},{9,8},{10,11... | collective-permute-start | bytes 1572872 | tf_op jit(solution)/shard_map/ppermute | solution.py:353
  5.4 3.4 %collective-permute-start.2 = (f32[1,16]{1,0:T(1,128)S(1)}, f32[1,16]{1,0:T(1,128)S(1)}, u32[]{:S(2)}, u32[]{:S(2)}) collective-permute-start(f32[1,16]{1,0:T(1,128)S(1)} %copy-done.6), channel_id=1, source_target_pairs={{0,8},{8,0},{16,24},{24,16},{1,9},{9,1},{17,25},{25,17},{2,10},{10... | collective-permute-start | bytes 200 | tf_op jit(solution)/shard_map/ppermute | solution.py:351
  8.8 5.2 %collective-permute-start.3 = (f32[1,16]{1,0:T(1,128)S(1)}, f32[1,16]{1,0:T(1,128)S(1)}, u32[]{:S(2)}, u32[]{:S(2)}) collective-permute-start(f32[1,16]{1,0:T(1,128)S(1)} %add.13.half_sum), channel_id=1, source_target_pairs={{8,16},{16,8},{24,0},{0,24},{9,17},{17,9},{25,1},{1,25},{10,18},{1... | collective-permute-start | bytes 200 | tf_op jit(solution)/shard_map/ppermute | solution.py:354
  18.6 11.8 %collective-permute-start.4 = (f32[904,128]{1,0:T(8,128)S(1)}, f32[904,128]{1,0:T(8,128)S(1)}, u32[]{:S(2)}, u32[]{:S(2)}) collective-permute-start(f32[904,128]{1,0:T(8,128)S(1)} %get-tuple-element.21), channel_id=1, source_target_pairs={{0,2},{2,0},{4,6},{6,4},{1,3},{3,1},{5,7},{7,5},{8,10},{10,8},{12,... | collective-permute-start | bytes 1388552 | tf_op jit(solution)/shard_map/ppermute | solution.py:379
  19.9 10.6 %collective-permute-start.5 = (f32[904,128]{1,0:T(8,128)S(1)}, f32[904,128]{1,0:T(8,128)S(1)}, u32[]{:S(2)}, u32[]{:S(2)}) collective-permute-start(f32[904,128]{1,0:T(8,128)S(1)} %get-tuple-element.22), channel_id=1, source_target_pairs={{2,4},{4,2},{6,0},{0,6},{3,5},{5,3},{7,1},{1,7},{10,12},{12,10},{1... | collective-permute-start | bytes 1388552 | tf_op jit(solution)/shard_map/ppermute | solution.py:380
  21.7 8.6 %collective-permute-start.6 = (f32[640,128]{1,0:T(8,128)S(1)}, f32[640,128]{1,0:T(8,128)S(1)}, u32[]{:S(2)}, u32[]{:S(2)}) collective-permute-start(f32[640,128]{1,0:T(8,128)S(1)} %get-tuple-element.23), channel_id=1, source_target_pairs={{0,32},{32,0},{64,96},{96,64},{1,33},{33,1},{65,97},{97,65},{2,34}... | collective-permute-start | bytes 983048 | tf_op jit(solution)/shard_map/ppermute | solution.py:381
  23.0 7.4 %collective-permute-start.7 = (f32[640,128]{1,0:T(8,128)S(1)}, f32[640,128]{1,0:T(8,128)S(1)}, u32[]{:S(2)}, u32[]{:S(2)}) collective-permute-start(f32[640,128]{1,0:T(8,128)S(1)} %get-tuple-element.24), channel_id=1, source_target_pairs={{0,128},{128,0},{1,129},{129,1},{2,130},{130,2},{3,131},{131,3},{4... | collective-permute-start | bytes 983048 | tf_op jit(solution)/shard_map/ppermute | solution.py:382
  23.7 6.6 %collective-permute-start.8 = (f32[8,128]{1,0:T(8,128)S(1)}, f32[8,128]{1,0:T(8,128)S(1)}, u32[]{:S(2)}, u32[]{:S(2)}) collective-permute-start(f32[8,128]{1,0:T(8,128)S(1)} %get-tuple-element.25.row_sum), channel_id=1, source_target_pairs={{0,4},{2,6},{4,0},{6,2},{1,5},{3,7},{5,1},{7,3},{8,12},{10,14},{12... | collective-permute-start | bytes 12296 | tf_op jit(solution)/shard_map/ppermute | solution.py:383
  51.6 7.6 %collective-permute-start.10 = (f32[136,128]{1,0:T(8,128)S(1)}, f32[136,128]{1,0:T(8,128)S(1)}, u32[]{:S(2)}, u32[]{:S(2)}) collective-permute-start(f32[136,128]{1,0:T(8,128)S(1)} %reduce_sum.9), channel_id=1, source_target_pairs={{0,8},{8,16},{16,24},{24,0},{1,9},{9,17},{17,25},{25,1},{2,10},{10... | collective-permute-start | bytes 208904 | tf_op jit(solution)/shard_map/ppermute | solution.py:389
  52.6 6.6 %collective-permute-start.11 = (f32[136,128]{1,0:T(8,128)S(1)}, f32[136,128]{1,0:T(8,128)S(1)}, u32[]{:S(2)}, u32[]{:S(2)}) collective-permute-start(f32[136,128]{1,0:T(8,128)S(1)} %reduce_sum.9), channel_id=1, source_target_pairs={{0,24},{8,0},{16,8},{24,16},{1,25},{9,1},{17,9},{25,17},{2,26},{10... | collective-permute-start | bytes 208904 | tf_op jit(solution)/shard_map/ppermute | solution.py:389
  55.3 7.3 %collective-permute-start.9 = (f32[136,128]{1,0:T(8,128)S(1)}, f32[136,128]{1,0:T(8,128)S(1)}, u32[]{:S(2)}, u32[]{:S(2)}) collective-permute-start(f32[136,128]{1,0:T(8,128)S(1)} %reduce_sum.9), channel_id=1, source_target_pairs={{0,16},{8,24},{16,0},{24,8},{1,17},{9,25},{17,1},{25,9},{2,18},{10... | collective-permute-start | bytes 208904 | tf_op jit(solution)/shard_map/ppermute | solution.py:389
  62.5 25.2 %copy-start.5 = (f32[1,256,256]{2,1,0:T(8,128)S(1)}, f32[1,256,256]{2,1,0:T(8,128)}, u32[]{:S(2)}) copy-start(f32[1,256,256]{2,1,0:T(8,128)} %param.15) | copy-start | bytes 786436
  62.6 25.1 %copy-start.3 = (f32[1,896,896]{2,1,0:T(8,128)S(1)}, f32[1,896,896]{2,1,0:T(8,128)}, u32[]{:S(2)}) copy-start(f32[1,896,896]{2,1,0:T(8,128)} %param.14) | copy-start | bytes 9633796
  80.7 7.1 %collective-permute-start.15 = (f32[512,128]{1,0:T(8,128)S(1)}, f32[512,128]{1,0:T(8,128)S(1)}, u32[]{:S(2)}, u32[]{:S(2)}) collective-permute-start(f32[512,128]{1,0:T(8,128)S(1)} %get-tuple-element.31), channel_id=1, source_target_pairs={{0,2},{2,0},{4,6},{6,4},{1,3},{3,1},{5,7},{7,5},{8,10},{10,8},{12,... | collective-permute-start | bytes 786440 | tf_op jit(solution)/shard_map/ppermute | solution.py:338
  83.2 4.6 %collective-permute-start.16 = (f32[384,128]{1,0:T(8,128)S(1)}, f32[384,128]{1,0:T(8,128)S(1)}, u32[]{:S(2)}, u32[]{:S(2)}) collective-permute-start(f32[384,128]{1,0:T(8,128)S(1)} %get-tuple-element.32), channel_id=1, source_target_pairs={{0,32},{32,0},{64,96},{96,64},{1,33},{33,1},{65,97},{97,65},{2,34}... | collective-permute-start | bytes 589832 | tf_op jit(solution)/shard_map/ppermute | solution.py:338
  83.2 13.9 %collective-permute-start.12 = (f32[512,128]{1,0:T(8,128)S(1)}, f32[512,128]{1,0:T(8,128)S(1)}, u32[]{:S(2)}, u32[]{:S(2)}) collective-permute-start(f32[512,128]{1,0:T(8,128)S(1)} %get-tuple-element.26), channel_id=1, source_target_pairs={{0,128},{128,0},{1,129},{129,1},{2,130},{130,2},{3,131},{131,3},{4... | collective-permute-start | bytes 786440 | tf_op jit(solution)/shard_map/ppermute | solution.py:338
  83.9 13.2 %collective-permute-start.13 = (f32[384,128]{1,0:T(8,128)S(1)}, f32[384,128]{1,0:T(8,128)S(1)}, u32[]{:S(2)}, u32[]{:S(2)}) collective-permute-start(f32[384,128]{1,0:T(8,128)S(1)} %get-tuple-element.27), channel_id=1, source_target_pairs={{2,4},{4,2},{6,0},{0,6},{3,5},{5,3},{7,1},{1,7},{10,12},{12,10},{1... | collective-permute-start | bytes 589832 | tf_op jit(solution)/shard_map/ppermute | solution.py:338
  84.7 12.4 %collective-permute-start.14 = (f32[384,128]{1,0:T(8,128)S(1)}, f32[384,128]{1,0:T(8,128)S(1)}, u32[]{:S(2)}, u32[]{:S(2)}) collective-permute-start(f32[384,128]{1,0:T(8,128)S(1)} %get-tuple-element.28), channel_id=1, source_target_pairs={{32,64},{64,32},{96,0},{0,96},{33,65},{65,33},{97,1},{1,97},{34,66... | collective-permute-start | bytes 589832 | tf_op jit(solution)/shard_map/ppermute | solution.py:338
  90.3 9.0 %collective-permute-start.17 = (f32[1,128]{1,0:T(1,128)S(1)}, f32[1,128]{1,0:T(1,128)S(1)}, u32[]{:S(2)}, u32[]{:S(2)}) collective-permute-start(f32[1,128]{1,0:T(1,128)S(1)} %get-tuple-element.34.curvature), channel_id=1, source_target_pairs={{0,1},{1,0},{2,3},{3,2},{4,5},{5,4},{6,7},{7,6},{8,9},{9,8},{10,11... | collective-permute-start | bytes 1544 | tf_op jit(solution)/shard_map/ppermute | solution.py:405

commit v6 on v5

--- a/solution.py
+++ b/solution.py
@@ -64,8 +64,8 @@
 
 
 def factors_kernel(
-    feat, pair, psi, other, oth_pair, weights, half_sum, half_other, energies, energy, multiplicity,
-    keep, keep_0, to_a, to_0, to_2, to_3, row_sum, x_s, d_s, m_s, s_s, c_s, out, out_0
+    feat, pair, psi, other, oth_pair, weights, energies, energy, multiplicity,
+    keep, keep_0, to_a, to_0, to_2, to_3, x_s, d_s, m_s, s_s, c_s, out, out_0
 ):
     mp = lax.axis_index("c")
     own_row = pl.multiple_of(D + D * mp, D)
@@ -112,15 +112,13 @@
     s = s_s[l]
     mean = jnp.sum(energies[...], axis=1, keepdims=True) * (1.0 / WALK)
     shifted = mean + SHIFT
-    zh_sum = jnp.sum(half_sum[...] + half_other[...], axis=1, keepdims=True)
-    row_sum[...] = jnp.broadcast_to(zh_sum, (8, B))
     step = HALF // WALK
     for w in range(WALK):
         centered = energy[0, w] - mean
         for first in (w * step, HALF + w * step):
             rows = slice(first, first + step)
-            c_s[rows, :] = (centered * s_s[l, rows, :].astype(F32)).astype(BF16)
-    c = c_s[...]
+            c_s[0, rows, :], c_s[1, rows, :] = split(centered * s_s[l, rows, :].astype(F32))
+    c, c_low = c_s[0], c_s[1]
     h, p = x[:, :D], x[:, D:]
     row, col = square_iotas()
 
@@ -149,8 +147,8 @@
     put(11, hp[:B])
     put(12, hp[B:])
     put(10, dot_t(p, p))
-    hc, hs = dot_t(h, c), dot_t(h, s)
-    pc, ps = dot_t(p, c), dot_t(p, s)
+    hc, hs = dot_t(h, c) + dot_t(h, c_low), dot_t(h, s)
+    pc, ps = dot_t(p, c) + dot_t(p, c_low), dot_t(p, s)
     for j in range(2):
         cols = slice(j * B, (j + 1) * B)
         put_grad(19 + j, hc[:B, cols], hs[:B, cols])
@@ -169,7 +167,7 @@
     for i in range(2):
         for j in range(2):
             put(6 + 2 * i + j, mm[i * B : (i + 1) * B, D + j * B : D + (j + 1) * B])
-    totals = dot(pick, jnp.concatenate([p, c, s], 1))
+    totals = jnp.concatenate([dot(pick, p), dot(pick, c) + dot(pick, c_low), dot(pick, s)], 1)
     t_high, t_low = split(totals[:WALK] + totals[WALK:])
     side = dot_t(jnp.concatenate([both, both], 0), jnp.concatenate([t_high, t_low], 0))
     for i in range(4):
@@ -186,20 +184,22 @@
     keep[...] = out[0]
     keep_0[...] = out_0[0]
     grads = GRADS * B
-    to_a[:grads, :] = out[1, :grads, :]
-    to_0[:grads, :] = out_0[1]
-    to_a[grads:, :] = row_sum[...]
-    to_0[grads:, :] = row_sum[...]
+    to_a[...] = out[1, :grads, :]
+    to_0[...] = out_0[1]
     for target, (first, end) in zip((to_2, to_3), OUT_STREAMS):
         target[...] = out[1, first * B : end * B, :]
 
 
-def add_kernel(keep, keep_0, from_a, from_0, from_2, from_3, row_sum, row_two, total):
+def tie_kernel(stream, near, far, same_stream, total):
+    total[...] = near[...] + far[...]
+
+
+def add_kernel(keep, keep_0, from_a, from_0, from_2, from_3, near_sum, far_sum, total):
     grads = GRADS * B
-    energy = (row_sum[...] + row_two[...]) + (from_a[grads:, :] + from_0[grads:, :])
-    shifted = energy[:1, :] * (1.0 / 256.0) + SHIFT
-    plain = keep_0[...] + from_0[:grads, :]
-    total[:grads, :] = (keep[:grads, :] + from_a[:grads, :]) - shifted * plain
+    energy = jnp.sum(near_sum[...] + far_sum[...], axis=1, keepdims=True)
+    shifted = energy * (1.0 / 256.0) + SHIFT
+    plain = keep_0[...] + from_0[...]
+    total[:grads, :] = (keep[:grads, :] + from_a[...]) - shifted * plain
     for part, (first, end) in zip((from_2, from_3), OUT_STREAMS):
         rows = slice(first * B, end * B)
         total[rows, :] = keep[rows, :] + part[...]
@@ -348,19 +348,19 @@
     pair = pair_means.reshape(2, HALF, PAIR)
     swap = [(0, 1), (1, 0)]
 
-    half_sum = energies + lax.ppermute(energies, "zh", LOW)
+    two = [(0, 2), (1, 3), (2, 0), (3, 1)]
+    sum_2 = energies + lax.ppermute(energies, "x", two)
     other = lax.ppermute(jnp.concatenate([feat, psi], 1).astype(F32), "c", swap)
     oth_pair = lax.ppermute(pair.astype(F32), "c", swap)
-    half_other = lax.ppermute(half_sum, "zh", HIGH)
+    far_2 = lax.ppermute(sum_2, "zh", LOW)
 
     grads = GRADS * B
-    keep, keep_0, to_a, to_0, to_2, to_3, row_sum = call(
+    keep, keep_0, to_a, to_0, to_2, to_3 = call(
         factors_kernel,
         [((KEPT, B), F32), ((grads, B), F32)]
-        + [((grads + 8, B), F32)] * 2
-        + streams_of(OUT_STREAMS)
-        + [((8, B), F32)],
-        [V] * 9 + [S] * 2,
+        + [((grads, B), F32)] * 2
+        + streams_of(OUT_STREAMS),
+        [V] * 7 + [S] * 2,
         26,
         "factors",
         scratch=[
@@ -368,21 +368,30 @@
             pltpu.VMEM((2, ROWS, D), F32),
             pltpu.VMEM((2, 2 * WALK, D), BF16),
             pltpu.VMEM((2, ROWS, D), BF16),
-            pltpu.VMEM((ROWS, D), BF16),
+            pltpu.VMEM((2, ROWS, D), BF16),
             pltpu.VMEM((2, KEPT, B), F32),
             pltpu.VMEM((2, grads, B), F32),
         ],
         flops=2_500_000_000,
         moved=8_000_000,
-    )(feat, pair, psi, other, oth_pair, weights, half_sum, half_other, energies, energies, multiplicity)
-
+    )(feat, pair, psi, other, oth_pair, weights, energies, energies, multiplicity)
+
+    to_a, sum_4 = pl.pallas_call(
+        tie_kernel,
+        out_shape=(jax.ShapeDtypeStruct((grads, B), F32), jax.ShapeDtypeStruct((1, WALK), F32)),
+        in_specs=[pl.BlockSpec(memory_space=pl.ANY)] + [pl.BlockSpec(memory_space=V)] * 2,
+        out_specs=(pl.BlockSpec(memory_space=pl.ANY), pl.BlockSpec(memory_space=V)),
+        input_output_aliases={0: 0},
+        name="tie",
+    )(to_a, sum_2, far_2)
     from_a = lax.ppermute(to_a, "x", LOW)
     from_0 = lax.ppermute(to_0, "x", HIGH)
     from_2 = lax.ppermute(to_2, "y", LOW)
     from_3 = lax.ppermute(to_3, "zl", swap)
-    row_two = lax.ppermute(row_sum, "x", [(0, 2), (1, 3), (2, 0), (3, 1)])
+    sum_8 = sum_4 + lax.ppermute(sum_4, "zh", HIGH)
+    far_8 = lax.ppermute(sum_8, "x", LOW)
     (total,) = call(add_kernel, [((KEPT, B), F32)], [V] * 8, 8, "add", moved=3_000_000)(
-        keep, keep_0, from_a, from_0, from_2, from_3, row_sum, row_two
+        keep, keep_0, from_a, from_0, from_2, from_3, sum_8, far_8
     )
     mine = jnp.sum(same_parity(total).reshape(GROUP, CHUNK, B), axis=0)
     one, two, three = (

time: 100 us -> 105 us (1.050)
  waiting for transfers between devices: 13.8 us -> 18 us
  blocking collectives: 38.8 us -> 34.7 us
  Pallas kernels: 10.4 us -> 12.3 us
  local copies, waits for them, and re-layouts: 0.11 us -> 1.38 us
    all_to_all x2, blocking collectives: 38.8 us -> 34.7 us  [same_parity(): lax.all_to_all(value, axes, 0, 0, axis_index_groups=parity_groups(), tile...]
    ppermute x3, waiting for transfers between devices: 3.33 us -> 6.31 us  [body(): lax.ppermute(mine, 'zh', [(i, (i + k) % 4) for i in range(4)])]
    ppermute x1, starting transfers between devices: 6.84 us -> 9.58 us  [body(): other = lax.ppermute(curvature, 'c', swap)]
    ppermute x3, starting transfers between devices: 7.59 us -> 5.81 us  [body(): lax.ppermute(mine, 'zh', [(i, (i + k) % 4) for i in range(4)])]
    pallas_call x1 -> x2, Pallas kernels: 4.49 us -> 6.25 us  [the longest x1 4.99 us: body(): call(factors_kernel, [((KEPT, B), F32), ((grads, B), F32)] + [((grads, B)...]
    ppermute x5, starting transfers between devices: 5.15 us -> 3.84 us  [to_neighbours(): lax.ppermute(part, axis, pairs)]
    unnamed x14 -> x20, local copies, waits for them, and re-layouts: 0.03 us -> 1.31 us
    ppermute x3 -> x4, waiting for transfers between devices: 8.28 us -> 9.09 us  [the longest x1 4.77 us: body(): sum_8 = sum_4 + lax.ppermute(sum_4, 'zh', HIGH)]
  transfers between devices with their start and end apart: 18 -> 19, of which waited for: 6 -> 6; matrix products, arithmetic and copies ran while one was open for 0% -> 1% of each run, Pallas kernels for 5% -> 9%
where the time goes in v6:
time: 105 us
  blocking collectives  34.7 us (33%)
  starting transfers between devices  34.6 us (33%)
  waiting for transfers between devices  18 us (17%)
  Pallas kernels  12.3 us (12%)
  other arithmetic  2.07 us (2%)
  between operations  1.45 us (1%)
  local copies, waits for them, and re-layouts  1.38 us (1%)
    all_to_all x2, blocking collectives, same_parity(): lax.all_to_all(value, axes, 0, 0, axis_index_groups=parity_groups(), tile...  34.7 us
    ppermute x1, starting transfers between devices, body(): other = lax.ppermute(curvature, 'c', swap)  9.58 us
    ppermute x3, waiting for transfers between devices, body(): lax.ppermute(mine, 'zh', [(i, (i + k) % 4) for i in range(4)])  6.31 us
    ppermute x3, starting transfers between devices, body(): lax.ppermute(mine, 'zh', [(i, (i + k) % 4) for i in range(4)])  5.81 us
    pallas_call x1, Pallas kernels, body(): call(factors_kernel, [((KEPT, B), F32), ((grads, B), F32)] + [((grads, B)...  4.99 us
    ppermute x1, waiting for transfers between devices, body(): sum_8 = sum_4 + lax.ppermute(sum_4, 'zh', HIGH)  4.77 us
    ppermute x5, starting transfers between devices, to_neighbours(): lax.ppermute(part, axis, pairs)  3.84 us
    ppermute x1, starting transfers between devices, body(): other = lax.ppermute(jnp.concatenate([feat, psi], 1).astype(F32), 'c', swap)  3.33 us
  transfers between devices with their start and end apart: 19, of which 6 were waited for; matrix products, arithmetic and copies ran while one was open for 1% of the time, Pallas kernels for 9%

profile of v6, /device:TPU:1, one launch (start us, length us, event | category | flops | bytes accessed | tf_op | source)
XLA Modules:
  0.0 104.5 jit_solution(2502286848053547527)
XLA Ops:
  0.6 0.0 copy-start.1
  0.6 0.0 copy-start.7
  0.7 0.0 copy-start.2
  0.7 1.3 %maximum_convert_fusion = f32[512,512]{1,0:T(8,128)S(1)} fusion(bf16[512,256]{1,0:T(8,128)(2,1)} %bitcast.18, bf16[512,256]{1,0:T(8,128)(2,1)} %bitcast.16), kind=kLoop, calls=%fused_computation | loop fusion | flops 1048576 | bytes 1572864 | tf_op jit(solution)/shard_map/convert_element_type | solution.py:353
  2.0 3.3 %collective-permute-start = (f32[512,512]{1,0:T(8,128)S(1)}, f32[512,512]{1,0:T(8,128)S(1)}, u32[]{:S(2)}, u32[]{:S(2)}) collective-permute-start(f32[512,512]{1,0:T(8,128)S(1)} %maximum_convert_fusion), channel_id=1, source_target_pairs={{0,1},{1,0},{2,3},{3,2},{4,5},{5,4},{6,7},{7,6},{8,9},{9,8},{10,11... | collective-permute-start | bytes 3145736 | tf_op jit(solution)/shard_map/ppermute | solution.py:353
  5.3 0.0 copy-done.1
  5.3 0.1 collective-permute-start.1
  5.4 0.0 copy-done.7
  5.4 1.1 %collective-permute-start.2 = (f32[1,16]{1,0:T(1,128)S(1)}, f32[1,16]{1,0:T(1,128)S(1)}, u32[]{:S(2)}, u32[]{:S(2)}) collective-permute-start(f32[1,16]{1,0:T(1,128)S(1)} %copy-done.7), channel_id=1, source_target_pairs={{0,4},{2,6},{4,0},{6,2},{1,5},{3,7},{5,1},{7,3},{8,12},{10,14},{12... | collective-permute-start | bytes 200 | tf_op jit(solution)/shard_map/ppermute | solution.py:352
  7.2 2.2 %collective-permute-done.2 = f32[1,16]{1,0:T(1,128)S(1)} collective-permute-done((f32[1,16]{1,0:T(1,128)S(1)}, f32[1,16]{1,0:T(1,128)S(1)}, u32[]{:S(2)}, u32[]{:S(2)}) %collective-permute-start.2) | collective-permute-done | bytes 96 | tf_op jit(solution)/shard_map/ppermute | solution.py:352
  9.4 1.3 %collective-permute-start.3 = (f32[1,16]{1,0:T(1,128)S(1)}, f32[1,16]{1,0:T(1,128)S(1)}, u32[]{:S(2)}, u32[]{:S(2)}) collective-permute-start(f32[1,16]{1,0:T(1,128)S(1)} %add.16.near), channel_id=1, source_target_pairs={{0,8},{8,0},{16,24},{24,16},{1,9},{9,1},{17,25},{25,17},{2,10},{10... | collective-permute-start | bytes 200 | tf_op jit(solution)/shard_map/ppermute | solution.py:355
  10.7 0.0 collective-permute-done.1.oth_pair
  10.7 0.0 collective-permute-done.other
  10.7 0.0 copy-done.3
  10.7 0.0 copy-done.5
  10.7 5.0 %factors.1 = (f32[2176,128]{1,0:T(8,128)S(1)}, f32[896,128]{1,0:T(8,128)S(1)}, f32[896,128]{1,0:T(8,128)S(1)}, f32[896,128]{1,0:T(8,128)S(1)}, f32[640,128]{1,0:T(8,128)S(1)}, /*index=5*/f32[640,128]{1,0:T(8,128)S(1)}) custom-call(bf16[512,256]{1,0:T(8,128)(2,1)S(1)} %bitcast.17, bf16[2,512,128]{2,1,0:T(8,128)(2,1)S(1)} %bitcast.15, ...), custom_call_target="tpu_custom_call" | custom-call | flops 2500000000 | bytes 8000000 | tf_op jit(solution)/shard_map/factors/pallas_call | solution.py:358
  15.7 0.0 copy-start
  15.7 0.8 copy-done
  16.5 0.0 collective-permute-done.3.far
  16.5 0.5 copy-done.9
  17.0 1.3 %tie.1 = (f32[896,128]{1,0:T(8,128)}, f32[1,16]{1,0:T(1,128)}) custom-call(f32[896,128]{1,0:T(8,128)} %copy-done, f32[1,16]{1,0:T(1,128)} %copy-done.8, f32[1,16]{1,0:T(1,128)} %copy-done.9), custom_call_target="tpu_custom_call", output_to_operand_aliasing={{0}: (0, {})} | custom-call | tf_op jit(solution)/shard_map/tie/pallas_call | solution.py:379
  18.3 1.2 %collective-permute-start.4 = (f32[896,128]{1,0:T(8,128)}, f32[896,128]{1,0:T(8,128)S(1)}, u32[]{:S(2)}, u32[]{:S(2)}) collective-permute-start(f32[896,128]{1,0:T(8,128)} %get-tuple-element.23), channel_id=1, source_target_pairs={{0,2},{2,0},{4,6},{6,4},{1,3},{3,1},{5,7},{7,5},{8,10},{10,8},{12,... | collective-permute-start | bytes 1376264 | tf_op jit(solution)/shard_map/ppermute | solution.py:387
  19.5 1.8 %collective-permute-start.5 = (f32[896,128]{1,0:T(8,128)S(1)}, f32[896,128]{1,0:T(8,128)S(1)}, u32[]{:S(2)}, u32[]{:S(2)}) collective-permute-start(f32[896,128]{1,0:T(8,128)S(1)} %get-tuple-element.24), channel_id=1, source_target_pairs={{2,4},{4,2},{6,0},{0,6},{3,5},{5,3},{7,1},{1,7},{10,12},{12,10},{1... | collective-permute-start | bytes 1376264 | tf_op jit(solution)/shard_map/ppermute | solution.py:388
  21.3 1.3 %collective-permute-start.6 = (f32[640,128]{1,0:T(8,128)S(1)}, f32[640,128]{1,0:T(8,128)S(1)}, u32[]{:S(2)}, u32[]{:S(2)}) collective-permute-start(f32[640,128]{1,0:T(8,128)S(1)} %get-tuple-element.25), channel_id=1, source_target_pairs={{0,32},{32,0},{64,96},{96,64},{1,33},{33,1},{65,97},{97,65},{2,34}... | collective-permute-start | bytes 983048 | tf_op jit(solution)/shard_map/ppermute | solution.py:389
  22.6 1.6 %collective-permute-start.7 = (f32[640,128]{1,0:T(8,128)S(1)}, f32[640,128]{1,0:T(8,128)S(1)}, u32[]{:S(2)}, u32[]{:S(2)}) collective-permute-start(f32[640,128]{1,0:T(8,128)S(1)} %get-tuple-element.26), channel_id=1, source_target_pairs={{0,128},{128,0},{1,129},{129,1},{2,130},{130,2},{3,131},{131,3},{4... | collective-permute-start | bytes 983048 | tf_op jit(solution)/shard_map/ppermute | solution.py:390
  24.2 3.3 %collective-permute-start.8 = (f32[1,16]{1,0:T(1,128)}, f32[1,16]{1,0:T(1,128)S(1)}, u32[]{:S(2)}, u32[]{:S(2)}) collective-permute-start(f32[1,16]{1,0:T(1,128)} %get-tuple-element.27), channel_id=1, source_target_pairs={{8,16},{16,8},{24,0},{0,24},{9,17},{17,9},{25,1},{1,25},{10,18},{1... | collective-permute-start | bytes 200 | tf_op jit(solution)/shard_map/ppermute | solution.py:391
  27.5 4.8 %collective-permute-done.8 = f32[1,16]{1,0:T(1,128)S(1)} collective-permute-done((f32[1,16]{1,0:T(1,128)}, f32[1,16]{1,0:T(1,128)S(1)}, u32[]{:S(2)}, u32[]{:S(2)}) %collective-permute-start.8) | collective-permute-done | bytes 96 | tf_op jit(solution)/shard_map/ppermute | solution.py:391
  32.3 0.7 add.17.near_sum
  33.0 0.3 collective-permute-start.9
  33.3 2.1 %collective-permute-done.9.far_sum = f32[1,16]{1,0:T(1,128)S(1)} collective-permute-done((f32[1,16]{1,0:T(1,128)S(1)}, f32[1,16]{1,0:T(1,128)S(1)}, u32[]{:S(2)}, u32[]{:S(2)}) %collective-permute-start.9) | collective-permute-done | bytes 96 | tf_op jit(solution)/shard_map/ppermute | solution.py:392
  35.4 0.0 collective-permute-done.6.from_2
  35.4 0.0 collective-permute-done.7.from_3
  35.4 0.0 collective-permute-done.4.from_a
  35.4 0.0 collective-permute-done.5.from_0
  35.4 0.3 add.24
  35.7 18.1 %all_to_all.17 = f32[16,136,128]{2,1,0:T(8,128)S(1)} all-to-all(f32[16,136,128]{2,1,0:T(8,128)S(1)} %bitcast.13), channel_id=1, replica_groups={{0,4,34,38,64,68,98,102,130,134,160,164,194,198,224,228},{2,6,32,36,66,..., dimensions={0} | all-to-all | bytes 2228224 | tf_op jit(solution)/shard_map/all_to_all | solution.py:330
  53.8 0.1 reduce_sum.9
  53.9 1.1 %collective-permute-start.11 = (f32[136,128]{1,0:T(8,128)S(1)}, f32[136,128]{1,0:T(8,128)S(1)}, u32[]{:S(2)}, u32[]{:S(2)}) collective-permute-start(f32[136,128]{1,0:T(8,128)S(1)} %reduce_sum.9), channel_id=1, source_target_pairs={{0,8},{8,16},{16,24},{24,0},{1,9},{9,17},{17,25},{25,1},{2,10},{10... | collective-permute-start | bytes 208904 | tf_op jit(solution)/shard_map/ppermute | solution.py:398
  55.0 2.5 %collective-permute-start.12 = (f32[136,128]{1,0:T(8,128)S(1)}, f32[136,128]{1,0:T(8,128)S(1)}, u32[]{:S(2)}, u32[]{:S(2)}) collective-permute-start(f32[136,128]{1,0:T(8,128)S(1)} %reduce_sum.9), channel_id=1, source_target_pairs={{0,24},{8,0},{16,8},{24,16},{1,25},{9,1},{17,9},{25,17},{2,26},{10... | collective-permute-start | bytes 208904 | tf_op jit(solution)/shard_map/ppermute | solution.py:398
  57.5 2.2 %collective-permute-start.10 = (f32[136,128]{1,0:T(8,128)S(1)}, f32[136,128]{1,0:T(8,128)S(1)}, u32[]{:S(2)}, u32[]{:S(2)}) collective-permute-start(f32[136,128]{1,0:T(8,128)S(1)} %reduce_sum.9), channel_id=1, source_target_pairs={{0,16},{8,24},{16,0},{24,8},{1,17},{9,25},{17,1},{25,9},{2,18},{10... | collective-permute-start | bytes 208904 | tf_op jit(solution)/shard_map/ppermute | solution.py:398
  59.7 0.0 collective-permute-done.11
  59.7 0.1 collective-permute-done.12
  59.8 6.2 %collective-permute-done.10 = f32[136,128]{1,0:T(8,128)S(1)} collective-permute-done((f32[136,128]{1,0:T(8,128)S(1)}, f32[136,128]{1,0:T(8,128)S(1)}, u32[]{:S(2)}, u32[]{:S(2)}) %collective-permute-start.10) | collective-permute-done | bytes 69664 | tf_op jit(solution)/shard_map/ppermute | solution.py:398
  66.0 0.0 copy-start.6
  66.0 0.1 broadcast_in_dim.15
  66.1 0.0 copy-start.4
  66.1 16.6 %all_to_all.18 = f32[16,136,128]{2,1,0:T(8,128)S(1)} all-to-all(f32[16,136,128]{2,1,0:T(8,128)S(1)} %broadcast_in_dim.15), channel_id=1, replica_groups={{0,4,34,38,64,68,98,102,130,134,160,164,194,198,224,228},{2,6,32,36,66,..., dimensions={0} | all-to-all | bytes 2228224 | tf_op jit(solution)/shard_map/all_to_all | solution.py:330
  82.7 0.1 cut.1
  82.8 0.8 collective-permute-start.16
  83.6 0.5 collective-permute-start.17
  84.1 0.8 collective-permute-start.13
  84.8 0.7 collective-permute-start.14
  85.6 1.1 %collective-permute-start.15 = (f32[384,128]{1,0:T(8,128)S(1)}, f32[384,128]{1,0:T(8,128)S(1)}, u32[]{:S(2)}, u32[]{:S(2)}) collective-permute-start(f32[384,128]{1,0:T(8,128)S(1)} %get-tuple-element.30), channel_id=1, source_target_pairs={{32,64},{64,32},{96,0},{0,96},{33,65},{65,33},{97,1},{1,97},{34,66... | collective-permute-start | bytes 589832 | tf_op jit(solution)/shard_map/ppermute | solution.py:338
  86.6 2.6 %collective-permute-done.17.from_1 = f32[384,128]{1,0:T(8,128)S(1)} collective-permute-done((f32[384,128]{1,0:T(8,128)S(1)}, f32[384,128]{1,0:T(8,128)S(1)}, u32[]{:S(2)}, u32[]{:S(2)}) %collective-permute-start.17) | collective-permute-done | bytes 196640 | tf_op jit(solution)/shard_map/ppermute | solution.py:338
  89.2 0.0 collective-permute-done.16.from_0
  89.2 0.0 copy-done.4
  89.2 2.5 %natural.1 = (f32[896,256]{1,0:T(8,128)S(1)}, f32[1,128]{1,0:T(1,128)S(1)}) custom-call(f32[2176,128]{1,0:T(8,128)S(1)} %bitcast.11, f32[512,128]{1,0:T(8,128)S(1)} %collective-permute-done.16.from_0, f32[384,128]{1,0:T(8,128)S(1)} %collective-permute-done.17.from_1, f32[896,896]{1,0:T(8,128)S(1)} %bitcast.20, f32[256,256]{1,0:T(8,128)S(1)} %bitcast.21), custom_call_target="tpu_custom_call" | custom-call | flops 1500000000 | bytes 5000000 | tf_op jit(solution)/shard_map/natural/pallas_call | solution.py:405
  91.7 9.6 %collective-permute-start.18 = (f32[1,128]{1,0:T(1,128)S(1)}, f32[1,128]{1,0:T(1,128)S(1)}, u32[]{:S(2)}, u32[]{:S(2)}) collective-permute-start(f32[1,128]{1,0:T(1,128)S(1)} %get-tuple-element.36.curvature), channel_id=1, source_target_pairs={{0,1},{1,0},{2,3},{3,2},{4,5},{5,4},{6,7},{7,6},{8,9},{9,8},{10,11... | collective-permute-start | bytes 1544 | tf_op jit(solution)/shard_map/ppermute | solution.py:414
  101.3 0.0 collective-permute-done.14.from_3
  101.3 0.0 collective-permute-done.15.from_4
  101.3 0.0 collective-permute-done.13.from_2
  101.3 2.1 %unpack.1 = (f32[896,896]{1,0:T(8,128)}, f32[256,256]{1,0:T(8,128)}) custom-call(f32[2176,128]{1,0:T(8,128)S(1)} %bitcast.12, f32[512,128]{1,0:T(8,128)S(1)} %collective-permute-done.13.from_2, f32[384,128]{1,0:T(8,128)S(1)} %collective-permute-done.14.from_3, f32[384,128]{1,0:T(8,128)S(1)} %collective-permute-done.15.from_4), custom_call_target="tpu_custom_call" | custom-call | flops 10000000 | bytes 6000000 | tf_op jit(solution)/shard_map/unpack/pallas_call | solution.py:415
  103.5 0.0 collective-permute-done.18.other
  103.5 1.1 %scale.1 = f32[896,256]{1,0:T(8,128)} custom-call(f32[896,256]{1,0:T(8,128)S(1)} %get-tuple-element.35.natural, f32[1,128]{1,0:T(1,128)S(1)} %get-tuple-element.36.curvature, f32[1,128]{1,0:T(1,128)S(1)} %collective-permute-done.18.other), custom_call_target="tpu_custom_call" | custom-call | flops 1000000 | bytes 2000000 | tf_op jit(solution)/shard_map/scale/pallas_call | solution.py:424
  (10 shorter events, 0.1 us)
Async XLA Ops:
  0.6 4.7 %copy-start.1 = (bf16[1,2,16,32,128]{4,3,2,1,0:T(8,128)(2,1)S(1)}, bf16[1,2,16,32,128]{4,3,2,1,0:T(8,128)(2,1)}, u32[]{:S(2)}) copy-start(bf16[1,2,16,32,128]{4,3,2,1,0:T(8,128)(2,1)} %param.10) | copy-start | bytes 786436
  0.6 4.8 %copy-start.7 = (f32[1,16]{1,0:T(1,128)S(1)}, f32[1,16]{1,0:T(1,128)}, u32[]{:S(2)}) copy-start(f32[1,16]{1,0:T(1,128)} %energy.1) | copy-start | bytes 196
  0.7 10.0 %copy-start.2 = (bf16[1,16,32,256]{3,2,1,0:T(8,128)(2,1)S(1)}, bf16[1,16,32,256]{3,2,1,0:T(8,128)(2,1)}, u32[]{:S(2)}) copy-start(bf16[1,16,32,256]{3,2,1,0:T(8,128)(2,1)} %param.8) | copy-start | bytes 786436
  0.7 10.0 %copy-start.3 = (bf16[1,16,32,256]{3,2,1,0:T(8,128)(2,1)S(1)}, bf16[1,16,32,256]{3,2,1,0:T(8,128)(2,1)}, u32[]{:S(2)}) copy-start(bf16[1,16,32,256]{3,2,1,0:T(8,128)(2,1)} %param.9) | copy-start | bytes 786436
  0.7 10.0 %copy-start.5 = (bf16[2,896,256]{2,1,0:T(8,128)(2,1)S(1)}, bf16[2,896,256]{2,1,0:T(8,128)(2,1)}, u32[]{:S(2)}) copy-start(bf16[2,896,256]{2,1,0:T(8,128)(2,1)} %weights.1) | copy-start | bytes 2752516
  2.0 8.7 %collective-permute-start = (f32[512,512]{1,0:T(8,128)S(1)}, f32[512,512]{1,0:T(8,128)S(1)}, u32[]{:S(2)}, u32[]{:S(2)}) collective-permute-start(f32[512,512]{1,0:T(8,128)S(1)} %maximum_convert_fusion), channel_id=1, source_target_pairs={{0,1},{1,0},{2,3},{3,2},{4,5},{5,4},{6,7},{7,6},{8,9},{9,8},{10,11... | collective-permute-start | bytes 3145736 | tf_op jit(solution)/shard_map/ppermute | solution.py:353
  5.3 5.4 %collective-permute-start.1 = (f32[2,512,128]{2,1,0:T(8,128)S(1)}, f32[2,512,128]{2,1,0:T(8,128)S(1)}, u32[]{:S(2)}, u32[]{:S(2)}) collective-permute-start(f32[2,512,128]{2,1,0:T(8,128)S(1)} %convert_element_type.7), channel_id=1, source_target_pairs={{0,1},{1,0},{2,3},{3,2},{4,5},{5,4},{6,7},{7,6},{8,9},{9,8},{10,11... | collective-permute-start | bytes 1572872 | tf_op jit(solution)/shard_map/ppermute | solution.py:354
  5.4 4.0 %collective-permute-start.2 = (f32[1,16]{1,0:T(1,128)S(1)}, f32[1,16]{1,0:T(1,128)S(1)}, u32[]{:S(2)}, u32[]{:S(2)}) collective-permute-start(f32[1,16]{1,0:T(1,128)S(1)} %copy-done.7), channel_id=1, source_target_pairs={{0,4},{2,6},{4,0},{6,2},{1,5},{3,7},{5,1},{7,3},{8,12},{10,14},{12... | collective-permute-start | bytes 200 | tf_op jit(solution)/shard_map/ppermute | solution.py:352
  9.4 6.3 %copy-start.8 = (f32[1,16]{1,0:T(1,128)}, f32[1,16]{1,0:T(1,128)S(1)}, u32[]{:S(2)}) copy-start(f32[1,16]{1,0:T(1,128)S(1)} %add.16.near) | copy-start | bytes 196
  9.4 7.1 %collective-permute-start.3 = (f32[1,16]{1,0:T(1,128)S(1)}, f32[1,16]{1,0:T(1,128)S(1)}, u32[]{:S(2)}, u32[]{:S(2)}) collective-permute-start(f32[1,16]{1,0:T(1,128)S(1)} %add.16.near), channel_id=1, source_target_pairs={{0,8},{8,0},{16,24},{24,16},{1,9},{9,1},{17,25},{25,17},{2,10},{10... | collective-permute-start | bytes 200 | tf_op jit(solution)/shard_map/ppermute | solution.py:355
  15.7 0.8 copy-start
  16.5 0.5 copy-start.9
  18.3 17.1 %collective-permute-start.4 = (f32[896,128]{1,0:T(8,128)}, f32[896,128]{1,0:T(8,128)S(1)}, u32[]{:S(2)}, u32[]{:S(2)}) collective-permute-start(f32[896,128]{1,0:T(8,128)} %get-tuple-element.23), channel_id=1, source_target_pairs={{0,2},{2,0},{4,6},{6,4},{1,3},{3,1},{5,7},{7,5},{8,10},{10,8},{12,... | collective-permute-start | bytes 1376264 | tf_op jit(solution)/shard_map/ppermute | solution.py:387
  19.5 15.9 %collective-permute-start.5 = (f32[896,128]{1,0:T(8,128)S(1)}, f32[896,128]{1,0:T(8,128)S(1)}, u32[]{:S(2)}, u32[]{:S(2)}) collective-permute-start(f32[896,128]{1,0:T(8,128)S(1)} %get-tuple-element.24), channel_id=1, source_target_pairs={{2,4},{4,2},{6,0},{0,6},{3,5},{5,3},{7,1},{1,7},{10,12},{12,10},{1... | collective-permute-start | bytes 1376264 | tf_op jit(solution)/shard_map/ppermute | solution.py:388
  21.3 14.1 %collective-permute-start.6 = (f32[640,128]{1,0:T(8,128)S(1)}, f32[640,128]{1,0:T(8,128)S(1)}, u32[]{:S(2)}, u32[]{:S(2)}) collective-permute-start(f32[640,128]{1,0:T(8,128)S(1)} %get-tuple-element.25), channel_id=1, source_target_pairs={{0,32},{32,0},{64,96},{96,64},{1,33},{33,1},{65,97},{97,65},{2,34}... | collective-permute-start | bytes 983048 | tf_op jit(solution)/shard_map/ppermute | solution.py:389
  22.6 12.8 %collective-permute-start.7 = (f32[640,128]{1,0:T(8,128)S(1)}, f32[640,128]{1,0:T(8,128)S(1)}, u32[]{:S(2)}, u32[]{:S(2)}) collective-permute-start(f32[640,128]{1,0:T(8,128)S(1)} %get-tuple-element.26), channel_id=1, source_target_pairs={{0,128},{128,0},{1,129},{129,1},{2,130},{130,2},{3,131},{131,3},{4... | collective-permute-start | bytes 983048 | tf_op jit(solution)/shard_map/ppermute | solution.py:390
  24.2 8.1 %collective-permute-start.8 = (f32[1,16]{1,0:T(1,128)}, f32[1,16]{1,0:T(1,128)S(1)}, u32[]{:S(2)}, u32[]{:S(2)}) collective-permute-start(f32[1,16]{1,0:T(1,128)} %get-tuple-element.27), channel_id=1, source_target_pairs={{8,16},{16,8},{24,0},{0,24},{9,17},{17,9},{25,1},{1,25},{10,18},{1... | collective-permute-start | bytes 200 | tf_op jit(solution)/shard_map/ppermute | solution.py:391
  33.0 2.4 %collective-permute-start.9 = (f32[1,16]{1,0:T(1,128)S(1)}, f32[1,16]{1,0:T(1,128)S(1)}, u32[]{:S(2)}, u32[]{:S(2)}) collective-permute-start(f32[1,16]{1,0:T(1,128)S(1)} %add.17.near_sum), channel_id=1, source_target_pairs={{0,2},{2,0},{4,6},{6,4},{1,3},{3,1},{5,7},{7,5},{8,10},{10,8},{12,... | collective-permute-start | bytes 200 | tf_op jit(solution)/shard_map/ppermute | solution.py:392
  53.9 5.8 %collective-permute-start.11 = (f32[136,128]{1,0:T(8,128)S(1)}, f32[136,128]{1,0:T(8,128)S(1)}, u32[]{:S(2)}, u32[]{:S(2)}) collective-permute-start(f32[136,128]{1,0:T(8,128)S(1)} %reduce_sum.9), channel_id=1, source_target_pairs={{0,8},{8,16},{16,24},{24,0},{1,9},{9,17},{17,25},{25,1},{2,10},{10... | collective-permute-start | bytes 208904 | tf_op jit(solution)/shard_map/ppermute | solution.py:398
  55.0 4.8 %collective-permute-start.12 = (f32[136,128]{1,0:T(8,128)S(1)}, f32[136,128]{1,0:T(8,128)S(1)}, u32[]{:S(2)}, u32[]{:S(2)}) collective-permute-start(f32[136,128]{1,0:T(8,128)S(1)} %reduce_sum.9), channel_id=1, source_target_pairs={{0,24},{8,0},{16,8},{24,16},{1,25},{9,1},{17,9},{25,17},{2,26},{10... | collective-permute-start | bytes 208904 | tf_op jit(solution)/shard_map/ppermute | solution.py:398
  57.5 8.5 %collective-permute-start.10 = (f32[136,128]{1,0:T(8,128)S(1)}, f32[136,128]{1,0:T(8,128)S(1)}, u32[]{:S(2)}, u32[]{:S(2)}) collective-permute-start(f32[136,128]{1,0:T(8,128)S(1)} %reduce_sum.9), channel_id=1, source_target_pairs={{0,16},{8,24},{16,0},{24,8},{1,17},{9,25},{17,1},{25,9},{2,18},{10... | collective-permute-start | bytes 208904 | tf_op jit(solution)/shard_map/ppermute | solution.py:398
  66.0 23.2 %copy-start.6 = (f32[1,256,256]{2,1,0:T(8,128)S(1)}, f32[1,256,256]{2,1,0:T(8,128)}, u32[]{:S(2)}) copy-start(f32[1,256,256]{2,1,0:T(8,128)} %param.15) | copy-start | bytes 786436
  66.1 23.1 %copy-start.4 = (f32[1,896,896]{2,1,0:T(8,128)S(1)}, f32[1,896,896]{2,1,0:T(8,128)}, u32[]{:S(2)}) copy-start(f32[1,896,896]{2,1,0:T(8,128)} %param.14) | copy-start | bytes 9633796
  82.8 6.4 %collective-permute-start.16 = (f32[512,128]{1,0:T(8,128)S(1)}, f32[512,128]{1,0:T(8,128)S(1)}, u32[]{:S(2)}, u32[]{:S(2)}) collective-permute-start(f32[512,128]{1,0:T(8,128)S(1)} %get-tuple-element.33), channel_id=1, source_target_pairs={{0,2},{2,0},{4,6},{6,4},{1,3},{3,1},{5,7},{7,5},{8,10},{10,8},{12,... | collective-permute-start | bytes 786440 | tf_op jit(solution)/shard_map/ppermute | solution.py:338
  83.6 5.6 %collective-permute-start.17 = (f32[384,128]{1,0:T(8,128)S(1)}, f32[384,128]{1,0:T(8,128)S(1)}, u32[]{:S(2)}, u32[]{:S(2)}) collective-permute-start(f32[384,128]{1,0:T(8,128)S(1)} %get-tuple-element.34), channel_id=1, source_target_pairs={{0,32},{32,0},{64,96},{96,64},{1,33},{33,1},{65,97},{97,65},{2,34}... | collective-permute-start | bytes 589832 | tf_op jit(solution)/shard_map/ppermute | solution.py:338
  84.1 17.2 %collective-permute-start.13 = (f32[512,128]{1,0:T(8,128)S(1)}, f32[512,128]{1,0:T(8,128)S(1)}, u32[]{:S(2)}, u32[]{:S(2)}) collective-permute-start(f32[512,128]{1,0:T(8,128)S(1)} %get-tuple-element.28), channel_id=1, source_target_pairs={{0,128},{128,0},{1,129},{129,1},{2,130},{130,2},{3,131},{131,3},{4... | collective-permute-start | bytes 786440 | tf_op jit(solution)/shard_map/ppermute | solution.py:338
  84.8 16.5 %collective-permute-start.14 = (f32[384,128]{1,0:T(8,128)S(1)}, f32[384,128]{1,0:T(8,128)S(1)}, u32[]{:S(2)}, u32[]{:S(2)}) collective-permute-start(f32[384,128]{1,0:T(8,128)S(1)} %get-tuple-element.29), channel_id=1, source_target_pairs={{2,4},{4,2},{6,0},{0,6},{3,5},{5,3},{7,1},{1,7},{10,12},{12,10},{1... | collective-permute-start | bytes 589832 | tf_op jit(solution)/shard_map/ppermute | solution.py:338
  85.6 15.7 %collective-permute-start.15 = (f32[384,128]{1,0:T(8,128)S(1)}, f32[384,128]{1,0:T(8,128)S(1)}, u32[]{:S(2)}, u32[]{:S(2)}) collective-permute-start(f32[384,128]{1,0:T(8,128)S(1)} %get-tuple-element.30), channel_id=1, source_target_pairs={{32,64},{64,32},{96,0},{0,96},{33,65},{65,33},{97,1},{1,97},{34,66... | collective-permute-start | bytes 589832 | tf_op jit(solution)/shard_map/ppermute | solution.py:338
  91.7 11.7 %collective-permute-start.18 = (f32[1,128]{1,0:T(1,128)S(1)}, f32[1,128]{1,0:T(1,128)S(1)}, u32[]{:S(2)}, u32[]{:S(2)}) collective-permute-start(f32[1,128]{1,0:T(1,128)S(1)} %get-tuple-element.36.curvature), channel_id=1, source_target_pairs={{0,1},{1,0},{2,3},{3,2},{4,5},{5,4},{6,7},{7,6},{8,9},{9,8},{10,11... | collective-permute-start | bytes 1544 | tf_op jit(solution)/shard_map/ppermute | solution.py:414

commit v7 on v5

--- a/solution.py
+++ b/solution.py
@@ -64,8 +64,8 @@
 
 
 def factors_kernel(
-    feat, pair, psi, other, oth_pair, weights, half_sum, half_other, energies, energy, multiplicity,
-    keep, keep_0, to_a, to_0, to_2, to_3, row_sum, x_s, d_s, m_s, s_s, c_s, out, out_0
+    feat, pair, psi, other, oth_pair, weights, energies, energy, multiplicity,
+    keep, keep_0, to_a, to_0, to_2, to_3, x_s, d_s, m_s, s_s, w_s, out, out_0
 ):
     mp = lax.axis_index("c")
     own_row = pl.multiple_of(D + D * mp, D)
@@ -108,20 +108,24 @@
     l = mp
     mult = multiplicity[0].astype(F32)
     row_scale = mult * (1.0 / 16384.0)
-    x = x_s[l]
-    s = s_s[l]
     mean = jnp.sum(energies[...], axis=1, keepdims=True) * (1.0 / WALK)
     shifted = mean + SHIFT
-    zh_sum = jnp.sum(half_sum[...] + half_other[...], axis=1, keepdims=True)
-    row_sum[...] = jnp.broadcast_to(zh_sum, (8, B))
+    at_p, at_c, at_low, at_s = D, D + PAIR, 2 * D + PAIR, 3 * D + PAIR
+    w_s[:, :at_c] = x_s[l]
+    w_s[:, at_s:] = s_s[l]
     step = HALF // WALK
     for w in range(WALK):
         centered = energy[0, w] - mean
         for first in (w * step, HALF + w * step):
             rows = slice(first, first + step)
-            c_s[rows, :] = (centered * s_s[l, rows, :].astype(F32)).astype(BF16)
-    c = c_s[...]
-    h, p = x[:, :D], x[:, D:]
+            high, low = split(centered * w_s[rows, at_s:].astype(F32))
+            w_s[rows, at_c:at_low] = high
+            w_s[rows, at_low:at_s] = low
+    with_h = dot_t(w_s[:, :D], w_s[...])
+    with_p = dot_t(w_s[:, at_p:at_c], w_s[:, at_p:])
+    with_s = dot_t(w_s[:, at_s:], w_s[:, at_s:])
+    totals = dot(pick, w_s[:, at_p:])
+    totals = totals[:WALK] + totals[WALK:]
     row, col = square_iotas()
 
     parity = own_parity()
@@ -144,19 +148,20 @@
         put(slot + 1, full[:B, B:])
         lines[line] = jnp.sum(jnp.where(col == row, low, 0.0), axis=0, keepdims=True) * row_scale
 
-    put_symmetric(0, 0, dot_t(h, h))
-    hp = dot_t(h, p)
+    put_symmetric(0, 0, with_h[:, :D])
+    hp = with_h[:, at_p:at_c]
     put(11, hp[:B])
     put(12, hp[B:])
-    put(10, dot_t(p, p))
-    hc, hs = dot_t(h, c), dot_t(h, s)
-    pc, ps = dot_t(p, c), dot_t(p, s)
+    put(10, with_p[:, :PAIR])
+    hc, hs = with_h[:, at_c:at_low] + with_h[:, at_low:at_s], with_h[:, at_s:]
+    pc = with_p[:, PAIR : PAIR + D] + with_p[:, PAIR + D : PAIR + 2 * D]
+    ps = with_p[:, PAIR + 2 * D :]
     for j in range(2):
         cols = slice(j * B, (j + 1) * B)
         put_grad(19 + j, hc[:B, cols], hs[:B, cols])
         put_grad(21 + j, hc[B:, cols], hs[B:, cols])
         put_grad(31 + j, pc[:, cols], ps[:, cols])
-    put_symmetric(17, 3, dot_t(s, s))
+    put_symmetric(17, 3, with_s)
 
     means = m_s[l]
     up_first = mp == 0
@@ -169,8 +174,10 @@
     for i in range(2):
         for j in range(2):
             put(6 + 2 * i + j, mm[i * B : (i + 1) * B, D + j * B : D + (j + 1) * B])
-    totals = dot(pick, jnp.concatenate([p, c, s], 1))
-    t_high, t_low = split(totals[:WALK] + totals[WALK:])
+    totals = jnp.concatenate(
+        [totals[:, :PAIR], totals[:, PAIR : PAIR + D] + totals[:, PAIR + D : PAIR + 2 * D], totals[:, PAIR + 2 * D :]], 1
+    )
+    t_high, t_low = split(totals)
     side = dot_t(jnp.concatenate([both, both], 0), jnp.concatenate([t_high, t_low], 0))
     for i in range(4):
         rows = slice(i * B, (i + 1) * B)
@@ -186,12 +193,19 @@
     keep[...] = out[0]
     keep_0[...] = out_0[0]
     grads = GRADS * B
-    to_a[:grads, :] = out[1, :grads, :]
-    to_0[:grads, :] = out_0[1]
-    to_a[grads:, :] = row_sum[...]
-    to_0[grads:, :] = row_sum[...]
+    to_a[...] = out[1, :grads, :]
+    to_0[...] = out_0[1]
     for target, (first, end) in zip((to_2, to_3), OUT_STREAMS):
         target[...] = out[1, first * B : end * B, :]
+
+
+def tie_kernel(plain_a, plain_0, near, far, to_a, to_0, row_sum):
+    zh_sum = jnp.sum(near[...] + far[...], axis=1, keepdims=True)
+    row_sum[...] = jnp.broadcast_to(zh_sum, (8, B))
+    grads = GRADS * B
+    for source, target in ((plain_a, to_a), (plain_0, to_0)):
+        target[:grads, :] = source[...]
+        target[grads:, :] = row_sum[...]
 
 
 def add_kernel(keep, keep_0, from_a, from_0, from_2, from_3, row_sum, row_two, total):
@@ -224,11 +238,12 @@
     return read
 
 
-def unpack_kernel(kept, from_2, from_3, from_4, a_out, s_out):
+def unpack_kernel(kept, from_2, from_3, from_4, a_out, s_out, a_v, s_v, sems):
     row, col = square_iotas()
     read = reader(kept, (from_2, from_3, from_4), BACK_STREAMS[2:])
     lines = read(33, 8)
     inverse = 1.0 / lines[4:5, :]
+    copies = []
 
     def get(slot):
         return read(slot) * inverse
@@ -246,31 +261,50 @@
     def place(target, i, j, value):
         target[i * B : (i + 1) * B, j * B : (j + 1) * B] = value
 
+    def send(source, target, first, end):
+        rows = slice(first * B, end * B)
+        copy = pltpu.make_async_copy(source.at[rows], target.at[rows], sems.at[len(copies)])
+        copy.start()
+        copies.append(copy)
+
     ss = symmetric(17, 3)
-    hh = symmetric(0, 0)
     for i in range(2):
         for j in range(2):
-            place(s_out, i, j, ss[i][j])
-            place(a_out, i, j, hh[i][j])
+            place(s_v, i, j, ss[i][j])
+    send(s_v, s_out, 0, 2)
     uu = symmetric(2, 1)
     dd = symmetric(4, 2)
     ud = [[get(6 + 2 * i + j) for j in range(2)] for i in range(2)]
     du = [[ud[j][i].T for j in range(2)] for i in range(2)]
+    sides = [get(11 + i) for i in range(6)]
     for i in range(2):
         for j in range(2):
-            place(a_out, 2 + i, 2 + j, uu[i][j])
-            place(a_out, 4 + i, 4 + j, dd[i][j])
-            place(a_out, 2 + i, 4 + j, ud[i][j])
-            place(a_out, 4 + i, 2 + j, du[i][j])
-            place(a_out, i, 2 + j, (uu[i][j] + du[i][j]) * 0.5)
-            place(a_out, i, 4 + j, (ud[i][j] + dd[i][j]) * 0.5)
-            place(a_out, 2 + i, j, (uu[i][j] + ud[i][j]) * 0.5)
-            place(a_out, 4 + i, j, (du[i][j] + dd[i][j]) * 0.5)
-    place(a_out, 6, 6, get(10))
+            place(a_v, 2 + i, j, (uu[i][j] + ud[i][j]) * 0.5)
+            place(a_v, 2 + i, 2 + j, uu[i][j])
+            place(a_v, 2 + i, 4 + j, ud[i][j])
+        place(a_v, 2 + i, 6, sides[2 + i])
+    send(a_v, a_out, 2, 4)
+    for i in range(2):
+        for j in range(2):
+            place(a_v, 4 + i, j, (du[i][j] + dd[i][j]) * 0.5)
+            place(a_v, 4 + i, 2 + j, du[i][j])
+            place(a_v, 4 + i, 4 + j, dd[i][j])
+        place(a_v, 4 + i, 6, sides[4 + i])
+    send(a_v, a_out, 4, 6)
+    hh = symmetric(0, 0)
+    for i in range(2):
+        for j in range(2):
+            place(a_v, i, j, hh[i][j])
+            place(a_v, i, 2 + j, (uu[i][j] + du[i][j]) * 0.5)
+            place(a_v, i, 4 + j, (ud[i][j] + dd[i][j]) * 0.5)
+        place(a_v, i, 6, sides[i])
+    send(a_v, a_out, 0, 2)
     for i in range(6):
-        block = get(11 + i)
-        place(a_out, i, 6, block)
-        place(a_out, 6, i, block.T)
+        place(a_v, 6, i, sides[i].T)
+    place(a_v, 6, 6, get(10))
+    send(a_v, a_out, 6, 7)
+    for copy in copies:
+        copy.wait()
 
 
 def natural_kernel(kept, from_0, from_1, a_inverse, s_inverse, natural, curvature):
@@ -298,12 +332,12 @@
     direction[...] = natural[...] * lax.rsqrt(total * (1.0 / ENTRIES))
 
 
-def call(kernel, out_shapes, in_spaces, limit_mib, name, scratch=(), flops=0, moved=0):
+def call(kernel, out_shapes, in_spaces, limit_mib, name, scratch=(), flops=0, moved=0, out_space=pltpu.VMEM):
     return pl.pallas_call(
         kernel,
         out_shape=tuple(jax.ShapeDtypeStruct(shape, dtype) for shape, dtype in out_shapes),
         in_specs=[pl.BlockSpec(memory_space=space) for space in in_spaces],
-        out_specs=tuple(pl.BlockSpec(memory_space=pltpu.VMEM) for _ in out_shapes),
+        out_specs=tuple(pl.BlockSpec(memory_space=out_space) for _ in out_shapes),
         scratch_shapes=scratch,
         compiler_params=pltpu.CompilerParams(vmem_limit_bytes=limit_mib * 1024 * 1024),
         cost_estimate=pl.CostEstimate(flops=flops, bytes_accessed=moved, transcendentals=0),
@@ -348,19 +382,18 @@
     pair = pair_means.reshape(2, HALF, PAIR)
     swap = [(0, 1), (1, 0)]
 
-    half_sum = energies + lax.ppermute(energies, "zh", LOW)
+    sum_2 = energies + lax.ppermute(energies, "zh", LOW)
     other = lax.ppermute(jnp.concatenate([feat, psi], 1).astype(F32), "c", swap)
     oth_pair = lax.ppermute(pair.astype(F32), "c", swap)
-    half_other = lax.ppermute(half_sum, "zh", HIGH)
+    far_2 = lax.ppermute(sum_2, "zh", HIGH)
 
     grads = GRADS * B
-    keep, keep_0, to_a, to_0, to_2, to_3, row_sum = call(
+    keep, keep_0, to_a, to_0, to_2, to_3 = call(
         factors_kernel,
         [((KEPT, B), F32), ((grads, B), F32)]
-        + [((grads + 8, B), F32)] * 2
-        + streams_of(OUT_STREAMS)
-        + [((8, B), F32)],
-        [V] * 9 + [S] * 2,
+        + [((grads, B), F32)] * 2
+        + streams_of(OUT_STREAMS),
+        [V] * 7 + [S] * 2,
         26,
         "factors",
         scratch=[
@@ -368,14 +401,17 @@
             pltpu.VMEM((2, ROWS, D), F32),
             pltpu.VMEM((2, 2 * WALK, D), BF16),
             pltpu.VMEM((2, ROWS, D), BF16),
-            pltpu.VMEM((ROWS, D), BF16),
+            pltpu.VMEM((ROWS, 4 * D + PAIR), BF16),
             pltpu.VMEM((2, KEPT, B), F32),
             pltpu.VMEM((2, grads, B), F32),
         ],
         flops=2_500_000_000,
         moved=8_000_000,
-    )(feat, pair, psi, other, oth_pair, weights, half_sum, half_other, energies, energies, multiplicity)
-
+    )(feat, pair, psi, other, oth_pair, weights, energies, energies, multiplicity)
+
+    to_a, to_0, row_sum = call(
+        tie_kernel, [((grads + 8, B), F32)] * 2 + [((8, B), F32)], [V] * 4, 6, "tie", moved=2_000_000
+    )(to_a, to_0, sum_2, far_2)
     from_a = lax.ppermute(to_a, "x", LOW)
     from_0 = lax.ppermute(to_0, "x", HIGH)
     from_2 = lax.ppermute(to_2, "y", LOW)
@@ -409,6 +445,8 @@
         [V] * 4,
         14,
         "unpack",
+        scratch=[pltpu.VMEM((DIN, DIN), F32), pltpu.VMEM((D, D), F32), pltpu.SemaphoreType.DMA((5,))],
+        out_space=pl.ANY,
         flops=10_000_000,
         moved=6_000_000,
     )(kept, *parts[2:])

time: 100 us -> 101 us (1.010)
  starting transfers between devices: 34.4 us -> 30.5 us
  blocking collectives: 38.8 us -> 41.1 us
  waiting for transfers between devices: 13.8 us -> 15.7 us
    ppermute x3, waiting for transfers between devices: 3.33 us -> 6.55 us  [body(): lax.ppermute(mine, 'zh', [(i, (i + k) % 4) for i in range(4)])]
    ppermute x3, starting transfers between devices: 7.59 us -> 4.63 us  [body(): lax.ppermute(mine, 'zh', [(i, (i + k) % 4) for i in range(4)])]
    all_to_all x2, blocking collectives: 38.8 us -> 41.1 us  [same_parity(): lax.all_to_all(value, axes, 0, 0, axis_index_groups=parity_groups(), tile...]
    pallas_call x1 -> x2, Pallas kernels: 4.49 us -> 5.02 us  [the longest x1 4.94 us: body(): call(factors_kernel, [((KEPT, B), F32), ((grads, B), F32)] + [((grads, B)...]
  transfers between devices with their start and end apart: 18 -> 18, of which waited for: 6 -> 7; matrix products, arithmetic and copies ran while one was open for 0% -> 0% of each run, Pallas kernels for 5% -> 9%
where the time goes in v7:
time: 101 us
  blocking collectives  41.1 us (41%)
  starting transfers between devices  30.5 us (30%)
  waiting for transfers between devices  15.7 us (16%)
  Pallas kernels  10.8 us (11%)
  between operations  1.45 us (1%)
  other arithmetic  1.39 us (1%)
    all_to_all x2, blocking collectives, same_parity(): lax.all_to_all(value, axes, 0, 0, axis_index_groups=parity_groups(), tile...  41.1 us
    ppermute x1, waiting for transfers between devices, body(): row_two = lax.ppermute(row_sum, 'x', [(0, 2), (1, 3), (2, 0), (3, 1)])  6.57 us
    ppermute x3, waiting for transfers between devices, body(): lax.ppermute(mine, 'zh', [(i, (i + k) % 4) for i in range(4)])  6.55 us
    ppermute x1, starting transfers between devices, body(): other = lax.ppermute(curvature, 'c', swap)  6.23 us
    pallas_call x1, Pallas kernels, body(): call(factors_kernel, [((KEPT, B), F32), ((grads, B), F32)] + [((grads, B)...  4.94 us
    ppermute x5, starting transfers between devices, to_neighbours(): lax.ppermute(part, axis, pairs)  4.77 us
    ppermute x3, starting transfers between devices, body(): lax.ppermute(mine, 'zh', [(i, (i + k) % 4) for i in range(4)])  4.63 us
    ppermute x1, starting transfers between devices, body(): far_2 = lax.ppermute(sum_2, 'zh', HIGH)  4.28 us
  transfers between devices with their start and end apart: 18, of which 7 were waited for; matrix products, arithmetic and copies ran while one was open for 0% of the time, Pallas kernels for 9%

profile of v7, /device:TPU:1, one launch (start us, length us, event | category | flops | bytes accessed | tf_op | source)
XLA Modules:
  0.0 101.0 jit_solution(15736137419436996659)
XLA Ops:
  0.6 0.0 copy-start
  0.6 0.0 copy-start.6
  0.7 0.0 copy-start.1
  0.7 0.0 copy-start.2
  0.7 0.0 copy-start.4
  0.7 1.3 %maximum_convert_fusion = f32[512,512]{1,0:T(8,128)S(1)} fusion(bf16[512,256]{1,0:T(8,128)(2,1)} %bitcast.18, bf16[512,256]{1,0:T(8,128)(2,1)} %bitcast.16), kind=kLoop, calls=%fused_computation | loop fusion | flops 1048576 | bytes 1572864 | tf_op jit(solution)/shard_map/convert_element_type | solution.py:386
  2.0 3.3 %collective-permute-start = (f32[512,512]{1,0:T(8,128)S(1)}, f32[512,512]{1,0:T(8,128)S(1)}, u32[]{:S(2)}, u32[]{:S(2)}) collective-permute-start(f32[512,512]{1,0:T(8,128)S(1)} %maximum_convert_fusion), channel_id=1, source_target_pairs={{0,1},{1,0},{2,3},{3,2},{4,5},{5,4},{6,7},{7,6},{8,9},{9,8},{10,11... | collective-permute-start | bytes 3145736 | tf_op jit(solution)/shard_map/ppermute | solution.py:386
  5.3 0.0 copy-done
  5.3 0.1 collective-permute-start.1
  5.4 0.0 copy-done.6
  5.4 1.3 %collective-permute-start.2 = (f32[1,16]{1,0:T(1,128)S(1)}, f32[1,16]{1,0:T(1,128)S(1)}, u32[]{:S(2)}, u32[]{:S(2)}) collective-permute-start(f32[1,16]{1,0:T(1,128)S(1)} %copy-done.6), channel_id=1, source_target_pairs={{0,8},{8,0},{16,24},{24,16},{1,9},{9,1},{17,25},{25,17},{2,10},{10... | collective-permute-start | bytes 200 | tf_op jit(solution)/shard_map/ppermute | solution.py:385
  7.4 1.4 %collective-permute-done.2 = f32[1,16]{1,0:T(1,128)S(1)} collective-permute-done((f32[1,16]{1,0:T(1,128)S(1)}, f32[1,16]{1,0:T(1,128)S(1)}, u32[]{:S(2)}, u32[]{:S(2)}) %collective-permute-start.2) | collective-permute-done | bytes 96 | tf_op jit(solution)/shard_map/ppermute | solution.py:385
  8.8 4.3 %collective-permute-start.3 = (f32[1,16]{1,0:T(1,128)S(1)}, f32[1,16]{1,0:T(1,128)S(1)}, u32[]{:S(2)}, u32[]{:S(2)}) collective-permute-start(f32[1,16]{1,0:T(1,128)S(1)} %add.13.near), channel_id=1, source_target_pairs={{8,16},{16,8},{24,0},{0,24},{9,17},{17,9},{25,1},{1,25},{10,18},{1... | collective-permute-start | bytes 200 | tf_op jit(solution)/shard_map/ppermute | solution.py:388
  13.1 0.0 collective-permute-done.1.oth_pair
  13.1 0.0 collective-permute-done.other
  13.1 0.0 copy-done.1
  13.1 0.0 copy-done.2
  13.1 0.0 copy-done.4
  13.1 4.9 %factors.1 = (f32[2176,128]{1,0:T(8,128)S(1)}, f32[896,128]{1,0:T(8,128)S(1)}, f32[896,128]{1,0:T(8,128)S(1)}, f32[896,128]{1,0:T(8,128)S(1)}, f32[640,128]{1,0:T(8,128)S(1)}, /*index=5*/f32[640,128]{1,0:T(8,128)S(1)}) custom-call(bf16[512,256]{1,0:T(8,128)(2,1)S(1)} %bitcast.17, bf16[2,512,128]{2,1,0:T(8,128)(2,1)S(1)} %bitcast.15, ...), custom_call_target="tpu_custom_call" | custom-call | flops 2500000000 | bytes 8000000 | tf_op jit(solution)/shard_map/factors/pallas_call | solution.py:391
  18.1 0.0 collective-permute-done.3.far
  18.1 0.1 tie.1
  18.2 1.3 %collective-permute-start.4 = (f32[904,128]{1,0:T(8,128)S(1)}, f32[904,128]{1,0:T(8,128)S(1)}, u32[]{:S(2)}, u32[]{:S(2)}) collective-permute-start(f32[904,128]{1,0:T(8,128)S(1)} %get-tuple-element.25), channel_id=1, source_target_pairs={{0,2},{2,0},{4,6},{6,4},{1,3},{3,1},{5,7},{7,5},{8,10},{10,8},{12,... | collective-permute-start | bytes 1388552 | tf_op jit(solution)/shard_map/ppermute | solution.py:415
  19.5 1.8 %collective-permute-start.5 = (f32[904,128]{1,0:T(8,128)S(1)}, f32[904,128]{1,0:T(8,128)S(1)}, u32[]{:S(2)}, u32[]{:S(2)}) collective-permute-start(f32[904,128]{1,0:T(8,128)S(1)} %get-tuple-element.26), channel_id=1, source_target_pairs={{2,4},{4,2},{6,0},{0,6},{3,5},{5,3},{7,1},{1,7},{10,12},{12,10},{1... | collective-permute-start | bytes 1388552 | tf_op jit(solution)/shard_map/ppermute | solution.py:416
  21.3 1.3 %collective-permute-start.6 = (f32[640,128]{1,0:T(8,128)S(1)}, f32[640,128]{1,0:T(8,128)S(1)}, u32[]{:S(2)}, u32[]{:S(2)}) collective-permute-start(f32[640,128]{1,0:T(8,128)S(1)} %get-tuple-element.27), channel_id=1, source_target_pairs={{0,32},{32,0},{64,96},{96,64},{1,33},{33,1},{65,97},{97,65},{2,34}... | collective-permute-start | bytes 983048 | tf_op jit(solution)/shard_map/ppermute | solution.py:417
  22.6 0.7 collective-permute-start.7
  23.3 0.6 collective-permute-start.8
  23.9 6.6 %collective-permute-done.8.row_two = f32[8,128]{1,0:T(8,128)S(1)} collective-permute-done((f32[8,128]{1,0:T(8,128)S(1)}, f32[8,128]{1,0:T(8,128)S(1)}, u32[]{:S(2)}, u32[]{:S(2)}) %collective-permute-start.8) | collective-permute-done | bytes 4128 | tf_op jit(solution)/shard_map/ppermute | solution.py:419
  30.5 0.0 collective-permute-done.6.from_2
  30.5 0.0 collective-permute-done.7.from_3
  30.5 0.0 collective-permute-done.4.from_a
  30.5 0.1 collective-permute-done.5.from_0
  30.7 0.2 add.20
  30.8 21.6 %all_to_all.17 = f32[16,136,128]{2,1,0:T(8,128)S(1)} all-to-all(f32[16,136,128]{2,1,0:T(8,128)S(1)} %bitcast.13), channel_id=1, replica_groups={{0,4,34,38,64,68,98,102,130,134,160,164,194,198,224,228},{2,6,32,36,66,..., dimensions={0} | all-to-all | bytes 2228224 | tf_op jit(solution)/shard_map/all_to_all | solution.py:364
  52.4 0.1 reduce_sum.9
  52.5 1.2 %collective-permute-start.10 = (f32[136,128]{1,0:T(8,128)S(1)}, f32[136,128]{1,0:T(8,128)S(1)}, u32[]{:S(2)}, u32[]{:S(2)}) collective-permute-start(f32[136,128]{1,0:T(8,128)S(1)} %reduce_sum.9), channel_id=1, source_target_pairs={{0,8},{8,16},{16,24},{24,0},{1,9},{9,17},{17,25},{25,1},{2,10},{10... | collective-permute-start | bytes 208904 | tf_op jit(solution)/shard_map/ppermute | solution.py:425
  53.7 2.4 %collective-permute-start.11 = (f32[136,128]{1,0:T(8,128)S(1)}, f32[136,128]{1,0:T(8,128)S(1)}, u32[]{:S(2)}, u32[]{:S(2)}) collective-permute-start(f32[136,128]{1,0:T(8,128)S(1)} %reduce_sum.9), channel_id=1, source_target_pairs={{0,24},{8,0},{16,8},{24,16},{1,25},{9,1},{17,9},{25,17},{2,26},{10... | collective-permute-start | bytes 208904 | tf_op jit(solution)/shard_map/ppermute | solution.py:425
  56.1 1.0 collective-permute-start.9
  57.1 0.7 collective-permute-done.10
  57.9 0.8 collective-permute-done.11
  58.7 5.0 %collective-permute-done.9 = f32[136,128]{1,0:T(8,128)S(1)} collective-permute-done((f32[136,128]{1,0:T(8,128)S(1)}, f32[136,128]{1,0:T(8,128)S(1)}, u32[]{:S(2)}, u32[]{:S(2)}) %collective-permute-start.9) | collective-permute-done | bytes 69664 | tf_op jit(solution)/shard_map/ppermute | solution.py:425
  63.7 0.0 copy-start.5
  63.7 0.1 broadcast_in_dim.15
  63.8 0.0 copy-start.3
  63.8 19.5 %all_to_all.18 = f32[16,136,128]{2,1,0:T(8,128)S(1)} all-to-all(f32[16,136,128]{2,1,0:T(8,128)S(1)} %broadcast_in_dim.15), channel_id=1, replica_groups={{0,4,34,38,64,68,98,102,130,134,160,164,194,198,224,228},{2,6,32,36,66,..., dimensions={0} | all-to-all | bytes 2228224 | tf_op jit(solution)/shard_map/all_to_all | solution.py:364
  83.3 0.1 cut.1
  83.4 1.3 %collective-permute-start.15 = (f32[512,128]{1,0:T(8,128)S(1)}, f32[512,128]{1,0:T(8,128)S(1)}, u32[]{:S(2)}, u32[]{:S(2)}) collective-permute-start(f32[512,128]{1,0:T(8,128)S(1)} %get-tuple-element.35), channel_id=1, source_target_pairs={{0,2},{2,0},{4,6},{6,4},{1,3},{3,1},{5,7},{7,5},{8,10},{10,8},{12,... | collective-permute-start | bytes 786440 | tf_op jit(solution)/shard_map/ppermute | solution.py:372
  84.7 0.7 collective-permute-start.16
  85.4 1.5 %collective-permute-start.12 = (f32[512,128]{1,0:T(8,128)S(1)}, f32[512,128]{1,0:T(8,128)S(1)}, u32[]{:S(2)}, u32[]{:S(2)}) collective-permute-start(f32[512,128]{1,0:T(8,128)S(1)} %get-tuple-element.30), channel_id=1, source_target_pairs={{0,128},{128,0},{1,129},{129,1},{2,130},{130,2},{3,131},{131,3},{4... | collective-permute-start | bytes 786440 | tf_op jit(solution)/shard_map/ppermute | solution.py:372
  86.9 0.8 collective-permute-start.13
  87.7 0.5 collective-permute-start.14
  88.2 1.0 %collective-permute-done.16.from_1 = f32[384,128]{1,0:T(8,128)S(1)} collective-permute-done((f32[384,128]{1,0:T(8,128)S(1)}, f32[384,128]{1,0:T(8,128)S(1)}, u32[]{:S(2)}, u32[]{:S(2)}) %collective-permute-start.16) | collective-permute-done | bytes 196640 | tf_op jit(solution)/shard_map/ppermute | solution.py:372
  89.2 0.0 collective-permute-done.15.from_0
  89.2 0.0 copy-done.5
  89.2 0.0 copy-done.3
  89.2 2.5 %natural.1 = (f32[896,256]{1,0:T(8,128)S(1)}, f32[1,128]{1,0:T(1,128)S(1)}) custom-call(f32[2176,128]{1,0:T(8,128)S(1)} %bitcast.11, f32[512,128]{1,0:T(8,128)S(1)} %collective-permute-done.15.from_0, f32[384,128]{1,0:T(8,128)S(1)} %collective-permute-done.16.from_1, f32[896,896]{1,0:T(8,128)S(1)} %bitcast.20, f32[256,256]{1,0:T(8,128)S(1)} %bitcast.21), custom_call_target="tpu_custom_call" | custom-call | flops 1500000000 | bytes 5000000 | tf_op jit(solution)/shard_map/natural/pallas_call | solution.py:432
  91.7 6.2 %collective-permute-start.17 = (f32[1,128]{1,0:T(1,128)S(1)}, f32[1,128]{1,0:T(1,128)S(1)}, u32[]{:S(2)}, u32[]{:S(2)}) collective-permute-start(f32[1,128]{1,0:T(1,128)S(1)} %get-tuple-element.38.curvature), channel_id=1, source_target_pairs={{0,1},{1,0},{2,3},{3,2},{4,5},{5,4},{6,7},{7,6},{8,9},{9,8},{10,11... | collective-permute-start | bytes 1544 | tf_op jit(solution)/shard_map/ppermute | solution.py:441
  97.9 0.0 collective-permute-done.13.from_3
  97.9 0.0 collective-permute-done.14.from_4
  97.9 0.0 collective-permute-done.12.from_2
  97.9 2.0 %unpack.1 = (f32[896,896]{1,0:T(8,128)}, f32[256,256]{1,0:T(8,128)}) custom-call(f32[2176,128]{1,0:T(8,128)S(1)} %bitcast.12, f32[512,128]{1,0:T(8,128)S(1)} %collective-permute-done.12.from_2, f32[384,128]{1,0:T(8,128)S(1)} %collective-permute-done.13.from_3, f32[384,128]{1,0:T(8,128)S(1)} %collective-permute-done.14.from_4), custom_call_target="tpu_custom_call" | custom-call | flops 10000000 | bytes 6000000 | tf_op jit(solution)/shard_map/unpack/pallas_call | solution.py:442
  99.9 0.0 collective-permute-done.17.other
  99.9 1.1 %scale.1 = f32[896,256]{1,0:T(8,128)} custom-call(f32[896,256]{1,0:T(8,128)S(1)} %get-tuple-element.37.natural, f32[1,128]{1,0:T(1,128)S(1)} %get-tuple-element.38.curvature, f32[1,128]{1,0:T(1,128)S(1)} %collective-permute-done.17.other), custom_call_target="tpu_custom_call" | custom-call | flops 1000000 | bytes 2000000 | tf_op jit(solution)/shard_map/scale/pallas_call | solution.py:453
  (3 shorter events, 0.1 us)
Async XLA Ops:
  0.6 4.7 %copy-start = (bf16[1,2,16,32,128]{4,3,2,1,0:T(8,128)(2,1)S(1)}, bf16[1,2,16,32,128]{4,3,2,1,0:T(8,128)(2,1)}, u32[]{:S(2)}) copy-start(bf16[1,2,16,32,128]{4,3,2,1,0:T(8,128)(2,1)} %param.10) | copy-start | bytes 786436
  0.6 4.8 %copy-start.6 = (f32[1,16]{1,0:T(1,128)S(1)}, f32[1,16]{1,0:T(1,128)}, u32[]{:S(2)}) copy-start(f32[1,16]{1,0:T(1,128)} %energy.1) | copy-start | bytes 196
  0.7 12.5 %copy-start.1 = (bf16[1,16,32,256]{3,2,1,0:T(8,128)(2,1)S(1)}, bf16[1,16,32,256]{3,2,1,0:T(8,128)(2,1)}, u32[]{:S(2)}) copy-start(bf16[1,16,32,256]{3,2,1,0:T(8,128)(2,1)} %param.8) | copy-start | bytes 786436
  0.7 12.5 %copy-start.2 = (bf16[1,16,32,256]{3,2,1,0:T(8,128)(2,1)S(1)}, bf16[1,16,32,256]{3,2,1,0:T(8,128)(2,1)}, u32[]{:S(2)}) copy-start(bf16[1,16,32,256]{3,2,1,0:T(8,128)(2,1)} %param.9) | copy-start | bytes 786436
  0.7 12.5 %copy-start.4 = (bf16[2,896,256]{2,1,0:T(8,128)(2,1)S(1)}, bf16[2,896,256]{2,1,0:T(8,128)(2,1)}, u32[]{:S(2)}) copy-start(bf16[2,896,256]{2,1,0:T(8,128)(2,1)} %weights.1) | copy-start | bytes 2752516
  2.0 11.2 %collective-permute-start = (f32[512,512]{1,0:T(8,128)S(1)}, f32[512,512]{1,0:T(8,128)S(1)}, u32[]{:S(2)}, u32[]{:S(2)}) collective-permute-start(f32[512,512]{1,0:T(8,128)S(1)} %maximum_convert_fusion), channel_id=1, source_target_pairs={{0,1},{1,0},{2,3},{3,2},{4,5},{5,4},{6,7},{7,6},{8,9},{9,8},{10,11... | collective-permute-start | bytes 3145736 | tf_op jit(solution)/shard_map/ppermute | solution.py:386
  5.3 7.8 %collective-permute-start.1 = (f32[2,512,128]{2,1,0:T(8,128)S(1)}, f32[2,512,128]{2,1,0:T(8,128)S(1)}, u32[]{:S(2)}, u32[]{:S(2)}) collective-permute-start(f32[2,512,128]{2,1,0:T(8,128)S(1)} %convert_element_type.7), channel_id=1, source_target_pairs={{0,1},{1,0},{2,3},{3,2},{4,5},{5,4},{6,7},{7,6},{8,9},{9,8},{10,11... | collective-permute-start | bytes 1572872 | tf_op jit(solution)/shard_map/ppermute | solution.py:387
  5.4 3.4 %collective-permute-start.2 = (f32[1,16]{1,0:T(1,128)S(1)}, f32[1,16]{1,0:T(1,128)S(1)}, u32[]{:S(2)}, u32[]{:S(2)}) collective-permute-start(f32[1,16]{1,0:T(1,128)S(1)} %copy-done.6), channel_id=1, source_target_pairs={{0,8},{8,0},{16,24},{24,16},{1,9},{9,1},{17,25},{25,17},{2,10},{10... | collective-permute-start | bytes 200 | tf_op jit(solution)/shard_map/ppermute | solution.py:385
  8.8 9.3 %collective-permute-start.3 = (f32[1,16]{1,0:T(1,128)S(1)}, f32[1,16]{1,0:T(1,128)S(1)}, u32[]{:S(2)}, u32[]{:S(2)}) collective-permute-start(f32[1,16]{1,0:T(1,128)S(1)} %add.13.near), channel_id=1, source_target_pairs={{8,16},{16,8},{24,0},{0,24},{9,17},{17,9},{25,1},{1,25},{10,18},{1... | collective-permute-start | bytes 200 | tf_op jit(solution)/shard_map/ppermute | solution.py:388
  18.2 12.4 %collective-permute-start.4 = (f32[904,128]{1,0:T(8,128)S(1)}, f32[904,128]{1,0:T(8,128)S(1)}, u32[]{:S(2)}, u32[]{:S(2)}) collective-permute-start(f32[904,128]{1,0:T(8,128)S(1)} %get-tuple-element.25), channel_id=1, source_target_pairs={{0,2},{2,0},{4,6},{6,4},{1,3},{3,1},{5,7},{7,5},{8,10},{10,8},{12,... | collective-permute-start | bytes 1388552 | tf_op jit(solution)/shard_map/ppermute | solution.py:415
  19.5 11.2 %collective-permute-start.5 = (f32[904,128]{1,0:T(8,128)S(1)}, f32[904,128]{1,0:T(8,128)S(1)}, u32[]{:S(2)}, u32[]{:S(2)}) collective-permute-start(f32[904,128]{1,0:T(8,128)S(1)} %get-tuple-element.26), channel_id=1, source_target_pairs={{2,4},{4,2},{6,0},{0,6},{3,5},{5,3},{7,1},{1,7},{10,12},{12,10},{1... | collective-permute-start | bytes 1388552 | tf_op jit(solution)/shard_map/ppermute | solution.py:416
  21.3 9.2 %collective-permute-start.6 = (f32[640,128]{1,0:T(8,128)S(1)}, f32[640,128]{1,0:T(8,128)S(1)}, u32[]{:S(2)}, u32[]{:S(2)}) collective-permute-start(f32[640,128]{1,0:T(8,128)S(1)} %get-tuple-element.27), channel_id=1, source_target_pairs={{0,32},{32,0},{64,96},{96,64},{1,33},{33,1},{65,97},{97,65},{2,34}... | collective-permute-start | bytes 983048 | tf_op jit(solution)/shard_map/ppermute | solution.py:417
  22.6 8.0 %collective-permute-start.7 = (f32[640,128]{1,0:T(8,128)S(1)}, f32[640,128]{1,0:T(8,128)S(1)}, u32[]{:S(2)}, u32[]{:S(2)}) collective-permute-start(f32[640,128]{1,0:T(8,128)S(1)} %get-tuple-element.28), channel_id=1, source_target_pairs={{0,128},{128,0},{1,129},{129,1},{2,130},{130,2},{3,131},{131,3},{4... | collective-permute-start | bytes 983048 | tf_op jit(solution)/shard_map/ppermute | solution.py:418
  23.3 7.2 %collective-permute-start.8 = (f32[8,128]{1,0:T(8,128)S(1)}, f32[8,128]{1,0:T(8,128)S(1)}, u32[]{:S(2)}, u32[]{:S(2)}) collective-permute-start(f32[8,128]{1,0:T(8,128)S(1)} %get-tuple-element.29.row_sum), channel_id=1, source_target_pairs={{0,4},{2,6},{4,0},{6,2},{1,5},{3,7},{5,1},{7,3},{8,12},{10,14},{12... | collective-permute-start | bytes 12296 | tf_op jit(solution)/shard_map/ppermute | solution.py:419
  52.5 5.4 %collective-permute-start.10 = (f32[136,128]{1,0:T(8,128)S(1)}, f32[136,128]{1,0:T(8,128)S(1)}, u32[]{:S(2)}, u32[]{:S(2)}) collective-permute-start(f32[136,128]{1,0:T(8,128)S(1)} %reduce_sum.9), channel_id=1, source_target_pairs={{0,8},{8,16},{16,24},{24,0},{1,9},{9,17},{17,25},{25,1},{2,10},{10... | collective-permute-start | bytes 208904 | tf_op jit(solution)/shard_map/ppermute | solution.py:425
  53.7 4.9 %collective-permute-start.11 = (f32[136,128]{1,0:T(8,128)S(1)}, f32[136,128]{1,0:T(8,128)S(1)}, u32[]{:S(2)}, u32[]{:S(2)}) collective-permute-start(f32[136,128]{1,0:T(8,128)S(1)} %reduce_sum.9), channel_id=1, source_target_pairs={{0,24},{8,0},{16,8},{24,16},{1,25},{9,1},{17,9},{25,17},{2,26},{10... | collective-permute-start | bytes 208904 | tf_op jit(solution)/shard_map/ppermute | solution.py:425
  56.1 7.5 %collective-permute-start.9 = (f32[136,128]{1,0:T(8,128)S(1)}, f32[136,128]{1,0:T(8,128)S(1)}, u32[]{:S(2)}, u32[]{:S(2)}) collective-permute-start(f32[136,128]{1,0:T(8,128)S(1)} %reduce_sum.9), channel_id=1, source_target_pairs={{0,16},{8,24},{16,0},{24,8},{1,17},{9,25},{17,1},{25,9},{2,18},{10... | collective-permute-start | bytes 208904 | tf_op jit(solution)/shard_map/ppermute | solution.py:425
  63.7 25.5 %copy-start.5 = (f32[1,256,256]{2,1,0:T(8,128)S(1)}, f32[1,256,256]{2,1,0:T(8,128)}, u32[]{:S(2)}) copy-start(f32[1,256,256]{2,1,0:T(8,128)} %param.15) | copy-start | bytes 786436
  63.8 25.4 %copy-start.3 = (f32[1,896,896]{2,1,0:T(8,128)S(1)}, f32[1,896,896]{2,1,0:T(8,128)}, u32[]{:S(2)}) copy-start(f32[1,896,896]{2,1,0:T(8,128)} %param.14) | copy-start | bytes 9633796
  83.4 5.8 %collective-permute-start.15 = (f32[512,128]{1,0:T(8,128)S(1)}, f32[512,128]{1,0:T(8,128)S(1)}, u32[]{:S(2)}, u32[]{:S(2)}) collective-permute-start(f32[512,128]{1,0:T(8,128)S(1)} %get-tuple-element.35), channel_id=1, source_target_pairs={{0,2},{2,0},{4,6},{6,4},{1,3},{3,1},{5,7},{7,5},{8,10},{10,8},{12,... | collective-permute-start | bytes 786440 | tf_op jit(solution)/shard_map/ppermute | solution.py:372
  84.7 4.5 %collective-permute-start.16 = (f32[384,128]{1,0:T(8,128)S(1)}, f32[384,128]{1,0:T(8,128)S(1)}, u32[]{:S(2)}, u32[]{:S(2)}) collective-permute-start(f32[384,128]{1,0:T(8,128)S(1)} %get-tuple-element.36), channel_id=1, source_target_pairs={{0,32},{32,0},{64,96},{96,64},{1,33},{33,1},{65,97},{97,65},{2,34}... | collective-permute-start | bytes 589832 | tf_op jit(solution)/shard_map/ppermute | solution.py:372
  85.4 12.5 %collective-permute-start.12 = (f32[512,128]{1,0:T(8,128)S(1)}, f32[512,128]{1,0:T(8,128)S(1)}, u32[]{:S(2)}, u32[]{:S(2)}) collective-permute-start(f32[512,128]{1,0:T(8,128)S(1)} %get-tuple-element.30), channel_id=1, source_target_pairs={{0,128},{128,0},{1,129},{129,1},{2,130},{130,2},{3,131},{131,3},{4... | collective-permute-start | bytes 786440 | tf_op jit(solution)/shard_map/ppermute | solution.py:372
  86.9 11.0 %collective-permute-start.13 = (f32[384,128]{1,0:T(8,128)S(1)}, f32[384,128]{1,0:T(8,128)S(1)}, u32[]{:S(2)}, u32[]{:S(2)}) collective-permute-start(f32[384,128]{1,0:T(8,128)S(1)} %get-tuple-element.31), channel_id=1, source_target_pairs={{2,4},{4,2},{6,0},{0,6},{3,5},{5,3},{7,1},{1,7},{10,12},{12,10},{1... | collective-permute-start | bytes 589832 | tf_op jit(solution)/shard_map/ppermute | solution.py:372
  87.7 10.2 %collective-permute-start.14 = (f32[384,128]{1,0:T(8,128)S(1)}, f32[384,128]{1,0:T(8,128)S(1)}, u32[]{:S(2)}, u32[]{:S(2)}) collective-permute-start(f32[384,128]{1,0:T(8,128)S(1)} %get-tuple-element.32), channel_id=1, source_target_pairs={{32,64},{64,32},{96,0},{0,96},{33,65},{65,33},{97,1},{1,97},{34,66... | collective-permute-start | bytes 589832 | tf_op jit(solution)/shard_map/ppermute | solution.py:372
  91.7 8.2 %collective-permute-start.17 = (f32[1,128]{1,0:T(1,128)S(1)}, f32[1,128]{1,0:T(1,128)S(1)}, u32[]{:S(2)}, u32[]{:S(2)}) collective-permute-start(f32[1,128]{1,0:T(1,128)S(1)} %get-tuple-element.38.curvature), channel_id=1, source_target_pairs={{0,1},{1,0},{2,3},{3,2},{4,5},{5,4},{6,7},{7,6},{8,9},{9,8},{10,11... | collective-permute-start | bytes 1544 | tf_op jit(solution)/shard_map/ppermute | solution.py:441

commit v8 on v7

--- a/solution.py
+++ b/solution.py
@@ -14,8 +14,8 @@
 KEPT = SLOTS * B
 CHUNK = KEPT // GROUP
 GRADS, FACTORS = 7, 10
-OUT_STREAMS = ((7, 12), (12, 17))
-BACK_STREAMS = ((0, 4), (4, 7), (7, 11), (11, 14), (14, 17))
+OUT_STREAMS = ((0, 6), (6, 12), (12, 17))
+BACK_STREAMS = ((0, 4), (4, 7), (7, 12), (12, 15), (15, 17))
 ENTRIES = 2 * DIN * D
 SHIFT = 7.0
 
@@ -65,7 +65,7 @@
 
 def factors_kernel(
     feat, pair, psi, other, oth_pair, weights, energies, energy, multiplicity,
-    keep, keep_0, to_a, to_0, to_2, to_3, x_s, d_s, m_s, s_s, w_s, out, out_0
+    out, out_0, x_s, d_s, m_s, s_s, w_s
 ):
     mp = lax.axis_index("c")
     own_row = pl.multiple_of(D + D * mp, D)
@@ -190,33 +190,31 @@
     out[parity ^ 1, last:, :] = jnp.zeros((B, B), F32)
     for line, value in lines.items():
         out[parity ^ 1, last + line : last + line + 1, :] = value
-    keep[...] = out[0]
-    keep_0[...] = out_0[0]
-    grads = GRADS * B
-    to_a[...] = out[1, :grads, :]
-    to_0[...] = out_0[1]
-    for target, (first, end) in zip((to_2, to_3), OUT_STREAMS):
-        target[...] = out[1, first * B : end * B, :]
-
-
-def tie_kernel(plain_a, plain_0, near, far, to_a, to_0, row_sum):
+
+
+def tie_kernel(out, out_0, near, far, to_0, to_1, to_2, to_3, row_sum):
     zh_sum = jnp.sum(near[...] + far[...], axis=1, keepdims=True)
     row_sum[...] = jnp.broadcast_to(zh_sum, (8, B))
     grads = GRADS * B
-    for source, target in ((plain_a, to_a), (plain_0, to_0)):
-        target[:grads, :] = source[...]
-        target[grads:, :] = row_sum[...]
-
-
-def add_kernel(keep, keep_0, from_a, from_0, from_2, from_3, row_sum, row_two, total):
+    to_0[:grads, :] = out_0[1]
+    to_0[grads:, :] = row_sum[...]
+    for target, (first, end) in zip((to_1, to_2, to_3), OUT_STREAMS):
+        target[: (end - first) * B, :] = out[1, first * B : end * B, :]
+    to_1[OUT_STREAMS[0][1] * B :, :] = row_sum[...]
+
+
+def add_kernel(out, out_0, from_0, from_1, from_2, from_3, row_sum, row_two, total):
     grads = GRADS * B
-    energy = (row_sum[...] + row_two[...]) + (from_a[grads:, :] + from_0[grads:, :])
+    near, far = from_0[grads:, :], from_1[OUT_STREAMS[0][1] * B :, :]
+    energy = (row_sum[...] + row_two[...]) + (near + far)
     shifted = energy[:1, :] * (1.0 / 256.0) + SHIFT
-    plain = keep_0[...] + from_0[:grads, :]
-    total[:grads, :] = (keep[:grads, :] + from_a[:grads, :]) - shifted * plain
-    for part, (first, end) in zip((from_2, from_3), OUT_STREAMS):
-        rows = slice(first * B, end * B)
-        total[rows, :] = keep[rows, :] + part[...]
+    for part, (first, end) in zip((from_1, from_2, from_3), OUT_STREAMS):
+        for place in range(first, end):
+            rows = slice(place * B, (place + 1) * B)
+            value = out[0, rows, :] + part[(place - first) * B : (place - first + 1) * B, :]
+            if place < GRADS:
+                value = value - shifted * (out_0[0, rows, :] + from_0[rows, :])
+            total[rows, :] = value
 
 
 def cut_kernel(kept, to_0, to_1, to_2, to_3, to_4):
@@ -388,11 +386,9 @@
     far_2 = lax.ppermute(sum_2, "zh", HIGH)
 
     grads = GRADS * B
-    keep, keep_0, to_a, to_0, to_2, to_3 = call(
+    out, out_0 = call(
         factors_kernel,
-        [((KEPT, B), F32), ((grads, B), F32)]
-        + [((grads, B), F32)] * 2
-        + streams_of(OUT_STREAMS),
+        [((2, KEPT, B), F32), ((2, grads, B), F32)],
         [V] * 7 + [S] * 2,
         26,
         "factors",
@@ -402,23 +398,27 @@
             pltpu.VMEM((2, 2 * WALK, D), BF16),
             pltpu.VMEM((2, ROWS, D), BF16),
             pltpu.VMEM((ROWS, 4 * D + PAIR), BF16),
-            pltpu.VMEM((2, KEPT, B), F32),
-            pltpu.VMEM((2, grads, B), F32),
         ],
         flops=2_500_000_000,
         moved=8_000_000,
     )(feat, pair, psi, other, oth_pair, weights, energies, energies, multiplicity)
 
-    to_a, to_0, row_sum = call(
-        tie_kernel, [((grads + 8, B), F32)] * 2 + [((8, B), F32)], [V] * 4, 6, "tie", moved=2_000_000
-    )(to_a, to_0, sum_2, far_2)
-    from_a = lax.ppermute(to_a, "x", LOW)
-    from_0 = lax.ppermute(to_0, "x", HIGH)
+    sizes = [((end - first) * B, B) for first, end in OUT_STREAMS]
+    to_0, to_1, to_2, to_3, row_sum = call(
+        tie_kernel,
+        [((grads + 8, B), F32), ((sizes[0][0] + 8, B), F32), (sizes[1], F32), (sizes[2], F32), ((8, B), F32)],
+        [V] * 4,
+        8,
+        "tie",
+        moved=3_000_000,
+    )(out, out_0, sum_2, far_2)
+    from_0 = lax.ppermute(to_0, "x", LOW)
+    from_1 = lax.ppermute(to_1, "x", HIGH)
     from_2 = lax.ppermute(to_2, "y", LOW)
     from_3 = lax.ppermute(to_3, "zl", swap)
     row_two = lax.ppermute(row_sum, "x", [(0, 2), (1, 3), (2, 0), (3, 1)])
-    (total,) = call(add_kernel, [((KEPT, B), F32)], [V] * 8, 8, "add", moved=3_000_000)(
-        keep, keep_0, from_a, from_0, from_2, from_3, row_sum, row_two
+    (total,) = call(add_kernel, [((KEPT, B), F32)], [V] * 8, 10, "add", moved=3_000_000)(
+        out, out_0, from_0, from_1, from_2, from_3, row_sum, row_two
     )
     mine = jnp.sum(same_parity(total).reshape(GROUP, CHUNK, B), axis=0)
     one, two, three = (

time: 101 us -> 101 us (level)
  blocking collectives: 41.1 us -> 38.2 us
  waiting for transfers between devices: 15.7 us -> 17.3 us
    all_to_all x2, blocking collectives: 41.1 us -> 38.2 us  [same_parity(): lax.all_to_all(value, axes, 0, 0, axis_index_groups=parity_groups(), tile...]
  transfers between devices with their start and end apart: 18 -> 18, of which waited for: 7 -> 7; matrix products, arithmetic and copies ran while one was open for 0% -> 0% of each run, Pallas kernels for 9% -> 8%
where the time goes in v8:
time: 101 us; the launch traced here: 100 us
  blocking collectives  38.2 us (38%)
  starting transfers between devices  31.2 us (31%)
  waiting for transfers between devices  17.3 us (17%)
  Pallas kernels  10.6 us (10%)
  between operations  1.6 us (2%)
  other arithmetic  1.39 us (1%)
    all_to_all x2, blocking collectives, same_parity(): lax.all_to_all(value, axes, 0, 0, axis_index_groups=parity_groups(), tile...  38.2 us
    ppermute x1, starting transfers between devices, body(): other = lax.ppermute(curvature, 'c', swap)  7.21 us
    ppermute x3, waiting for transfers between devices, body(): lax.ppermute(mine, 'zh', [(i, (i + k) % 4) for i in range(4)])  6.6 us
    ppermute x1, waiting for transfers between devices, body(): row_two = lax.ppermute(row_sum, 'x', [(0, 2), (1, 3), (2, 0), (3, 1)])  6.58 us
    pallas_call x1, Pallas kernels, body(): call(factors_kernel, [((2, KEPT, B), F32), ((2, grads, B), F32)], [V] * 7...  4.73 us
    ppermute x3, starting transfers between devices, body(): lax.ppermute(mine, 'zh', [(i, (i + k) % 4) for i in range(4)])  4.6 us
    ppermute x5, starting transfers between devices, to_neighbours(): lax.ppermute(part, axis, pairs)  4.57 us
    ppermute x1, starting transfers between devices, body(): far_2 = lax.ppermute(sum_2, 'zh', HIGH)  4.28 us
  transfers between devices with their start and end apart: 18, of which 7 were waited for; matrix products, arithmetic and copies ran while one was open for 0% of the time, Pallas kernels for 8%

profile of v8, /device:TPU:1, one launch (start us, length us, event | category | flops | bytes accessed | tf_op | source)
XLA Modules:
  0.0 100.5 jit_solution(16076268579933721510)
XLA Ops:
  0.6 0.0 copy-start
  0.6 0.0 copy-start.6
  0.7 0.0 copy-start.1
  0.7 0.0 copy-start.2
  0.7 0.0 copy-start.4
  0.7 1.3 %maximum_convert_fusion = f32[512,512]{1,0:T(8,128)S(1)} fusion(bf16[512,256]{1,0:T(8,128)(2,1)} %bitcast.18, bf16[512,256]{1,0:T(8,128)(2,1)} %bitcast.16), kind=kLoop, calls=%fused_computation | loop fusion | flops 1048576 | bytes 1572864 | tf_op jit(solution)/shard_map/convert_element_type | solution.py:384
  2.0 3.3 %collective-permute-start = (f32[512,512]{1,0:T(8,128)S(1)}, f32[512,512]{1,0:T(8,128)S(1)}, u32[]{:S(2)}, u32[]{:S(2)}) collective-permute-start(f32[512,512]{1,0:T(8,128)S(1)} %maximum_convert_fusion), channel_id=1, source_target_pairs={{0,1},{1,0},{2,3},{3,2},{4,5},{5,4},{6,7},{7,6},{8,9},{9,8},{10,11... | collective-permute-start | bytes 3145736 | tf_op jit(solution)/shard_map/ppermute | solution.py:384
  5.3 0.0 copy-done
  5.3 0.1 collective-permute-start.1
  5.4 0.0 copy-done.6
  5.4 1.3 %collective-permute-start.2 = (f32[1,16]{1,0:T(1,128)S(1)}, f32[1,16]{1,0:T(1,128)S(1)}, u32[]{:S(2)}, u32[]{:S(2)}) collective-permute-start(f32[1,16]{1,0:T(1,128)S(1)} %copy-done.6), channel_id=1, source_target_pairs={{0,8},{8,0},{16,24},{24,16},{1,9},{9,1},{17,25},{25,17},{2,10},{10... | collective-permute-start | bytes 200 | tf_op jit(solution)/shard_map/ppermute | solution.py:383
  7.4 1.4 %collective-permute-done.2 = f32[1,16]{1,0:T(1,128)S(1)} collective-permute-done((f32[1,16]{1,0:T(1,128)S(1)}, f32[1,16]{1,0:T(1,128)S(1)}, u32[]{:S(2)}, u32[]{:S(2)}) %collective-permute-start.2) | collective-permute-done | bytes 96 | tf_op jit(solution)/shard_map/ppermute | solution.py:383
  8.8 4.3 %collective-permute-start.3 = (f32[1,16]{1,0:T(1,128)S(1)}, f32[1,16]{1,0:T(1,128)S(1)}, u32[]{:S(2)}, u32[]{:S(2)}) collective-permute-start(f32[1,16]{1,0:T(1,128)S(1)} %add.13.near), channel_id=1, source_target_pairs={{8,16},{16,8},{24,0},{0,24},{9,17},{17,9},{25,1},{1,25},{10,18},{1... | collective-permute-start | bytes 200 | tf_op jit(solution)/shard_map/ppermute | solution.py:386
  13.1 0.0 collective-permute-done.1.oth_pair
  13.1 0.0 collective-permute-done.other
  13.1 0.0 copy-done.1
  13.1 0.0 copy-done.2
  13.1 0.0 copy-done.4
  13.1 4.7 %factors.1 = (f32[2,2176,128]{2,1,0:T(8,128)S(1)}, f32[2,896,128]{2,1,0:T(8,128)S(1)}) custom-call(bf16[512,256]{1,0:T(8,128)(2,1)S(1)} %bitcast.17, bf16[2,512,128]{2,1,0:T(8,128)(2,1)S(1)} %bitcast.15, bf16[512,256]{1,0:T(8,128)(2,1)S(1)} %bitcast.19, f32[512,512]{1,0:T(8,128)S(1)} %collective-permute-done.other, ...), custom_call_target="tpu_custom_call" | custom-call | flops 2500000000 | bytes 8000000 | tf_op jit(solution)/shard_map/factors/pallas_call | solution.py:389
  17.9 0.0 collective-permute-done.3.far
  17.9 0.1 tie.1
  18.0 1.3 %collective-permute-start.4 = (f32[904,128]{1,0:T(8,128)S(1)}, f32[904,128]{1,0:T(8,128)S(1)}, u32[]{:S(2)}, u32[]{:S(2)}) collective-permute-start(f32[904,128]{1,0:T(8,128)S(1)} %get-tuple-element.21), channel_id=1, source_target_pairs={{0,2},{2,0},{4,6},{6,4},{1,3},{3,1},{5,7},{7,5},{8,10},{10,8},{12,... | collective-permute-start | bytes 1388552 | tf_op jit(solution)/shard_map/ppermute | solution.py:415
  19.3 1.8 %collective-permute-start.5 = (f32[776,128]{1,0:T(8,128)S(1)}, f32[776,128]{1,0:T(8,128)S(1)}, u32[]{:S(2)}, u32[]{:S(2)}) collective-permute-start(f32[776,128]{1,0:T(8,128)S(1)} %get-tuple-element.22), channel_id=1, source_target_pairs={{2,4},{4,2},{6,0},{0,6},{3,5},{5,3},{7,1},{1,7},{10,12},{12,10},{1... | collective-permute-start | bytes 1191944 | tf_op jit(solution)/shard_map/ppermute | solution.py:416
  21.1 1.3 %collective-permute-start.6 = (f32[768,128]{1,0:T(8,128)S(1)}, f32[768,128]{1,0:T(8,128)S(1)}, u32[]{:S(2)}, u32[]{:S(2)}) collective-permute-start(f32[768,128]{1,0:T(8,128)S(1)} %get-tuple-element.23), channel_id=1, source_target_pairs={{0,32},{32,0},{64,96},{96,64},{1,33},{33,1},{65,97},{97,65},{2,34}... | collective-permute-start | bytes 1179656 | tf_op jit(solution)/shard_map/ppermute | solution.py:417
  22.4 0.7 collective-permute-start.7
  23.2 0.6 collective-permute-start.8
  23.8 6.6 %collective-permute-done.8.row_two = f32[8,128]{1,0:T(8,128)S(1)} collective-permute-done((f32[8,128]{1,0:T(8,128)S(1)}, f32[8,128]{1,0:T(8,128)S(1)}, u32[]{:S(2)}, u32[]{:S(2)}) %collective-permute-start.8) | collective-permute-done | bytes 4128 | tf_op jit(solution)/shard_map/ppermute | solution.py:419
  30.4 0.0 collective-permute-done.7.from_3
  30.4 0.0 collective-permute-done.6.from_2
  30.4 0.0 collective-permute-done.5.from_1
  30.4 0.0 collective-permute-done.4.from_0
  30.4 0.2 add.20
  30.6 20.1 %all_to_all.17 = f32[16,136,128]{2,1,0:T(8,128)S(1)} all-to-all(f32[16,136,128]{2,1,0:T(8,128)S(1)} %bitcast.13), channel_id=1, replica_groups={{0,4,34,38,64,68,98,102,130,134,160,164,194,198,224,228},{2,6,32,36,66,..., dimensions={0} | all-to-all | bytes 2228224 | tf_op jit(solution)/shard_map/all_to_all | solution.py:362
  50.7 0.1 reduce_sum.9
  50.8 1.2 %collective-permute-start.10 = (f32[136,128]{1,0:T(8,128)S(1)}, f32[136,128]{1,0:T(8,128)S(1)}, u32[]{:S(2)}, u32[]{:S(2)}) collective-permute-start(f32[136,128]{1,0:T(8,128)S(1)} %reduce_sum.9), channel_id=1, source_target_pairs={{0,8},{8,16},{16,24},{24,0},{1,9},{9,17},{17,25},{25,1},{2,10},{10... | collective-permute-start | bytes 208904 | tf_op jit(solution)/shard_map/ppermute | solution.py:425
  52.0 2.4 %collective-permute-start.11 = (f32[136,128]{1,0:T(8,128)S(1)}, f32[136,128]{1,0:T(8,128)S(1)}, u32[]{:S(2)}, u32[]{:S(2)}) collective-permute-start(f32[136,128]{1,0:T(8,128)S(1)} %reduce_sum.9), channel_id=1, source_target_pairs={{0,24},{8,0},{16,8},{24,16},{1,25},{9,1},{17,9},{25,17},{2,26},{10... | collective-permute-start | bytes 208904 | tf_op jit(solution)/shard_map/ppermute | solution.py:425
  54.4 1.0 collective-permute-start.9
  55.4 0.8 collective-permute-done.10
  56.2 0.5 collective-permute-done.11
  56.7 5.2 %collective-permute-done.9 = f32[136,128]{1,0:T(8,128)S(1)} collective-permute-done((f32[136,128]{1,0:T(8,128)S(1)}, f32[136,128]{1,0:T(8,128)S(1)}, u32[]{:S(2)}, u32[]{:S(2)}) %collective-permute-start.9) | collective-permute-done | bytes 69664 | tf_op jit(solution)/shard_map/ppermute | solution.py:425
  62.0 0.0 copy-start.5
  62.0 0.1 broadcast_in_dim.15
  62.1 0.0 copy-start.3
  62.1 18.1 %all_to_all.18 = f32[16,136,128]{2,1,0:T(8,128)S(1)} all-to-all(f32[16,136,128]{2,1,0:T(8,128)S(1)} %broadcast_in_dim.15), channel_id=1, replica_groups={{0,4,34,38,64,68,98,102,130,134,160,164,194,198,224,228},{2,6,32,36,66,..., dimensions={0} | all-to-all | bytes 2228224 | tf_op jit(solution)/shard_map/all_to_all | solution.py:362
  80.2 0.1 cut.1
  80.2 1.7 %collective-permute-start.15 = (f32[512,128]{1,0:T(8,128)S(1)}, f32[512,128]{1,0:T(8,128)S(1)}, u32[]{:S(2)}, u32[]{:S(2)}) collective-permute-start(f32[512,128]{1,0:T(8,128)S(1)} %get-tuple-element.31), channel_id=1, source_target_pairs={{0,2},{2,0},{4,6},{6,4},{1,3},{3,1},{5,7},{7,5},{8,10},{10,8},{12,... | collective-permute-start | bytes 786440 | tf_op jit(solution)/shard_map/ppermute | solution.py:370
  81.9 0.0 collective-permute-start.16
  82.0 1.1 %collective-permute-start.12 = (f32[640,128]{1,0:T(8,128)S(1)}, f32[640,128]{1,0:T(8,128)S(1)}, u32[]{:S(2)}, u32[]{:S(2)}) collective-permute-start(f32[640,128]{1,0:T(8,128)S(1)} %get-tuple-element.26), channel_id=1, source_target_pairs={{0,128},{128,0},{1,129},{129,1},{2,130},{130,2},{3,131},{131,3},{4... | collective-permute-start | bytes 983048 | tf_op jit(solution)/shard_map/ppermute | solution.py:370
  83.1 1.0 %collective-permute-start.13 = (f32[384,128]{1,0:T(8,128)S(1)}, f32[384,128]{1,0:T(8,128)S(1)}, u32[]{:S(2)}, u32[]{:S(2)}) collective-permute-start(f32[384,128]{1,0:T(8,128)S(1)} %get-tuple-element.27), channel_id=1, source_target_pairs={{2,4},{4,2},{6,0},{0,6},{3,5},{5,3},{7,1},{1,7},{10,12},{12,10},{1... | collective-permute-start | bytes 589832 | tf_op jit(solution)/shard_map/ppermute | solution.py:370
  84.1 0.7 collective-permute-start.14
  84.8 1.9 %collective-permute-done.16.from_1 = f32[384,128]{1,0:T(8,128)S(1)} collective-permute-done((f32[384,128]{1,0:T(8,128)S(1)}, f32[384,128]{1,0:T(8,128)S(1)}, u32[]{:S(2)}, u32[]{:S(2)}) %collective-permute-start.16) | collective-permute-done | bytes 196640 | tf_op jit(solution)/shard_map/ppermute | solution.py:370
  86.8 0.0 collective-permute-done.15.from_0
  86.8 0.0 copy-done.5
  86.8 0.0 copy-done.3
  86.8 2.5 %natural.1 = (f32[896,256]{1,0:T(8,128)S(1)}, f32[1,128]{1,0:T(1,128)S(1)}) custom-call(f32[2176,128]{1,0:T(8,128)S(1)} %bitcast.11, f32[512,128]{1,0:T(8,128)S(1)} %collective-permute-done.15.from_0, f32[384,128]{1,0:T(8,128)S(1)} %collective-permute-done.16.from_1, f32[896,896]{1,0:T(8,128)S(1)} %bitcast.20, f32[256,256]{1,0:T(8,128)S(1)} %bitcast.21), custom_call_target="tpu_custom_call" | custom-call | flops 1500000000 | bytes 5000000 | tf_op jit(solution)/shard_map/natural/pallas_call | solution.py:432
  89.3 7.2 %collective-permute-start.17 = (f32[1,128]{1,0:T(1,128)S(1)}, f32[1,128]{1,0:T(1,128)S(1)}, u32[]{:S(2)}, u32[]{:S(2)}) collective-permute-start(f32[1,128]{1,0:T(1,128)S(1)} %get-tuple-element.34.curvature), channel_id=1, source_target_pairs={{0,1},{1,0},{2,3},{3,2},{4,5},{5,4},{6,7},{7,6},{8,9},{9,8},{10,11... | collective-permute-start | bytes 1544 | tf_op jit(solution)/shard_map/ppermute | solution.py:441
  96.5 0.8 collective-permute-done.17.other
  97.3 1.1 %scale.1 = f32[896,256]{1,0:T(8,128)} custom-call(f32[896,256]{1,0:T(8,128)S(1)} %get-tuple-element.33.natural, f32[1,128]{1,0:T(1,128)S(1)} %get-tuple-element.34.curvature, f32[1,128]{1,0:T(1,128)S(1)} %collective-permute-done.17.other), custom_call_target="tpu_custom_call" | custom-call | flops 1000000 | bytes 2000000 | tf_op jit(solution)/shard_map/scale/pallas_call | solution.py:453
  98.3 0.0 collective-permute-done.14.from_4
  98.4 0.0 collective-permute-done.13.from_3
  98.4 0.0 collective-permute-done.12.from_2
  98.4 2.0 %unpack.1 = (f32[896,896]{1,0:T(8,128)}, f32[256,256]{1,0:T(8,128)}) custom-call(f32[2176,128]{1,0:T(8,128)S(1)} %bitcast.12, f32[640,128]{1,0:T(8,128)S(1)} %collective-permute-done.12.from_2, f32[384,128]{1,0:T(8,128)S(1)} %collective-permute-done.13.from_3, f32[256,128]{1,0:T(8,128)S(1)} %collective-permute-done.14.from_4), custom_call_target="tpu_custom_call" | custom-call | flops 10000000 | bytes 6000000 | tf_op jit(solution)/shard_map/unpack/pallas_call | solution.py:442
  (3 shorter events, 0.1 us)
Async XLA Ops:
  0.6 4.7 %copy-start = (bf16[1,2,16,32,128]{4,3,2,1,0:T(8,128)(2,1)S(1)}, bf16[1,2,16,32,128]{4,3,2,1,0:T(8,128)(2,1)}, u32[]{:S(2)}) copy-start(bf16[1,2,16,32,128]{4,3,2,1,0:T(8,128)(2,1)} %param.10) | copy-start | bytes 786436
  0.6 4.8 %copy-start.6 = (f32[1,16]{1,0:T(1,128)S(1)}, f32[1,16]{1,0:T(1,128)}, u32[]{:S(2)}) copy-start(f32[1,16]{1,0:T(1,128)} %energy.1) | copy-start | bytes 196
  0.7 12.5 %copy-start.1 = (bf16[1,16,32,256]{3,2,1,0:T(8,128)(2,1)S(1)}, bf16[1,16,32,256]{3,2,1,0:T(8,128)(2,1)}, u32[]{:S(2)}) copy-start(bf16[1,16,32,256]{3,2,1,0:T(8,128)(2,1)} %param.8) | copy-start | bytes 786436
  0.7 12.5 %copy-start.2 = (bf16[1,16,32,256]{3,2,1,0:T(8,128)(2,1)S(1)}, bf16[1,16,32,256]{3,2,1,0:T(8,128)(2,1)}, u32[]{:S(2)}) copy-start(bf16[1,16,32,256]{3,2,1,0:T(8,128)(2,1)} %param.9) | copy-start | bytes 786436
  0.7 12.5 %copy-start.4 = (bf16[2,896,256]{2,1,0:T(8,128)(2,1)S(1)}, bf16[2,896,256]{2,1,0:T(8,128)(2,1)}, u32[]{:S(2)}) copy-start(bf16[2,896,256]{2,1,0:T(8,128)(2,1)} %weights.1) | copy-start | bytes 2752516
  2.0 11.2 %collective-permute-start = (f32[512,512]{1,0:T(8,128)S(1)}, f32[512,512]{1,0:T(8,128)S(1)}, u32[]{:S(2)}, u32[]{:S(2)}) collective-permute-start(f32[512,512]{1,0:T(8,128)S(1)} %maximum_convert_fusion), channel_id=1, source_target_pairs={{0,1},{1,0},{2,3},{3,2},{4,5},{5,4},{6,7},{7,6},{8,9},{9,8},{10,11... | collective-permute-start | bytes 3145736 | tf_op jit(solution)/shard_map/ppermute | solution.py:384
  5.3 7.8 %collective-permute-start.1 = (f32[2,512,128]{2,1,0:T(8,128)S(1)}, f32[2,512,128]{2,1,0:T(8,128)S(1)}, u32[]{:S(2)}, u32[]{:S(2)}) collective-permute-start(f32[2,512,128]{2,1,0:T(8,128)S(1)} %convert_element_type.7), channel_id=1, source_target_pairs={{0,1},{1,0},{2,3},{3,2},{4,5},{5,4},{6,7},{7,6},{8,9},{9,8},{10,11... | collective-permute-start | bytes 1572872 | tf_op jit(solution)/shard_map/ppermute | solution.py:385
  5.4 3.4 %collective-permute-start.2 = (f32[1,16]{1,0:T(1,128)S(1)}, f32[1,16]{1,0:T(1,128)S(1)}, u32[]{:S(2)}, u32[]{:S(2)}) collective-permute-start(f32[1,16]{1,0:T(1,128)S(1)} %copy-done.6), channel_id=1, source_target_pairs={{0,8},{8,0},{16,24},{24,16},{1,9},{9,1},{17,25},{25,17},{2,10},{10... | collective-permute-start | bytes 200 | tf_op jit(solution)/shard_map/ppermute | solution.py:383
  8.8 9.1 %collective-permute-start.3 = (f32[1,16]{1,0:T(1,128)S(1)}, f32[1,16]{1,0:T(1,128)S(1)}, u32[]{:S(2)}, u32[]{:S(2)}) collective-permute-start(f32[1,16]{1,0:T(1,128)S(1)} %add.13.near), channel_id=1, source_target_pairs={{8,16},{16,8},{24,0},{0,24},{9,17},{17,9},{25,1},{1,25},{10,18},{1... | collective-permute-start | bytes 200 | tf_op jit(solution)/shard_map/ppermute | solution.py:386
  18.0 12.4 %collective-permute-start.4 = (f32[904,128]{1,0:T(8,128)S(1)}, f32[904,128]{1,0:T(8,128)S(1)}, u32[]{:S(2)}, u32[]{:S(2)}) collective-permute-start(f32[904,128]{1,0:T(8,128)S(1)} %get-tuple-element.21), channel_id=1, source_target_pairs={{0,2},{2,0},{4,6},{6,4},{1,3},{3,1},{5,7},{7,5},{8,10},{10,8},{12,... | collective-permute-start | bytes 1388552 | tf_op jit(solution)/shard_map/ppermute | solution.py:415
  19.3 11.1 %collective-permute-start.5 = (f32[776,128]{1,0:T(8,128)S(1)}, f32[776,128]{1,0:T(8,128)S(1)}, u32[]{:S(2)}, u32[]{:S(2)}) collective-permute-start(f32[776,128]{1,0:T(8,128)S(1)} %get-tuple-element.22), channel_id=1, source_target_pairs={{2,4},{4,2},{6,0},{0,6},{3,5},{5,3},{7,1},{1,7},{10,12},{12,10},{1... | collective-permute-start | bytes 1191944 | tf_op jit(solution)/shard_map/ppermute | solution.py:416
  21.1 9.3 %collective-permute-start.6 = (f32[768,128]{1,0:T(8,128)S(1)}, f32[768,128]{1,0:T(8,128)S(1)}, u32[]{:S(2)}, u32[]{:S(2)}) collective-permute-start(f32[768,128]{1,0:T(8,128)S(1)} %get-tuple-element.23), channel_id=1, source_target_pairs={{0,32},{32,0},{64,96},{96,64},{1,33},{33,1},{65,97},{97,65},{2,34}... | collective-permute-start | bytes 1179656 | tf_op jit(solution)/shard_map/ppermute | solution.py:417
  22.4 8.0 %collective-permute-start.7 = (f32[640,128]{1,0:T(8,128)S(1)}, f32[640,128]{1,0:T(8,128)S(1)}, u32[]{:S(2)}, u32[]{:S(2)}) collective-permute-start(f32[640,128]{1,0:T(8,128)S(1)} %get-tuple-element.24), channel_id=1, source_target_pairs={{0,128},{128,0},{1,129},{129,1},{2,130},{130,2},{3,131},{131,3},{4... | collective-permute-start | bytes 983048 | tf_op jit(solution)/shard_map/ppermute | solution.py:418
  23.2 7.2 %collective-permute-start.8 = (f32[8,128]{1,0:T(8,128)S(1)}, f32[8,128]{1,0:T(8,128)S(1)}, u32[]{:S(2)}, u32[]{:S(2)}) collective-permute-start(f32[8,128]{1,0:T(8,128)S(1)} %get-tuple-element.25.row_sum), channel_id=1, source_target_pairs={{0,4},{2,6},{4,0},{6,2},{1,5},{3,7},{5,1},{7,3},{8,12},{10,14},{12... | collective-permute-start | bytes 12296 | tf_op jit(solution)/shard_map/ppermute | solution.py:419
  50.8 5.4 %collective-permute-start.10 = (f32[136,128]{1,0:T(8,128)S(1)}, f32[136,128]{1,0:T(8,128)S(1)}, u32[]{:S(2)}, u32[]{:S(2)}) collective-permute-start(f32[136,128]{1,0:T(8,128)S(1)} %reduce_sum.9), channel_id=1, source_target_pairs={{0,8},{8,16},{16,24},{24,0},{1,9},{9,17},{17,25},{25,1},{2,10},{10... | collective-permute-start | bytes 208904 | tf_op jit(solution)/shard_map/ppermute | solution.py:425
  52.0 4.7 %collective-permute-start.11 = (f32[136,128]{1,0:T(8,128)S(1)}, f32[136,128]{1,0:T(8,128)S(1)}, u32[]{:S(2)}, u32[]{:S(2)}) collective-permute-start(f32[136,128]{1,0:T(8,128)S(1)} %reduce_sum.9), channel_id=1, source_target_pairs={{0,24},{8,0},{16,8},{24,16},{1,25},{9,1},{17,9},{25,17},{2,26},{10... | collective-permute-start | bytes 208904 | tf_op jit(solution)/shard_map/ppermute | solution.py:425
  54.4 7.6 %collective-permute-start.9 = (f32[136,128]{1,0:T(8,128)S(1)}, f32[136,128]{1,0:T(8,128)S(1)}, u32[]{:S(2)}, u32[]{:S(2)}) collective-permute-start(f32[136,128]{1,0:T(8,128)S(1)} %reduce_sum.9), channel_id=1, source_target_pairs={{0,16},{8,24},{16,0},{24,8},{1,17},{9,25},{17,1},{25,9},{2,18},{10... | collective-permute-start | bytes 208904 | tf_op jit(solution)/shard_map/ppermute | solution.py:425
  62.0 24.8 %copy-start.5 = (f32[1,256,256]{2,1,0:T(8,128)S(1)}, f32[1,256,256]{2,1,0:T(8,128)}, u32[]{:S(2)}) copy-start(f32[1,256,256]{2,1,0:T(8,128)} %param.15) | copy-start | bytes 786436
  62.1 24.7 %copy-start.3 = (f32[1,896,896]{2,1,0:T(8,128)S(1)}, f32[1,896,896]{2,1,0:T(8,128)}, u32[]{:S(2)}) copy-start(f32[1,896,896]{2,1,0:T(8,128)} %param.14) | copy-start | bytes 9633796
  80.2 6.5 %collective-permute-start.15 = (f32[512,128]{1,0:T(8,128)S(1)}, f32[512,128]{1,0:T(8,128)S(1)}, u32[]{:S(2)}, u32[]{:S(2)}) collective-permute-start(f32[512,128]{1,0:T(8,128)S(1)} %get-tuple-element.31), channel_id=1, source_target_pairs={{0,2},{2,0},{4,6},{6,4},{1,3},{3,1},{5,7},{7,5},{8,10},{10,8},{12,... | collective-permute-start | bytes 786440 | tf_op jit(solution)/shard_map/ppermute | solution.py:370
  81.9 4.8 %collective-permute-start.16 = (f32[384,128]{1,0:T(8,128)S(1)}, f32[384,128]{1,0:T(8,128)S(1)}, u32[]{:S(2)}, u32[]{:S(2)}) collective-permute-start(f32[384,128]{1,0:T(8,128)S(1)} %get-tuple-element.32), channel_id=1, source_target_pairs={{0,32},{32,0},{64,96},{96,64},{1,33},{33,1},{65,97},{97,65},{2,34}... | collective-permute-start | bytes 589832 | tf_op jit(solution)/shard_map/ppermute | solution.py:370
  82.0 16.4 %collective-permute-start.12 = (f32[640,128]{1,0:T(8,128)S(1)}, f32[640,128]{1,0:T(8,128)S(1)}, u32[]{:S(2)}, u32[]{:S(2)}) collective-permute-start(f32[640,128]{1,0:T(8,128)S(1)} %get-tuple-element.26), channel_id=1, source_target_pairs={{0,128},{128,0},{1,129},{129,1},{2,130},{130,2},{3,131},{131,3},{4... | collective-permute-start | bytes 983048 | tf_op jit(solution)/shard_map/ppermute | solution.py:370
  83.1 15.3 %collective-permute-start.13 = (f32[384,128]{1,0:T(8,128)S(1)}, f32[384,128]{1,0:T(8,128)S(1)}, u32[]{:S(2)}, u32[]{:S(2)}) collective-permute-start(f32[384,128]{1,0:T(8,128)S(1)} %get-tuple-element.27), channel_id=1, source_target_pairs={{2,4},{4,2},{6,0},{0,6},{3,5},{5,3},{7,1},{1,7},{10,12},{12,10},{1... | collective-permute-start | bytes 589832 | tf_op jit(solution)/shard_map/ppermute | solution.py:370
  84.1 14.2 %collective-permute-start.14 = (f32[256,128]{1,0:T(8,128)S(1)}, f32[256,128]{1,0:T(8,128)S(1)}, u32[]{:S(2)}, u32[]{:S(2)}) collective-permute-start(f32[256,128]{1,0:T(8,128)S(1)} %get-tuple-element.28), channel_id=1, source_target_pairs={{32,64},{64,32},{96,0},{0,96},{33,65},{65,33},{97,1},{1,97},{34,66... | collective-permute-start | bytes 393224 | tf_op jit(solution)/shard_map/ppermute | solution.py:370
  89.3 8.0 %collective-permute-start.17 = (f32[1,128]{1,0:T(1,128)S(1)}, f32[1,128]{1,0:T(1,128)S(1)}, u32[]{:S(2)}, u32[]{:S(2)}) collective-permute-start(f32[1,128]{1,0:T(1,128)S(1)} %get-tuple-element.34.curvature), channel_id=1, source_target_pairs={{0,1},{1,0},{2,3},{3,2},{4,5},{5,4},{6,7},{7,6},{8,9},{9,8},{10,11... | collective-permute-start | bytes 1544 | tf_op jit(solution)/shard_map/ppermute | solution.py:441

commit v9 on v8

--- a/solution.py
+++ b/solution.py
@@ -192,22 +192,16 @@
         out[parity ^ 1, last + line : last + line + 1, :] = value
 
 
-def tie_kernel(out, out_0, near, far, to_0, to_1, to_2, to_3, row_sum):
-    zh_sum = jnp.sum(near[...] + far[...], axis=1, keepdims=True)
-    row_sum[...] = jnp.broadcast_to(zh_sum, (8, B))
-    grads = GRADS * B
-    to_0[:grads, :] = out_0[1]
-    to_0[grads:, :] = row_sum[...]
+def tie_kernel(out, out_0, near, far, to_0, to_1, to_2, to_3, sums):
+    sums[...] = near[...] + far[...]
+    to_0[...] = out_0[1]
     for target, (first, end) in zip((to_1, to_2, to_3), OUT_STREAMS):
-        target[: (end - first) * B, :] = out[1, first * B : end * B, :]
-    to_1[OUT_STREAMS[0][1] * B :, :] = row_sum[...]
-
-
-def add_kernel(out, out_0, from_0, from_1, from_2, from_3, row_sum, row_two, total):
-    grads = GRADS * B
-    near, far = from_0[grads:, :], from_1[OUT_STREAMS[0][1] * B :, :]
-    energy = (row_sum[...] + row_two[...]) + (near + far)
-    shifted = energy[:1, :] * (1.0 / 256.0) + SHIFT
+        target[...] = out[1, first * B : end * B, :]
+
+
+def add_kernel(out, out_0, from_0, from_1, from_2, from_3, sums, sums_1, total):
+    known = jnp.where(lax.axis_index("c") == 0, sums_1[...], sums[...])
+    shifted = jnp.sum(known, axis=1, keepdims=True) * (1.0 / 256.0) + SHIFT
     for part, (first, end) in zip((from_1, from_2, from_3), OUT_STREAMS):
         for place in range(first, end):
             rows = slice(place * B, (place + 1) * B)
@@ -370,6 +364,10 @@
     return [lax.ppermute(part, axis, pairs) for part, (axis, pairs) in zip(parts, ways)]
 
 
+def core_1(value, axis, pairs):
+    return lax.ppermute(value, (axis, "c"), [(2 * a + 1, 2 * b + 1) for a, b in pairs])
+
+
 def streams_of(streams):
     return [(((end - first) * B, B), F32) for first, end in streams]
 
@@ -380,10 +378,12 @@
     pair = pair_means.reshape(2, HALF, PAIR)
     swap = [(0, 1), (1, 0)]
 
-    sum_2 = energies + lax.ppermute(energies, "zh", LOW)
+    sums = energies
+    for axis, pairs in (("zh", LOW), ("x", LOW), ("x", HIGH)):
+        sums = sums + core_1(sums, axis, pairs)
     other = lax.ppermute(jnp.concatenate([feat, psi], 1).astype(F32), "c", swap)
     oth_pair = lax.ppermute(pair.astype(F32), "c", swap)
-    far_2 = lax.ppermute(sum_2, "zh", HIGH)
+    far = core_1(sums, "zh", HIGH)
 
     grads = GRADS * B
     out, out_0 = call(
@@ -403,22 +403,21 @@
         moved=8_000_000,
     )(feat, pair, psi, other, oth_pair, weights, energies, energies, multiplicity)
 
-    sizes = [((end - first) * B, B) for first, end in OUT_STREAMS]
-    to_0, to_1, to_2, to_3, row_sum = call(
+    to_0, to_1, to_2, to_3, sums = call(
         tie_kernel,
-        [((grads + 8, B), F32), ((sizes[0][0] + 8, B), F32), (sizes[1], F32), (sizes[2], F32), ((8, B), F32)],
+        [((grads, B), F32)] + streams_of(OUT_STREAMS) + [((1, WALK), F32)],
         [V] * 4,
         8,
         "tie",
         moved=3_000_000,
-    )(out, out_0, sum_2, far_2)
+    )(out, out_0, sums, far)
     from_0 = lax.ppermute(to_0, "x", LOW)
     from_1 = lax.ppermute(to_1, "x", HIGH)
     from_2 = lax.ppermute(to_2, "y", LOW)
     from_3 = lax.ppermute(to_3, "zl", swap)
-    row_two = lax.ppermute(row_sum, "x", [(0, 2), (1, 3), (2, 0), (3, 1)])
+    sums_1 = lax.ppermute(sums, "c", [(1, 0)])
     (total,) = call(add_kernel, [((KEPT, B), F32)], [V] * 8, 10, "add", moved=3_000_000)(
-        out, out_0, from_0, from_1, from_2, from_3, row_sum, row_two
+        out, out_0, from_0, from_1, from_2, from_3, sums, sums_1
     )
     mine = jnp.sum(same_parity(total).reshape(GROUP, CHUNK, B), axis=0)
     one, two, three = (

time: 101 us -> 113 us (1.12)
  blocking collectives: 38.2 us -> 43.1 us
  starting transfers between devices: 31.2 us -> 35.5 us
  waiting for transfers between devices: 17.3 us -> 20.5 us
    ppermute x3 -> x5, starting transfers between devices: 6.26 us -> 15.8 us  [the longest x4 14.6 us: core_1(): lax.ppermute(value, (axis, 'c'), [(2 * a + 1, 2 * b + 1) for a, b in pairs])]
    all_to_all x2, blocking collectives: 38.2 us -> 43.1 us  [same_parity(): lax.all_to_all(value, axes, 0, 0, axis_index_groups=parity_groups(), tile...]
    ppermute x1, starting transfers between devices: 7.21 us -> 2.83 us  [body(): other = lax.ppermute(curvature, 'c', swap)]
    ppermute x1, waiting for transfers between devices: 0.01 us -> 3.1 us  [body(): from_3 = lax.ppermute(to_3, 'zl', swap)]
    ppermute x1, starting transfers between devices: 1.3 us -> 0.13 us  [body(): from_0 = lax.ppermute(to_0, 'x', LOW)]
    ppermute x3 -> x5, waiting for transfers between devices: 7.96 us -> 6.98 us  [the longest x4 6.18 us: core_1(): lax.ppermute(value, (axis, 'c'), [(2 * a + 1, 2 * b + 1) for a, b in pairs])]
  transfers between devices with their start and end apart: 18 -> 20, of which waited for: 7 -> 10; matrix products, arithmetic and copies ran while one was open for 0% -> 0% of each run, Pallas kernels for 8% -> 7%
where the time goes in v9:
time: 113 us
  blocking collectives  43.1 us (38%)
  starting transfers between devices  35.5 us (31%)
  waiting for transfers between devices  20.5 us (18%)
  Pallas kernels  10.6 us (9%)
  between operations  1.66 us (1%)
  other arithmetic  1.39 us (1%)
    all_to_all x2, blocking collectives, same_parity(): lax.all_to_all(value, axes, 0, 0, axis_index_groups=parity_groups(), tile...  43.1 us
    ppermute x4, starting transfers between devices, core_1(): lax.ppermute(value, (axis, 'c'), [(2 * a + 1, 2 * b + 1) for a, b in pairs])  14.6 us
    ppermute x3, waiting for transfers between devices, body(): lax.ppermute(mine, 'zh', [(i, (i + k) % 4) for i in range(4)])  7.54 us
    ppermute x4, waiting for transfers between devices, core_1(): lax.ppermute(value, (axis, 'c'), [(2 * a + 1, 2 * b + 1) for a, b in pairs])  6.18 us
    pallas_call x1, Pallas kernels, body(): call(factors_kernel, [((2, KEPT, B), F32), ((2, grads, B), F32)], [V] * 7...  4.73 us
    ppermute x3, starting transfers between devices, body(): lax.ppermute(mine, 'zh', [(i, (i + k) % 4) for i in range(4)])  4.69 us
    ppermute x5, starting transfers between devices, to_neighbours(): lax.ppermute(part, axis, pairs)  3.96 us
    ppermute x1, starting transfers between devices, body(): other = lax.ppermute(jnp.concatenate([feat, psi], 1).astype(F32), 'c', swap)  3.33 us
  transfers between devices with their start and end apart: 20, of which 10 were waited for; matrix products, arithmetic and copies ran while one was open for 0% of the time, Pallas kernels for 7%

profile of v9, /device:TPU:1, one launch (start us, length us, event | category | flops | bytes accessed | tf_op | source)
XLA Modules:
  0.0 112.8 jit_solution(11891624260955486591)
XLA Ops:
  0.6 0.0 copy-start
  0.6 0.0 copy-start.6
  0.7 0.0 copy-start.1
  0.7 0.0 copy-start.2
  0.7 0.0 copy-start.4
  0.7 1.3 %maximum_convert_fusion = f32[512,512]{1,0:T(8,128)S(1)} fusion(bf16[512,256]{1,0:T(8,128)(2,1)} %bitcast.18, bf16[512,256]{1,0:T(8,128)(2,1)} %bitcast.16), kind=kLoop, calls=%fused_computation | loop fusion | flops 1048576 | bytes 1572864 | tf_op jit(solution)/shard_map/convert_element_type | solution.py:384
  2.0 3.3 %collective-permute-start = (f32[512,512]{1,0:T(8,128)S(1)}, f32[512,512]{1,0:T(8,128)S(1)}, u32[]{:S(2)}, u32[]{:S(2)}) collective-permute-start(f32[512,512]{1,0:T(8,128)S(1)} %maximum_convert_fusion), channel_id=1, source_target_pairs={{0,1},{1,0},{2,3},{3,2},{4,5},{5,4},{6,7},{7,6},{8,9},{9,8},{10,11... | collective-permute-start | bytes 3145736 | tf_op jit(solution)/shard_map/ppermute | solution.py:384
  5.3 0.0 copy-done
  5.3 0.1 collective-permute-start.1
  5.4 0.0 copy-done.6
  5.4 3.2 %collective-permute-start.2 = (f32[1,16]{1,0:T(1,128)S(1)}, f32[1,16]{1,0:T(1,128)S(1)}, u32[]{:S(2)}, u32[]{:S(2)}) collective-permute-start(f32[1,16]{1,0:T(1,128)S(1)} %copy-done.6), channel_id=1, source_target_pairs={{1,9},{9,1},{17,25},{25,17},{3,11},{11,3},{19,27},{27,19},{5,13},{... | collective-permute-start | bytes 200 | tf_op jit(solution)/shard_map/ppermute | solution.py:368
  8.6 2.0 %collective-permute-done.2 = f32[1,16]{1,0:T(1,128)S(1)} collective-permute-done((f32[1,16]{1,0:T(1,128)S(1)}, f32[1,16]{1,0:T(1,128)S(1)}, u32[]{:S(2)}, u32[]{:S(2)}) %collective-permute-start.2) | collective-permute-done | bytes 96 | tf_op jit(solution)/shard_map/ppermute | solution.py:368
  10.6 2.0 %collective-permute-start.3 = (f32[1,16]{1,0:T(1,128)S(1)}, f32[1,16]{1,0:T(1,128)S(1)}, u32[]{:S(2)}, u32[]{:S(2)}) collective-permute-start(f32[1,16]{1,0:T(1,128)S(1)} %add.19), channel_id=1, source_target_pairs={{1,3},{3,1},{5,7},{7,5},{9,11},{11,9},{13,15},{15,13},{17,19},{19,... | collective-permute-start | bytes 200 | tf_op jit(solution)/shard_map/ppermute | solution.py:368
  12.6 2.3 %collective-permute-done.3 = f32[1,16]{1,0:T(1,128)S(1)} collective-permute-done((f32[1,16]{1,0:T(1,128)S(1)}, f32[1,16]{1,0:T(1,128)S(1)}, u32[]{:S(2)}, u32[]{:S(2)}) %collective-permute-start.3) | collective-permute-done | bytes 96 | tf_op jit(solution)/shard_map/ppermute | solution.py:368
  14.9 3.3 %collective-permute-start.4 = (f32[1,16]{1,0:T(1,128)S(1)}, f32[1,16]{1,0:T(1,128)S(1)}, u32[]{:S(2)}, u32[]{:S(2)}) collective-permute-start(f32[1,16]{1,0:T(1,128)S(1)} %add.20), channel_id=1, source_target_pairs={{3,5},{5,3},{7,1},{1,7},{11,13},{13,11},{15,9},{9,15},{19,21},{21,... | collective-permute-start | bytes 200 | tf_op jit(solution)/shard_map/ppermute | solution.py:368
  18.8 1.9 %collective-permute-done.4 = f32[1,16]{1,0:T(1,128)S(1)} collective-permute-done((f32[1,16]{1,0:T(1,128)S(1)}, f32[1,16]{1,0:T(1,128)S(1)}, u32[]{:S(2)}, u32[]{:S(2)}) %collective-permute-start.4) | collective-permute-done | bytes 96 | tf_op jit(solution)/shard_map/ppermute | solution.py:368
  20.8 6.1 %collective-permute-start.5 = (f32[1,16]{1,0:T(1,128)S(1)}, f32[1,16]{1,0:T(1,128)S(1)}, u32[]{:S(2)}, u32[]{:S(2)}) collective-permute-start(f32[1,16]{1,0:T(1,128)S(1)} %add.21.near), channel_id=1, source_target_pairs={{9,17},{17,9},{25,1},{1,25},{11,19},{19,11},{27,3},{3,27},{13,21},... | collective-permute-start | bytes 200 | tf_op jit(solution)/shard_map/ppermute | solution.py:368
  26.9 0.0 collective-permute-done.1.oth_pair
  26.9 0.0 collective-permute-done.other
  26.9 0.0 copy-done.1
  26.9 0.0 copy-done.2
  26.9 0.0 copy-done.4
  26.9 4.7 %factors.1 = (f32[2,2176,128]{2,1,0:T(8,128)S(1)}, f32[2,896,128]{2,1,0:T(8,128)S(1)}) custom-call(bf16[512,256]{1,0:T(8,128)(2,1)S(1)} %bitcast.17, bf16[2,512,128]{2,1,0:T(8,128)(2,1)S(1)} %bitcast.15, bf16[512,256]{1,0:T(8,128)(2,1)S(1)} %bitcast.19, f32[512,512]{1,0:T(8,128)S(1)} %collective-permute-done.other, ...), custom_call_target="tpu_custom_call" | custom-call | flops 2500000000 | bytes 8000000 | tf_op jit(solution)/shard_map/factors/pallas_call | solution.py:389
  31.7 0.0 collective-permute-done.5.far
  31.7 0.1 tie.1
  31.8 0.1 collective-permute-start.6
  31.9 2.6 %collective-permute-start.7 = (f32[768,128]{1,0:T(8,128)S(1)}, f32[768,128]{1,0:T(8,128)S(1)}, u32[]{:S(2)}, u32[]{:S(2)}) collective-permute-start(f32[768,128]{1,0:T(8,128)S(1)} %get-tuple-element.22), channel_id=1, source_target_pairs={{2,4},{4,2},{6,0},{0,6},{3,5},{5,3},{7,1},{1,7},{10,12},{12,10},{1... | collective-permute-start | bytes 1179656 | tf_op jit(solution)/shard_map/ppermute | solution.py:415
  34.5 1.3 %collective-permute-start.8 = (f32[768,128]{1,0:T(8,128)S(1)}, f32[768,128]{1,0:T(8,128)S(1)}, u32[]{:S(2)}, u32[]{:S(2)}) collective-permute-start(f32[768,128]{1,0:T(8,128)S(1)} %get-tuple-element.23), channel_id=1, source_target_pairs={{0,32},{32,0},{64,96},{96,64},{1,33},{33,1},{65,97},{97,65},{2,34}... | collective-permute-start | bytes 1179656 | tf_op jit(solution)/shard_map/ppermute | solution.py:416
  35.8 0.7 collective-permute-start.9
  36.5 1.3 %collective-permute-start.10 = (f32[1,16]{1,0:T(1,128)S(1)}, f32[1,16]{1,0:T(1,128)S(1)}, u32[]{:S(2)}, u32[]{:S(2)}) collective-permute-start(f32[1,16]{1,0:T(1,128)S(1)} %get-tuple-element.25.sums), channel_id=1, source_target_pairs={{1,0},{3,2},{5,4},{7,6},{9,8},{11,10},{13,12},{15,14},{17,16},{19,... | collective-permute-start | bytes 200 | tf_op jit(solution)/shard_map/ppermute | solution.py:418
  37.8 0.8 collective-permute-done.10.sums_1
  38.6 3.1 %collective-permute-done.9.from_3 = f32[640,128]{1,0:T(8,128)S(1)} collective-permute-done((f32[640,128]{1,0:T(8,128)S(1)}, f32[640,128]{1,0:T(8,128)S(1)}, u32[]{:S(2)}, u32[]{:S(2)}) %collective-permute-start.9) | collective-permute-done | bytes 327712 | tf_op jit(solution)/shard_map/ppermute | solution.py:417
  41.7 0.0 collective-permute-done.7.from_1
  41.7 0.0 collective-permute-done.8.from_2
  41.7 0.0 collective-permute-done.6.from_0
  41.7 0.2 add.28
  41.9 21.5 %all_to_all.17 = f32[16,136,128]{2,1,0:T(8,128)S(1)} all-to-all(f32[16,136,128]{2,1,0:T(8,128)S(1)} %bitcast.13), channel_id=1, replica_groups={{0,4,34,38,64,68,98,102,130,134,160,164,194,198,224,228},{2,6,32,36,66,..., dimensions={0} | all-to-all | bytes 2228224 | tf_op jit(solution)/shard_map/all_to_all | solution.py:356
  63.5 0.1 reduce_sum.9
  63.5 1.3 %collective-permute-start.12 = (f32[136,128]{1,0:T(8,128)S(1)}, f32[136,128]{1,0:T(8,128)S(1)}, u32[]{:S(2)}, u32[]{:S(2)}) collective-permute-start(f32[136,128]{1,0:T(8,128)S(1)} %reduce_sum.9), channel_id=1, source_target_pairs={{0,8},{8,16},{16,24},{24,0},{1,9},{9,17},{17,25},{25,1},{2,10},{10... | collective-permute-start | bytes 208904 | tf_op jit(solution)/shard_map/ppermute | solution.py:424
  64.8 2.4 %collective-permute-start.13 = (f32[136,128]{1,0:T(8,128)S(1)}, f32[136,128]{1,0:T(8,128)S(1)}, u32[]{:S(2)}, u32[]{:S(2)}) collective-permute-start(f32[136,128]{1,0:T(8,128)S(1)} %reduce_sum.9), channel_id=1, source_target_pairs={{0,24},{8,0},{16,8},{24,16},{1,25},{9,1},{17,9},{25,17},{2,26},{10... | collective-permute-start | bytes 208904 | tf_op jit(solution)/shard_map/ppermute | solution.py:424
  67.2 1.0 collective-permute-start.11
  68.2 1.2 %collective-permute-done.12 = f32[136,128]{1,0:T(8,128)S(1)} collective-permute-done((f32[136,128]{1,0:T(8,128)S(1)}, f32[136,128]{1,0:T(8,128)S(1)}, u32[]{:S(2)}, u32[]{:S(2)}) %collective-permute-start.12) | collective-permute-done | bytes 69664 | tf_op jit(solution)/shard_map/ppermute | solution.py:424
  69.5 0.0 collective-permute-done.13
  69.5 6.3 %collective-permute-done.11 = f32[136,128]{1,0:T(8,128)S(1)} collective-permute-done((f32[136,128]{1,0:T(8,128)S(1)}, f32[136,128]{1,0:T(8,128)S(1)}, u32[]{:S(2)}, u32[]{:S(2)}) %collective-permute-start.11) | collective-permute-done | bytes 69664 | tf_op jit(solution)/shard_map/ppermute | solution.py:424
  75.8 0.0 copy-start.5
  75.8 0.1 broadcast_in_dim.15
  75.9 0.0 copy-start.3
  75.9 21.5 %all_to_all.18 = f32[16,136,128]{2,1,0:T(8,128)S(1)} all-to-all(f32[16,136,128]{2,1,0:T(8,128)S(1)} %broadcast_in_dim.15), channel_id=1, replica_groups={{0,4,34,38,64,68,98,102,130,134,160,164,194,198,224,228},{2,6,32,36,66,..., dimensions={0} | all-to-all | bytes 2228224 | tf_op jit(solution)/shard_map/all_to_all | solution.py:356
  97.4 0.1 cut.1
  97.5 0.2 collective-permute-start.17
  97.7 0.5 collective-permute-start.18
  98.1 1.6 %collective-permute-start.14 = (f32[640,128]{1,0:T(8,128)S(1)}, f32[640,128]{1,0:T(8,128)S(1)}, u32[]{:S(2)}, u32[]{:S(2)}) collective-permute-start(f32[640,128]{1,0:T(8,128)S(1)} %get-tuple-element.26), channel_id=1, source_target_pairs={{0,128},{128,0},{1,129},{129,1},{2,130},{130,2},{3,131},{131,3},{4... | collective-permute-start | bytes 983048 | tf_op jit(solution)/shard_map/ppermute | solution.py:364
  99.8 0.4 collective-permute-start.15
  100.2 1.3 %collective-permute-start.16 = (f32[256,128]{1,0:T(8,128)S(1)}, f32[256,128]{1,0:T(8,128)S(1)}, u32[]{:S(2)}, u32[]{:S(2)}) collective-permute-start(f32[256,128]{1,0:T(8,128)S(1)} %get-tuple-element.28), channel_id=1, source_target_pairs={{32,64},{64,32},{96,0},{0,96},{33,65},{65,33},{97,1},{1,97},{34,66... | collective-permute-start | bytes 393224 | tf_op jit(solution)/shard_map/ppermute | solution.py:364
  101.4 0.7 collective-permute-done.18.from_1
  102.2 1.3 %collective-permute-done.17.from_0 = f32[512,128]{1,0:T(8,128)S(1)} collective-permute-done((f32[512,128]{1,0:T(8,128)S(1)}, f32[512,128]{1,0:T(8,128)S(1)}, u32[]{:S(2)}, u32[]{:S(2)}) %collective-permute-start.17) | collective-permute-done | bytes 262176 | tf_op jit(solution)/shard_map/ppermute | solution.py:364
  103.5 2.5 %natural.1 = (f32[896,256]{1,0:T(8,128)S(1)}, f32[1,128]{1,0:T(1,128)S(1)}) custom-call(f32[2176,128]{1,0:T(8,128)S(1)} %bitcast.11, f32[512,128]{1,0:T(8,128)S(1)} %collective-permute-done.17.from_0, f32[384,128]{1,0:T(8,128)S(1)} %collective-permute-done.18.from_1, f32[896,896]{1,0:T(8,128)S(1)} %bitcast.20, f32[256,256]{1,0:T(8,128)S(1)} %bitcast.21), custom_call_target="tpu_custom_call" | custom-call | flops 1500000000 | bytes 5000000 | tf_op jit(solution)/shard_map/natural/pallas_call | solution.py:431
  106.0 2.8 %collective-permute-start.19 = (f32[1,128]{1,0:T(1,128)S(1)}, f32[1,128]{1,0:T(1,128)S(1)}, u32[]{:S(2)}, u32[]{:S(2)}) collective-permute-start(f32[1,128]{1,0:T(1,128)S(1)} %get-tuple-element.34.curvature), channel_id=1, source_target_pairs={{0,1},{1,0},{2,3},{3,2},{4,5},{5,4},{6,7},{7,6},{8,9},{9,8},{10,11... | collective-permute-start | bytes 1544 | tf_op jit(solution)/shard_map/ppermute | solution.py:440
  108.8 0.8 collective-permute-done.19.other
  109.6 1.1 scale.1
  110.7 0.0 collective-permute-done.16.from_4
  110.7 0.0 collective-permute-done.15.from_3
  110.7 0.0 collective-permute-done.14.from_2
  110.7 2.0 %unpack.1 = (f32[896,896]{1,0:T(8,128)}, f32[256,256]{1,0:T(8,128)}) custom-call(f32[2176,128]{1,0:T(8,128)S(1)} %bitcast.12, f32[640,128]{1,0:T(8,128)S(1)} %collective-permute-done.14.from_2, f32[384,128]{1,0:T(8,128)S(1)} %collective-permute-done.15.from_3, f32[256,128]{1,0:T(8,128)S(1)} %collective-permute-done.16.from_4), custom_call_target="tpu_custom_call" | custom-call | flops 10000000 | bytes 6000000 | tf_op jit(solution)/shard_map/unpack/pallas_call | solution.py:441
  (7 shorter events, 0.1 us)
Async XLA Ops:
  0.6 4.7 %copy-start = (bf16[1,2,16,32,128]{4,3,2,1,0:T(8,128)(2,1)S(1)}, bf16[1,2,16,32,128]{4,3,2,1,0:T(8,128)(2,1)}, u32[]{:S(2)}) copy-start(bf16[1,2,16,32,128]{4,3,2,1,0:T(8,128)(2,1)} %param.10) | copy-start | bytes 786436
  0.6 4.8 %copy-start.6 = (f32[1,16]{1,0:T(1,128)S(1)}, f32[1,16]{1,0:T(1,128)}, u32[]{:S(2)}) copy-start(f32[1,16]{1,0:T(1,128)} %energy.1) | copy-start | bytes 196
  0.7 26.3 %copy-start.1 = (bf16[1,16,32,256]{3,2,1,0:T(8,128)(2,1)S(1)}, bf16[1,16,32,256]{3,2,1,0:T(8,128)(2,1)}, u32[]{:S(2)}) copy-start(bf16[1,16,32,256]{3,2,1,0:T(8,128)(2,1)} %param.8) | copy-start | bytes 786436
  0.7 26.3 %copy-start.2 = (bf16[1,16,32,256]{3,2,1,0:T(8,128)(2,1)S(1)}, bf16[1,16,32,256]{3,2,1,0:T(8,128)(2,1)}, u32[]{:S(2)}) copy-start(bf16[1,16,32,256]{3,2,1,0:T(8,128)(2,1)} %param.9) | copy-start | bytes 786436
  0.7 26.3 %copy-start.4 = (bf16[2,896,256]{2,1,0:T(8,128)(2,1)S(1)}, bf16[2,896,256]{2,1,0:T(8,128)(2,1)}, u32[]{:S(2)}) copy-start(bf16[2,896,256]{2,1,0:T(8,128)(2,1)} %weights.1) | copy-start | bytes 2752516
  2.0 24.9 %collective-permute-start = (f32[512,512]{1,0:T(8,128)S(1)}, f32[512,512]{1,0:T(8,128)S(1)}, u32[]{:S(2)}, u32[]{:S(2)}) collective-permute-start(f32[512,512]{1,0:T(8,128)S(1)} %maximum_convert_fusion), channel_id=1, source_target_pairs={{0,1},{1,0},{2,3},{3,2},{4,5},{5,4},{6,7},{7,6},{8,9},{9,8},{10,11... | collective-permute-start | bytes 3145736 | tf_op jit(solution)/shard_map/ppermute | solution.py:384
  5.3 21.6 %collective-permute-start.1 = (f32[2,512,128]{2,1,0:T(8,128)S(1)}, f32[2,512,128]{2,1,0:T(8,128)S(1)}, u32[]{:S(2)}, u32[]{:S(2)}) collective-permute-start(f32[2,512,128]{2,1,0:T(8,128)S(1)} %convert_element_type.7), channel_id=1, source_target_pairs={{0,1},{1,0},{2,3},{3,2},{4,5},{5,4},{6,7},{7,6},{8,9},{9,8},{10,11... | collective-permute-start | bytes 1572872 | tf_op jit(solution)/shard_map/ppermute | solution.py:385
  5.4 5.2 %collective-permute-start.2 = (f32[1,16]{1,0:T(1,128)S(1)}, f32[1,16]{1,0:T(1,128)S(1)}, u32[]{:S(2)}, u32[]{:S(2)}) collective-permute-start(f32[1,16]{1,0:T(1,128)S(1)} %copy-done.6), channel_id=1, source_target_pairs={{1,9},{9,1},{17,25},{25,17},{3,11},{11,3},{19,27},{27,19},{5,13},{... | collective-permute-start | bytes 200 | tf_op jit(solution)/shard_map/ppermute | solution.py:368
  10.6 4.3 %collective-permute-start.3 = (f32[1,16]{1,0:T(1,128)S(1)}, f32[1,16]{1,0:T(1,128)S(1)}, u32[]{:S(2)}, u32[]{:S(2)}) collective-permute-start(f32[1,16]{1,0:T(1,128)S(1)} %add.19), channel_id=1, source_target_pairs={{1,3},{3,1},{5,7},{7,5},{9,11},{11,9},{13,15},{15,13},{17,19},{19,... | collective-permute-start | bytes 200 | tf_op jit(solution)/shard_map/ppermute | solution.py:368
  14.9 5.8 %collective-permute-start.4 = (f32[1,16]{1,0:T(1,128)S(1)}, f32[1,16]{1,0:T(1,128)S(1)}, u32[]{:S(2)}, u32[]{:S(2)}) collective-permute-start(f32[1,16]{1,0:T(1,128)S(1)} %add.20), channel_id=1, source_target_pairs={{3,5},{5,3},{7,1},{1,7},{11,13},{13,11},{15,9},{9,15},{19,21},{21,... | collective-permute-start | bytes 200 | tf_op jit(solution)/shard_map/ppermute | solution.py:368
  20.8 10.9 %collective-permute-start.5 = (f32[1,16]{1,0:T(1,128)S(1)}, f32[1,16]{1,0:T(1,128)S(1)}, u32[]{:S(2)}, u32[]{:S(2)}) collective-permute-start(f32[1,16]{1,0:T(1,128)S(1)} %add.21.near), channel_id=1, source_target_pairs={{9,17},{17,9},{25,1},{1,25},{11,19},{19,11},{27,3},{3,27},{13,21},... | collective-permute-start | bytes 200 | tf_op jit(solution)/shard_map/ppermute | solution.py:368
  31.8 9.9 %collective-permute-start.6 = (f32[896,128]{1,0:T(8,128)S(1)}, f32[896,128]{1,0:T(8,128)S(1)}, u32[]{:S(2)}, u32[]{:S(2)}) collective-permute-start(f32[896,128]{1,0:T(8,128)S(1)} %get-tuple-element.21), channel_id=1, source_target_pairs={{0,2},{2,0},{4,6},{6,4},{1,3},{3,1},{5,7},{7,5},{8,10},{10,8},{12,... | collective-permute-start | bytes 1376264 | tf_op jit(solution)/shard_map/ppermute | solution.py:414
  31.9 9.8 %collective-permute-start.7 = (f32[768,128]{1,0:T(8,128)S(1)}, f32[768,128]{1,0:T(8,128)S(1)}, u32[]{:S(2)}, u32[]{:S(2)}) collective-permute-start(f32[768,128]{1,0:T(8,128)S(1)} %get-tuple-element.22), channel_id=1, source_target_pairs={{2,4},{4,2},{6,0},{0,6},{3,5},{5,3},{7,1},{1,7},{10,12},{12,10},{1... | collective-permute-start | bytes 1179656 | tf_op jit(solution)/shard_map/ppermute | solution.py:415
  34.5 7.2 %collective-permute-start.8 = (f32[768,128]{1,0:T(8,128)S(1)}, f32[768,128]{1,0:T(8,128)S(1)}, u32[]{:S(2)}, u32[]{:S(2)}) collective-permute-start(f32[768,128]{1,0:T(8,128)S(1)} %get-tuple-element.23), channel_id=1, source_target_pairs={{0,32},{32,0},{64,96},{96,64},{1,33},{33,1},{65,97},{97,65},{2,34}... | collective-permute-start | bytes 1179656 | tf_op jit(solution)/shard_map/ppermute | solution.py:416
  35.8 5.9 %collective-permute-start.9 = (f32[640,128]{1,0:T(8,128)S(1)}, f32[640,128]{1,0:T(8,128)S(1)}, u32[]{:S(2)}, u32[]{:S(2)}) collective-permute-start(f32[640,128]{1,0:T(8,128)S(1)} %get-tuple-element.24), channel_id=1, source_target_pairs={{0,128},{128,0},{1,129},{129,1},{2,130},{130,2},{3,131},{131,3},{4... | collective-permute-start | bytes 983048 | tf_op jit(solution)/shard_map/ppermute | solution.py:417
  36.5 2.1 %collective-permute-start.10 = (f32[1,16]{1,0:T(1,128)S(1)}, f32[1,16]{1,0:T(1,128)S(1)}, u32[]{:S(2)}, u32[]{:S(2)}) collective-permute-start(f32[1,16]{1,0:T(1,128)S(1)} %get-tuple-element.25.sums), channel_id=1, source_target_pairs={{1,0},{3,2},{5,4},{7,6},{9,8},{11,10},{13,12},{15,14},{17,16},{19,... | collective-permute-start | bytes 200 | tf_op jit(solution)/shard_map/ppermute | solution.py:418
  63.5 5.9 %collective-permute-start.12 = (f32[136,128]{1,0:T(8,128)S(1)}, f32[136,128]{1,0:T(8,128)S(1)}, u32[]{:S(2)}, u32[]{:S(2)}) collective-permute-start(f32[136,128]{1,0:T(8,128)S(1)} %reduce_sum.9), channel_id=1, source_target_pairs={{0,8},{8,16},{16,24},{24,0},{1,9},{9,17},{17,25},{25,1},{2,10},{10... | collective-permute-start | bytes 208904 | tf_op jit(solution)/shard_map/ppermute | solution.py:424
  64.8 4.7 %collective-permute-start.13 = (f32[136,128]{1,0:T(8,128)S(1)}, f32[136,128]{1,0:T(8,128)S(1)}, u32[]{:S(2)}, u32[]{:S(2)}) collective-permute-start(f32[136,128]{1,0:T(8,128)S(1)} %reduce_sum.9), channel_id=1, source_target_pairs={{0,24},{8,0},{16,8},{24,16},{1,25},{9,1},{17,9},{25,17},{2,26},{10... | collective-permute-start | bytes 208904 | tf_op jit(solution)/shard_map/ppermute | solution.py:424
  67.2 8.6 %collective-permute-start.11 = (f32[136,128]{1,0:T(8,128)S(1)}, f32[136,128]{1,0:T(8,128)S(1)}, u32[]{:S(2)}, u32[]{:S(2)}) collective-permute-start(f32[136,128]{1,0:T(8,128)S(1)} %reduce_sum.9), channel_id=1, source_target_pairs={{0,16},{8,24},{16,0},{24,8},{1,17},{9,25},{17,1},{25,9},{2,18},{10... | collective-permute-start | bytes 208904 | tf_op jit(solution)/shard_map/ppermute | solution.py:424
  75.8 27.7 %copy-start.5 = (f32[1,256,256]{2,1,0:T(8,128)S(1)}, f32[1,256,256]{2,1,0:T(8,128)}, u32[]{:S(2)}) copy-start(f32[1,256,256]{2,1,0:T(8,128)} %param.15) | copy-start | bytes 786436
  75.9 27.6 %copy-start.3 = (f32[1,896,896]{2,1,0:T(8,128)S(1)}, f32[1,896,896]{2,1,0:T(8,128)}, u32[]{:S(2)}) copy-start(f32[1,896,896]{2,1,0:T(8,128)} %param.14) | copy-start | bytes 9633796
  97.5 6.0 %collective-permute-start.17 = (f32[512,128]{1,0:T(8,128)S(1)}, f32[512,128]{1,0:T(8,128)S(1)}, u32[]{:S(2)}, u32[]{:S(2)}) collective-permute-start(f32[512,128]{1,0:T(8,128)S(1)} %get-tuple-element.31), channel_id=1, source_target_pairs={{0,2},{2,0},{4,6},{6,4},{1,3},{3,1},{5,7},{7,5},{8,10},{10,8},{12,... | collective-permute-start | bytes 786440 | tf_op jit(solution)/shard_map/ppermute | solution.py:364
  97.7 4.5 %collective-permute-start.18 = (f32[384,128]{1,0:T(8,128)S(1)}, f32[384,128]{1,0:T(8,128)S(1)}, u32[]{:S(2)}, u32[]{:S(2)}) collective-permute-start(f32[384,128]{1,0:T(8,128)S(1)} %get-tuple-element.32), channel_id=1, source_target_pairs={{0,32},{32,0},{64,96},{96,64},{1,33},{33,1},{65,97},{97,65},{2,34}... | collective-permute-start | bytes 589832 | tf_op jit(solution)/shard_map/ppermute | solution.py:364
  98.1 12.6 %collective-permute-start.14 = (f32[640,128]{1,0:T(8,128)S(1)}, f32[640,128]{1,0:T(8,128)S(1)}, u32[]{:S(2)}, u32[]{:S(2)}) collective-permute-start(f32[640,128]{1,0:T(8,128)S(1)} %get-tuple-element.26), channel_id=1, source_target_pairs={{0,128},{128,0},{1,129},{129,1},{2,130},{130,2},{3,131},{131,3},{4... | collective-permute-start | bytes 983048 | tf_op jit(solution)/shard_map/ppermute | solution.py:364
  99.8 10.9 %collective-permute-start.15 = (f32[384,128]{1,0:T(8,128)S(1)}, f32[384,128]{1,0:T(8,128)S(1)}, u32[]{:S(2)}, u32[]{:S(2)}) collective-permute-start(f32[384,128]{1,0:T(8,128)S(1)} %get-tuple-element.27), channel_id=1, source_target_pairs={{2,4},{4,2},{6,0},{0,6},{3,5},{5,3},{7,1},{1,7},{10,12},{12,10},{1... | collective-permute-start | bytes 589832 | tf_op jit(solution)/shard_map/ppermute | solution.py:364
  100.2 10.5 %collective-permute-start.16 = (f32[256,128]{1,0:T(8,128)S(1)}, f32[256,128]{1,0:T(8,128)S(1)}, u32[]{:S(2)}, u32[]{:S(2)}) collective-permute-start(f32[256,128]{1,0:T(8,128)S(1)} %get-tuple-element.28), channel_id=1, source_target_pairs={{32,64},{64,32},{96,0},{0,96},{33,65},{65,33},{97,1},{1,97},{34,66... | collective-permute-start | bytes 393224 | tf_op jit(solution)/shard_map/ppermute | solution.py:364
  106.0 3.6 %collective-permute-start.19 = (f32[1,128]{1,0:T(1,128)S(1)}, f32[1,128]{1,0:T(1,128)S(1)}, u32[]{:S(2)}, u32[]{:S(2)}) collective-permute-start(f32[1,128]{1,0:T(1,128)S(1)} %get-tuple-element.34.curvature), channel_id=1, source_target_pairs={{0,1},{1,0},{2,3},{3,2},{4,5},{5,4},{6,7},{7,6},{8,9},{9,8},{10,11... | collective-permute-start | bytes 1544 | tf_op jit(solution)/shard_map/ppermute | solution.py:440

commit v10 on v8

--- a/solution.py
+++ b/solution.py
@@ -63,15 +63,12 @@
     return half, place + GRADS
 
 
-def factors_kernel(
-    feat, pair, psi, other, oth_pair, weights, energies, energy, multiplicity,
-    out, out_0, x_s, d_s, m_s, s_s, w_s
-):
+def forward_kernel(feat, pair, oth_feat, oth_pair, weights, x_s, d_s, m_s):
     mp = lax.axis_index("c")
     own_row = pl.multiple_of(D + D * mp, D)
     oth_row = pl.multiple_of(2 * D - D * mp, D)
     x_s[0, :HALF, :D] = feat[...]
-    x_s[0, HALF:, :D] = other[:, :D].astype(BF16)
+    x_s[0, HALF:, :D] = oth_feat[...].astype(BF16)
     for l in range(2):
         x_s[l, :HALF, D:] = pair[l]
         x_s[l, HALF:, D:] = oth_pair[l].astype(BF16)
@@ -93,15 +90,25 @@
             if l == 0:
                 x_s[1, rows, :D] = (x_s[0, rows, :D].astype(F32) + t).astype(BF16)
 
+
+def pair_kernel(after, near, far, sums):
+    sums[...] = near[...] + far[...]
+
+
+def factors_kernel(x_s, d_s, m_s, psi, oth_psi, weights, energies, energy, multiplicity, out, out_0, s_s, w_s):
+    mp = lax.axis_index("c")
+    own_row = pl.multiple_of(D + D * mp, D)
+    oth_row = pl.multiple_of(2 * D - D * mp, D)
+    pick = walker_table()
     s_s[1, :HALF, :] = (psi[...].astype(F32) * d_s[1, :HALF, :]).astype(BF16)
-    s_s[1, HALF:, :] = (other[:, D : 2 * D] * d_s[1, HALF:, :]).astype(BF16)
+    s_s[1, HALF:, :] = (oth_psi[...] * d_s[1, HALF:, :]).astype(BF16)
     q_both = dot(pick, s_s[1])
     q_high, q_low = split(q_both[:WALK] + q_both[WALK:])
     for half in range(2):
         rows = slice(half * HALF, (half + 1) * HALF)
         w_spin = weights[1, pl.ds(own_row if half == 0 else oth_row, D), :]
         spin = (dot_nt(q_high, w_spin) + dot_nt(q_low, w_spin)) * (1.0 / 32.0)
-        up = psi[...].astype(F32) if half == 0 else other[:, D : 2 * D]
+        up = psi[...].astype(F32) if half == 0 else oth_psi[...]
         u = up + dot_nt(s_s[1, rows, :], weights[1, :D, :]) + per_walker(spin)
         s_s[0, rows, :] = (u * d_s[0, rows, :]).astype(BF16)
 
@@ -236,7 +243,7 @@
     return read
 
 
-def unpack_kernel(kept, from_2, from_3, from_4, a_out, s_out, a_v, s_v, sems):
+def unpack_kernel(kept, from_2, from_3, from_4, a_out, s_out, done, a_v, s_v, sems):
     row, col = square_iotas()
     read = reader(kept, (from_2, from_3, from_4), BACK_STREAMS[2:])
     lines = read(33, 8)
@@ -303,6 +310,7 @@
     send(a_v, a_out, 6, 7)
     for copy in copies:
         copy.wait()
+    done[...] = inverse
 
 
 def natural_kernel(kept, from_0, from_1, a_inverse, s_inverse, natural, curvature):
@@ -325,17 +333,17 @@
     curvature[...] = jnp.broadcast_to(jnp.sum(total, axis=1, keepdims=True), (1, B))
 
 
-def scale_kernel(natural, curvature, other, direction):
+def scale_kernel(natural, curvature, other, after, direction):
     total = curvature[:, :1] + other[:, :1]
     direction[...] = natural[...] * lax.rsqrt(total * (1.0 / ENTRIES))
 
 
-def call(kernel, out_shapes, in_spaces, limit_mib, name, scratch=(), flops=0, moved=0, out_space=pltpu.VMEM):
+def call(kernel, out_shapes, in_spaces, limit_mib, name, scratch=(), flops=0, moved=0, out_spaces=None):
     return pl.pallas_call(
         kernel,
         out_shape=tuple(jax.ShapeDtypeStruct(shape, dtype) for shape, dtype in out_shapes),
         in_specs=[pl.BlockSpec(memory_space=space) for space in in_spaces],
-        out_specs=tuple(pl.BlockSpec(memory_space=out_space) for _ in out_shapes),
+        out_specs=tuple(pl.BlockSpec(memory_space=space) for space in out_spaces or [V] * len(out_shapes)),
         scratch_shapes=scratch,
         compiler_params=pltpu.CompilerParams(vmem_limit_bytes=limit_mib * 1024 * 1024),
         cost_estimate=pl.CostEstimate(flops=flops, bytes_accessed=moved, transcendentals=0),
@@ -380,9 +388,21 @@
     pair = pair_means.reshape(2, HALF, PAIR)
     swap = [(0, 1), (1, 0)]
 
-    sum_2 = energies + lax.ppermute(energies, "zh", LOW)
-    other = lax.ppermute(jnp.concatenate([feat, psi], 1).astype(F32), "c", swap)
+    oth_feat = lax.ppermute(feat.astype(F32), "c", swap)
     oth_pair = lax.ppermute(pair.astype(F32), "c", swap)
+    far_1 = lax.ppermute(energies, "zh", LOW)
+    oth_psi = lax.ppermute(psi.astype(F32), "c", swap)
+
+    x_s, d_s, m_s = call(
+        forward_kernel,
+        [((2, ROWS, D + PAIR), BF16), ((2, ROWS, D), F32), ((2, 2 * WALK, D), BF16)],
+        [V] * 5,
+        16,
+        "forward",
+        flops=1_000_000_000,
+        moved=6_000_000,
+    )(feat, pair, oth_feat, oth_pair, weights)
+    (sum_2,) = call(pair_kernel, [((1, WALK), F32)], [V] * 3, 4, "pair")(m_s, energies, far_1)
     far_2 = lax.ppermute(sum_2, "zh", HIGH)
 
     grads = GRADS * B
@@ -390,18 +410,15 @@
         factors_kernel,
         [((2, KEPT, B), F32), ((2, grads, B), F32)],
         [V] * 7 + [S] * 2,
-        26,
+        24,
         "factors",
         scratch=[
-            pltpu.VMEM((2, ROWS, D + PAIR), BF16),
-            pltpu.VMEM((2, ROWS, D), F32),
-            pltpu.VMEM((2, 2 * WALK, D), BF16),
             pltpu.VMEM((2, ROWS, D), BF16),
             pltpu.VMEM((ROWS, 4 * D + PAIR), BF16),
         ],
         flops=2_500_000_000,
         moved=8_000_000,
-    )(feat, pair, psi, other, oth_pair, weights, energies, energies, multiplicity)
+    )(x_s, d_s, m_s, psi, oth_psi, weights, energies, energies, multiplicity)
 
     sizes = [((end - first) * B, B) for first, end in OUT_STREAMS]
     to_0, to_1, to_2, to_3, row_sum = call(
@@ -439,20 +456,20 @@
         moved=5_000_000,
     )(kept, *parts[:2], a_inverse[0], s_inverse[0])
     other = lax.ppermute(curvature, "c", swap)
-    a_sum, s_sum = call(
+    a_sum, s_sum, done = call(
         unpack_kernel,
-        [((DIN, DIN), F32), ((D, D), F32)],
+        [((DIN, DIN), F32), ((D, D), F32), ((1, B), F32)],
         [V] * 4,
         14,
         "unpack",
         scratch=[pltpu.VMEM((DIN, DIN), F32), pltpu.VMEM((D, D), F32), pltpu.SemaphoreType.DMA((5,))],
-        out_space=pl.ANY,
+        out_spaces=(pl.ANY, pl.ANY, V),
         flops=10_000_000,
         moved=6_000_000,
     )(kept, *parts[2:])
     (direction,) = call(
-        scale_kernel, [((DIN, D), F32)], [V] * 3, 6, "scale", flops=1_000_000, moved=2_000_000
-    )(natural, curvature, other)
+        scale_kernel, [((DIN, D), F32)], [V] * 4, 6, "scale", flops=1_000_000, moved=2_000_000
+    )(natural, curvature, other, done)
     return a_sum[None], s_sum[None], direction[None]
 
 

time: 101 us -> 97.3 us (0.963)
  waiting for transfers between devices: 17.3 us -> 13.7 us
  blocking collectives: 38.2 us -> 36.5 us
  starting transfers between devices: 31.2 us -> 32.5 us
    ppermute x1, starting transfers between devices: 0.11 us -> 3.33 us  [body(): oth_pair = lax.ppermute(pair.astype(F32), 'c', swap)]
    ppermute x2 -> x3, starting transfers between devices: 4.66 us -> 1.96 us  [the longest x1 1.28 us: body(): far_1 = lax.ppermute(energies, 'zh', LOW)]
    all_to_all x2, blocking collectives: 38.2 us -> 36.5 us  [same_parity(): lax.all_to_all(value, axes, 0, 0, axis_index_groups=parity_groups(), tile...]
    ppermute x3, waiting for transfers between devices: 6.6 us -> 5.05 us  [body(): lax.ppermute(mine, 'zh', [(i, (i + k) % 4) for i in range(4)])]
    pallas_call x1, Pallas kernels: 4.73 us -> 3.24 us  [body(): call(factors_kernel, [((2, KEPT, B), F32), ((2, grads, B), F32)], [V] * 7...]
    ppermute x2 -> x3, waiting for transfers between devices: 1.39 us -> 0.01 us  [the longest x1 0.01 us: body(): oth_feat = lax.ppermute(feat.astype(F32), 'c', swap)]
    pallas_call x2 -> x4, Pallas kernels: 3.02 us -> 4.39 us  [the longest x1 1.96 us: body(): call(unpack_kernel, [((DIN, DIN), F32), ((D, D), F32), ((1, B), F32)], [V...]
    ppermute x5, starting transfers between devices: 4.57 us -> 5.89 us  [to_neighbours(): lax.ppermute(part, axis, pairs)]
  transfers between devices with their start and end apart: 18 -> 19, of which waited for: 7 -> 5; matrix products, arithmetic and copies ran while one was open for 0% -> 1% of each run, Pallas kernels for 8% -> 9%
where the time goes in v10:
time: 97.3 us; the launch traced here: 97.1 us
  blocking collectives  36.5 us (38%)
  starting transfers between devices  32.5 us (33%)
  waiting for transfers between devices  13.7 us (14%)
  Pallas kernels  10.5 us (11%)
  other arithmetic  2.22 us (2%)
  between operations  1.5 us (2%)
    all_to_all x2, blocking collectives, same_parity(): lax.all_to_all(value, axes, 0, 0, axis_index_groups=parity_groups(), tile...  36.5 us
    ppermute x1, waiting for transfers between devices, body(): row_two = lax.ppermute(row_sum, 'x', [(0, 2), (1, 3), (2, 0), (3, 1)])  6.93 us
    ppermute x1, starting transfers between devices, body(): other = lax.ppermute(curvature, 'c', swap)  6.67 us
    ppermute x5, starting transfers between devices, to_neighbours(): lax.ppermute(part, axis, pairs)  5.89 us
    ppermute x3, waiting for transfers between devices, body(): lax.ppermute(mine, 'zh', [(i, (i + k) % 4) for i in range(4)])  5.05 us
    ppermute x3, starting transfers between devices, body(): lax.ppermute(mine, 'zh', [(i, (i + k) % 4) for i in range(4)])  4.63 us
    ppermute x1, starting transfers between devices, body(): far_2 = lax.ppermute(sum_2, 'zh', HIGH)  4.29 us
    ppermute x1, starting transfers between devices, body(): oth_pair = lax.ppermute(pair.astype(F32), 'c', swap)  3.33 us
  transfers between devices with their start and end apart: 19, of which 5 were waited for; matrix products, arithmetic and copies ran while one was open for 1% of the time, Pallas kernels for 9%

profile of v10, /device:TPU:1, one launch (start us, length us, event | category | flops | bytes accessed | tf_op | source)
XLA Modules:
  0.0 97.1 jit_solution(11122592572016842582)
XLA Ops:
  0.6 0.0 copy-start.1
  0.6 0.0 copy-start
  0.7 0.0 copy-start.2
  0.7 0.0 copy-start.3
  0.7 0.0 copy-start.5
  0.7 1.1 %convert_element_type.10 = f32[2,512,128]{2,1,0:T(8,128)S(1)} convert(bf16[2,512,128]{2,1,0:T(8,128)(2,1)} %bitcast.17) | non-fusion elementwise | flops 131072 | bytes 786432 | tf_op jit(solution)/shard_map/convert_element_type | solution.py:392
  1.8 3.3 %collective-permute-start.1 = (f32[2,512,128]{2,1,0:T(8,128)S(1)}, f32[2,512,128]{2,1,0:T(8,128)S(1)}, u32[]{:S(2)}, u32[]{:S(2)}) collective-permute-start(f32[2,512,128]{2,1,0:T(8,128)S(1)} %convert_element_type.10), channel_id=1, source_target_pairs={{0,1},{1,0},{2,3},{3,2},{4,5},{5,4},{6,7},{7,6},{8,9},{9,8},{10,11... | collective-permute-start | bytes 1572872 | tf_op jit(solution)/shard_map/ppermute | solution.py:392
  5.1 1.0 %bitcast_convert_fusion.1 = f32[512,256]{1,0:T(8,128)S(1)} fusion(bf16[1,16,32,256]{3,2,1,0:T(8,128)(2,1)} %param.8), kind=kLoop, calls=%fused_computation.2 | loop fusion | flops 131072 | bytes 786432 | tf_op jit(solution)/shard_map/convert_element_type | solution.py:391
  6.1 0.1 collective-permute-start
  6.2 0.0 copy-done.2
  6.2 0.1 bitcast_convert_fusion
  6.3 0.6 collective-permute-start.2
  6.8 0.0 copy-done.3
  6.9 1.3 %collective-permute-start.3 = (f32[1,16]{1,0:T(1,128)S(1)}, f32[1,16]{1,0:T(1,128)S(1)}, u32[]{:S(2)}, u32[]{:S(2)}) collective-permute-start(f32[1,16]{1,0:T(1,128)S(1)} %copy-done.3), channel_id=1, source_target_pairs={{0,8},{8,0},{16,24},{24,16},{1,9},{9,1},{17,25},{25,17},{2,10},{10... | collective-permute-start | bytes 200 | tf_op jit(solution)/shard_map/ppermute | solution.py:393
  8.8 0.0 collective-permute-done.1.oth_pair
  8.8 0.0 collective-permute-done.oth_feat
  8.8 0.0 copy-done.1
  8.8 0.0 copy-done
  8.8 1.4 %forward.1 = (bf16[2,1024,384]{2,1,0:T(8,128)(2,1)S(1)}, f32[2,1024,256]{2,1,0:T(8,128)S(1)}, bf16[2,32,256]{2,1,0:T(8,128)(2,1)S(1)}) custom-call(bf16[512,256]{1,0:T(8,128)(2,1)S(1)} %bitcast.16, bf16[2,512,128]{2,1,0:T(8,128)(2,1)S(1)} %bitcast.18, f32[512,256]{1,0:T(8,128)S(1)} %collective-permute-done.oth_feat, ...), custom_call_target="tpu_custom_call" | custom-call | flops 1000000000 | bytes 6000000 | tf_op jit(solution)/shard_map/forward/pallas_call | solution.py:396
  10.2 0.0 collective-permute-done.3.far
  10.2 4.3 %collective-permute-start.4 = (f32[1,16]{1,0:T(1,128)S(1)}, f32[1,16]{1,0:T(1,128)S(1)}, u32[]{:S(2)}, u32[]{:S(2)}) collective-permute-start(f32[1,16]{1,0:T(1,128)S(1)} %pair.1.near), channel_id=1, source_target_pairs={{8,16},{16,8},{24,0},{0,24},{9,17},{17,9},{25,1},{1,25},{10,18},{1... | collective-permute-start | bytes 200 | tf_op jit(solution)/shard_map/ppermute | solution.py:406
  14.5 0.0 collective-permute-done.2.oth_psi
  14.5 3.2 %factors.1 = (f32[2,2176,128]{2,1,0:T(8,128)S(1)}, f32[2,896,128]{2,1,0:T(8,128)S(1)}) custom-call(bf16[2,1024,384]{2,1,0:T(8,128)(2,1)S(1)} %get-tuple-element.23.x_s, f32[2,1024,256]{2,1,0:T(8,128)S(1)} %get-tuple-element.24.d_s, bf16[2,32,256]{2,1,0:T(8,128)(2,1)S(1)} %get-tuple-element.25.m_s.after, bf16[512,256]{1,0:T(8,128)(2,1)S(1)} %bitcast.19, ...), custom_call_target="tpu_custom_call" | custom-call | flops 2500000000 | bytes 8000000 | tf_op jit(solution)/shard_map/factors/pallas_call | solution.py:409
  17.8 0.0 collective-permute-done.4.far
  17.8 0.1 tie.1
  17.9 1.3 %collective-permute-start.5 = (f32[904,128]{1,0:T(8,128)S(1)}, f32[904,128]{1,0:T(8,128)S(1)}, u32[]{:S(2)}, u32[]{:S(2)}) collective-permute-start(f32[904,128]{1,0:T(8,128)S(1)} %get-tuple-element.28), channel_id=1, source_target_pairs={{0,2},{2,0},{4,6},{6,4},{1,3},{3,1},{5,7},{7,5},{8,10},{10,8},{12,... | collective-permute-start | bytes 1388552 | tf_op jit(solution)/shard_map/ppermute | solution.py:432
  19.2 1.8 %collective-permute-start.6 = (f32[776,128]{1,0:T(8,128)S(1)}, f32[776,128]{1,0:T(8,128)S(1)}, u32[]{:S(2)}, u32[]{:S(2)}) collective-permute-start(f32[776,128]{1,0:T(8,128)S(1)} %get-tuple-element.29), channel_id=1, source_target_pairs={{2,4},{4,2},{6,0},{0,6},{3,5},{5,3},{7,1},{1,7},{10,12},{12,10},{1... | collective-permute-start | bytes 1191944 | tf_op jit(solution)/shard_map/ppermute | solution.py:433
  21.0 1.3 %collective-permute-start.7 = (f32[768,128]{1,0:T(8,128)S(1)}, f32[768,128]{1,0:T(8,128)S(1)}, u32[]{:S(2)}, u32[]{:S(2)}) collective-permute-start(f32[768,128]{1,0:T(8,128)S(1)} %get-tuple-element.30), channel_id=1, source_target_pairs={{0,32},{32,0},{64,96},{96,64},{1,33},{33,1},{65,97},{97,65},{2,34}... | collective-permute-start | bytes 1179656 | tf_op jit(solution)/shard_map/ppermute | solution.py:434
  22.3 0.7 collective-permute-start.8
  23.0 0.6 collective-permute-start.9
  23.7 6.9 %collective-permute-done.9.row_two = f32[8,128]{1,0:T(8,128)S(1)} collective-permute-done((f32[8,128]{1,0:T(8,128)S(1)}, f32[8,128]{1,0:T(8,128)S(1)}, u32[]{:S(2)}, u32[]{:S(2)}) %collective-permute-start.9) | collective-permute-done | bytes 4128 | tf_op jit(solution)/shard_map/ppermute | solution.py:436
  30.6 0.0 collective-permute-done.8.from_3
  30.6 0.0 collective-permute-done.7.from_2
  30.6 0.0 collective-permute-done.6.from_1
  30.6 0.0 collective-permute-done.5.from_0
  30.6 0.2 add.16
  30.8 20.4 %all_to_all.17 = f32[16,136,128]{2,1,0:T(8,128)S(1)} all-to-all(f32[16,136,128]{2,1,0:T(8,128)S(1)} %bitcast.15), channel_id=1, replica_groups={{0,4,34,38,64,68,98,102,130,134,160,164,194,198,224,228},{2,6,32,36,66,..., dimensions={0} | all-to-all | bytes 2228224 | tf_op jit(solution)/shard_map/all_to_all | solution.py:370
  51.3 0.1 reduce_sum.9
  51.3 0.9 collective-permute-start.10
  52.3 1.1 %collective-permute-start.11 = (f32[136,128]{1,0:T(8,128)S(1)}, f32[136,128]{1,0:T(8,128)S(1)}, u32[]{:S(2)}, u32[]{:S(2)}) collective-permute-start(f32[136,128]{1,0:T(8,128)S(1)} %reduce_sum.9), channel_id=1, source_target_pairs={{0,8},{8,16},{16,24},{24,0},{1,9},{9,17},{17,25},{25,1},{2,10},{10... | collective-permute-start | bytes 208904 | tf_op jit(solution)/shard_map/ppermute | solution.py:442
  53.4 2.5 %collective-permute-start.12 = (f32[136,128]{1,0:T(8,128)S(1)}, f32[136,128]{1,0:T(8,128)S(1)}, u32[]{:S(2)}, u32[]{:S(2)}) collective-permute-start(f32[136,128]{1,0:T(8,128)S(1)} %reduce_sum.9), channel_id=1, source_target_pairs={{0,24},{8,0},{16,8},{24,16},{1,25},{9,1},{17,9},{25,17},{2,26},{10... | collective-permute-start | bytes 208904 | tf_op jit(solution)/shard_map/ppermute | solution.py:442
  56.0 3.0 %collective-permute-done.10 = f32[136,128]{1,0:T(8,128)S(1)} collective-permute-done((f32[136,128]{1,0:T(8,128)S(1)}, f32[136,128]{1,0:T(8,128)S(1)}, u32[]{:S(2)}, u32[]{:S(2)}) %collective-permute-start.10) | collective-permute-done | bytes 69664 | tf_op jit(solution)/shard_map/ppermute | solution.py:442
  58.9 0.4 collective-permute-done.11
  59.3 1.7 %collective-permute-done.12 = f32[136,128]{1,0:T(8,128)S(1)} collective-permute-done((f32[136,128]{1,0:T(8,128)S(1)}, f32[136,128]{1,0:T(8,128)S(1)}, u32[]{:S(2)}, u32[]{:S(2)}) %collective-permute-start.12) | collective-permute-done | bytes 69664 | tf_op jit(solution)/shard_map/ppermute | solution.py:442
  61.0 0.0 copy-start.6
  61.0 0.1 broadcast_in_dim.15
  61.1 0.0 copy-start.4
  61.1 16.1 %all_to_all.18 = f32[16,136,128]{2,1,0:T(8,128)S(1)} all-to-all(f32[16,136,128]{2,1,0:T(8,128)S(1)} %broadcast_in_dim.15), channel_id=1, replica_groups={{0,4,34,38,64,68,98,102,130,134,160,164,194,198,224,228},{2,6,32,36,66,..., dimensions={0} | all-to-all | bytes 2228224 | tf_op jit(solution)/shard_map/all_to_all | solution.py:370
  77.2 0.1 cut.1
  77.3 3.0 %collective-permute-start.16 = (f32[512,128]{1,0:T(8,128)S(1)}, f32[512,128]{1,0:T(8,128)S(1)}, u32[]{:S(2)}, u32[]{:S(2)}) collective-permute-start(f32[512,128]{1,0:T(8,128)S(1)} %get-tuple-element.38), channel_id=1, source_target_pairs={{0,2},{2,0},{4,6},{6,4},{1,3},{3,1},{5,7},{7,5},{8,10},{10,8},{12,... | collective-permute-start | bytes 786440 | tf_op jit(solution)/shard_map/ppermute | solution.py:378
  80.3 0.4 collective-permute-start.17
  80.7 1.1 %collective-permute-start.13 = (f32[640,128]{1,0:T(8,128)S(1)}, f32[640,128]{1,0:T(8,128)S(1)}, u32[]{:S(2)}, u32[]{:S(2)}) collective-permute-start(f32[640,128]{1,0:T(8,128)S(1)} %get-tuple-element.33), channel_id=1, source_target_pairs={{0,128},{128,0},{1,129},{129,1},{2,130},{130,2},{3,131},{131,3},{4... | collective-permute-start | bytes 983048 | tf_op jit(solution)/shard_map/ppermute | solution.py:378
  81.8 0.9 collective-permute-start.14
  82.7 0.5 collective-permute-start.15
  83.2 1.7 %collective-permute-done.17.from_1 = f32[384,128]{1,0:T(8,128)S(1)} collective-permute-done((f32[384,128]{1,0:T(8,128)S(1)}, f32[384,128]{1,0:T(8,128)S(1)}, u32[]{:S(2)}, u32[]{:S(2)}) %collective-permute-start.17) | collective-permute-done | bytes 196640 | tf_op jit(solution)/shard_map/ppermute | solution.py:378
  84.9 0.0 collective-permute-done.16.from_0
  84.9 2.5 %natural.1 = (f32[896,256]{1,0:T(8,128)S(1)}, f32[1,128]{1,0:T(1,128)S(1)}) custom-call(f32[2176,128]{1,0:T(8,128)S(1)} %bitcast.13, f32[512,128]{1,0:T(8,128)S(1)} %collective-permute-done.16.from_0, f32[384,128]{1,0:T(8,128)S(1)} %collective-permute-done.17.from_1, f32[896,896]{1,0:T(8,128)S(1)} %bitcast.20, f32[256,256]{1,0:T(8,128)S(1)} %bitcast.21), custom_call_target="tpu_custom_call" | custom-call | flops 1500000000 | bytes 5000000 | tf_op jit(solution)/shard_map/natural/pallas_call | solution.py:449
  87.4 6.7 %collective-permute-start.18 = (f32[1,128]{1,0:T(1,128)S(1)}, f32[1,128]{1,0:T(1,128)S(1)}, u32[]{:S(2)}, u32[]{:S(2)}) collective-permute-start(f32[1,128]{1,0:T(1,128)S(1)} %get-tuple-element.41.curvature), channel_id=1, source_target_pairs={{0,1},{1,0},{2,3},{3,2},{4,5},{5,4},{6,7},{7,6},{8,9},{9,8},{10,11... | collective-permute-start | bytes 1544 | tf_op jit(solution)/shard_map/ppermute | solution.py:458
  94.1 0.0 collective-permute-done.15.from_4
  94.1 0.0 collective-permute-done.14.from_3
  94.1 0.0 collective-permute-done.13.from_2
  94.1 2.0 %unpack.1 = (f32[896,896]{1,0:T(8,128)}, f32[256,256]{1,0:T(8,128)}, f32[1,128]{1,0:T(1,128)S(1)}) custom-call(f32[2176,128]{1,0:T(8,128)S(1)} %bitcast.14, f32[640,128]{1,0:T(8,128)S(1)} %collective-permute-done.13.from_2, f32[384,128]{1,0:T(8,128)S(1)} %collective-permute-done.14.from_3, f32[256,128]{1,0:T(8,128)S(1)} %collective-permute-done.15.from_4), custom_call_target="tpu_custom_call" | custom-call | flops 10000000 | bytes 6000000 | tf_op jit(solution)/shard_map/unpack/pallas_call | solution.py:459
  96.0 0.0 collective-permute-done.18.other
  96.1 1.1 %scale.1 = f32[896,256]{1,0:T(8,128)} custom-call(f32[896,256]{1,0:T(8,128)S(1)} %get-tuple-element.40.natural, f32[1,128]{1,0:T(1,128)S(1)} %get-tuple-element.41.curvature, f32[1,128]{1,0:T(1,128)S(1)} %collective-permute-done.18.other, f32[1,128]{1,0:T(1,128)S(1)} %get-tuple-element.42.after), custom_call_target="tpu_custom_call" | custom-call | flops 1000000 | bytes 2000000 | tf_op jit(solution)/shard_map/scale/pallas_call | solution.py:470
  (5 shorter events, 0.0 us)
Async XLA Ops:
  0.6 8.2 %copy-start.1 = (bf16[1,2,16,32,128]{4,3,2,1,0:T(8,128)(2,1)S(1)}, bf16[1,2,16,32,128]{4,3,2,1,0:T(8,128)(2,1)}, u32[]{:S(2)}) copy-start(bf16[1,2,16,32,128]{4,3,2,1,0:T(8,128)(2,1)} %param.10) | copy-start | bytes 786436
  0.6 8.2 %copy-start = (bf16[1,16,32,256]{3,2,1,0:T(8,128)(2,1)S(1)}, bf16[1,16,32,256]{3,2,1,0:T(8,128)(2,1)}, u32[]{:S(2)}) copy-start(bf16[1,16,32,256]{3,2,1,0:T(8,128)(2,1)} %param.8) | copy-start | bytes 786436
  0.7 5.6 %copy-start.2 = (bf16[1,16,32,256]{3,2,1,0:T(8,128)(2,1)S(1)}, bf16[1,16,32,256]{3,2,1,0:T(8,128)(2,1)}, u32[]{:S(2)}) copy-start(bf16[1,16,32,256]{3,2,1,0:T(8,128)(2,1)} %param.9) | copy-start | bytes 786436
  0.7 6.2 %copy-start.3 = (f32[1,16]{1,0:T(1,128)S(1)}, f32[1,16]{1,0:T(1,128)}, u32[]{:S(2)}) copy-start(f32[1,16]{1,0:T(1,128)} %near.1) | copy-start | bytes 196
  0.7 8.2 %copy-start.5 = (bf16[2,896,256]{2,1,0:T(8,128)(2,1)S(1)}, bf16[2,896,256]{2,1,0:T(8,128)(2,1)}, u32[]{:S(2)}) copy-start(bf16[2,896,256]{2,1,0:T(8,128)(2,1)} %weights.3) | copy-start | bytes 2752516
  1.8 7.0 %collective-permute-start.1 = (f32[2,512,128]{2,1,0:T(8,128)S(1)}, f32[2,512,128]{2,1,0:T(8,128)S(1)}, u32[]{:S(2)}, u32[]{:S(2)}) collective-permute-start(f32[2,512,128]{2,1,0:T(8,128)S(1)} %convert_element_type.10), channel_id=1, source_target_pairs={{0,1},{1,0},{2,3},{3,2},{4,5},{5,4},{6,7},{7,6},{8,9},{9,8},{10,11... | collective-permute-start | bytes 1572872 | tf_op jit(solution)/shard_map/ppermute | solution.py:392
  6.1 2.7 %collective-permute-start = (f32[512,256]{1,0:T(8,128)S(1)}, f32[512,256]{1,0:T(8,128)S(1)}, u32[]{:S(2)}, u32[]{:S(2)}) collective-permute-start(f32[512,256]{1,0:T(8,128)S(1)} %bitcast_convert_fusion.1), channel_id=1, source_target_pairs={{0,1},{1,0},{2,3},{3,2},{4,5},{5,4},{6,7},{7,6},{8,9},{9,8},{10,11... | collective-permute-start | bytes 1572872 | tf_op jit(solution)/shard_map/ppermute | solution.py:391
  6.3 8.2 %collective-permute-start.2 = (f32[512,256]{1,0:T(8,128)S(1)}, f32[512,256]{1,0:T(8,128)S(1)}, u32[]{:S(2)}, u32[]{:S(2)}) collective-permute-start(f32[512,256]{1,0:T(8,128)S(1)} %bitcast_convert_fusion), channel_id=1, source_target_pairs={{0,1},{1,0},{2,3},{3,2},{4,5},{5,4},{6,7},{7,6},{8,9},{9,8},{10,11... | collective-permute-start | bytes 1572872 | tf_op jit(solution)/shard_map/ppermute | solution.py:394
  6.9 3.4 %collective-permute-start.3 = (f32[1,16]{1,0:T(1,128)S(1)}, f32[1,16]{1,0:T(1,128)S(1)}, u32[]{:S(2)}, u32[]{:S(2)}) collective-permute-start(f32[1,16]{1,0:T(1,128)S(1)} %copy-done.3), channel_id=1, source_target_pairs={{0,8},{8,0},{16,24},{24,16},{1,9},{9,1},{17,25},{25,17},{2,10},{10... | collective-permute-start | bytes 200 | tf_op jit(solution)/shard_map/ppermute | solution.py:393
  10.2 7.5 %collective-permute-start.4 = (f32[1,16]{1,0:T(1,128)S(1)}, f32[1,16]{1,0:T(1,128)S(1)}, u32[]{:S(2)}, u32[]{:S(2)}) collective-permute-start(f32[1,16]{1,0:T(1,128)S(1)} %pair.1.near), channel_id=1, source_target_pairs={{8,16},{16,8},{24,0},{0,24},{9,17},{17,9},{25,1},{1,25},{10,18},{1... | collective-permute-start | bytes 200 | tf_op jit(solution)/shard_map/ppermute | solution.py:406
  17.9 12.7 %collective-permute-start.5 = (f32[904,128]{1,0:T(8,128)S(1)}, f32[904,128]{1,0:T(8,128)S(1)}, u32[]{:S(2)}, u32[]{:S(2)}) collective-permute-start(f32[904,128]{1,0:T(8,128)S(1)} %get-tuple-element.28), channel_id=1, source_target_pairs={{0,2},{2,0},{4,6},{6,4},{1,3},{3,1},{5,7},{7,5},{8,10},{10,8},{12,... | collective-permute-start | bytes 1388552 | tf_op jit(solution)/shard_map/ppermute | solution.py:432
  19.2 11.4 %collective-permute-start.6 = (f32[776,128]{1,0:T(8,128)S(1)}, f32[776,128]{1,0:T(8,128)S(1)}, u32[]{:S(2)}, u32[]{:S(2)}) collective-permute-start(f32[776,128]{1,0:T(8,128)S(1)} %get-tuple-element.29), channel_id=1, source_target_pairs={{2,4},{4,2},{6,0},{0,6},{3,5},{5,3},{7,1},{1,7},{10,12},{12,10},{1... | collective-permute-start | bytes 1191944 | tf_op jit(solution)/shard_map/ppermute | solution.py:433
  21.0 9.6 %collective-permute-start.7 = (f32[768,128]{1,0:T(8,128)S(1)}, f32[768,128]{1,0:T(8,128)S(1)}, u32[]{:S(2)}, u32[]{:S(2)}) collective-permute-start(f32[768,128]{1,0:T(8,128)S(1)} %get-tuple-element.30), channel_id=1, source_target_pairs={{0,32},{32,0},{64,96},{96,64},{1,33},{33,1},{65,97},{97,65},{2,34}... | collective-permute-start | bytes 1179656 | tf_op jit(solution)/shard_map/ppermute | solution.py:434
  22.3 8.3 %collective-permute-start.8 = (f32[640,128]{1,0:T(8,128)S(1)}, f32[640,128]{1,0:T(8,128)S(1)}, u32[]{:S(2)}, u32[]{:S(2)}) collective-permute-start(f32[640,128]{1,0:T(8,128)S(1)} %get-tuple-element.31), channel_id=1, source_target_pairs={{0,128},{128,0},{1,129},{129,1},{2,130},{130,2},{3,131},{131,3},{4... | collective-permute-start | bytes 983048 | tf_op jit(solution)/shard_map/ppermute | solution.py:435
  23.0 7.6 %collective-permute-start.9 = (f32[8,128]{1,0:T(8,128)S(1)}, f32[8,128]{1,0:T(8,128)S(1)}, u32[]{:S(2)}, u32[]{:S(2)}) collective-permute-start(f32[8,128]{1,0:T(8,128)S(1)} %get-tuple-element.32.row_sum), channel_id=1, source_target_pairs={{0,4},{2,6},{4,0},{6,2},{1,5},{3,7},{5,1},{7,3},{8,12},{10,14},{12... | collective-permute-start | bytes 12296 | tf_op jit(solution)/shard_map/ppermute | solution.py:436
  51.3 7.6 %collective-permute-start.10 = (f32[136,128]{1,0:T(8,128)S(1)}, f32[136,128]{1,0:T(8,128)S(1)}, u32[]{:S(2)}, u32[]{:S(2)}) collective-permute-start(f32[136,128]{1,0:T(8,128)S(1)} %reduce_sum.9), channel_id=1, source_target_pairs={{0,16},{8,24},{16,0},{24,8},{1,17},{9,25},{17,1},{25,9},{2,18},{10... | collective-permute-start | bytes 208904 | tf_op jit(solution)/shard_map/ppermute | solution.py:442
  52.3 7.0 %collective-permute-start.11 = (f32[136,128]{1,0:T(8,128)S(1)}, f32[136,128]{1,0:T(8,128)S(1)}, u32[]{:S(2)}, u32[]{:S(2)}) collective-permute-start(f32[136,128]{1,0:T(8,128)S(1)} %reduce_sum.9), channel_id=1, source_target_pairs={{0,8},{8,16},{16,24},{24,0},{1,9},{9,17},{17,25},{25,1},{2,10},{10... | collective-permute-start | bytes 208904 | tf_op jit(solution)/shard_map/ppermute | solution.py:442
  53.4 7.6 %collective-permute-start.12 = (f32[136,128]{1,0:T(8,128)S(1)}, f32[136,128]{1,0:T(8,128)S(1)}, u32[]{:S(2)}, u32[]{:S(2)}) collective-permute-start(f32[136,128]{1,0:T(8,128)S(1)} %reduce_sum.9), channel_id=1, source_target_pairs={{0,24},{8,0},{16,8},{24,16},{1,25},{9,1},{17,9},{25,17},{2,26},{10... | collective-permute-start | bytes 208904 | tf_op jit(solution)/shard_map/ppermute | solution.py:442
  61.0 23.9 %copy-start.6 = (f32[1,256,256]{2,1,0:T(8,128)S(1)}, f32[1,256,256]{2,1,0:T(8,128)}, u32[]{:S(2)}) copy-start(f32[1,256,256]{2,1,0:T(8,128)} %param.15) | copy-start | bytes 786436
  61.1 23.8 %copy-start.4 = (f32[1,896,896]{2,1,0:T(8,128)S(1)}, f32[1,896,896]{2,1,0:T(8,128)}, u32[]{:S(2)}) copy-start(f32[1,896,896]{2,1,0:T(8,128)} %param.14) | copy-start | bytes 9633796
  77.3 7.6 %collective-permute-start.16 = (f32[512,128]{1,0:T(8,128)S(1)}, f32[512,128]{1,0:T(8,128)S(1)}, u32[]{:S(2)}, u32[]{:S(2)}) collective-permute-start(f32[512,128]{1,0:T(8,128)S(1)} %get-tuple-element.38), channel_id=1, source_target_pairs={{0,2},{2,0},{4,6},{6,4},{1,3},{3,1},{5,7},{7,5},{8,10},{10,8},{12,... | collective-permute-start | bytes 786440 | tf_op jit(solution)/shard_map/ppermute | solution.py:378
  80.3 4.6 %collective-permute-start.17 = (f32[384,128]{1,0:T(8,128)S(1)}, f32[384,128]{1,0:T(8,128)S(1)}, u32[]{:S(2)}, u32[]{:S(2)}) collective-permute-start(f32[384,128]{1,0:T(8,128)S(1)} %get-tuple-element.39), channel_id=1, source_target_pairs={{0,32},{32,0},{64,96},{96,64},{1,33},{33,1},{65,97},{97,65},{2,34}... | collective-permute-start | bytes 589832 | tf_op jit(solution)/shard_map/ppermute | solution.py:378
  80.7 13.4 %collective-permute-start.13 = (f32[640,128]{1,0:T(8,128)S(1)}, f32[640,128]{1,0:T(8,128)S(1)}, u32[]{:S(2)}, u32[]{:S(2)}) collective-permute-start(f32[640,128]{1,0:T(8,128)S(1)} %get-tuple-element.33), channel_id=1, source_target_pairs={{0,128},{128,0},{1,129},{129,1},{2,130},{130,2},{3,131},{131,3},{4... | collective-permute-start | bytes 983048 | tf_op jit(solution)/shard_map/ppermute | solution.py:378
  81.8 12.3 %collective-permute-start.14 = (f32[384,128]{1,0:T(8,128)S(1)}, f32[384,128]{1,0:T(8,128)S(1)}, u32[]{:S(2)}, u32[]{:S(2)}) collective-permute-start(f32[384,128]{1,0:T(8,128)S(1)} %get-tuple-element.34), channel_id=1, source_target_pairs={{2,4},{4,2},{6,0},{0,6},{3,5},{5,3},{7,1},{1,7},{10,12},{12,10},{1... | collective-permute-start | bytes 589832 | tf_op jit(solution)/shard_map/ppermute | solution.py:378
  82.7 11.4 %collective-permute-start.15 = (f32[256,128]{1,0:T(8,128)S(1)}, f32[256,128]{1,0:T(8,128)S(1)}, u32[]{:S(2)}, u32[]{:S(2)}) collective-permute-start(f32[256,128]{1,0:T(8,128)S(1)} %get-tuple-element.35), channel_id=1, source_target_pairs={{32,64},{64,32},{96,0},{0,96},{33,65},{65,33},{97,1},{1,97},{34,66... | collective-permute-start | bytes 393224 | tf_op jit(solution)/shard_map/ppermute | solution.py:378
  87.4 8.7 %collective-permute-start.18 = (f32[1,128]{1,0:T(1,128)S(1)}, f32[1,128]{1,0:T(1,128)S(1)}, u32[]{:S(2)}, u32[]{:S(2)}) collective-permute-start(f32[1,128]{1,0:T(1,128)S(1)} %get-tuple-element.41.curvature), channel_id=1, source_target_pairs={{0,1},{1,0},{2,3},{3,2},{4,5},{5,4},{6,7},{7,6},{8,9},{9,8},{10,11... | collective-permute-start | bytes 1544 | tf_op jit(solution)/shard_map/ppermute | solution.py:458

commit v11 on v8

--- a/solution.py
+++ b/solution.py
@@ -192,8 +192,9 @@
         out[parity ^ 1, last + line : last + line + 1, :] = value
 
 
-def tie_kernel(out, out_0, near, far, to_0, to_1, to_2, to_3, row_sum):
-    zh_sum = jnp.sum(near[...] + far[...], axis=1, keepdims=True)
+def tie_kernel(out, out_0, own, one, two, three, to_0, to_1, to_2, to_3, row_sum):
+    four = (own[...] + two[...]) + (one[...] + three[...])
+    zh_sum = jnp.sum(four, axis=1, keepdims=True)
     row_sum[...] = jnp.broadcast_to(zh_sum, (8, B))
     grads = GRADS * B
     to_0[:grads, :] = out_0[1]
@@ -236,7 +237,7 @@
     return read
 
 
-def unpack_kernel(kept, from_2, from_3, from_4, a_out, s_out, a_v, s_v, sems):
+def unpack_kernel(kept, from_2, from_3, from_4, a_out, s_out, done, a_v, s_v, sems):
     row, col = square_iotas()
     read = reader(kept, (from_2, from_3, from_4), BACK_STREAMS[2:])
     lines = read(33, 8)
@@ -303,6 +304,7 @@
     send(a_v, a_out, 6, 7)
     for copy in copies:
         copy.wait()
+    done[...] = inverse
 
 
 def natural_kernel(kept, from_0, from_1, a_inverse, s_inverse, natural, curvature):
@@ -325,17 +327,17 @@
     curvature[...] = jnp.broadcast_to(jnp.sum(total, axis=1, keepdims=True), (1, B))
 
 
-def scale_kernel(natural, curvature, other, direction):
+def scale_kernel(natural, curvature, other, after, direction):
     total = curvature[:, :1] + other[:, :1]
     direction[...] = natural[...] * lax.rsqrt(total * (1.0 / ENTRIES))
 
 
-def call(kernel, out_shapes, in_spaces, limit_mib, name, scratch=(), flops=0, moved=0, out_space=pltpu.VMEM):
+def call(kernel, out_shapes, in_spaces, limit_mib, name, scratch=(), flops=0, moved=0, out_spaces=None):
     return pl.pallas_call(
         kernel,
         out_shape=tuple(jax.ShapeDtypeStruct(shape, dtype) for shape, dtype in out_shapes),
         in_specs=[pl.BlockSpec(memory_space=space) for space in in_spaces],
-        out_specs=tuple(pl.BlockSpec(memory_space=out_space) for _ in out_shapes),
+        out_specs=tuple(pl.BlockSpec(memory_space=space) for space in out_spaces or [V] * len(out_shapes)),
         scratch_shapes=scratch,
         compiler_params=pltpu.CompilerParams(vmem_limit_bytes=limit_mib * 1024 * 1024),
         cost_estimate=pl.CostEstimate(flops=flops, bytes_accessed=moved, transcendentals=0),
@@ -370,6 +372,10 @@
     return [lax.ppermute(part, axis, pairs) for part, (axis, pairs) in zip(parts, ways)]
 
 
+def turned(value):
+    return [lax.ppermute(value, "zh", [(i, (i + k) % 4) for i in range(4)]) for k in (1, 2, 3)]
+
+
 def streams_of(streams):
     return [(((end - first) * B, B), F32) for first, end in streams]
 
@@ -380,10 +386,9 @@
     pair = pair_means.reshape(2, HALF, PAIR)
     swap = [(0, 1), (1, 0)]
 
-    sum_2 = energies + lax.ppermute(energies, "zh", LOW)
     other = lax.ppermute(jnp.concatenate([feat, psi], 1).astype(F32), "c", swap)
     oth_pair = lax.ppermute(pair.astype(F32), "c", swap)
-    far_2 = lax.ppermute(sum_2, "zh", HIGH)
+    row = turned(energies)
 
     grads = GRADS * B
     out, out_0 = call(
@@ -407,11 +412,11 @@
     to_0, to_1, to_2, to_3, row_sum = call(
         tie_kernel,
         [((grads + 8, B), F32), ((sizes[0][0] + 8, B), F32), (sizes[1], F32), (sizes[2], F32), ((8, B), F32)],
-        [V] * 4,
+        [V] * 6,
         8,
         "tie",
         moved=3_000_000,
-    )(out, out_0, sum_2, far_2)
+    )(out, out_0, energies, *row)
     from_0 = lax.ppermute(to_0, "x", LOW)
     from_1 = lax.ppermute(to_1, "x", HIGH)
     from_2 = lax.ppermute(to_2, "y", LOW)
@@ -421,9 +426,7 @@
         out, out_0, from_0, from_1, from_2, from_3, row_sum, row_two
     )
     mine = jnp.sum(same_parity(total).reshape(GROUP, CHUNK, B), axis=0)
-    one, two, three = (
-        lax.ppermute(mine, "zh", [(i, (i + k) % 4) for i in range(4)]) for k in (1, 2, 3)
-    )
+    one, two, three = turned(mine)
     mine = (mine + two) + (one + three)
     kept = same_parity(jnp.broadcast_to(mine[None], (GROUP, CHUNK, B)).reshape(KEPT, B))
     parts = call(cut_kernel, streams_of(BACK_STREAMS), [V], 6, "cut", moved=2_200_000)(kept)
@@ -439,20 +442,20 @@
         moved=5_000_000,
     )(kept, *parts[:2], a_inverse[0], s_inverse[0])
     other = lax.ppermute(curvature, "c", swap)
-    a_sum, s_sum = call(
+    a_sum, s_sum, done = call(
         unpack_kernel,
-        [((DIN, DIN), F32), ((D, D), F32)],
+        [((DIN, DIN), F32), ((D, D), F32), ((1, B), F32)],
         [V] * 4,
         14,
         "unpack",
         scratch=[pltpu.VMEM((DIN, DIN), F32), pltpu.VMEM((D, D), F32), pltpu.SemaphoreType.DMA((5,))],
-        out_space=pl.ANY,
+        out_spaces=(pl.ANY, pl.ANY, V),
         flops=10_000_000,
         moved=6_000_000,
     )(kept, *parts[2:])
     (direction,) = call(
-        scale_kernel, [((DIN, D), F32)], [V] * 3, 6, "scale", flops=1_000_000, moved=2_000_000
-    )(natural, curvature, other)
+        scale_kernel, [((DIN, D), F32)], [V] * 4, 6, "scale", flops=1_000_000, moved=2_000_000
+    )(natural, curvature, other, done)
     return a_sum[None], s_sum[None], direction[None]
 
 

time: 101 us -> 102 us (level)
  waiting for transfers between devices: 17.3 us -> 13.8 us
  blocking collectives: 38.2 us -> 41.2 us
  starting transfers between devices: 31.2 us -> 33.4 us
    ppermute x5 -> x6, starting transfers between devices: 10.2 us -> 14.4 us  [turned(): lax.ppermute(value, 'zh', [(i, (i + k) % 4) for i in range(4)])]
    all_to_all x2, blocking collectives: 38.2 us -> 41.2 us  [same_parity(): lax.all_to_all(value, axes, 0, 0, axis_index_groups=parity_groups(), tile...]
    ppermute x5 -> x6, waiting for transfers between devices: 7.99 us -> 5.8 us  [turned(): lax.ppermute(value, 'zh', [(i, (i + k) % 4) for i in range(4)])]
    ppermute x1, starting transfers between devices: 7.21 us -> 5.35 us  [body(): other = lax.ppermute(curvature, 'c', swap)]
    ppermute x5, waiting for transfers between devices: 1.95 us -> 0.87 us  [to_neighbours(): lax.ppermute(part, axis, pairs)]
  transfers between devices with their start and end apart: 18 -> 19, of which waited for: 7 -> 4; matrix products, arithmetic and copies ran while one was open for 0% -> 0% of each run, Pallas kernels for 8% -> 9%
where the time goes in v11:
time: 102 us
  blocking collectives  41.2 us (40%)
  starting transfers between devices  33.4 us (33%)
  waiting for transfers between devices  13.8 us (14%)
  Pallas kernels  10.6 us (10%)
  between operations  1.5 us (1%)
  other arithmetic  1.38 us (1%)
    all_to_all x2, blocking collectives, same_parity(): lax.all_to_all(value, axes, 0, 0, axis_index_groups=parity_groups(), tile...  41.2 us
    ppermute x6, starting transfers between devices, turned(): lax.ppermute(value, 'zh', [(i, (i + k) % 4) for i in range(4)])  14.4 us
    ppermute x1, waiting for transfers between devices, body(): row_two = lax.ppermute(row_sum, 'x', [(0, 2), (1, 3), (2, 0), (3, 1)])  7.16 us
    ppermute x6, waiting for transfers between devices, turned(): lax.ppermute(value, 'zh', [(i, (i + k) % 4) for i in range(4)])  5.8 us
    ppermute x1, starting transfers between devices, body(): other = lax.ppermute(curvature, 'c', swap)  5.35 us
    pallas_call x1, Pallas kernels, body(): call(factors_kernel, [((2, KEPT, B), F32), ((2, grads, B), F32)], [V] * 7...  4.73 us
    ppermute x5, starting transfers between devices, to_neighbours(): lax.ppermute(part, axis, pairs)  4.44 us
    ppermute x1, starting transfers between devices, body(): other = lax.ppermute(jnp.concatenate([feat, psi], 1).astype(F32), 'c', swap)  3.33 us
  transfers between devices with their start and end apart: 19, of which 4 were waited for; matrix products, arithmetic and copies ran while one was open for 0% of the time, Pallas kernels for 9%

profile of v11, /device:TPU:1, one launch (start us, length us, event | category | flops | bytes accessed | tf_op | source)
XLA Modules:
  0.0 102.1 jit_solution(13068167269391026703)
XLA Ops:
  0.6 0.0 copy-start
  0.6 0.0 copy-start.3
  0.7 0.0 copy-start.1
  0.7 0.0 copy-start.2
  0.7 0.0 copy-start.5
  0.7 1.3 %maximum_convert_fusion = f32[512,512]{1,0:T(8,128)S(1)} fusion(bf16[512,256]{1,0:T(8,128)(2,1)} %bitcast.18, bf16[512,256]{1,0:T(8,128)(2,1)} %bitcast.16), kind=kLoop, calls=%fused_computation | loop fusion | flops 1048576 | bytes 1572864 | tf_op jit(solution)/shard_map/convert_element_type | solution.py:389
  2.0 3.3 %collective-permute-start = (f32[512,512]{1,0:T(8,128)S(1)}, f32[512,512]{1,0:T(8,128)S(1)}, u32[]{:S(2)}, u32[]{:S(2)}) collective-permute-start(f32[512,512]{1,0:T(8,128)S(1)} %maximum_convert_fusion), channel_id=1, source_target_pairs={{0,1},{1,0},{2,3},{3,2},{4,5},{5,4},{6,7},{7,6},{8,9},{9,8},{10,11... | collective-permute-start | bytes 3145736 | tf_op jit(solution)/shard_map/ppermute | solution.py:389
  5.3 0.0 copy-done
  5.3 0.1 collective-permute-start.1
  5.4 0.0 copy-done.3
  5.4 1.3 %collective-permute-start.2 = (f32[1,16]{1,0:T(1,128)S(1)}, f32[1,16]{1,0:T(1,128)S(1)}, u32[]{:S(2)}, u32[]{:S(2)}) collective-permute-start(f32[1,16]{1,0:T(1,128)S(1)} %copy-done.3), channel_id=1, source_target_pairs={{0,8},{8,16},{16,24},{24,0},{1,9},{9,17},{17,25},{25,1},{2,10},{10... | collective-permute-start | bytes 200 | tf_op jit(solution)/shard_map/ppermute | solution.py:376
  6.8 5.1 %collective-permute-start.3 = (f32[1,16]{1,0:T(1,128)S(1)}, f32[1,16]{1,0:T(1,128)S(1)}, u32[]{:S(2)}, u32[]{:S(2)}) collective-permute-start(f32[1,16]{1,0:T(1,128)S(1)} %copy-done.3), channel_id=1, source_target_pairs={{0,16},{8,24},{16,0},{24,8},{1,17},{9,25},{17,1},{25,9},{2,18},{10... | collective-permute-start | bytes 200 | tf_op jit(solution)/shard_map/ppermute | solution.py:376
  11.9 2.4 %collective-permute-start.4 = (f32[1,16]{1,0:T(1,128)S(1)}, f32[1,16]{1,0:T(1,128)S(1)}, u32[]{:S(2)}, u32[]{:S(2)}) collective-permute-start(f32[1,16]{1,0:T(1,128)S(1)} %copy-done.3), channel_id=1, source_target_pairs={{0,24},{8,0},{16,8},{24,16},{1,25},{9,1},{17,9},{25,17},{2,26},{10... | collective-permute-start | bytes 200 | tf_op jit(solution)/shard_map/ppermute | solution.py:376
  14.9 0.0 collective-permute-done.1.oth_pair
  14.9 0.0 collective-permute-done.other
  14.9 0.0 copy-done.1
  14.9 0.0 copy-done.2
  15.0 0.0 copy-done.5
  15.0 4.7 %factors.1 = (f32[2,2176,128]{2,1,0:T(8,128)S(1)}, f32[2,896,128]{2,1,0:T(8,128)S(1)}) custom-call(bf16[512,256]{1,0:T(8,128)(2,1)S(1)} %bitcast.17, bf16[2,512,128]{2,1,0:T(8,128)(2,1)S(1)} %bitcast.15, bf16[512,256]{1,0:T(8,128)(2,1)S(1)} %bitcast.19, f32[512,512]{1,0:T(8,128)S(1)} %collective-permute-done.other, ...), custom_call_target="tpu_custom_call" | custom-call | flops 2500000000 | bytes 8000000 | tf_op jit(solution)/shard_map/factors/pallas_call | solution.py:394
  19.7 0.0 collective-permute-done.2.one
  19.7 0.0 collective-permute-done.3.two
  19.7 0.0 collective-permute-done.4.three
  19.7 0.1 tie.1
  19.9 1.3 %collective-permute-start.5 = (f32[904,128]{1,0:T(8,128)S(1)}, f32[904,128]{1,0:T(8,128)S(1)}, u32[]{:S(2)}, u32[]{:S(2)}) collective-permute-start(f32[904,128]{1,0:T(8,128)S(1)} %get-tuple-element.22), channel_id=1, source_target_pairs={{0,2},{2,0},{4,6},{6,4},{1,3},{3,1},{5,7},{7,5},{8,10},{10,8},{12,... | collective-permute-start | bytes 1388552 | tf_op jit(solution)/shard_map/ppermute | solution.py:420
  21.1 1.8 %collective-permute-start.6 = (f32[776,128]{1,0:T(8,128)S(1)}, f32[776,128]{1,0:T(8,128)S(1)}, u32[]{:S(2)}, u32[]{:S(2)}) collective-permute-start(f32[776,128]{1,0:T(8,128)S(1)} %get-tuple-element.23), channel_id=1, source_target_pairs={{2,4},{4,2},{6,0},{0,6},{3,5},{5,3},{7,1},{1,7},{10,12},{12,10},{1... | collective-permute-start | bytes 1191944 | tf_op jit(solution)/shard_map/ppermute | solution.py:421
  23.0 1.3 %collective-permute-start.7 = (f32[768,128]{1,0:T(8,128)S(1)}, f32[768,128]{1,0:T(8,128)S(1)}, u32[]{:S(2)}, u32[]{:S(2)}) collective-permute-start(f32[768,128]{1,0:T(8,128)S(1)} %get-tuple-element.24), channel_id=1, source_target_pairs={{0,32},{32,0},{64,96},{96,64},{1,33},{33,1},{65,97},{97,65},{2,34}... | collective-permute-start | bytes 1179656 | tf_op jit(solution)/shard_map/ppermute | solution.py:422
  24.3 0.7 collective-permute-start.8
  25.0 0.6 collective-permute-start.9
  25.6 7.2 %collective-permute-done.9.row_two = f32[8,128]{1,0:T(8,128)S(1)} collective-permute-done((f32[8,128]{1,0:T(8,128)S(1)}, f32[8,128]{1,0:T(8,128)S(1)}, u32[]{:S(2)}, u32[]{:S(2)}) %collective-permute-start.9) | collective-permute-done | bytes 4128 | tf_op jit(solution)/shard_map/ppermute | solution.py:424
  32.8 0.0 collective-permute-done.8.from_3
  32.8 0.0 collective-permute-done.7.from_2
  32.8 0.0 collective-permute-done.6.from_1
  32.8 0.0 collective-permute-done.5.from_0
  32.8 0.2 add.16
  33.0 20.9 %all_to_all.17 = f32[16,136,128]{2,1,0:T(8,128)S(1)} all-to-all(f32[16,136,128]{2,1,0:T(8,128)S(1)} %bitcast.13), channel_id=1, replica_groups={{0,4,34,38,64,68,98,102,130,134,160,164,194,198,224,228},{2,6,32,36,66,..., dimensions={0} | all-to-all | bytes 2228224 | tf_op jit(solution)/shard_map/all_to_all | solution.py:364
  53.9 0.1 reduce_sum.9
  54.0 0.1 collective-permute-start.11
  54.1 3.6 %collective-permute-start.12 = (f32[136,128]{1,0:T(8,128)S(1)}, f32[136,128]{1,0:T(8,128)S(1)}, u32[]{:S(2)}, u32[]{:S(2)}) collective-permute-start(f32[136,128]{1,0:T(8,128)S(1)} %reduce_sum.9), channel_id=1, source_target_pairs={{0,24},{8,0},{16,8},{24,16},{1,25},{9,1},{17,9},{25,17},{2,26},{10... | collective-permute-start | bytes 208904 | tf_op jit(solution)/shard_map/ppermute | solution.py:376
  57.6 1.9 %collective-permute-start.10 = (f32[136,128]{1,0:T(8,128)S(1)}, f32[136,128]{1,0:T(8,128)S(1)}, u32[]{:S(2)}, u32[]{:S(2)}) collective-permute-start(f32[136,128]{1,0:T(8,128)S(1)} %reduce_sum.9), channel_id=1, source_target_pairs={{0,16},{8,24},{16,0},{24,8},{1,17},{9,25},{17,1},{25,9},{2,18},{10... | collective-permute-start | bytes 208904 | tf_op jit(solution)/shard_map/ppermute | solution.py:376
  59.6 0.0 collective-permute-done.11
  59.6 0.1 collective-permute-done.12
  59.6 5.7 %collective-permute-done.10 = f32[136,128]{1,0:T(8,128)S(1)} collective-permute-done((f32[136,128]{1,0:T(8,128)S(1)}, f32[136,128]{1,0:T(8,128)S(1)}, u32[]{:S(2)}, u32[]{:S(2)}) %collective-permute-start.10) | collective-permute-done | bytes 69664 | tf_op jit(solution)/shard_map/ppermute | solution.py:376
  65.4 0.0 copy-start.6
  65.4 0.1 broadcast_in_dim.15
  65.5 0.0 copy-start.4
  65.5 20.3 %all_to_all.18 = f32[16,136,128]{2,1,0:T(8,128)S(1)} all-to-all(f32[16,136,128]{2,1,0:T(8,128)S(1)} %broadcast_in_dim.15), channel_id=1, replica_groups={{0,4,34,38,64,68,98,102,130,134,160,164,194,198,224,228},{2,6,32,36,66,..., dimensions={0} | all-to-all | bytes 2228224 | tf_op jit(solution)/shard_map/all_to_all | solution.py:364
  85.8 0.1 cut.1
  85.9 0.1 collective-permute-start.16
  86.0 0.3 collective-permute-start.17
  86.3 1.9 %collective-permute-start.13 = (f32[640,128]{1,0:T(8,128)S(1)}, f32[640,128]{1,0:T(8,128)S(1)}, u32[]{:S(2)}, u32[]{:S(2)}) collective-permute-start(f32[640,128]{1,0:T(8,128)S(1)} %get-tuple-element.27), channel_id=1, source_target_pairs={{0,128},{128,0},{1,129},{129,1},{2,130},{130,2},{3,131},{131,3},{4... | collective-permute-start | bytes 983048 | tf_op jit(solution)/shard_map/ppermute | solution.py:372
  88.2 0.5 collective-permute-start.14
  88.7 1.6 %collective-permute-start.15 = (f32[256,128]{1,0:T(8,128)S(1)}, f32[256,128]{1,0:T(8,128)S(1)}, u32[]{:S(2)}, u32[]{:S(2)}) collective-permute-start(f32[256,128]{1,0:T(8,128)S(1)} %get-tuple-element.29), channel_id=1, source_target_pairs={{32,64},{64,32},{96,0},{0,96},{33,65},{65,33},{97,1},{1,97},{34,66... | collective-permute-start | bytes 393224 | tf_op jit(solution)/shard_map/ppermute | solution.py:372
  90.3 0.3 collective-permute-done.17.from_1
  90.6 0.6 collective-permute-done.16.from_0
  91.2 0.0 copy-done.6
  91.2 0.0 copy-done.4
  91.2 2.5 %natural.1 = (f32[896,256]{1,0:T(8,128)S(1)}, f32[1,128]{1,0:T(1,128)S(1)}) custom-call(f32[2176,128]{1,0:T(8,128)S(1)} %bitcast.11, f32[512,128]{1,0:T(8,128)S(1)} %collective-permute-done.16.from_0, f32[384,128]{1,0:T(8,128)S(1)} %collective-permute-done.17.from_1, f32[896,896]{1,0:T(8,128)S(1)} %bitcast.20, f32[256,256]{1,0:T(8,128)S(1)} %bitcast.21), custom_call_target="tpu_custom_call" | custom-call | flops 1500000000 | bytes 5000000 | tf_op jit(solution)/shard_map/natural/pallas_call | solution.py:435
  93.7 5.3 %collective-permute-start.18 = (f32[1,128]{1,0:T(1,128)S(1)}, f32[1,128]{1,0:T(1,128)S(1)}, u32[]{:S(2)}, u32[]{:S(2)}) collective-permute-start(f32[1,128]{1,0:T(1,128)S(1)} %get-tuple-element.35.curvature), channel_id=1, source_target_pairs={{0,1},{1,0},{2,3},{3,2},{4,5},{5,4},{6,7},{7,6},{8,9},{9,8},{10,11... | collective-permute-start | bytes 1544 | tf_op jit(solution)/shard_map/ppermute | solution.py:444
  99.0 0.0 collective-permute-done.15.from_4
  99.0 0.0 collective-permute-done.14.from_3
  99.0 0.0 collective-permute-done.13.from_2
  99.0 2.0 %unpack.1 = (f32[896,896]{1,0:T(8,128)}, f32[256,256]{1,0:T(8,128)}, f32[1,128]{1,0:T(1,128)S(1)}) custom-call(f32[2176,128]{1,0:T(8,128)S(1)} %bitcast.12, f32[640,128]{1,0:T(8,128)S(1)} %collective-permute-done.13.from_2, f32[384,128]{1,0:T(8,128)S(1)} %collective-permute-done.14.from_3, f32[256,128]{1,0:T(8,128)S(1)} %collective-permute-done.15.from_4), custom_call_target="tpu_custom_call" | custom-call | flops 10000000 | bytes 6000000 | tf_op jit(solution)/shard_map/unpack/pallas_call | solution.py:445
  101.0 0.0 collective-permute-done.18.other
  101.0 1.1 %scale.1 = f32[896,256]{1,0:T(8,128)} custom-call(f32[896,256]{1,0:T(8,128)S(1)} %get-tuple-element.34.natural, f32[1,128]{1,0:T(1,128)S(1)} %get-tuple-element.35.curvature, f32[1,128]{1,0:T(1,128)S(1)} %collective-permute-done.18.other, f32[1,128]{1,0:T(1,128)S(1)} %get-tuple-element.36.after), custom_call_target="tpu_custom_call" | custom-call | flops 1000000 | bytes 2000000 | tf_op jit(solution)/shard_map/scale/pallas_call | solution.py:456
  (2 shorter events, 0.1 us)
Async XLA Ops:
  0.6 4.7 %copy-start = (bf16[1,2,16,32,128]{4,3,2,1,0:T(8,128)(2,1)S(1)}, bf16[1,2,16,32,128]{4,3,2,1,0:T(8,128)(2,1)}, u32[]{:S(2)}) copy-start(bf16[1,2,16,32,128]{4,3,2,1,0:T(8,128)(2,1)} %param.10) | copy-start | bytes 786436
  0.6 4.8 %copy-start.3 = (f32[1,16]{1,0:T(1,128)S(1)}, f32[1,16]{1,0:T(1,128)}, u32[]{:S(2)}) copy-start(f32[1,16]{1,0:T(1,128)} %own.1) | copy-start | bytes 196
  0.7 14.3 %copy-start.1 = (bf16[1,16,32,256]{3,2,1,0:T(8,128)(2,1)S(1)}, bf16[1,16,32,256]{3,2,1,0:T(8,128)(2,1)}, u32[]{:S(2)}) copy-start(bf16[1,16,32,256]{3,2,1,0:T(8,128)(2,1)} %param.8) | copy-start | bytes 786436
  0.7 14.3 %copy-start.2 = (bf16[1,16,32,256]{3,2,1,0:T(8,128)(2,1)S(1)}, bf16[1,16,32,256]{3,2,1,0:T(8,128)(2,1)}, u32[]{:S(2)}) copy-start(bf16[1,16,32,256]{3,2,1,0:T(8,128)(2,1)} %param.9) | copy-start | bytes 786436
  0.7 14.3 %copy-start.5 = (bf16[2,896,256]{2,1,0:T(8,128)(2,1)S(1)}, bf16[2,896,256]{2,1,0:T(8,128)(2,1)}, u32[]{:S(2)}) copy-start(bf16[2,896,256]{2,1,0:T(8,128)(2,1)} %weights.1) | copy-start | bytes 2752516
  2.0 13.0 %collective-permute-start = (f32[512,512]{1,0:T(8,128)S(1)}, f32[512,512]{1,0:T(8,128)S(1)}, u32[]{:S(2)}, u32[]{:S(2)}) collective-permute-start(f32[512,512]{1,0:T(8,128)S(1)} %maximum_convert_fusion), channel_id=1, source_target_pairs={{0,1},{1,0},{2,3},{3,2},{4,5},{5,4},{6,7},{7,6},{8,9},{9,8},{10,11... | collective-permute-start | bytes 3145736 | tf_op jit(solution)/shard_map/ppermute | solution.py:389
  5.3 9.6 %collective-permute-start.1 = (f32[2,512,128]{2,1,0:T(8,128)S(1)}, f32[2,512,128]{2,1,0:T(8,128)S(1)}, u32[]{:S(2)}, u32[]{:S(2)}) collective-permute-start(f32[2,512,128]{2,1,0:T(8,128)S(1)} %convert_element_type.7), channel_id=1, source_target_pairs={{0,1},{1,0},{2,3},{3,2},{4,5},{5,4},{6,7},{7,6},{8,9},{9,8},{10,11... | collective-permute-start | bytes 1572872 | tf_op jit(solution)/shard_map/ppermute | solution.py:390
  5.4 14.3 %collective-permute-start.2 = (f32[1,16]{1,0:T(1,128)S(1)}, f32[1,16]{1,0:T(1,128)S(1)}, u32[]{:S(2)}, u32[]{:S(2)}) collective-permute-start(f32[1,16]{1,0:T(1,128)S(1)} %copy-done.3), channel_id=1, source_target_pairs={{0,8},{8,16},{16,24},{24,0},{1,9},{9,17},{17,25},{25,1},{2,10},{10... | collective-permute-start | bytes 200 | tf_op jit(solution)/shard_map/ppermute | solution.py:376
  6.8 12.9 %collective-permute-start.3 = (f32[1,16]{1,0:T(1,128)S(1)}, f32[1,16]{1,0:T(1,128)S(1)}, u32[]{:S(2)}, u32[]{:S(2)}) collective-permute-start(f32[1,16]{1,0:T(1,128)S(1)} %copy-done.3), channel_id=1, source_target_pairs={{0,16},{8,24},{16,0},{24,8},{1,17},{9,25},{17,1},{25,9},{2,18},{10... | collective-permute-start | bytes 200 | tf_op jit(solution)/shard_map/ppermute | solution.py:376
  11.9 7.8 %collective-permute-start.4 = (f32[1,16]{1,0:T(1,128)S(1)}, f32[1,16]{1,0:T(1,128)S(1)}, u32[]{:S(2)}, u32[]{:S(2)}) collective-permute-start(f32[1,16]{1,0:T(1,128)S(1)} %copy-done.3), channel_id=1, source_target_pairs={{0,24},{8,0},{16,8},{24,16},{1,25},{9,1},{17,9},{25,17},{2,26},{10... | collective-permute-start | bytes 200 | tf_op jit(solution)/shard_map/ppermute | solution.py:376
  19.9 13.0 %collective-permute-start.5 = (f32[904,128]{1,0:T(8,128)S(1)}, f32[904,128]{1,0:T(8,128)S(1)}, u32[]{:S(2)}, u32[]{:S(2)}) collective-permute-start(f32[904,128]{1,0:T(8,128)S(1)} %get-tuple-element.22), channel_id=1, source_target_pairs={{0,2},{2,0},{4,6},{6,4},{1,3},{3,1},{5,7},{7,5},{8,10},{10,8},{12,... | collective-permute-start | bytes 1388552 | tf_op jit(solution)/shard_map/ppermute | solution.py:420
  21.1 11.7 %collective-permute-start.6 = (f32[776,128]{1,0:T(8,128)S(1)}, f32[776,128]{1,0:T(8,128)S(1)}, u32[]{:S(2)}, u32[]{:S(2)}) collective-permute-start(f32[776,128]{1,0:T(8,128)S(1)} %get-tuple-element.23), channel_id=1, source_target_pairs={{2,4},{4,2},{6,0},{0,6},{3,5},{5,3},{7,1},{1,7},{10,12},{12,10},{1... | collective-permute-start | bytes 1191944 | tf_op jit(solution)/shard_map/ppermute | solution.py:421
  23.0 9.8 %collective-permute-start.7 = (f32[768,128]{1,0:T(8,128)S(1)}, f32[768,128]{1,0:T(8,128)S(1)}, u32[]{:S(2)}, u32[]{:S(2)}) collective-permute-start(f32[768,128]{1,0:T(8,128)S(1)} %get-tuple-element.24), channel_id=1, source_target_pairs={{0,32},{32,0},{64,96},{96,64},{1,33},{33,1},{65,97},{97,65},{2,34}... | collective-permute-start | bytes 1179656 | tf_op jit(solution)/shard_map/ppermute | solution.py:422
  24.3 8.5 %collective-permute-start.8 = (f32[640,128]{1,0:T(8,128)S(1)}, f32[640,128]{1,0:T(8,128)S(1)}, u32[]{:S(2)}, u32[]{:S(2)}) collective-permute-start(f32[640,128]{1,0:T(8,128)S(1)} %get-tuple-element.25), channel_id=1, source_target_pairs={{0,128},{128,0},{1,129},{129,1},{2,130},{130,2},{3,131},{131,3},{4... | collective-permute-start | bytes 983048 | tf_op jit(solution)/shard_map/ppermute | solution.py:423
  25.0 7.8 %collective-permute-start.9 = (f32[8,128]{1,0:T(8,128)S(1)}, f32[8,128]{1,0:T(8,128)S(1)}, u32[]{:S(2)}, u32[]{:S(2)}) collective-permute-start(f32[8,128]{1,0:T(8,128)S(1)} %get-tuple-element.26.row_sum), channel_id=1, source_target_pairs={{0,4},{2,6},{4,0},{6,2},{1,5},{3,7},{5,1},{7,3},{8,12},{10,14},{12... | collective-permute-start | bytes 12296 | tf_op jit(solution)/shard_map/ppermute | solution.py:424
  54.0 5.6 %collective-permute-start.11 = (f32[136,128]{1,0:T(8,128)S(1)}, f32[136,128]{1,0:T(8,128)S(1)}, u32[]{:S(2)}, u32[]{:S(2)}) collective-permute-start(f32[136,128]{1,0:T(8,128)S(1)} %reduce_sum.9), channel_id=1, source_target_pairs={{0,8},{8,16},{16,24},{24,0},{1,9},{9,17},{17,25},{25,1},{2,10},{10... | collective-permute-start | bytes 208904 | tf_op jit(solution)/shard_map/ppermute | solution.py:376
  54.1 5.6 %collective-permute-start.12 = (f32[136,128]{1,0:T(8,128)S(1)}, f32[136,128]{1,0:T(8,128)S(1)}, u32[]{:S(2)}, u32[]{:S(2)}) collective-permute-start(f32[136,128]{1,0:T(8,128)S(1)} %reduce_sum.9), channel_id=1, source_target_pairs={{0,24},{8,0},{16,8},{24,16},{1,25},{9,1},{17,9},{25,17},{2,26},{10... | collective-permute-start | bytes 208904 | tf_op jit(solution)/shard_map/ppermute | solution.py:376
  57.6 7.7 %collective-permute-start.10 = (f32[136,128]{1,0:T(8,128)S(1)}, f32[136,128]{1,0:T(8,128)S(1)}, u32[]{:S(2)}, u32[]{:S(2)}) collective-permute-start(f32[136,128]{1,0:T(8,128)S(1)} %reduce_sum.9), channel_id=1, source_target_pairs={{0,16},{8,24},{16,0},{24,8},{1,17},{9,25},{17,1},{25,9},{2,18},{10... | collective-permute-start | bytes 208904 | tf_op jit(solution)/shard_map/ppermute | solution.py:376
  65.4 25.8 %copy-start.6 = (f32[1,256,256]{2,1,0:T(8,128)S(1)}, f32[1,256,256]{2,1,0:T(8,128)}, u32[]{:S(2)}) copy-start(f32[1,256,256]{2,1,0:T(8,128)} %param.15) | copy-start | bytes 786436
  65.5 25.7 %copy-start.4 = (f32[1,896,896]{2,1,0:T(8,128)S(1)}, f32[1,896,896]{2,1,0:T(8,128)}, u32[]{:S(2)}) copy-start(f32[1,896,896]{2,1,0:T(8,128)} %param.14) | copy-start | bytes 9633796
  85.9 5.3 %collective-permute-start.16 = (f32[512,128]{1,0:T(8,128)S(1)}, f32[512,128]{1,0:T(8,128)S(1)}, u32[]{:S(2)}, u32[]{:S(2)}) collective-permute-start(f32[512,128]{1,0:T(8,128)S(1)} %get-tuple-element.32), channel_id=1, source_target_pairs={{0,2},{2,0},{4,6},{6,4},{1,3},{3,1},{5,7},{7,5},{8,10},{10,8},{12,... | collective-permute-start | bytes 786440 | tf_op jit(solution)/shard_map/ppermute | solution.py:372
  86.0 4.6 %collective-permute-start.17 = (f32[384,128]{1,0:T(8,128)S(1)}, f32[384,128]{1,0:T(8,128)S(1)}, u32[]{:S(2)}, u32[]{:S(2)}) collective-permute-start(f32[384,128]{1,0:T(8,128)S(1)} %get-tuple-element.33), channel_id=1, source_target_pairs={{0,32},{32,0},{64,96},{96,64},{1,33},{33,1},{65,97},{97,65},{2,34}... | collective-permute-start | bytes 589832 | tf_op jit(solution)/shard_map/ppermute | solution.py:372
  86.3 12.8 %collective-permute-start.13 = (f32[640,128]{1,0:T(8,128)S(1)}, f32[640,128]{1,0:T(8,128)S(1)}, u32[]{:S(2)}, u32[]{:S(2)}) collective-permute-start(f32[640,128]{1,0:T(8,128)S(1)} %get-tuple-element.27), channel_id=1, source_target_pairs={{0,128},{128,0},{1,129},{129,1},{2,130},{130,2},{3,131},{131,3},{4... | collective-permute-start | bytes 983048 | tf_op jit(solution)/shard_map/ppermute | solution.py:372
  88.2 10.9 %collective-permute-start.14 = (f32[384,128]{1,0:T(8,128)S(1)}, f32[384,128]{1,0:T(8,128)S(1)}, u32[]{:S(2)}, u32[]{:S(2)}) collective-permute-start(f32[384,128]{1,0:T(8,128)S(1)} %get-tuple-element.28), channel_id=1, source_target_pairs={{2,4},{4,2},{6,0},{0,6},{3,5},{5,3},{7,1},{1,7},{10,12},{12,10},{1... | collective-permute-start | bytes 589832 | tf_op jit(solution)/shard_map/ppermute | solution.py:372
  88.7 10.3 %collective-permute-start.15 = (f32[256,128]{1,0:T(8,128)S(1)}, f32[256,128]{1,0:T(8,128)S(1)}, u32[]{:S(2)}, u32[]{:S(2)}) collective-permute-start(f32[256,128]{1,0:T(8,128)S(1)} %get-tuple-element.29), channel_id=1, source_target_pairs={{32,64},{64,32},{96,0},{0,96},{33,65},{65,33},{97,1},{1,97},{34,66... | collective-permute-start | bytes 393224 | tf_op jit(solution)/shard_map/ppermute | solution.py:372
  93.7 7.3 %collective-permute-start.18 = (f32[1,128]{1,0:T(1,128)S(1)}, f32[1,128]{1,0:T(1,128)S(1)}, u32[]{:S(2)}, u32[]{:S(2)}) collective-permute-start(f32[1,128]{1,0:T(1,128)S(1)} %get-tuple-element.35.curvature), channel_id=1, source_target_pairs={{0,1},{1,0},{2,3},{3,2},{4,5},{5,4},{6,7},{7,6},{8,9},{9,8},{10,11... | collective-permute-start | bytes 1544 | tf_op jit(solution)/shard_map/ppermute | solution.py:444

commit v12 on v10

--- a/solution.py
+++ b/solution.py
@@ -14,8 +14,9 @@
 KEPT = SLOTS * B
 CHUNK = KEPT // GROUP
 GRADS, FACTORS = 7, 10
-OUT_STREAMS = ((0, 6), (6, 12), (12, 17))
-BACK_STREAMS = ((0, 4), (4, 7), (7, 12), (12, 15), (15, 17))
+OUT_STREAMS = ((0, 9), (9, 17))
+PLAIN_STREAMS = ((0, 4), (4, 7))
+BACK_STREAMS = ((0, 6), (6, 11), (11, 14), (14, 17))
 ENTRIES = 2 * DIN * D
 SHIFT = 7.0
 
@@ -202,30 +203,36 @@
 def tie_kernel(out, out_0, near, far, to_0, to_1, to_2, to_3, row_sum):
     zh_sum = jnp.sum(near[...] + far[...], axis=1, keepdims=True)
     row_sum[...] = jnp.broadcast_to(zh_sum, (8, B))
-    grads = GRADS * B
-    to_0[:grads, :] = out_0[1]
-    to_0[grads:, :] = row_sum[...]
-    for target, (first, end) in zip((to_1, to_2, to_3), OUT_STREAMS):
-        target[: (end - first) * B, :] = out[1, first * B : end * B, :]
-    to_1[OUT_STREAMS[0][1] * B :, :] = row_sum[...]
+    for target, (first, end) in zip((to_0, to_1), OUT_STREAMS):
+        target[...] = out[1, first * B : end * B, :]
+    for target, (first, end) in zip((to_2, to_3), PLAIN_STREAMS):
+        rows = (end - first) * B
+        target[:rows, :] = out_0[1, first * B : end * B, :]
+        target[rows:, :] = row_sum[...]
 
 
 def add_kernel(out, out_0, from_0, from_1, from_2, from_3, row_sum, row_two, total):
-    grads = GRADS * B
-    near, far = from_0[grads:, :], from_1[OUT_STREAMS[0][1] * B :, :]
-    energy = (row_sum[...] + row_two[...]) + (near + far)
+    energy = row_sum[...] + row_two[...]
+    near = [
+        part[(end - first) * B :, :] for part, (first, end) in zip((from_2, from_3), PLAIN_STREAMS)
+    ]
+    energy = energy + (near[0] + near[1])
     shifted = energy[:1, :] * (1.0 / 256.0) + SHIFT
-    for part, (first, end) in zip((from_1, from_2, from_3), OUT_STREAMS):
+    plain = [None] * GRADS
+    for part, (first, end) in zip((from_2, from_3), PLAIN_STREAMS):
+        for place in range(first, end):
+            plain[place] = part[(place - first) * B : (place - first + 1) * B, :]
+    for part, (first, end) in zip((from_0, from_1), OUT_STREAMS):
         for place in range(first, end):
             rows = slice(place * B, (place + 1) * B)
             value = out[0, rows, :] + part[(place - first) * B : (place - first + 1) * B, :]
             if place < GRADS:
-                value = value - shifted * (out_0[0, rows, :] + from_0[rows, :])
+                value = value - shifted * (out_0[0, rows, :] + plain[place])
             total[rows, :] = value
 
 
-def cut_kernel(kept, to_0, to_1, to_2, to_3, to_4):
-    for target, (first, end) in zip((to_0, to_1, to_2, to_3, to_4), BACK_STREAMS):
+def cut_kernel(kept, to_0, to_1, to_2, to_3):
+    for target, (first, end) in zip((to_0, to_1, to_2, to_3), BACK_STREAMS):
         target[...] = kept[first * B : end * B, :]
 
 
@@ -243,9 +250,9 @@
     return read
 
 
-def unpack_kernel(kept, from_2, from_3, from_4, a_out, s_out, done, a_v, s_v, sems):
+def unpack_kernel(kept, from_1, from_2, from_3, a_out, s_out, done, a_v, s_v, sems):
     row, col = square_iotas()
-    read = reader(kept, (from_2, from_3, from_4), BACK_STREAMS[2:])
+    read = reader(kept, (from_1, from_2, from_3), BACK_STREAMS[1:])
     lines = read(33, 8)
     inverse = 1.0 / lines[4:5, :]
     copies = []
@@ -373,9 +380,18 @@
 LOW, HIGH = [(0, 1), (1, 0), (2, 3), (3, 2)], [(1, 2), (2, 1), (3, 0), (0, 3)]
 
 
-def to_neighbours(parts):
-    ways = (("x", LOW), ("y", LOW), ("zl", [(0, 1), (1, 0)]), ("x", HIGH), ("y", HIGH))
-    return [lax.ppermute(part, axis, pairs) for part, (axis, pairs) in zip(parts, ways)]
+def over_y(part):
+    pairs = [(2 * a, 2 * b) for a, b in LOW] + [(2 * a + 1, 2 * b + 1) for a, b in HIGH]
+    return lax.ppermute(part, ("y", "c"), pairs)
+
+
+def over_z(part):
+    def index(z, c):
+        return (z % 2 * 4 + z // 2) * 2 + c
+
+    pairs = [(index(z, 0), index(z ^ 1, 0)) for z in range(8)]
+    pairs += [(index(z, 1), index((z + (1 if z % 2 else -1)) % 8, 1)) for z in range(8)]
+    return lax.ppermute(part, ("zl", "zh", "c"), pairs)
 
 
 def streams_of(streams):
@@ -420,19 +436,18 @@
         moved=8_000_000,
     )(x_s, d_s, m_s, psi, oth_psi, weights, energies, energies, multiplicity)
 
-    sizes = [((end - first) * B, B) for first, end in OUT_STREAMS]
+    sizes = [((end - first) * B + 8, B) for first, end in PLAIN_STREAMS]
     to_0, to_1, to_2, to_3, row_sum = call(
         tie_kernel,
-        [((grads + 8, B), F32), ((sizes[0][0] + 8, B), F32), (sizes[1], F32), (sizes[2], F32), ((8, B), F32)],
+        streams_of(OUT_STREAMS) + [(sizes[0], F32), (sizes[1], F32), ((8, B), F32)],
         [V] * 4,
         8,
         "tie",
         moved=3_000_000,
     )(out, out_0, sum_2, far_2)
-    from_0 = lax.ppermute(to_0, "x", LOW)
-    from_1 = lax.ppermute(to_1, "x", HIGH)
-    from_2 = lax.ppermute(to_2, "y", LOW)
-    from_3 = lax.ppermute(to_3, "zl", swap)
+    from_0, from_1 = over_y(to_0), over_z(to_1)
+    from_2 = lax.ppermute(to_2, "x", LOW)
+    from_3 = lax.ppermute(to_3, "x", HIGH)
     row_two = lax.ppermute(row_sum, "x", [(0, 2), (1, 3), (2, 0), (3, 1)])
     (total,) = call(add_kernel, [((KEPT, B), F32)], [V] * 8, 10, "add", moved=3_000_000)(
         out, out_0, from_0, from_1, from_2, from_3, row_sum, row_two
@@ -444,7 +459,7 @@
     mine = (mine + two) + (one + three)
     kept = same_parity(jnp.broadcast_to(mine[None], (GROUP, CHUNK, B)).reshape(KEPT, B))
     parts = call(cut_kernel, streams_of(BACK_STREAMS), [V], 6, "cut", moved=2_200_000)(kept)
-    parts = to_neighbours(parts)
+    parts = over_y(parts[0]), over_z(parts[1]), lax.ppermute(parts[2], "x", LOW), lax.ppermute(parts[3], "x", HIGH)
 
     natural, curvature = call(
         natural_kernel,
@@ -466,7 +481,7 @@
         out_spaces=(pl.ANY, pl.ANY, V),
         flops=10_000_000,
         moved=6_000_000,
-    )(kept, *parts[2:])
+    )(kept, *parts[1:])
     (direction,) = call(
         scale_kernel, [((DIN, D), F32)], [V] * 4, 6, "scale", flops=1_000_000, moved=2_000_000
     )(natural, curvature, other, done)

time: 97.3 us -> 100 us (1.028)
  blocking collectives: 36.5 us -> 40.1 us
  starting transfers between devices: 32.5 us -> 30.4 us
  waiting for transfers between devices: 13.7 us -> 15 us
    ppermute x1, starting transfers between devices: 6.67 us -> 2.52 us  [body(): other = lax.ppermute(curvature, 'c', swap)]
    all_to_all x2, blocking collectives: 36.5 us -> 40.1 us  [same_parity(): lax.all_to_all(value, axes, 0, 0, axis_index_groups=parity_groups(), tile...]
    ppermute x9 -> x8, waiting for transfers between devices: 1.72 us -> 5.07 us  [the longest x2 5.06 us: over_z(): return lax.ppermute(part, ('zl', 'zh', 'c'), pairs)]
    ppermute x1, waiting for transfers between devices: 6.93 us -> 5.75 us  [body(): row_two = lax.ppermute(row_sum, 'x', [(0, 2), (1, 3), (2, 0), (3, 1)])]
    ppermute x9 -> x8, starting transfers between devices: 11 us -> 12.2 us  [the longest x2 6.32 us: over_y(): return lax.ppermute(part, ('y', 'c'), pairs)]
  transfers between devices with their start and end apart: 19 -> 18, of which waited for: 5 -> 4; matrix products, arithmetic and copies ran while one was open for 1% -> 1% of each run, Pallas kernels for 9% -> 9%
where the time goes in v12:
time: 100 us; the launch traced here: 99.9 us
  blocking collectives  40.1 us (40%)
  starting transfers between devices  30.4 us (30%)
  waiting for transfers between devices  15 us (15%)
  Pallas kernels  10.5 us (10%)
  other arithmetic  2.22 us (2%)
  between operations  1.5 us (2%)
    all_to_all x2, blocking collectives, same_parity(): lax.all_to_all(value, axes, 0, 0, axis_index_groups=parity_groups(), tile...  40.1 us
    ppermute x2, starting transfers between devices, over_y(): return lax.ppermute(part, ('y', 'c'), pairs)  6.32 us
    ppermute x1, waiting for transfers between devices, body(): row_two = lax.ppermute(row_sum, 'x', [(0, 2), (1, 3), (2, 0), (3, 1)])  5.75 us
    ppermute x3, starting transfers between devices, body(): lax.ppermute(mine, 'zh', [(i, (i + k) % 4) for i in range(4)])  5.48 us
    ppermute x2, waiting for transfers between devices, over_z(): return lax.ppermute(part, ('zl', 'zh', 'c'), pairs)  5.06 us
    ppermute x1, starting transfers between devices, body(): far_2 = lax.ppermute(sum_2, 'zh', HIGH)  4.29 us
    ppermute x3, waiting for transfers between devices, body(): lax.ppermute(mine, 'zh', [(i, (i + k) % 4) for i in range(4)])  4.2 us
    ppermute x1, starting transfers between devices, body(): oth_pair = lax.ppermute(pair.astype(F32), 'c', swap)  3.33 us
  transfers between devices with their start and end apart: 18, of which 4 were waited for; matrix products, arithmetic and copies ran while one was open for 1% of the time, Pallas kernels for 9%

profile of v12, /device:TPU:1, one launch (start us, length us, event | category | flops | bytes accessed | tf_op | source)
XLA Modules:
  0.0 99.9 jit_solution(15329669470345784029)
XLA Ops:
  0.6 0.0 copy-start.1
  0.6 0.0 copy-start
  0.7 0.0 copy-start.2
  0.7 0.0 copy-start.3
  0.7 0.0 copy-start.5
  0.7 1.1 %convert_element_type.10 = f32[2,512,128]{2,1,0:T(8,128)S(1)} convert(bf16[2,512,128]{2,1,0:T(8,128)(2,1)} %bitcast.17) | non-fusion elementwise | flops 131072 | bytes 786432 | tf_op jit(solution)/shard_map/convert_element_type | solution.py:408
  1.8 3.3 %collective-permute-start.1 = (f32[2,512,128]{2,1,0:T(8,128)S(1)}, f32[2,512,128]{2,1,0:T(8,128)S(1)}, u32[]{:S(2)}, u32[]{:S(2)}) collective-permute-start(f32[2,512,128]{2,1,0:T(8,128)S(1)} %convert_element_type.10), channel_id=1, source_target_pairs={{0,1},{1,0},{2,3},{3,2},{4,5},{5,4},{6,7},{7,6},{8,9},{9,8},{10,11... | collective-permute-start | bytes 1572872 | tf_op jit(solution)/shard_map/ppermute | solution.py:408
  5.1 1.0 bitcast_convert_fusion.1
  6.1 0.1 collective-permute-start
  6.2 0.0 copy-done.2
  6.2 0.1 bitcast_convert_fusion
  6.3 0.6 collective-permute-start.2
  6.8 0.0 copy-done.3
  6.9 1.3 %collective-permute-start.3 = (f32[1,16]{1,0:T(1,128)S(1)}, f32[1,16]{1,0:T(1,128)S(1)}, u32[]{:S(2)}, u32[]{:S(2)}) collective-permute-start(f32[1,16]{1,0:T(1,128)S(1)} %copy-done.3), channel_id=1, source_target_pairs={{0,8},{8,0},{16,24},{24,16},{1,9},{9,1},{17,25},{25,17},{2,10},{10... | collective-permute-start | bytes 200 | tf_op jit(solution)/shard_map/ppermute | solution.py:409
  8.8 0.0 collective-permute-done.1.oth_pair
  8.8 0.0 collective-permute-done.oth_feat
  8.8 0.0 copy-done.1
  8.8 0.0 copy-done
  8.8 0.0 copy-done.5
  8.8 1.4 %forward.1 = (bf16[2,1024,384]{2,1,0:T(8,128)(2,1)S(1)}, f32[2,1024,256]{2,1,0:T(8,128)S(1)}, bf16[2,32,256]{2,1,0:T(8,128)(2,1)S(1)}) custom-call(bf16[512,256]{1,0:T(8,128)(2,1)S(1)} %bitcast.16, bf16[2,512,128]{2,1,0:T(8,128)(2,1)S(1)} %bitcast.18, f32[512,256]{1,0:T(8,128)S(1)} %collective-permute-done.oth_feat, ...), custom_call_target="tpu_custom_call" | custom-call | flops 1000000000 | bytes 6000000 | tf_op jit(solution)/shard_map/forward/pallas_call | solution.py:412
  10.2 0.0 collective-permute-done.3.far
  10.2 4.3 %collective-permute-start.4 = (f32[1,16]{1,0:T(1,128)S(1)}, f32[1,16]{1,0:T(1,128)S(1)}, u32[]{:S(2)}, u32[]{:S(2)}) collective-permute-start(f32[1,16]{1,0:T(1,128)S(1)} %pair.1.near), channel_id=1, source_target_pairs={{8,16},{16,8},{24,0},{0,24},{9,17},{17,9},{25,1},{1,25},{10,18},{1... | collective-permute-start | bytes 200 | tf_op jit(solution)/shard_map/ppermute | solution.py:422
  14.5 0.0 collective-permute-done.2.oth_psi
  14.5 3.2 %factors.1 = (f32[2,2176,128]{2,1,0:T(8,128)S(1)}, f32[2,896,128]{2,1,0:T(8,128)S(1)}) custom-call(bf16[2,1024,384]{2,1,0:T(8,128)(2,1)S(1)} %get-tuple-element.22.x_s, f32[2,1024,256]{2,1,0:T(8,128)S(1)} %get-tuple-element.23.d_s, bf16[2,32,256]{2,1,0:T(8,128)(2,1)S(1)} %get-tuple-element.24.m_s.after, bf16[512,256]{1,0:T(8,128)(2,1)S(1)} %bitcast.19, ...), custom_call_target="tpu_custom_call" | custom-call | flops 2500000000 | bytes 8000000 | tf_op jit(solution)/shard_map/factors/pallas_call | solution.py:425
  17.8 0.0 collective-permute-done.4.far
  17.8 0.1 tie.1
  17.9 2.8 %collective-permute-start.5 = (f32[1152,128]{1,0:T(8,128)S(1)}, f32[1152,128]{1,0:T(8,128)S(1)}, u32[]{:S(2)}, u32[]{:S(2)}) collective-permute-start(f32[1152,128]{1,0:T(8,128)S(1)} %get-tuple-element.27), channel_id=1, source_target_pairs={{0,32},{32,0},{64,96},{96,64},{33,65},{65,33},{97,1},{1,97},{2,34}... | collective-permute-start | bytes 1769480 | tf_op jit(solution)/shard_map/ppermute | solution.py:385
  20.7 0.8 collective-permute-start.6
  21.5 1.2 %collective-permute-start.7 = (f32[520,128]{1,0:T(8,128)S(1)}, f32[520,128]{1,0:T(8,128)S(1)}, u32[]{:S(2)}, u32[]{:S(2)}) collective-permute-start(f32[520,128]{1,0:T(8,128)S(1)} %get-tuple-element.29), channel_id=1, source_target_pairs={{0,2},{2,0},{4,6},{6,4},{1,3},{3,1},{5,7},{7,5},{8,10},{10,8},{12,... | collective-permute-start | bytes 798728 | tf_op jit(solution)/shard_map/ppermute | solution.py:449
  22.7 1.8 %collective-permute-start.8 = (f32[392,128]{1,0:T(8,128)S(1)}, f32[392,128]{1,0:T(8,128)S(1)}, u32[]{:S(2)}, u32[]{:S(2)}) collective-permute-start(f32[392,128]{1,0:T(8,128)S(1)} %get-tuple-element.30), channel_id=1, source_target_pairs={{2,4},{4,2},{6,0},{0,6},{3,5},{5,3},{7,1},{1,7},{10,12},{12,10},{1... | collective-permute-start | bytes 602120 | tf_op jit(solution)/shard_map/ppermute | solution.py:450
  24.5 0.6 collective-permute-start.9
  25.2 5.7 %collective-permute-done.9.row_two = f32[8,128]{1,0:T(8,128)S(1)} collective-permute-done((f32[8,128]{1,0:T(8,128)S(1)}, f32[8,128]{1,0:T(8,128)S(1)}, u32[]{:S(2)}, u32[]{:S(2)}) %collective-permute-start.9) | collective-permute-done | bytes 4128 | tf_op jit(solution)/shard_map/ppermute | solution.py:451
  30.9 0.0 collective-permute-done.8.from_3
  30.9 0.0 collective-permute-done.7.from_2
  30.9 0.0 collective-permute-done.6.from_1
  30.9 0.0 collective-permute-done.5.from_0
  30.9 0.2 add.16
  31.1 20.3 %all_to_all.17 = f32[16,136,128]{2,1,0:T(8,128)S(1)} all-to-all(f32[16,136,128]{2,1,0:T(8,128)S(1)} %bitcast.15), channel_id=1, replica_groups={{0,4,34,38,64,68,98,102,130,134,160,164,194,198,224,228},{2,6,32,36,66,..., dimensions={0} | all-to-all | bytes 2228224 | tf_op jit(solution)/shard_map/all_to_all | solution.py:377
  51.5 0.1 reduce_sum.9
  51.5 1.9 %collective-permute-start.10 = (f32[136,128]{1,0:T(8,128)S(1)}, f32[136,128]{1,0:T(8,128)S(1)}, u32[]{:S(2)}, u32[]{:S(2)}) collective-permute-start(f32[136,128]{1,0:T(8,128)S(1)} %reduce_sum.9), channel_id=1, source_target_pairs={{0,16},{8,24},{16,0},{24,8},{1,17},{9,25},{17,1},{25,9},{2,18},{10... | collective-permute-start | bytes 208904 | tf_op jit(solution)/shard_map/ppermute | solution.py:457
  53.4 0.9 collective-permute-start.11
  54.3 2.7 %collective-permute-start.12 = (f32[136,128]{1,0:T(8,128)S(1)}, f32[136,128]{1,0:T(8,128)S(1)}, u32[]{:S(2)}, u32[]{:S(2)}) collective-permute-start(f32[136,128]{1,0:T(8,128)S(1)} %reduce_sum.9), channel_id=1, source_target_pairs={{0,24},{8,0},{16,8},{24,16},{1,25},{9,1},{17,9},{25,17},{2,26},{10... | collective-permute-start | bytes 208904 | tf_op jit(solution)/shard_map/ppermute | solution.py:457
  57.0 2.5 %collective-permute-done.10 = f32[136,128]{1,0:T(8,128)S(1)} collective-permute-done((f32[136,128]{1,0:T(8,128)S(1)}, f32[136,128]{1,0:T(8,128)S(1)}, u32[]{:S(2)}, u32[]{:S(2)}) %collective-permute-start.10) | collective-permute-done | bytes 69664 | tf_op jit(solution)/shard_map/ppermute | solution.py:457
  59.5 0.0 collective-permute-done.11
  59.5 1.7 %collective-permute-done.12 = f32[136,128]{1,0:T(8,128)S(1)} collective-permute-done((f32[136,128]{1,0:T(8,128)S(1)}, f32[136,128]{1,0:T(8,128)S(1)}, u32[]{:S(2)}, u32[]{:S(2)}) %collective-permute-start.12) | collective-permute-done | bytes 69664 | tf_op jit(solution)/shard_map/ppermute | solution.py:457
  61.2 0.0 copy-start.6
  61.2 0.1 broadcast_in_dim.15
  61.3 0.0 copy-start.4
  61.3 19.8 %all_to_all.18 = f32[16,136,128]{2,1,0:T(8,128)S(1)} all-to-all(f32[16,136,128]{2,1,0:T(8,128)S(1)} %broadcast_in_dim.15), channel_id=1, replica_groups={{0,4,34,38,64,68,98,102,130,134,160,164,194,198,224,228},{2,6,32,36,66,..., dimensions={0} | all-to-all | bytes 2228224 | tf_op jit(solution)/shard_map/all_to_all | solution.py:377
  81.1 0.1 cut.1
  81.2 3.5 %collective-permute-start.16 = (f32[768,128]{1,0:T(8,128)S(1)}, f32[768,128]{1,0:T(8,128)S(1)}, u32[]{:S(2)}, u32[]{:S(2)}) collective-permute-start(f32[768,128]{1,0:T(8,128)S(1)} %get-tuple-element.37), channel_id=1, source_target_pairs={{0,32},{32,0},{64,96},{96,64},{33,65},{65,33},{97,1},{1,97},{2,34}... | collective-permute-start | bytes 1179656 | tf_op jit(solution)/shard_map/ppermute | solution.py:385
  84.7 0.0 collective-permute-start.13
  84.7 0.9 collective-permute-start.14
  85.6 1.1 %collective-permute-start.15 = (f32[384,128]{1,0:T(8,128)S(1)}, f32[384,128]{1,0:T(8,128)S(1)}, u32[]{:S(2)}, u32[]{:S(2)}) collective-permute-start(f32[384,128]{1,0:T(8,128)S(1)} %get-tuple-element.34), channel_id=1, source_target_pairs={{2,4},{4,2},{6,0},{0,6},{3,5},{5,3},{7,1},{1,7},{10,12},{12,10},{1... | collective-permute-start | bytes 589832 | tf_op jit(solution)/shard_map/ppermute | solution.py:462
  86.7 5.1 %collective-permute-done.13.from_1 = f32[640,128]{1,0:T(8,128)S(1)} collective-permute-done((f32[640,128]{1,0:T(8,128)S(1)}, f32[640,128]{1,0:T(8,128)S(1)}, u32[]{:S(2)}, u32[]{:S(2)}) %collective-permute-start.13) | collective-permute-done | bytes 327712 | tf_op jit(solution)/shard_map/ppermute | solution.py:394
  91.8 0.0 collective-permute-done.16.from_0
  91.8 0.0 copy-done.6
  91.8 2.5 %natural.1 = (f32[896,256]{1,0:T(8,128)S(1)}, f32[1,128]{1,0:T(1,128)S(1)}) custom-call(f32[2176,128]{1,0:T(8,128)S(1)} %bitcast.13, f32[768,128]{1,0:T(8,128)S(1)} %collective-permute-done.16.from_0, f32[640,128]{1,0:T(8,128)S(1)} %collective-permute-done.13.from_1, f32[896,896]{1,0:T(8,128)S(1)} %bitcast.20, f32[256,256]{1,0:T(8,128)S(1)} %bitcast.21), custom_call_target="tpu_custom_call" | custom-call | flops 1500000000 | bytes 5000000 | tf_op jit(solution)/shard_map/natural/pallas_call | solution.py:464
  94.3 2.5 %collective-permute-start.17 = (f32[1,128]{1,0:T(1,128)S(1)}, f32[1,128]{1,0:T(1,128)S(1)}, u32[]{:S(2)}, u32[]{:S(2)}) collective-permute-start(f32[1,128]{1,0:T(1,128)S(1)} %get-tuple-element.39.curvature), channel_id=1, source_target_pairs={{0,1},{1,0},{2,3},{3,2},{4,5},{5,4},{6,7},{7,6},{8,9},{9,8},{10,11... | collective-permute-start | bytes 1544 | tf_op jit(solution)/shard_map/ppermute | solution.py:473
  96.8 0.0 collective-permute-done.14.from_2
  96.8 0.0 collective-permute-done.15.from_3
  96.8 2.0 %unpack.1 = (f32[896,896]{1,0:T(8,128)}, f32[256,256]{1,0:T(8,128)}, f32[1,128]{1,0:T(1,128)S(1)}) custom-call(f32[2176,128]{1,0:T(8,128)S(1)} %bitcast.14, f32[640,128]{1,0:T(8,128)S(1)} %collective-permute-done.13.from_1, f32[384,128]{1,0:T(8,128)S(1)} %collective-permute-done.14.from_2, f32[384,128]{1,0:T(8,128)S(1)} %collective-permute-done.15.from_3), custom_call_target="tpu_custom_call" | custom-call | flops 10000000 | bytes 6000000 | tf_op jit(solution)/shard_map/unpack/pallas_call | solution.py:474
  98.8 0.0 collective-permute-done.17.other
  98.8 1.1 %scale.1 = f32[896,256]{1,0:T(8,128)} custom-call(f32[896,256]{1,0:T(8,128)S(1)} %get-tuple-element.38.natural, f32[1,128]{1,0:T(1,128)S(1)} %get-tuple-element.39.curvature, f32[1,128]{1,0:T(1,128)S(1)} %collective-permute-done.17.other, f32[1,128]{1,0:T(1,128)S(1)} %get-tuple-element.40.after), custom_call_target="tpu_custom_call" | custom-call | flops 1000000 | bytes 2000000 | tf_op jit(solution)/shard_map/scale/pallas_call | solution.py:485
  (3 shorter events, 0.0 us)
Async XLA Ops:
  0.6 8.2 %copy-start.1 = (bf16[1,2,16,32,128]{4,3,2,1,0:T(8,128)(2,1)S(1)}, bf16[1,2,16,32,128]{4,3,2,1,0:T(8,128)(2,1)}, u32[]{:S(2)}) copy-start(bf16[1,2,16,32,128]{4,3,2,1,0:T(8,128)(2,1)} %param.10) | copy-start | bytes 786436
  0.6 8.2 %copy-start = (bf16[1,16,32,256]{3,2,1,0:T(8,128)(2,1)S(1)}, bf16[1,16,32,256]{3,2,1,0:T(8,128)(2,1)}, u32[]{:S(2)}) copy-start(bf16[1,16,32,256]{3,2,1,0:T(8,128)(2,1)} %param.8) | copy-start | bytes 786436
  0.7 5.6 %copy-start.2 = (bf16[1,16,32,256]{3,2,1,0:T(8,128)(2,1)S(1)}, bf16[1,16,32,256]{3,2,1,0:T(8,128)(2,1)}, u32[]{:S(2)}) copy-start(bf16[1,16,32,256]{3,2,1,0:T(8,128)(2,1)} %param.9) | copy-start | bytes 786436
  0.7 6.2 %copy-start.3 = (f32[1,16]{1,0:T(1,128)S(1)}, f32[1,16]{1,0:T(1,128)}, u32[]{:S(2)}) copy-start(f32[1,16]{1,0:T(1,128)} %near.1) | copy-start | bytes 196
  0.7 8.2 %copy-start.5 = (bf16[2,896,256]{2,1,0:T(8,128)(2,1)S(1)}, bf16[2,896,256]{2,1,0:T(8,128)(2,1)}, u32[]{:S(2)}) copy-start(bf16[2,896,256]{2,1,0:T(8,128)(2,1)} %weights.3) | copy-start | bytes 2752516
  1.8 7.0 %collective-permute-start.1 = (f32[2,512,128]{2,1,0:T(8,128)S(1)}, f32[2,512,128]{2,1,0:T(8,128)S(1)}, u32[]{:S(2)}, u32[]{:S(2)}) collective-permute-start(f32[2,512,128]{2,1,0:T(8,128)S(1)} %convert_element_type.10), channel_id=1, source_target_pairs={{0,1},{1,0},{2,3},{3,2},{4,5},{5,4},{6,7},{7,6},{8,9},{9,8},{10,11... | collective-permute-start | bytes 1572872 | tf_op jit(solution)/shard_map/ppermute | solution.py:408
  6.1 2.7 %collective-permute-start = (f32[512,256]{1,0:T(8,128)S(1)}, f32[512,256]{1,0:T(8,128)S(1)}, u32[]{:S(2)}, u32[]{:S(2)}) collective-permute-start(f32[512,256]{1,0:T(8,128)S(1)} %bitcast_convert_fusion.1), channel_id=1, source_target_pairs={{0,1},{1,0},{2,3},{3,2},{4,5},{5,4},{6,7},{7,6},{8,9},{9,8},{10,11... | collective-permute-start | bytes 1572872 | tf_op jit(solution)/shard_map/ppermute | solution.py:407
  6.3 8.2 %collective-permute-start.2 = (f32[512,256]{1,0:T(8,128)S(1)}, f32[512,256]{1,0:T(8,128)S(1)}, u32[]{:S(2)}, u32[]{:S(2)}) collective-permute-start(f32[512,256]{1,0:T(8,128)S(1)} %bitcast_convert_fusion), channel_id=1, source_target_pairs={{0,1},{1,0},{2,3},{3,2},{4,5},{5,4},{6,7},{7,6},{8,9},{9,8},{10,11... | collective-permute-start | bytes 1572872 | tf_op jit(solution)/shard_map/ppermute | solution.py:410
  6.9 3.4 %collective-permute-start.3 = (f32[1,16]{1,0:T(1,128)S(1)}, f32[1,16]{1,0:T(1,128)S(1)}, u32[]{:S(2)}, u32[]{:S(2)}) collective-permute-start(f32[1,16]{1,0:T(1,128)S(1)} %copy-done.3), channel_id=1, source_target_pairs={{0,8},{8,0},{16,24},{24,16},{1,9},{9,1},{17,25},{25,17},{2,10},{10... | collective-permute-start | bytes 200 | tf_op jit(solution)/shard_map/ppermute | solution.py:409
  10.2 7.5 %collective-permute-start.4 = (f32[1,16]{1,0:T(1,128)S(1)}, f32[1,16]{1,0:T(1,128)S(1)}, u32[]{:S(2)}, u32[]{:S(2)}) collective-permute-start(f32[1,16]{1,0:T(1,128)S(1)} %pair.1.near), channel_id=1, source_target_pairs={{8,16},{16,8},{24,0},{0,24},{9,17},{17,9},{25,1},{1,25},{10,18},{1... | collective-permute-start | bytes 200 | tf_op jit(solution)/shard_map/ppermute | solution.py:422
  17.9 13.0 %collective-permute-start.5 = (f32[1152,128]{1,0:T(8,128)S(1)}, f32[1152,128]{1,0:T(8,128)S(1)}, u32[]{:S(2)}, u32[]{:S(2)}) collective-permute-start(f32[1152,128]{1,0:T(8,128)S(1)} %get-tuple-element.27), channel_id=1, source_target_pairs={{0,32},{32,0},{64,96},{96,64},{33,65},{65,33},{97,1},{1,97},{2,34}... | collective-permute-start | bytes 1769480 | tf_op jit(solution)/shard_map/ppermute | solution.py:385
  20.7 10.2 %collective-permute-start.6 = (f32[1024,128]{1,0:T(8,128)S(1)}, f32[1024,128]{1,0:T(8,128)S(1)}, u32[]{:S(2)}, u32[]{:S(2)}) collective-permute-start(f32[1024,128]{1,0:T(8,128)S(1)} %get-tuple-element.28), channel_id=1, source_target_pairs={{0,128},{128,0},{8,136},{136,8},{16,144},{144,16},{24,152},{152,24... | collective-permute-start | bytes 1572872 | tf_op jit(solution)/shard_map/ppermute | solution.py:394
  21.5 9.4 %collective-permute-start.7 = (f32[520,128]{1,0:T(8,128)S(1)}, f32[520,128]{1,0:T(8,128)S(1)}, u32[]{:S(2)}, u32[]{:S(2)}) collective-permute-start(f32[520,128]{1,0:T(8,128)S(1)} %get-tuple-element.29), channel_id=1, source_target_pairs={{0,2},{2,0},{4,6},{6,4},{1,3},{3,1},{5,7},{7,5},{8,10},{10,8},{12,... | collective-permute-start | bytes 798728 | tf_op jit(solution)/shard_map/ppermute | solution.py:449
  22.7 8.2 %collective-permute-start.8 = (f32[392,128]{1,0:T(8,128)S(1)}, f32[392,128]{1,0:T(8,128)S(1)}, u32[]{:S(2)}, u32[]{:S(2)}) collective-permute-start(f32[392,128]{1,0:T(8,128)S(1)} %get-tuple-element.30), channel_id=1, source_target_pairs={{2,4},{4,2},{6,0},{0,6},{3,5},{5,3},{7,1},{1,7},{10,12},{12,10},{1... | collective-permute-start | bytes 602120 | tf_op jit(solution)/shard_map/ppermute | solution.py:450
  24.5 6.4 %collective-permute-start.9 = (f32[8,128]{1,0:T(8,128)S(1)}, f32[8,128]{1,0:T(8,128)S(1)}, u32[]{:S(2)}, u32[]{:S(2)}) collective-permute-start(f32[8,128]{1,0:T(8,128)S(1)} %get-tuple-element.31.row_sum), channel_id=1, source_target_pairs={{0,4},{2,6},{4,0},{6,2},{1,5},{3,7},{5,1},{7,3},{8,12},{10,14},{12... | collective-permute-start | bytes 12296 | tf_op jit(solution)/shard_map/ppermute | solution.py:451
  51.5 8.0 %collective-permute-start.10 = (f32[136,128]{1,0:T(8,128)S(1)}, f32[136,128]{1,0:T(8,128)S(1)}, u32[]{:S(2)}, u32[]{:S(2)}) collective-permute-start(f32[136,128]{1,0:T(8,128)S(1)} %reduce_sum.9), channel_id=1, source_target_pairs={{0,16},{8,24},{16,0},{24,8},{1,17},{9,25},{17,1},{25,9},{2,18},{10... | collective-permute-start | bytes 208904 | tf_op jit(solution)/shard_map/ppermute | solution.py:457
  53.4 6.1 %collective-permute-start.11 = (f32[136,128]{1,0:T(8,128)S(1)}, f32[136,128]{1,0:T(8,128)S(1)}, u32[]{:S(2)}, u32[]{:S(2)}) collective-permute-start(f32[136,128]{1,0:T(8,128)S(1)} %reduce_sum.9), channel_id=1, source_target_pairs={{0,8},{8,16},{16,24},{24,0},{1,9},{9,17},{17,25},{25,1},{2,10},{10... | collective-permute-start | bytes 208904 | tf_op jit(solution)/shard_map/ppermute | solution.py:457
  54.3 6.9 %collective-permute-start.12 = (f32[136,128]{1,0:T(8,128)S(1)}, f32[136,128]{1,0:T(8,128)S(1)}, u32[]{:S(2)}, u32[]{:S(2)}) collective-permute-start(f32[136,128]{1,0:T(8,128)S(1)} %reduce_sum.9), channel_id=1, source_target_pairs={{0,24},{8,0},{16,8},{24,16},{1,25},{9,1},{17,9},{25,17},{2,26},{10... | collective-permute-start | bytes 208904 | tf_op jit(solution)/shard_map/ppermute | solution.py:457
  61.2 30.6 %copy-start.6 = (f32[1,256,256]{2,1,0:T(8,128)S(1)}, f32[1,256,256]{2,1,0:T(8,128)}, u32[]{:S(2)}) copy-start(f32[1,256,256]{2,1,0:T(8,128)} %param.15) | copy-start | bytes 786436
  61.3 30.5 %copy-start.4 = (f32[1,896,896]{2,1,0:T(8,128)S(1)}, f32[1,896,896]{2,1,0:T(8,128)}, u32[]{:S(2)}) copy-start(f32[1,896,896]{2,1,0:T(8,128)} %param.14) | copy-start | bytes 9633796
  81.2 10.6 %collective-permute-start.16 = (f32[768,128]{1,0:T(8,128)S(1)}, f32[768,128]{1,0:T(8,128)S(1)}, u32[]{:S(2)}, u32[]{:S(2)}) collective-permute-start(f32[768,128]{1,0:T(8,128)S(1)} %get-tuple-element.37), channel_id=1, source_target_pairs={{0,32},{32,0},{64,96},{96,64},{33,65},{65,33},{97,1},{1,97},{2,34}... | collective-permute-start | bytes 1179656 | tf_op jit(solution)/shard_map/ppermute | solution.py:385
  84.7 7.1 %collective-permute-start.13 = (f32[640,128]{1,0:T(8,128)S(1)}, f32[640,128]{1,0:T(8,128)S(1)}, u32[]{:S(2)}, u32[]{:S(2)}) collective-permute-start(f32[640,128]{1,0:T(8,128)S(1)} %get-tuple-element.32), channel_id=1, source_target_pairs={{0,128},{128,0},{8,136},{136,8},{16,144},{144,16},{24,152},{152,24... | collective-permute-start | bytes 983048 | tf_op jit(solution)/shard_map/ppermute | solution.py:394
  84.7 12.2 %collective-permute-start.14 = (f32[384,128]{1,0:T(8,128)S(1)}, f32[384,128]{1,0:T(8,128)S(1)}, u32[]{:S(2)}, u32[]{:S(2)}) collective-permute-start(f32[384,128]{1,0:T(8,128)S(1)} %get-tuple-element.33), channel_id=1, source_target_pairs={{0,2},{2,0},{4,6},{6,4},{1,3},{3,1},{5,7},{7,5},{8,10},{10,8},{12,... | collective-permute-start | bytes 589832 | tf_op jit(solution)/shard_map/ppermute | solution.py:462
  85.6 11.2 %collective-permute-start.15 = (f32[384,128]{1,0:T(8,128)S(1)}, f32[384,128]{1,0:T(8,128)S(1)}, u32[]{:S(2)}, u32[]{:S(2)}) collective-permute-start(f32[384,128]{1,0:T(8,128)S(1)} %get-tuple-element.34), channel_id=1, source_target_pairs={{2,4},{4,2},{6,0},{0,6},{3,5},{5,3},{7,1},{1,7},{10,12},{12,10},{1... | collective-permute-start | bytes 589832 | tf_op jit(solution)/shard_map/ppermute | solution.py:462
  94.3 4.5 %collective-permute-start.17 = (f32[1,128]{1,0:T(1,128)S(1)}, f32[1,128]{1,0:T(1,128)S(1)}, u32[]{:S(2)}, u32[]{:S(2)}) collective-permute-start(f32[1,128]{1,0:T(1,128)S(1)} %get-tuple-element.39.curvature), channel_id=1, source_target_pairs={{0,1},{1,0},{2,3},{3,2},{4,5},{5,4},{6,7},{7,6},{8,9},{9,8},{10,11... | collective-permute-start | bytes 1544 | tf_op jit(solution)/shard_map/ppermute | solution.py:473

commit v13 on v10

--- a/solution.py
+++ b/solution.py
@@ -243,7 +243,9 @@
     return read
 
 
-def unpack_kernel(kept, from_2, from_3, from_4, a_out, s_out, done, a_v, s_v, sems):
+def finish_kernel(
+    kept, from_2, from_3, from_4, natural, curvature, other, a_out, s_out, direction, a_v, s_v, d_v, sems
+):
     row, col = square_iotas()
     read = reader(kept, (from_2, from_3, from_4), BACK_STREAMS[2:])
     lines = read(33, 8)
@@ -308,9 +310,11 @@
         place(a_v, 6, i, sides[i].T)
     place(a_v, 6, 6, get(10))
     send(a_v, a_out, 6, 7)
+    total = curvature[:, :1] + other[:, :1]
+    d_v[...] = natural[...] * lax.rsqrt(total * (1.0 / ENTRIES))
+    send(d_v, direction, 0, 7)
     for copy in copies:
         copy.wait()
-    done[...] = inverse
 
 
 def natural_kernel(kept, from_0, from_1, a_inverse, s_inverse, natural, curvature):
@@ -321,21 +325,17 @@
     )
     g_high, g_low = split(grad)
     s_high, s_low = split(s_inverse[...])
-    half = dot(g_high, s_high) + (dot(g_high, s_low) + dot(g_low, s_high))
+    half = dot(jnp.concatenate([g_high, g_high, g_low], 1), jnp.concatenate([s_high, s_low, s_high], 0))
     h_high, h_low = split(half)
+    h_terms = jnp.concatenate([h_high, h_low, h_high], 0)
     total = jnp.zeros((1, D), F32)
     for i in range(7):
         rows = slice(i * B, (i + 1) * B)
         a_high, a_low = split(a_inverse[rows, :])
-        part = dot(a_high, h_high) + (dot(a_high, h_low) + dot(a_low, h_high))
+        part = dot(jnp.concatenate([a_high, a_high, a_low], 1), h_terms)
         natural[rows, :] = part
         total = total + jnp.sum(part * grad[rows, :], axis=0, keepdims=True)
     curvature[...] = jnp.broadcast_to(jnp.sum(total, axis=1, keepdims=True), (1, B))
-
-
-def scale_kernel(natural, curvature, other, after, direction):
-    total = curvature[:, :1] + other[:, :1]
-    direction[...] = natural[...] * lax.rsqrt(total * (1.0 / ENTRIES))
 
 
 def call(kernel, out_shapes, in_spaces, limit_mib, name, scratch=(), flops=0, moved=0, out_spaces=None):
@@ -456,20 +456,22 @@
         moved=5_000_000,
     )(kept, *parts[:2], a_inverse[0], s_inverse[0])
     other = lax.ppermute(curvature, "c", swap)
-    a_sum, s_sum, done = call(
-        unpack_kernel,
-        [((DIN, DIN), F32), ((D, D), F32), ((1, B), F32)],
-        [V] * 4,
-        14,
-        "unpack",
-        scratch=[pltpu.VMEM((DIN, DIN), F32), pltpu.VMEM((D, D), F32), pltpu.SemaphoreType.DMA((5,))],
-        out_spaces=(pl.ANY, pl.ANY, V),
+    a_sum, s_sum, direction = call(
+        finish_kernel,
+        [((DIN, DIN), F32), ((D, D), F32), ((DIN, D), F32)],
+        [V] * 7,
+        16,
+        "finish",
+        scratch=[
+            pltpu.VMEM((DIN, DIN), F32),
+            pltpu.VMEM((D, D), F32),
+            pltpu.VMEM((DIN, D), F32),
+            pltpu.SemaphoreType.DMA((6,)),
+        ],
+        out_spaces=(pl.ANY,) * 3,
         flops=10_000_000,
-        moved=6_000_000,
-    )(kept, *parts[2:])
-    (direction,) = call(
-        scale_kernel, [((DIN, D), F32)], [V] * 4, 6, "scale", flops=1_000_000, moved=2_000_000
-    )(natural, curvature, other, done)
+        moved=7_000_000,
+    )(kept, *parts[2:], natural, curvature, other)
     return a_sum[None], s_sum[None], direction[None]
 
 

time: 97.3 us -> 97.4 us (level)
    pallas_call x2 -> x1, Pallas kernels: 3.02 us -> 2.32 us  [body(): call(finish_kernel, [((DIN, DIN), F32), ((D, D), F32), ((DIN, D), F32)],...]
  transfers between devices with their start and end apart: 19 -> 19, of which waited for: 5 -> 6; matrix products, arithmetic and copies ran while one was open for 1% -> 1% of each run, Pallas kernels for 9% -> 7%
where the time goes in v13:
time: 97.4 us; the launch traced here: 97.2 us
  blocking collectives  36.5 us (37%)
  starting transfers between devices  32.5 us (33%)
  waiting for transfers between devices  14.5 us (15%)
  Pallas kernels  9.66 us (10%)
  other arithmetic  2.22 us (2%)
  between operations  1.65 us (2%)
    all_to_all x2, blocking collectives, same_parity(): lax.all_to_all(value, axes, 0, 0, axis_index_groups=parity_groups(), tile...  36.5 us
    ppermute x1, waiting for transfers between devices, body(): row_two = lax.ppermute(row_sum, 'x', [(0, 2), (1, 3), (2, 0), (3, 1)])  6.93 us
    ppermute x1, starting transfers between devices, body(): other = lax.ppermute(curvature, 'c', swap)  6.66 us
    ppermute x5, starting transfers between devices, to_neighbours(): lax.ppermute(part, axis, pairs)  5.89 us
    ppermute x3, waiting for transfers between devices, body(): lax.ppermute(mine, 'zh', [(i, (i + k) % 4) for i in range(4)])  5.05 us
    ppermute x3, starting transfers between devices, body(): lax.ppermute(mine, 'zh', [(i, (i + k) % 4) for i in range(4)])  4.63 us
    ppermute x1, starting transfers between devices, body(): far_2 = lax.ppermute(sum_2, 'zh', HIGH)  4.29 us
    ppermute x1, starting transfers between devices, body(): oth_pair = lax.ppermute(pair.astype(F32), 'c', swap)  3.33 us
  transfers between devices with their start and end apart: 19, of which 6 were waited for; matrix products, arithmetic and copies ran while one was open for 1% of the time, Pallas kernels for 7%

profile of v13, /device:TPU:1, one launch (start us, length us, event | category | flops | bytes accessed | tf_op | source)
XLA Modules:
  0.0 97.2 jit_solution(11199266550452928276)
XLA Ops:
  0.6 0.0 copy-start.1
  0.6 0.0 copy-start
  0.7 0.0 copy-start.2
  0.7 0.0 copy-start.3
  0.7 0.0 copy-start.5
  0.7 1.1 %convert_element_type.10 = f32[2,512,128]{2,1,0:T(8,128)S(1)} convert(bf16[2,512,128]{2,1,0:T(8,128)(2,1)} %bitcast.17) | non-fusion elementwise | flops 131072 | bytes 786432 | tf_op jit(solution)/shard_map/convert_element_type | solution.py:392
  1.8 3.3 %collective-permute-start.1 = (f32[2,512,128]{2,1,0:T(8,128)S(1)}, f32[2,512,128]{2,1,0:T(8,128)S(1)}, u32[]{:S(2)}, u32[]{:S(2)}) collective-permute-start(f32[2,512,128]{2,1,0:T(8,128)S(1)} %convert_element_type.10), channel_id=1, source_target_pairs={{0,1},{1,0},{2,3},{3,2},{4,5},{5,4},{6,7},{7,6},{8,9},{9,8},{10,11... | collective-permute-start | bytes 1572872 | tf_op jit(solution)/shard_map/ppermute | solution.py:392
  5.1 1.0 %bitcast_convert_fusion.1 = f32[512,256]{1,0:T(8,128)S(1)} fusion(bf16[1,16,32,256]{3,2,1,0:T(8,128)(2,1)} %param.8), kind=kLoop, calls=%fused_computation.2 | loop fusion | flops 131072 | bytes 786432 | tf_op jit(solution)/shard_map/convert_element_type | solution.py:391
  6.1 0.1 collective-permute-start
  6.2 0.0 copy-done.2
  6.2 0.1 bitcast_convert_fusion
  6.3 0.6 collective-permute-start.2
  6.8 0.0 copy-done.3
  6.9 1.3 %collective-permute-start.3 = (f32[1,16]{1,0:T(1,128)S(1)}, f32[1,16]{1,0:T(1,128)S(1)}, u32[]{:S(2)}, u32[]{:S(2)}) collective-permute-start(f32[1,16]{1,0:T(1,128)S(1)} %copy-done.3), channel_id=1, source_target_pairs={{0,8},{8,0},{16,24},{24,16},{1,9},{9,1},{17,25},{25,17},{2,10},{10... | collective-permute-start | bytes 200 | tf_op jit(solution)/shard_map/ppermute | solution.py:393
  8.8 0.0 collective-permute-done.1.oth_pair
  8.8 0.0 collective-permute-done.oth_feat
  8.8 0.0 copy-done.1
  8.8 0.0 copy-done
  8.8 0.0 copy-done.5
  8.8 1.4 %forward.1 = (bf16[2,1024,384]{2,1,0:T(8,128)(2,1)S(1)}, f32[2,1024,256]{2,1,0:T(8,128)S(1)}, bf16[2,32,256]{2,1,0:T(8,128)(2,1)S(1)}) custom-call(bf16[512,256]{1,0:T(8,128)(2,1)S(1)} %bitcast.16, bf16[2,512,128]{2,1,0:T(8,128)(2,1)S(1)} %bitcast.18, f32[512,256]{1,0:T(8,128)S(1)} %collective-permute-done.oth_feat, ...), custom_call_target="tpu_custom_call" | custom-call | flops 1000000000 | bytes 6000000 | tf_op jit(solution)/shard_map/forward/pallas_call | solution.py:396
  10.2 0.0 collective-permute-done.3.far
  10.2 4.3 %collective-permute-start.4 = (f32[1,16]{1,0:T(1,128)S(1)}, f32[1,16]{1,0:T(1,128)S(1)}, u32[]{:S(2)}, u32[]{:S(2)}) collective-permute-start(f32[1,16]{1,0:T(1,128)S(1)} %pair.1.near), channel_id=1, source_target_pairs={{8,16},{16,8},{24,0},{0,24},{9,17},{17,9},{25,1},{1,25},{10,18},{1... | collective-permute-start | bytes 200 | tf_op jit(solution)/shard_map/ppermute | solution.py:406
  14.5 0.0 collective-permute-done.2.oth_psi
  14.5 3.2 %factors.1 = (f32[2,2176,128]{2,1,0:T(8,128)S(1)}, f32[2,896,128]{2,1,0:T(8,128)S(1)}) custom-call(bf16[2,1024,384]{2,1,0:T(8,128)(2,1)S(1)} %get-tuple-element.23.x_s, f32[2,1024,256]{2,1,0:T(8,128)S(1)} %get-tuple-element.24.d_s, bf16[2,32,256]{2,1,0:T(8,128)(2,1)S(1)} %get-tuple-element.25.m_s.after, bf16[512,256]{1,0:T(8,128)(2,1)S(1)} %bitcast.19, ...), custom_call_target="tpu_custom_call" | custom-call | flops 2500000000 | bytes 8000000 | tf_op jit(solution)/shard_map/factors/pallas_call | solution.py:409
  17.8 0.0 collective-permute-done.4.far
  17.8 0.1 tie.1
  17.9 1.3 %collective-permute-start.5 = (f32[904,128]{1,0:T(8,128)S(1)}, f32[904,128]{1,0:T(8,128)S(1)}, u32[]{:S(2)}, u32[]{:S(2)}) collective-permute-start(f32[904,128]{1,0:T(8,128)S(1)} %get-tuple-element.28), channel_id=1, source_target_pairs={{0,2},{2,0},{4,6},{6,4},{1,3},{3,1},{5,7},{7,5},{8,10},{10,8},{12,... | collective-permute-start | bytes 1388552 | tf_op jit(solution)/shard_map/ppermute | solution.py:432
  19.2 1.8 %collective-permute-start.6 = (f32[776,128]{1,0:T(8,128)S(1)}, f32[776,128]{1,0:T(8,128)S(1)}, u32[]{:S(2)}, u32[]{:S(2)}) collective-permute-start(f32[776,128]{1,0:T(8,128)S(1)} %get-tuple-element.29), channel_id=1, source_target_pairs={{2,4},{4,2},{6,0},{0,6},{3,5},{5,3},{7,1},{1,7},{10,12},{12,10},{1... | collective-permute-start | bytes 1191944 | tf_op jit(solution)/shard_map/ppermute | solution.py:433
  21.0 1.3 %collective-permute-start.7 = (f32[768,128]{1,0:T(8,128)S(1)}, f32[768,128]{1,0:T(8,128)S(1)}, u32[]{:S(2)}, u32[]{:S(2)}) collective-permute-start(f32[768,128]{1,0:T(8,128)S(1)} %get-tuple-element.30), channel_id=1, source_target_pairs={{0,32},{32,0},{64,96},{96,64},{1,33},{33,1},{65,97},{97,65},{2,34}... | collective-permute-start | bytes 1179656 | tf_op jit(solution)/shard_map/ppermute | solution.py:434
  22.3 0.7 collective-permute-start.8
  23.0 0.6 collective-permute-start.9
  23.7 6.9 %collective-permute-done.9.row_two = f32[8,128]{1,0:T(8,128)S(1)} collective-permute-done((f32[8,128]{1,0:T(8,128)S(1)}, f32[8,128]{1,0:T(8,128)S(1)}, u32[]{:S(2)}, u32[]{:S(2)}) %collective-permute-start.9) | collective-permute-done | bytes 4128 | tf_op jit(solution)/shard_map/ppermute | solution.py:436
  30.6 0.0 collective-permute-done.8.from_3
  30.6 0.0 collective-permute-done.7.from_2
  30.6 0.0 collective-permute-done.6.from_1
  30.6 0.0 collective-permute-done.5.from_0
  30.6 0.2 add.16
  30.8 20.4 %all_to_all.17 = f32[16,136,128]{2,1,0:T(8,128)S(1)} all-to-all(f32[16,136,128]{2,1,0:T(8,128)S(1)} %bitcast.15), channel_id=1, replica_groups={{0,4,34,38,64,68,98,102,130,134,160,164,194,198,224,228},{2,6,32,36,66,..., dimensions={0} | all-to-all | bytes 2228224 | tf_op jit(solution)/shard_map/all_to_all | solution.py:370
  51.3 0.1 reduce_sum.9
  51.3 0.9 collective-permute-start.10
  52.3 1.1 %collective-permute-start.11 = (f32[136,128]{1,0:T(8,128)S(1)}, f32[136,128]{1,0:T(8,128)S(1)}, u32[]{:S(2)}, u32[]{:S(2)}) collective-permute-start(f32[136,128]{1,0:T(8,128)S(1)} %reduce_sum.9), channel_id=1, source_target_pairs={{0,8},{8,16},{16,24},{24,0},{1,9},{9,17},{17,25},{25,1},{2,10},{10... | collective-permute-start | bytes 208904 | tf_op jit(solution)/shard_map/ppermute | solution.py:442
  53.4 2.5 %collective-permute-start.12 = (f32[136,128]{1,0:T(8,128)S(1)}, f32[136,128]{1,0:T(8,128)S(1)}, u32[]{:S(2)}, u32[]{:S(2)}) collective-permute-start(f32[136,128]{1,0:T(8,128)S(1)} %reduce_sum.9), channel_id=1, source_target_pairs={{0,24},{8,0},{16,8},{24,16},{1,25},{9,1},{17,9},{25,17},{2,26},{10... | collective-permute-start | bytes 208904 | tf_op jit(solution)/shard_map/ppermute | solution.py:442
  56.0 3.0 %collective-permute-done.10 = f32[136,128]{1,0:T(8,128)S(1)} collective-permute-done((f32[136,128]{1,0:T(8,128)S(1)}, f32[136,128]{1,0:T(8,128)S(1)}, u32[]{:S(2)}, u32[]{:S(2)}) %collective-permute-start.10) | collective-permute-done | bytes 69664 | tf_op jit(solution)/shard_map/ppermute | solution.py:442
  58.9 0.4 collective-permute-done.11
  59.3 1.7 %collective-permute-done.12 = f32[136,128]{1,0:T(8,128)S(1)} collective-permute-done((f32[136,128]{1,0:T(8,128)S(1)}, f32[136,128]{1,0:T(8,128)S(1)}, u32[]{:S(2)}, u32[]{:S(2)}) %collective-permute-start.12) | collective-permute-done | bytes 69664 | tf_op jit(solution)/shard_map/ppermute | solution.py:442
  61.0 0.0 copy-start.6
  61.0 0.1 broadcast_in_dim.15
  61.1 0.0 copy-start.4
  61.1 16.1 %all_to_all.18 = f32[16,136,128]{2,1,0:T(8,128)S(1)} all-to-all(f32[16,136,128]{2,1,0:T(8,128)S(1)} %broadcast_in_dim.15), channel_id=1, replica_groups={{0,4,34,38,64,68,98,102,130,134,160,164,194,198,224,228},{2,6,32,36,66,..., dimensions={0} | all-to-all | bytes 2228224 | tf_op jit(solution)/shard_map/all_to_all | solution.py:370
  77.2 0.1 cut.1
  77.3 3.0 %collective-permute-start.16 = (f32[512,128]{1,0:T(8,128)S(1)}, f32[512,128]{1,0:T(8,128)S(1)}, u32[]{:S(2)}, u32[]{:S(2)}) collective-permute-start(f32[512,128]{1,0:T(8,128)S(1)} %get-tuple-element.36), channel_id=1, source_target_pairs={{0,2},{2,0},{4,6},{6,4},{1,3},{3,1},{5,7},{7,5},{8,10},{10,8},{12,... | collective-permute-start | bytes 786440 | tf_op jit(solution)/shard_map/ppermute | solution.py:378
  80.3 0.4 collective-permute-start.17
  80.7 1.1 %collective-permute-start.13 = (f32[640,128]{1,0:T(8,128)S(1)}, f32[640,128]{1,0:T(8,128)S(1)}, u32[]{:S(2)}, u32[]{:S(2)}) collective-permute-start(f32[640,128]{1,0:T(8,128)S(1)} %get-tuple-element.33), channel_id=1, source_target_pairs={{0,128},{128,0},{1,129},{129,1},{2,130},{130,2},{3,131},{131,3},{4... | collective-permute-start | bytes 983048 | tf_op jit(solution)/shard_map/ppermute | solution.py:378
  81.8 0.9 collective-permute-start.14
  82.7 0.5 collective-permute-start.15
  83.2 1.7 %collective-permute-done.17.from_1 = f32[384,128]{1,0:T(8,128)S(1)} collective-permute-done((f32[384,128]{1,0:T(8,128)S(1)}, f32[384,128]{1,0:T(8,128)S(1)}, u32[]{:S(2)}, u32[]{:S(2)}) %collective-permute-start.17) | collective-permute-done | bytes 196640 | tf_op jit(solution)/shard_map/ppermute | solution.py:378
  84.9 0.0 collective-permute-done.16.from_0
  84.9 2.4 %natural.1 = (f32[896,256]{1,0:T(8,128)S(1)}, f32[1,128]{1,0:T(1,128)S(1)}) custom-call(f32[2176,128]{1,0:T(8,128)S(1)} %bitcast.13, f32[512,128]{1,0:T(8,128)S(1)} %collective-permute-done.16.from_0, f32[384,128]{1,0:T(8,128)S(1)} %collective-permute-done.17.from_1, f32[896,896]{1,0:T(8,128)S(1)} %bitcast.20, f32[256,256]{1,0:T(8,128)S(1)} %bitcast.21), custom_call_target="tpu_custom_call" | custom-call | flops 1500000000 | bytes 5000000 | tf_op jit(solution)/shard_map/natural/pallas_call | solution.py:449
  87.3 6.7 %collective-permute-start.18 = (f32[1,128]{1,0:T(1,128)S(1)}, f32[1,128]{1,0:T(1,128)S(1)}, u32[]{:S(2)}, u32[]{:S(2)}) collective-permute-start(f32[1,128]{1,0:T(1,128)S(1)} %get-tuple-element.39.curvature), channel_id=1, source_target_pairs={{0,1},{1,0},{2,3},{3,2},{4,5},{5,4},{6,7},{7,6},{8,9},{9,8},{10,11... | collective-permute-start | bytes 1544 | tf_op jit(solution)/shard_map/ppermute | solution.py:458
  93.9 0.0 collective-permute-done.15.from_4
  93.9 0.0 collective-permute-done.14.from_3
  93.9 0.8 collective-permute-done.18.other
  94.8 0.0 collective-permute-done.13.from_2
  94.8 2.3 %finish.1 = (f32[896,896]{1,0:T(8,128)}, f32[256,256]{1,0:T(8,128)}, f32[896,256]{1,0:T(8,128)}) custom-call(f32[2176,128]{1,0:T(8,128)S(1)} %bitcast.14, f32[640,128]{1,0:T(8,128)S(1)} %collective-permute-done.13.from_2, f32[384,128]{1,0:T(8,128)S(1)} %collective-permute-done.14.from_3, f32[256,128]{1,0:T(8,128)S(1)} %collective-permute-done.15.from_4, ...), custom_call_target="tpu_custom_call" | custom-call | flops 10000000 | bytes 7000000 | tf_op jit(solution)/shard_map/finish/pallas_call | solution.py:459
  (4 shorter events, 0.0 us)
Async XLA Ops:
  0.6 8.2 %copy-start.1 = (bf16[1,2,16,32,128]{4,3,2,1,0:T(8,128)(2,1)S(1)}, bf16[1,2,16,32,128]{4,3,2,1,0:T(8,128)(2,1)}, u32[]{:S(2)}) copy-start(bf16[1,2,16,32,128]{4,3,2,1,0:T(8,128)(2,1)} %param.10) | copy-start | bytes 786436
  0.6 8.2 %copy-start = (bf16[1,16,32,256]{3,2,1,0:T(8,128)(2,1)S(1)}, bf16[1,16,32,256]{3,2,1,0:T(8,128)(2,1)}, u32[]{:S(2)}) copy-start(bf16[1,16,32,256]{3,2,1,0:T(8,128)(2,1)} %param.8) | copy-start | bytes 786436
  0.7 5.6 %copy-start.2 = (bf16[1,16,32,256]{3,2,1,0:T(8,128)(2,1)S(1)}, bf16[1,16,32,256]{3,2,1,0:T(8,128)(2,1)}, u32[]{:S(2)}) copy-start(bf16[1,16,32,256]{3,2,1,0:T(8,128)(2,1)} %param.9) | copy-start | bytes 786436
  0.7 6.2 %copy-start.3 = (f32[1,16]{1,0:T(1,128)S(1)}, f32[1,16]{1,0:T(1,128)}, u32[]{:S(2)}) copy-start(f32[1,16]{1,0:T(1,128)} %near.1) | copy-start | bytes 196
  0.7 8.2 %copy-start.5 = (bf16[2,896,256]{2,1,0:T(8,128)(2,1)S(1)}, bf16[2,896,256]{2,1,0:T(8,128)(2,1)}, u32[]{:S(2)}) copy-start(bf16[2,896,256]{2,1,0:T(8,128)(2,1)} %weights.3) | copy-start | bytes 2752516
  1.8 7.0 %collective-permute-start.1 = (f32[2,512,128]{2,1,0:T(8,128)S(1)}, f32[2,512,128]{2,1,0:T(8,128)S(1)}, u32[]{:S(2)}, u32[]{:S(2)}) collective-permute-start(f32[2,512,128]{2,1,0:T(8,128)S(1)} %convert_element_type.10), channel_id=1, source_target_pairs={{0,1},{1,0},{2,3},{3,2},{4,5},{5,4},{6,7},{7,6},{8,9},{9,8},{10,11... | collective-permute-start | bytes 1572872 | tf_op jit(solution)/shard_map/ppermute | solution.py:392
  6.1 2.7 %collective-permute-start = (f32[512,256]{1,0:T(8,128)S(1)}, f32[512,256]{1,0:T(8,128)S(1)}, u32[]{:S(2)}, u32[]{:S(2)}) collective-permute-start(f32[512,256]{1,0:T(8,128)S(1)} %bitcast_convert_fusion.1), channel_id=1, source_target_pairs={{0,1},{1,0},{2,3},{3,2},{4,5},{5,4},{6,7},{7,6},{8,9},{9,8},{10,11... | collective-permute-start | bytes 1572872 | tf_op jit(solution)/shard_map/ppermute | solution.py:391
  6.3 8.2 %collective-permute-start.2 = (f32[512,256]{1,0:T(8,128)S(1)}, f32[512,256]{1,0:T(8,128)S(1)}, u32[]{:S(2)}, u32[]{:S(2)}) collective-permute-start(f32[512,256]{1,0:T(8,128)S(1)} %bitcast_convert_fusion), channel_id=1, source_target_pairs={{0,1},{1,0},{2,3},{3,2},{4,5},{5,4},{6,7},{7,6},{8,9},{9,8},{10,11... | collective-permute-start | bytes 1572872 | tf_op jit(solution)/shard_map/ppermute | solution.py:394
  6.9 3.4 %collective-permute-start.3 = (f32[1,16]{1,0:T(1,128)S(1)}, f32[1,16]{1,0:T(1,128)S(1)}, u32[]{:S(2)}, u32[]{:S(2)}) collective-permute-start(f32[1,16]{1,0:T(1,128)S(1)} %copy-done.3), channel_id=1, source_target_pairs={{0,8},{8,0},{16,24},{24,16},{1,9},{9,1},{17,25},{25,17},{2,10},{10... | collective-permute-start | bytes 200 | tf_op jit(solution)/shard_map/ppermute | solution.py:393
  10.2 7.5 %collective-permute-start.4 = (f32[1,16]{1,0:T(1,128)S(1)}, f32[1,16]{1,0:T(1,128)S(1)}, u32[]{:S(2)}, u32[]{:S(2)}) collective-permute-start(f32[1,16]{1,0:T(1,128)S(1)} %pair.1.near), channel_id=1, source_target_pairs={{8,16},{16,8},{24,0},{0,24},{9,17},{17,9},{25,1},{1,25},{10,18},{1... | collective-permute-start | bytes 200 | tf_op jit(solution)/shard_map/ppermute | solution.py:406
  17.9 12.7 %collective-permute-start.5 = (f32[904,128]{1,0:T(8,128)S(1)}, f32[904,128]{1,0:T(8,128)S(1)}, u32[]{:S(2)}, u32[]{:S(2)}) collective-permute-start(f32[904,128]{1,0:T(8,128)S(1)} %get-tuple-element.28), channel_id=1, source_target_pairs={{0,2},{2,0},{4,6},{6,4},{1,3},{3,1},{5,7},{7,5},{8,10},{10,8},{12,... | collective-permute-start | bytes 1388552 | tf_op jit(solution)/shard_map/ppermute | solution.py:432
  19.2 11.4 %collective-permute-start.6 = (f32[776,128]{1,0:T(8,128)S(1)}, f32[776,128]{1,0:T(8,128)S(1)}, u32[]{:S(2)}, u32[]{:S(2)}) collective-permute-start(f32[776,128]{1,0:T(8,128)S(1)} %get-tuple-element.29), channel_id=1, source_target_pairs={{2,4},{4,2},{6,0},{0,6},{3,5},{5,3},{7,1},{1,7},{10,12},{12,10},{1... | collective-permute-start | bytes 1191944 | tf_op jit(solution)/shard_map/ppermute | solution.py:433
  21.0 9.6 %collective-permute-start.7 = (f32[768,128]{1,0:T(8,128)S(1)}, f32[768,128]{1,0:T(8,128)S(1)}, u32[]{:S(2)}, u32[]{:S(2)}) collective-permute-start(f32[768,128]{1,0:T(8,128)S(1)} %get-tuple-element.30), channel_id=1, source_target_pairs={{0,32},{32,0},{64,96},{96,64},{1,33},{33,1},{65,97},{97,65},{2,34}... | collective-permute-start | bytes 1179656 | tf_op jit(solution)/shard_map/ppermute | solution.py:434
  22.3 8.3 %collective-permute-start.8 = (f32[640,128]{1,0:T(8,128)S(1)}, f32[640,128]{1,0:T(8,128)S(1)}, u32[]{:S(2)}, u32[]{:S(2)}) collective-permute-start(f32[640,128]{1,0:T(8,128)S(1)} %get-tuple-element.31), channel_id=1, source_target_pairs={{0,128},{128,0},{1,129},{129,1},{2,130},{130,2},{3,131},{131,3},{4... | collective-permute-start | bytes 983048 | tf_op jit(solution)/shard_map/ppermute | solution.py:435
  23.0 7.6 %collective-permute-start.9 = (f32[8,128]{1,0:T(8,128)S(1)}, f32[8,128]{1,0:T(8,128)S(1)}, u32[]{:S(2)}, u32[]{:S(2)}) collective-permute-start(f32[8,128]{1,0:T(8,128)S(1)} %get-tuple-element.32.row_sum), channel_id=1, source_target_pairs={{0,4},{2,6},{4,0},{6,2},{1,5},{3,7},{5,1},{7,3},{8,12},{10,14},{12... | collective-permute-start | bytes 12296 | tf_op jit(solution)/shard_map/ppermute | solution.py:436
  51.3 7.6 %collective-permute-start.10 = (f32[136,128]{1,0:T(8,128)S(1)}, f32[136,128]{1,0:T(8,128)S(1)}, u32[]{:S(2)}, u32[]{:S(2)}) collective-permute-start(f32[136,128]{1,0:T(8,128)S(1)} %reduce_sum.9), channel_id=1, source_target_pairs={{0,16},{8,24},{16,0},{24,8},{1,17},{9,25},{17,1},{25,9},{2,18},{10... | collective-permute-start | bytes 208904 | tf_op jit(solution)/shard_map/ppermute | solution.py:442
  52.3 7.0 %collective-permute-start.11 = (f32[136,128]{1,0:T(8,128)S(1)}, f32[136,128]{1,0:T(8,128)S(1)}, u32[]{:S(2)}, u32[]{:S(2)}) collective-permute-start(f32[136,128]{1,0:T(8,128)S(1)} %reduce_sum.9), channel_id=1, source_target_pairs={{0,8},{8,16},{16,24},{24,0},{1,9},{9,17},{17,25},{25,1},{2,10},{10... | collective-permute-start | bytes 208904 | tf_op jit(solution)/shard_map/ppermute | solution.py:442
  53.4 7.6 %collective-permute-start.12 = (f32[136,128]{1,0:T(8,128)S(1)}, f32[136,128]{1,0:T(8,128)S(1)}, u32[]{:S(2)}, u32[]{:S(2)}) collective-permute-start(f32[136,128]{1,0:T(8,128)S(1)} %reduce_sum.9), channel_id=1, source_target_pairs={{0,24},{8,0},{16,8},{24,16},{1,25},{9,1},{17,9},{25,17},{2,26},{10... | collective-permute-start | bytes 208904 | tf_op jit(solution)/shard_map/ppermute | solution.py:442
  61.0 23.9 %copy-start.6 = (f32[1,256,256]{2,1,0:T(8,128)S(1)}, f32[1,256,256]{2,1,0:T(8,128)}, u32[]{:S(2)}) copy-start(f32[1,256,256]{2,1,0:T(8,128)} %param.15) | copy-start | bytes 786436
  61.1 23.8 %copy-start.4 = (f32[1,896,896]{2,1,0:T(8,128)S(1)}, f32[1,896,896]{2,1,0:T(8,128)}, u32[]{:S(2)}) copy-start(f32[1,896,896]{2,1,0:T(8,128)} %param.14) | copy-start | bytes 9633796
  77.3 7.6 %collective-permute-start.16 = (f32[512,128]{1,0:T(8,128)S(1)}, f32[512,128]{1,0:T(8,128)S(1)}, u32[]{:S(2)}, u32[]{:S(2)}) collective-permute-start(f32[512,128]{1,0:T(8,128)S(1)} %get-tuple-element.36), channel_id=1, source_target_pairs={{0,2},{2,0},{4,6},{6,4},{1,3},{3,1},{5,7},{7,5},{8,10},{10,8},{12,... | collective-permute-start | bytes 786440 | tf_op jit(solution)/shard_map/ppermute | solution.py:378
  80.3 4.6 %collective-permute-start.17 = (f32[384,128]{1,0:T(8,128)S(1)}, f32[384,128]{1,0:T(8,128)S(1)}, u32[]{:S(2)}, u32[]{:S(2)}) collective-permute-start(f32[384,128]{1,0:T(8,128)S(1)} %get-tuple-element.37), channel_id=1, source_target_pairs={{0,32},{32,0},{64,96},{96,64},{1,33},{33,1},{65,97},{97,65},{2,34}... | collective-permute-start | bytes 589832 | tf_op jit(solution)/shard_map/ppermute | solution.py:378
  80.7 14.0 %collective-permute-start.13 = (f32[640,128]{1,0:T(8,128)S(1)}, f32[640,128]{1,0:T(8,128)S(1)}, u32[]{:S(2)}, u32[]{:S(2)}) collective-permute-start(f32[640,128]{1,0:T(8,128)S(1)} %get-tuple-element.33), channel_id=1, source_target_pairs={{0,128},{128,0},{1,129},{129,1},{2,130},{130,2},{3,131},{131,3},{4... | collective-permute-start | bytes 983048 | tf_op jit(solution)/shard_map/ppermute | solution.py:378
  81.8 12.2 %collective-permute-start.14 = (f32[384,128]{1,0:T(8,128)S(1)}, f32[384,128]{1,0:T(8,128)S(1)}, u32[]{:S(2)}, u32[]{:S(2)}) collective-permute-start(f32[384,128]{1,0:T(8,128)S(1)} %get-tuple-element.34), channel_id=1, source_target_pairs={{2,4},{4,2},{6,0},{0,6},{3,5},{5,3},{7,1},{1,7},{10,12},{12,10},{1... | collective-permute-start | bytes 589832 | tf_op jit(solution)/shard_map/ppermute | solution.py:378
  82.7 11.3 %collective-permute-start.15 = (f32[256,128]{1,0:T(8,128)S(1)}, f32[256,128]{1,0:T(8,128)S(1)}, u32[]{:S(2)}, u32[]{:S(2)}) collective-permute-start(f32[256,128]{1,0:T(8,128)S(1)} %get-tuple-element.35), channel_id=1, source_target_pairs={{32,64},{64,32},{96,0},{0,96},{33,65},{65,33},{97,1},{1,97},{34,66... | collective-permute-start | bytes 393224 | tf_op jit(solution)/shard_map/ppermute | solution.py:378
  87.3 7.5 %collective-permute-start.18 = (f32[1,128]{1,0:T(1,128)S(1)}, f32[1,128]{1,0:T(1,128)S(1)}, u32[]{:S(2)}, u32[]{:S(2)}) collective-permute-start(f32[1,128]{1,0:T(1,128)S(1)} %get-tuple-element.39.curvature), channel_id=1, source_target_pairs={{0,1},{1,0},{2,3},{3,2},{4,5},{5,4},{6,7},{7,6},{8,9},{9,8},{10,11... | collective-permute-start | bytes 1544 | tf_op jit(solution)/shard_map/ppermute | solution.py:458

commit v14 on v13

--- a/solution.py
+++ b/solution.py
@@ -13,8 +13,12 @@
 SLOTS = 17
 KEPT = SLOTS * B
 CHUNK = KEPT // GROUP
-GRADS, FACTORS = 7, 10
-OUT_STREAMS = ((0, 6), (6, 12), (12, 17))
+HALVES = (
+    (19, 20, 21, 23, 24, 25, 26, 0, 1, 10, 11, 2, 3, 6, 7, 13, 14),
+    (22, 31, 32, 27, 28, 29, 30, 12, 17, 18, 33, 4, 5, 8, 9, 15, 16),
+)
+GRADS, FACTORS = 3, 4
+DIRECT = (0, 1, 2, 7, 8, 9, 10)
 BACK_STREAMS = ((0, 4), (4, 7), (7, 12), (12, 15), (15, 17))
 ENTRIES = 2 * DIN * D
 SHIFT = 7.0
@@ -56,11 +60,8 @@
 
 
 def place_of(slot):
-    if 19 <= slot < 33:
-        half, place = divmod(slot - 19, GRADS)
-        return half, place
-    half, place = divmod(slot if slot < 19 else 19, FACTORS)
-    return half, place + GRADS
+    half = 0 if slot in HALVES[0] else 1
+    return half, HALVES[half].index(slot)
 
 
 def forward_kernel(feat, pair, oth_feat, oth_pair, weights, x_s, d_s, m_s):
@@ -95,7 +96,7 @@
     sums[...] = near[...] + far[...]
 
 
-def factors_kernel(x_s, d_s, m_s, psi, oth_psi, weights, energies, energy, multiplicity, out, out_0, s_s, w_s):
+def factors_kernel(x_s, d_s, m_s, psi, oth_psi, weights, energies, energy, multiplicity, out, out_0, fac, s_s, w_s):
     mp = lax.axis_index("c")
     own_row = pl.multiple_of(D + D * mp, D)
     oth_row = pl.multiple_of(2 * D - D * mp, D)
@@ -131,15 +132,15 @@
     with_h = dot_t(w_s[:, :D], w_s[...])
     with_p = dot_t(w_s[:, at_p:at_c], w_s[:, at_p:])
     with_s = dot_t(w_s[:, at_s:], w_s[:, at_s:])
-    totals = dot(pick, w_s[:, at_p:])
-    totals = totals[:WALK] + totals[WALK:]
+    p_sum, s_sum = dot(pick, w_s[:, at_p:at_c]), dot(pick, w_s[:, at_s:])
     row, col = square_iotas()
 
     parity = own_parity()
 
     def put(slot, value):
         half, place = place_of(slot)
-        out[parity ^ half, place * B : (place + 1) * B, :] = value * row_scale
+        first = DIRECT.index(place) * B
+        out[parity ^ half, first : first + B, :] = value * row_scale
 
     def put_grad(slot, centered, plain):
         half, place = place_of(slot)
@@ -170,58 +171,87 @@
         put_grad(31 + j, pc[:, cols], ps[:, cols])
     put_symmetric(17, 3, with_s)
 
-    means = m_s[l]
+    means = m_s[l].astype(F32)
     up_first = mp == 0
-    up = jnp.where(up_first, means[:WALK].astype(F32), means[WALK:].astype(F32)).astype(BF16)
-    down = jnp.where(up_first, means[WALK:].astype(F32), means[:WALK].astype(F32)).astype(BF16)
-    both = jnp.concatenate([up, down], 1)
-    mm = dot_t(both, both) * 64.0
-    put_symmetric(2, 1, mm[:D, :D])
-    put_symmetric(4, 2, mm[D:, D:])
-    for i in range(2):
-        for j in range(2):
-            put(6 + 2 * i + j, mm[i * B : (i + 1) * B, D + j * B : D + (j + 1) * B])
-    totals = jnp.concatenate(
-        [totals[:, :PAIR], totals[:, PAIR : PAIR + D] + totals[:, PAIR + D : PAIR + 2 * D], totals[:, PAIR + 2 * D :]], 1
-    )
-    t_high, t_low = split(totals)
-    side = dot_t(jnp.concatenate([both, both], 0), jnp.concatenate([t_high, t_low], 0))
-    for i in range(4):
-        rows = slice(i * B, (i + 1) * B)
-        put(13 + i, side[rows, :B])
-        for j in range(2):
-            at = (1 + j) * B
-            put_grad(23 + 2 * i + j, side[rows, at : at + B], side[rows, at + D : at + D + B])
+    up = jnp.where(up_first, means[:WALK], means[WALK:])
+    down = jnp.where(up_first, means[WALK:], means[:WALK])
+    p_sum, s_sum = p_sum[:WALK] + p_sum[WALK:], s_sum[:WALK] + s_sum[WALK:]
+    for j, value in enumerate(
+        (up[:, :B], up[:, B:], down[:, :B], down[:, B:], p_sum, s_sum[:, :B], s_sum[:, B:])
+    ):
+        fac[j * WALK : (j + 1) * WALK, :] = value
+    for w in range(WALK):
+        fac[7 * WALK + w : 7 * WALK + w + 1, :] = jnp.full((1, B), energy[0, w], F32)
+
     lines[4] = jnp.full((1, B), mult * (1.0 / 16.0), F32)
-    last = KEPT - B
-    out[parity ^ 1, last:, :] = jnp.zeros((B, B), F32)
+    half, place = place_of(33)
+    first = DIRECT.index(place) * B
+    out[parity ^ half, first : first + B, :] = jnp.zeros((B, B), F32)
     for line, value in lines.items():
-        out[parity ^ 1, last + line : last + line + 1, :] = value
-
-
-def tie_kernel(out, out_0, near, far, to_0, to_1, to_2, to_3, row_sum):
+        out[parity ^ half, first + line : first + line + 1, :] = value
+
+
+def tie_kernel(out, out_0, fac, near, far, to_0, to_1, to_2, row_sum):
     zh_sum = jnp.sum(near[...] + far[...], axis=1, keepdims=True)
     row_sum[...] = jnp.broadcast_to(zh_sum, (8, B))
     grads = GRADS * B
-    to_0[:grads, :] = out_0[1]
-    to_0[grads:, :] = row_sum[...]
-    for target, (first, end) in zip((to_1, to_2, to_3), OUT_STREAMS):
-        target[: (end - first) * B, :] = out[1, first * B : end * B, :]
-    to_1[OUT_STREAMS[0][1] * B :, :] = row_sum[...]
-
-
-def add_kernel(out, out_0, from_0, from_1, from_2, from_3, row_sum, row_two, total):
+    to_0[:B, :] = fac[...]
+    to_0[B : B + grads, :] = out_0[1]
+    to_0[B + grads :, :] = row_sum[...]
+    to_1[:grads, :] = out[1, :grads, :]
+    to_1[grads:, :] = row_sum[...]
+    to_2[...] = out[1, grads:, :]
+
+
+def add_kernel(out, out_0, fac, from_0, from_1, from_2, row_sum, row_two, multiplicity, total):
+    parity = own_parity()
     grads = GRADS * B
-    near, far = from_0[grads:, :], from_1[OUT_STREAMS[0][1] * B :, :]
-    energy = (row_sum[...] + row_two[...]) + (near + far)
-    shifted = energy[:1, :] * (1.0 / 256.0) + SHIFT
-    for part, (first, end) in zip((from_1, from_2, from_3), OUT_STREAMS):
-        for place in range(first, end):
-            rows = slice(place * B, (place + 1) * B)
-            value = out[0, rows, :] + part[(place - first) * B : (place - first + 1) * B, :]
-            if place < GRADS:
-                value = value - shifted * (out_0[0, rows, :] + from_0[rows, :])
-            total[rows, :] = value
+    energy = (row_sum[...] + row_two[...]) + (from_0[B + grads :, :] + from_1[grads:, :])
+    mean = energy[:1, :] * (1.0 / 256.0)
+    plain = out_0[0] + from_0[B : B + grads, :]
+    total[:grads, :] = (out[0, :grads, :] + from_1[:grads, :]) - (mean + SHIFT) * plain
+    first = DIRECT[GRADS] * B
+    total[first : first + FACTORS * B, :] = out[0, grads:, :] + from_2[...]
+
+    def part(j):
+        rows = slice(j * WALK, (j + 1) * WALK)
+        return jnp.concatenate([fac[rows, :], from_0[rows, :]], 0)
+
+    row_scale = multiplicity[0].astype(F32) * (1.0 / 16384.0)
+    both = jnp.concatenate([part(j) for j in range(4)], 1).astype(BF16)
+    centered = part(7) - mean
+    sums = jnp.concatenate([part(4), part(5) * centered, part(6) * centered], 1)
+    high, low = split(sums)
+    side = dot_t(jnp.concatenate([both, both], 0), jnp.concatenate([high, low], 0)) * row_scale
+    mm = dot_t(both, both) * (64.0 * row_scale)
+    row, col = square_iotas()
+    blocks, lines = {}, {}
+    for slot, line, full in ((2, 1, mm[:D, :D]), (4, 2, mm[D:, D:])):
+        last = full[B:, B:]
+        blocks[slot] = jnp.where(col >= row, full[:B, :B], last)
+        blocks[slot + 1] = full[:B, B:]
+        lines[line] = jnp.sum(jnp.where(col == row, last, 0.0), axis=0, keepdims=True)
+    for i in range(2):
+        for j in range(2):
+            blocks[6 + 2 * i + j] = mm[i * B : (i + 1) * B, D + j * B : D + (j + 1) * B]
+    for i in range(4):
+        rows = slice(i * B, (i + 1) * B)
+        blocks[13 + i] = side[rows, :B]
+        for j in range(2):
+            blocks[23 + 2 * i + j] = side[rows, (1 + j) * B : (2 + j) * B]
+
+    for half in range(2):
+
+        @pl.when(parity == half)
+        def _():
+            for slot, value in blocks.items():
+                if place_of(slot)[0] == half:
+                    place = place_of(slot)[1]
+                    total[place * B : (place + 1) * B, :] = value
+            if half == place_of(33)[0]:
+                base = place_of(33)[1] * B
+                for line, value in lines.items():
+                    total[base + line : base + line + 1, :] = value
 
 
 def cut_kernel(kept, to_0, to_1, to_2, to_3, to_4):
@@ -406,9 +436,9 @@
     far_2 = lax.ppermute(sum_2, "zh", HIGH)
 
     grads = GRADS * B
-    out, out_0 = call(
+    out, out_0, fac = call(
         factors_kernel,
-        [((2, KEPT, B), F32), ((2, grads, B), F32)],
+        [((2, len(DIRECT) * B, B), F32), ((2, grads, B), F32), ((B, B), F32)],
         [V] * 7 + [S] * 2,
         24,
         "factors",
@@ -420,23 +450,21 @@
         moved=8_000_000,
     )(x_s, d_s, m_s, psi, oth_psi, weights, energies, energies, multiplicity)
 
-    sizes = [((end - first) * B, B) for first, end in OUT_STREAMS]
-    to_0, to_1, to_2, to_3, row_sum = call(
+    to_0, to_1, to_2, row_sum = call(
         tie_kernel,
-        [((grads + 8, B), F32), ((sizes[0][0] + 8, B), F32), (sizes[1], F32), (sizes[2], F32), ((8, B), F32)],
-        [V] * 4,
-        8,
+        [((B + grads + 8, B), F32), ((grads + 8, B), F32), ((FACTORS * B, B), F32), ((8, B), F32)],
+        [V] * 5,
+        6,
         "tie",
-        moved=3_000_000,
-    )(out, out_0, sum_2, far_2)
+        moved=2_000_000,
+    )(out, out_0, fac, sum_2, far_2)
     from_0 = lax.ppermute(to_0, "x", LOW)
+    from_2 = lax.ppermute(to_2, "y", LOW)
     from_1 = lax.ppermute(to_1, "x", HIGH)
-    from_2 = lax.ppermute(to_2, "y", LOW)
-    from_3 = lax.ppermute(to_3, "zl", swap)
     row_two = lax.ppermute(row_sum, "x", [(0, 2), (1, 3), (2, 0), (3, 1)])
-    (total,) = call(add_kernel, [((KEPT, B), F32)], [V] * 8, 10, "add", moved=3_000_000)(
-        out, out_0, from_0, from_1, from_2, from_3, row_sum, row_two
-    )
+    (total,) = call(
+        add_kernel, [((KEPT, B), F32)], [V] * 8 + [S], 12, "add", flops=50_000_000, moved=3_000_000
+    )(out, out_0, fac, from_0, from_1, from_2, row_sum, row_two, multiplicity)
     mine = jnp.sum(same_parity(total).reshape(GROUP, CHUNK, B), axis=0)
     one, two, three = (
         lax.ppermute(mine, "zh", [(i, (i + k) % 4) for i in range(4)]) for k in (1, 2, 3)

time: 97.4 us -> 94.3 us (0.968)
  starting transfers between devices: 32.5 us -> 28.1 us
  blocking collectives: 36.5 us -> 40.6 us
  waiting for transfers between devices: 14.5 us -> 12 us
    all_to_all x2, blocking collectives: 36.5 us -> 40.6 us  [same_parity(): lax.all_to_all(value, axes, 0, 0, axis_index_groups=parity_groups(), tile...]
    ppermute x1, waiting for transfers between devices: 6.93 us -> 3.46 us  [body(): row_two = lax.ppermute(row_sum, 'x', [(0, 2), (1, 3), (2, 0), (3, 1)])]
    ppermute x1, starting transfers between devices: 3.33 us -> 0.1 us  [body(): oth_pair = lax.ppermute(pair.astype(F32), 'c', swap)]
    ppermute x1, starting transfers between devices: 0.1 us -> 3.33 us  [body(): oth_feat = lax.ppermute(feat.astype(F32), 'c', swap)]
    ppermute x5, starting transfers between devices: 5.89 us -> 2.81 us  [to_neighbours(): lax.ppermute(part, axis, pairs)]
  transfers between devices with their start and end apart: 19 -> 18, of which waited for: 6 -> 7; matrix products, arithmetic and copies ran while one was open for 1% -> 1% of each run, Pallas kernels for 7% -> 7%
where the time goes in v14:
time: 94.3 us; the launch traced here: 94.2 us
  blocking collectives  40.6 us (43%)
  starting transfers between devices  28.1 us (30%)
  waiting for transfers between devices  12 us (13%)
  Pallas kernels  9.51 us (10%)
  other arithmetic  2.22 us (2%)
  between operations  1.65 us (2%)
    all_to_all x2, blocking collectives, same_parity(): lax.all_to_all(value, axes, 0, 0, axis_index_groups=parity_groups(), tile...  40.6 us
    ppermute x1, starting transfers between devices, body(): other = lax.ppermute(curvature, 'c', swap)  6.15 us
    ppermute x3, waiting for transfers between devices, body(): lax.ppermute(mine, 'zh', [(i, (i + k) % 4) for i in range(4)])  4.97 us
    ppermute x3, starting transfers between devices, body(): lax.ppermute(mine, 'zh', [(i, (i + k) % 4) for i in range(4)])  4.58 us
    ppermute x1, starting transfers between devices, body(): far_2 = lax.ppermute(sum_2, 'zh', HIGH)  4.29 us
    ppermute x1, waiting for transfers between devices, body(): row_two = lax.ppermute(row_sum, 'x', [(0, 2), (1, 3), (2, 0), (3, 1)])  3.46 us
    ppermute x1, starting transfers between devices, body(): oth_feat = lax.ppermute(feat.astype(F32), 'c', swap)  3.33 us
    ppermute x5, starting transfers between devices, to_neighbours(): lax.ppermute(part, axis, pairs)  2.81 us
  transfers between devices with their start and end apart: 18, of which 7 were waited for; matrix products, arithmetic and copies ran while one was open for 1% of the time, Pallas kernels for 7%

profile of v14, /device:TPU:1, one launch (start us, length us, event | category | flops | bytes accessed | tf_op | source)
XLA Modules:
  0.0 94.2 jit_solution(10945775846023860930)
XLA Ops:
  0.6 0.0 copy-start
  0.6 0.0 copy-start.1
  0.7 0.0 copy-start.2
  0.7 0.0 copy-start.3
  0.7 0.0 copy-start.5
  0.7 1.1 %bitcast_convert_fusion.1 = f32[512,256]{1,0:T(8,128)S(1)} fusion(bf16[1,16,32,256]{3,2,1,0:T(8,128)(2,1)} %param.8), kind=kLoop, calls=%fused_computation.2 | loop fusion | flops 131072 | bytes 786432 | tf_op jit(solution)/shard_map/convert_element_type | solution.py:421
  1.8 3.3 %collective-permute-start = (f32[512,256]{1,0:T(8,128)S(1)}, f32[512,256]{1,0:T(8,128)S(1)}, u32[]{:S(2)}, u32[]{:S(2)}) collective-permute-start(f32[512,256]{1,0:T(8,128)S(1)} %bitcast_convert_fusion.1), channel_id=1, source_target_pairs={{0,1},{1,0},{2,3},{3,2},{4,5},{5,4},{6,7},{7,6},{8,9},{9,8},{10,11... | collective-permute-start | bytes 1572872 | tf_op jit(solution)/shard_map/ppermute | solution.py:421
  5.1 1.0 %convert_element_type.10 = f32[2,512,128]{2,1,0:T(8,128)S(1)} convert(bf16[2,512,128]{2,1,0:T(8,128)(2,1)} %bitcast.17) | non-fusion elementwise | flops 131072 | bytes 786432 | tf_op jit(solution)/shard_map/convert_element_type | solution.py:422
  6.1 0.1 collective-permute-start.1
  6.2 0.0 copy-done.2
  6.2 0.1 bitcast_convert_fusion
  6.3 0.6 collective-permute-start.2
  6.8 0.0 copy-done.3
  6.9 1.3 %collective-permute-start.3 = (f32[1,16]{1,0:T(1,128)S(1)}, f32[1,16]{1,0:T(1,128)S(1)}, u32[]{:S(2)}, u32[]{:S(2)}) collective-permute-start(f32[1,16]{1,0:T(1,128)S(1)} %copy-done.3), channel_id=1, source_target_pairs={{0,8},{8,0},{16,24},{24,16},{1,9},{9,1},{17,25},{25,17},{2,10},{10... | collective-permute-start | bytes 200 | tf_op jit(solution)/shard_map/ppermute | solution.py:423
  8.8 0.0 collective-permute-done.oth_feat
  8.8 0.0 collective-permute-done.1.oth_pair
  8.8 0.0 copy-done
  8.8 0.0 copy-done.1
  8.8 0.0 copy-done.5
  8.8 1.4 %forward.1 = (bf16[2,1024,384]{2,1,0:T(8,128)(2,1)S(1)}, f32[2,1024,256]{2,1,0:T(8,128)S(1)}, bf16[2,32,256]{2,1,0:T(8,128)(2,1)S(1)}) custom-call(bf16[512,256]{1,0:T(8,128)(2,1)S(1)} %bitcast.16, bf16[2,512,128]{2,1,0:T(8,128)(2,1)S(1)} %bitcast.18, f32[512,256]{1,0:T(8,128)S(1)} %collective-permute-done.oth_feat, ...), custom_call_target="tpu_custom_call" | custom-call | flops 1000000000 | bytes 6000000 | tf_op jit(solution)/shard_map/forward/pallas_call | solution.py:426
  10.2 0.0 collective-permute-done.3.far
  10.2 4.3 %collective-permute-start.4 = (f32[1,16]{1,0:T(1,128)S(1)}, f32[1,16]{1,0:T(1,128)S(1)}, u32[]{:S(2)}, u32[]{:S(2)}) collective-permute-start(f32[1,16]{1,0:T(1,128)S(1)} %pair.1.near), channel_id=1, source_target_pairs={{8,16},{16,8},{24,0},{0,24},{9,17},{17,9},{25,1},{1,25},{10,18},{1... | collective-permute-start | bytes 200 | tf_op jit(solution)/shard_map/ppermute | solution.py:436
  14.5 0.0 collective-permute-done.2.oth_psi
  14.5 2.8 %factors.1 = (f32[2,896,128]{2,1,0:T(8,128)S(1)}, f32[2,384,128]{2,1,0:T(8,128)S(1)}, f32[128,128]{1,0:T(8,128)S(1)}) custom-call(bf16[2,1024,384]{2,1,0:T(8,128)(2,1)S(1)} %get-tuple-element.23.x_s, f32[2,1024,256]{2,1,0:T(8,128)S(1)} %get-tuple-element.24.d_s, bf16[2,32,256]{2,1,0:T(8,128)(2,1)S(1)} %get-tuple-element.25.m_s.after, ...), custom_call_target="tpu_custom_call" | custom-call | flops 2500000000 | bytes 8000000 | tf_op jit(solution)/shard_map/factors/pallas_call | solution.py:439
  17.3 0.0 collective-permute-done.4.far
  17.3 0.1 tie.1
  17.4 1.3 %collective-permute-start.5 = (f32[520,128]{1,0:T(8,128)S(1)}, f32[520,128]{1,0:T(8,128)S(1)}, u32[]{:S(2)}, u32[]{:S(2)}) collective-permute-start(f32[520,128]{1,0:T(8,128)S(1)} %get-tuple-element.29), channel_id=1, source_target_pairs={{0,2},{2,0},{4,6},{6,4},{1,3},{3,1},{5,7},{7,5},{8,10},{10,8},{12,... | collective-permute-start | bytes 798728 | tf_op jit(solution)/shard_map/ppermute | solution.py:461
  18.7 1.3 %collective-permute-start.7 = (f32[512,128]{1,0:T(8,128)S(1)}, f32[512,128]{1,0:T(8,128)S(1)}, u32[]{:S(2)}, u32[]{:S(2)}) collective-permute-start(f32[512,128]{1,0:T(8,128)S(1)} %get-tuple-element.31), channel_id=1, source_target_pairs={{0,32},{32,0},{64,96},{96,64},{1,33},{33,1},{65,97},{97,65},{2,34}... | collective-permute-start | bytes 786440 | tf_op jit(solution)/shard_map/ppermute | solution.py:462
  20.0 1.8 %collective-permute-start.6 = (f32[392,128]{1,0:T(8,128)S(1)}, f32[392,128]{1,0:T(8,128)S(1)}, u32[]{:S(2)}, u32[]{:S(2)}) collective-permute-start(f32[392,128]{1,0:T(8,128)S(1)} %get-tuple-element.30), channel_id=1, source_target_pairs={{2,4},{4,2},{6,0},{0,6},{3,5},{5,3},{7,1},{1,7},{10,12},{12,10},{1... | collective-permute-start | bytes 602120 | tf_op jit(solution)/shard_map/ppermute | solution.py:463
  21.8 0.6 collective-permute-start.8
  22.4 3.5 %collective-permute-done.8.row_two = f32[8,128]{1,0:T(8,128)S(1)} collective-permute-done((f32[8,128]{1,0:T(8,128)S(1)}, f32[8,128]{1,0:T(8,128)S(1)}, u32[]{:S(2)}, u32[]{:S(2)}) %collective-permute-start.8) | collective-permute-done | bytes 4128 | tf_op jit(solution)/shard_map/ppermute | solution.py:464
  25.9 0.0 collective-permute-done.6.from_1
  25.9 0.0 collective-permute-done.7.from_2
  25.9 0.0 collective-permute-done.5.from_0
  25.9 0.5 add.16
  26.4 21.0 %all_to_all.17 = f32[16,136,128]{2,1,0:T(8,128)S(1)} all-to-all(f32[16,136,128]{2,1,0:T(8,128)S(1)} %bitcast.15), channel_id=1, replica_groups={{0,4,34,38,64,68,98,102,130,134,160,164,194,198,224,228},{2,6,32,36,66,..., dimensions={0} | all-to-all | bytes 2228224 | tf_op jit(solution)/shard_map/all_to_all | solution.py:400
  47.5 0.1 reduce_sum.9
  47.5 0.9 collective-permute-start.11
  48.4 1.5 %collective-permute-start.10 = (f32[136,128]{1,0:T(8,128)S(1)}, f32[136,128]{1,0:T(8,128)S(1)}, u32[]{:S(2)}, u32[]{:S(2)}) collective-permute-start(f32[136,128]{1,0:T(8,128)S(1)} %reduce_sum.9), channel_id=1, source_target_pairs={{0,8},{8,16},{16,24},{24,0},{1,9},{9,17},{17,25},{25,1},{2,10},{10... | collective-permute-start | bytes 208904 | tf_op jit(solution)/shard_map/ppermute | solution.py:470
  50.0 2.1 %collective-permute-start.9 = (f32[136,128]{1,0:T(8,128)S(1)}, f32[136,128]{1,0:T(8,128)S(1)}, u32[]{:S(2)}, u32[]{:S(2)}) collective-permute-start(f32[136,128]{1,0:T(8,128)S(1)} %reduce_sum.9), channel_id=1, source_target_pairs={{0,16},{8,24},{16,0},{24,8},{1,17},{9,25},{17,1},{25,9},{2,18},{10... | collective-permute-start | bytes 208904 | tf_op jit(solution)/shard_map/ppermute | solution.py:470
  52.1 0.3 collective-permute-done.11
  52.4 1.3 %collective-permute-done.10 = f32[136,128]{1,0:T(8,128)S(1)} collective-permute-done((f32[136,128]{1,0:T(8,128)S(1)}, f32[136,128]{1,0:T(8,128)S(1)}, u32[]{:S(2)}, u32[]{:S(2)}) %collective-permute-start.10) | collective-permute-done | bytes 69664 | tf_op jit(solution)/shard_map/ppermute | solution.py:470
  53.7 3.3 %collective-permute-done.9 = f32[136,128]{1,0:T(8,128)S(1)} collective-permute-done((f32[136,128]{1,0:T(8,128)S(1)}, f32[136,128]{1,0:T(8,128)S(1)}, u32[]{:S(2)}, u32[]{:S(2)}) %collective-permute-start.9) | collective-permute-done | bytes 69664 | tf_op jit(solution)/shard_map/ppermute | solution.py:470
  57.1 0.0 copy-start.6
  57.1 0.1 broadcast_in_dim.15
  57.2 0.0 copy-start.4
  57.2 19.6 %all_to_all.18 = f32[16,136,128]{2,1,0:T(8,128)S(1)} all-to-all(f32[16,136,128]{2,1,0:T(8,128)S(1)} %broadcast_in_dim.15), channel_id=1, replica_groups={{0,4,34,38,64,68,98,102,130,134,160,164,194,198,224,228},{2,6,32,36,66,..., dimensions={0} | all-to-all | bytes 2228224 | tf_op jit(solution)/shard_map/all_to_all | solution.py:400
  76.8 0.1 cut.1
  76.8 0.3 collective-permute-start.15
  77.1 0.4 collective-permute-start.16
  77.5 0.0 collective-permute-start.12
  77.5 0.9 collective-permute-start.13
  78.4 1.2 %collective-permute-start.14 = (f32[256,128]{1,0:T(8,128)S(1)}, f32[256,128]{1,0:T(8,128)S(1)}, u32[]{:S(2)}, u32[]{:S(2)}) collective-permute-start(f32[256,128]{1,0:T(8,128)S(1)} %get-tuple-element.35), channel_id=1, source_target_pairs={{32,64},{64,32},{96,0},{0,96},{33,65},{65,33},{97,1},{1,97},{34,66... | collective-permute-start | bytes 393224 | tf_op jit(solution)/shard_map/ppermute | solution.py:408
  79.7 2.1 %collective-permute-done.16.from_1 = f32[384,128]{1,0:T(8,128)S(1)} collective-permute-done((f32[384,128]{1,0:T(8,128)S(1)}, f32[384,128]{1,0:T(8,128)S(1)}, u32[]{:S(2)}, u32[]{:S(2)}) %collective-permute-start.16) | collective-permute-done | bytes 196640 | tf_op jit(solution)/shard_map/ppermute | solution.py:408
  81.8 0.6 collective-permute-done.15.from_0
  82.3 0.0 copy-done.6
  82.3 0.0 copy-done.4
  82.3 2.4 %natural.1 = (f32[896,256]{1,0:T(8,128)S(1)}, f32[1,128]{1,0:T(1,128)S(1)}) custom-call(f32[2176,128]{1,0:T(8,128)S(1)} %bitcast.13, f32[512,128]{1,0:T(8,128)S(1)} %collective-permute-done.15.from_0, f32[384,128]{1,0:T(8,128)S(1)} %collective-permute-done.16.from_1, f32[896,896]{1,0:T(8,128)S(1)} %bitcast.20, f32[256,256]{1,0:T(8,128)S(1)} %bitcast.21), custom_call_target="tpu_custom_call" | custom-call | flops 1500000000 | bytes 5000000 | tf_op jit(solution)/shard_map/natural/pallas_call | solution.py:477
  84.7 6.2 %collective-permute-start.17 = (f32[1,128]{1,0:T(1,128)S(1)}, f32[1,128]{1,0:T(1,128)S(1)}, u32[]{:S(2)}, u32[]{:S(2)}) collective-permute-start(f32[1,128]{1,0:T(1,128)S(1)} %get-tuple-element.39.curvature), channel_id=1, source_target_pairs={{0,1},{1,0},{2,3},{3,2},{4,5},{5,4},{6,7},{7,6},{8,9},{9,8},{10,11... | collective-permute-start | bytes 1544 | tf_op jit(solution)/shard_map/ppermute | solution.py:486
  90.8 0.0 collective-permute-done.14.from_4
  90.9 0.0 collective-permute-done.13.from_3
  90.9 0.8 collective-permute-done.17.other
  91.7 0.0 collective-permute-done.12.from_2
  91.7 2.3 %finish.1 = (f32[896,896]{1,0:T(8,128)}, f32[256,256]{1,0:T(8,128)}, f32[896,256]{1,0:T(8,128)}) custom-call(f32[2176,128]{1,0:T(8,128)S(1)} %bitcast.14, f32[640,128]{1,0:T(8,128)S(1)} %collective-permute-done.12.from_2, f32[384,128]{1,0:T(8,128)S(1)} %collective-permute-done.13.from_3, f32[256,128]{1,0:T(8,128)S(1)} %collective-permute-done.14.from_4, ...), custom_call_target="tpu_custom_call" | custom-call | flops 10000000 | bytes 7000000 | tf_op jit(solution)/shard_map/finish/pallas_call | solution.py:487
  (2 shorter events, 0.0 us)
Async XLA Ops:
  0.6 8.2 %copy-start = (bf16[1,16,32,256]{3,2,1,0:T(8,128)(2,1)S(1)}, bf16[1,16,32,256]{3,2,1,0:T(8,128)(2,1)}, u32[]{:S(2)}) copy-start(bf16[1,16,32,256]{3,2,1,0:T(8,128)(2,1)} %param.8) | copy-start | bytes 786436
  0.6 8.2 %copy-start.1 = (bf16[1,2,16,32,128]{4,3,2,1,0:T(8,128)(2,1)S(1)}, bf16[1,2,16,32,128]{4,3,2,1,0:T(8,128)(2,1)}, u32[]{:S(2)}) copy-start(bf16[1,2,16,32,128]{4,3,2,1,0:T(8,128)(2,1)} %param.10) | copy-start | bytes 786436
  0.7 5.6 %copy-start.2 = (bf16[1,16,32,256]{3,2,1,0:T(8,128)(2,1)S(1)}, bf16[1,16,32,256]{3,2,1,0:T(8,128)(2,1)}, u32[]{:S(2)}) copy-start(bf16[1,16,32,256]{3,2,1,0:T(8,128)(2,1)} %param.9) | copy-start | bytes 786436
  0.7 6.2 %copy-start.3 = (f32[1,16]{1,0:T(1,128)S(1)}, f32[1,16]{1,0:T(1,128)}, u32[]{:S(2)}) copy-start(f32[1,16]{1,0:T(1,128)} %near.1) | copy-start | bytes 196
  0.7 8.2 %copy-start.5 = (bf16[2,896,256]{2,1,0:T(8,128)(2,1)S(1)}, bf16[2,896,256]{2,1,0:T(8,128)(2,1)}, u32[]{:S(2)}) copy-start(bf16[2,896,256]{2,1,0:T(8,128)(2,1)} %weights.3) | copy-start | bytes 2752516
  1.8 7.0 %collective-permute-start = (f32[512,256]{1,0:T(8,128)S(1)}, f32[512,256]{1,0:T(8,128)S(1)}, u32[]{:S(2)}, u32[]{:S(2)}) collective-permute-start(f32[512,256]{1,0:T(8,128)S(1)} %bitcast_convert_fusion.1), channel_id=1, source_target_pairs={{0,1},{1,0},{2,3},{3,2},{4,5},{5,4},{6,7},{7,6},{8,9},{9,8},{10,11... | collective-permute-start | bytes 1572872 | tf_op jit(solution)/shard_map/ppermute | solution.py:421
  6.1 2.7 %collective-permute-start.1 = (f32[2,512,128]{2,1,0:T(8,128)S(1)}, f32[2,512,128]{2,1,0:T(8,128)S(1)}, u32[]{:S(2)}, u32[]{:S(2)}) collective-permute-start(f32[2,512,128]{2,1,0:T(8,128)S(1)} %convert_element_type.10), channel_id=1, source_target_pairs={{0,1},{1,0},{2,3},{3,2},{4,5},{5,4},{6,7},{7,6},{8,9},{9,8},{10,11... | collective-permute-start | bytes 1572872 | tf_op jit(solution)/shard_map/ppermute | solution.py:422
  6.3 8.2 %collective-permute-start.2 = (f32[512,256]{1,0:T(8,128)S(1)}, f32[512,256]{1,0:T(8,128)S(1)}, u32[]{:S(2)}, u32[]{:S(2)}) collective-permute-start(f32[512,256]{1,0:T(8,128)S(1)} %bitcast_convert_fusion), channel_id=1, source_target_pairs={{0,1},{1,0},{2,3},{3,2},{4,5},{5,4},{6,7},{7,6},{8,9},{9,8},{10,11... | collective-permute-start | bytes 1572872 | tf_op jit(solution)/shard_map/ppermute | solution.py:424
  6.9 3.4 %collective-permute-start.3 = (f32[1,16]{1,0:T(1,128)S(1)}, f32[1,16]{1,0:T(1,128)S(1)}, u32[]{:S(2)}, u32[]{:S(2)}) collective-permute-start(f32[1,16]{1,0:T(1,128)S(1)} %copy-done.3), channel_id=1, source_target_pairs={{0,8},{8,0},{16,24},{24,16},{1,9},{9,1},{17,25},{25,17},{2,10},{10... | collective-permute-start | bytes 200 | tf_op jit(solution)/shard_map/ppermute | solution.py:423
  10.2 7.1 %collective-permute-start.4 = (f32[1,16]{1,0:T(1,128)S(1)}, f32[1,16]{1,0:T(1,128)S(1)}, u32[]{:S(2)}, u32[]{:S(2)}) collective-permute-start(f32[1,16]{1,0:T(1,128)S(1)} %pair.1.near), channel_id=1, source_target_pairs={{8,16},{16,8},{24,0},{0,24},{9,17},{17,9},{25,1},{1,25},{10,18},{1... | collective-permute-start | bytes 200 | tf_op jit(solution)/shard_map/ppermute | solution.py:436
  17.4 8.5 %collective-permute-start.5 = (f32[520,128]{1,0:T(8,128)S(1)}, f32[520,128]{1,0:T(8,128)S(1)}, u32[]{:S(2)}, u32[]{:S(2)}) collective-permute-start(f32[520,128]{1,0:T(8,128)S(1)} %get-tuple-element.29), channel_id=1, source_target_pairs={{0,2},{2,0},{4,6},{6,4},{1,3},{3,1},{5,7},{7,5},{8,10},{10,8},{12,... | collective-permute-start | bytes 798728 | tf_op jit(solution)/shard_map/ppermute | solution.py:461
  18.7 7.2 %collective-permute-start.7 = (f32[512,128]{1,0:T(8,128)S(1)}, f32[512,128]{1,0:T(8,128)S(1)}, u32[]{:S(2)}, u32[]{:S(2)}) collective-permute-start(f32[512,128]{1,0:T(8,128)S(1)} %get-tuple-element.31), channel_id=1, source_target_pairs={{0,32},{32,0},{64,96},{96,64},{1,33},{33,1},{65,97},{97,65},{2,34}... | collective-permute-start | bytes 786440 | tf_op jit(solution)/shard_map/ppermute | solution.py:462
  20.0 5.9 %collective-permute-start.6 = (f32[392,128]{1,0:T(8,128)S(1)}, f32[392,128]{1,0:T(8,128)S(1)}, u32[]{:S(2)}, u32[]{:S(2)}) collective-permute-start(f32[392,128]{1,0:T(8,128)S(1)} %get-tuple-element.30), channel_id=1, source_target_pairs={{2,4},{4,2},{6,0},{0,6},{3,5},{5,3},{7,1},{1,7},{10,12},{12,10},{1... | collective-permute-start | bytes 602120 | tf_op jit(solution)/shard_map/ppermute | solution.py:463
  21.8 4.1 %collective-permute-start.8 = (f32[8,128]{1,0:T(8,128)S(1)}, f32[8,128]{1,0:T(8,128)S(1)}, u32[]{:S(2)}, u32[]{:S(2)}) collective-permute-start(f32[8,128]{1,0:T(8,128)S(1)} %get-tuple-element.32.row_sum), channel_id=1, source_target_pairs={{0,4},{2,6},{4,0},{6,2},{1,5},{3,7},{5,1},{7,3},{8,12},{10,14},{12... | collective-permute-start | bytes 12296 | tf_op jit(solution)/shard_map/ppermute | solution.py:464
  47.5 4.9 %collective-permute-start.11 = (f32[136,128]{1,0:T(8,128)S(1)}, f32[136,128]{1,0:T(8,128)S(1)}, u32[]{:S(2)}, u32[]{:S(2)}) collective-permute-start(f32[136,128]{1,0:T(8,128)S(1)} %reduce_sum.9), channel_id=1, source_target_pairs={{0,24},{8,0},{16,8},{24,16},{1,25},{9,1},{17,9},{25,17},{2,26},{10... | collective-permute-start | bytes 208904 | tf_op jit(solution)/shard_map/ppermute | solution.py:470
  48.4 5.3 %collective-permute-start.10 = (f32[136,128]{1,0:T(8,128)S(1)}, f32[136,128]{1,0:T(8,128)S(1)}, u32[]{:S(2)}, u32[]{:S(2)}) collective-permute-start(f32[136,128]{1,0:T(8,128)S(1)} %reduce_sum.9), channel_id=1, source_target_pairs={{0,8},{8,16},{16,24},{24,0},{1,9},{9,17},{17,25},{25,1},{2,10},{10... | collective-permute-start | bytes 208904 | tf_op jit(solution)/shard_map/ppermute | solution.py:470
  50.0 7.1 %collective-permute-start.9 = (f32[136,128]{1,0:T(8,128)S(1)}, f32[136,128]{1,0:T(8,128)S(1)}, u32[]{:S(2)}, u32[]{:S(2)}) collective-permute-start(f32[136,128]{1,0:T(8,128)S(1)} %reduce_sum.9), channel_id=1, source_target_pairs={{0,16},{8,24},{16,0},{24,8},{1,17},{9,25},{17,1},{25,9},{2,18},{10... | collective-permute-start | bytes 208904 | tf_op jit(solution)/shard_map/ppermute | solution.py:470
  57.1 25.2 %copy-start.6 = (f32[1,256,256]{2,1,0:T(8,128)S(1)}, f32[1,256,256]{2,1,0:T(8,128)}, u32[]{:S(2)}) copy-start(f32[1,256,256]{2,1,0:T(8,128)} %param.15) | copy-start | bytes 786436
  57.2 25.1 %copy-start.4 = (f32[1,896,896]{2,1,0:T(8,128)S(1)}, f32[1,896,896]{2,1,0:T(8,128)}, u32[]{:S(2)}) copy-start(f32[1,896,896]{2,1,0:T(8,128)} %param.14) | copy-start | bytes 9633796
  76.8 5.5 %collective-permute-start.15 = (f32[512,128]{1,0:T(8,128)S(1)}, f32[512,128]{1,0:T(8,128)S(1)}, u32[]{:S(2)}, u32[]{:S(2)}) collective-permute-start(f32[512,128]{1,0:T(8,128)S(1)} %get-tuple-element.36), channel_id=1, source_target_pairs={{0,2},{2,0},{4,6},{6,4},{1,3},{3,1},{5,7},{7,5},{8,10},{10,8},{12,... | collective-permute-start | bytes 786440 | tf_op jit(solution)/shard_map/ppermute | solution.py:408
  77.1 4.7 %collective-permute-start.16 = (f32[384,128]{1,0:T(8,128)S(1)}, f32[384,128]{1,0:T(8,128)S(1)}, u32[]{:S(2)}, u32[]{:S(2)}) collective-permute-start(f32[384,128]{1,0:T(8,128)S(1)} %get-tuple-element.37), channel_id=1, source_target_pairs={{0,32},{32,0},{64,96},{96,64},{1,33},{33,1},{65,97},{97,65},{2,34}... | collective-permute-start | bytes 589832 | tf_op jit(solution)/shard_map/ppermute | solution.py:408
  77.5 14.2 %collective-permute-start.12 = (f32[640,128]{1,0:T(8,128)S(1)}, f32[640,128]{1,0:T(8,128)S(1)}, u32[]{:S(2)}, u32[]{:S(2)}) collective-permute-start(f32[640,128]{1,0:T(8,128)S(1)} %get-tuple-element.33), channel_id=1, source_target_pairs={{0,128},{128,0},{1,129},{129,1},{2,130},{130,2},{3,131},{131,3},{4... | collective-permute-start | bytes 983048 | tf_op jit(solution)/shard_map/ppermute | solution.py:408
  77.5 13.3 %collective-permute-start.13 = (f32[384,128]{1,0:T(8,128)S(1)}, f32[384,128]{1,0:T(8,128)S(1)}, u32[]{:S(2)}, u32[]{:S(2)}) collective-permute-start(f32[384,128]{1,0:T(8,128)S(1)} %get-tuple-element.34), channel_id=1, source_target_pairs={{2,4},{4,2},{6,0},{0,6},{3,5},{5,3},{7,1},{1,7},{10,12},{12,10},{1... | collective-permute-start | bytes 589832 | tf_op jit(solution)/shard_map/ppermute | solution.py:408
  78.4 12.4 %collective-permute-start.14 = (f32[256,128]{1,0:T(8,128)S(1)}, f32[256,128]{1,0:T(8,128)S(1)}, u32[]{:S(2)}, u32[]{:S(2)}) collective-permute-start(f32[256,128]{1,0:T(8,128)S(1)} %get-tuple-element.35), channel_id=1, source_target_pairs={{32,64},{64,32},{96,0},{0,96},{33,65},{65,33},{97,1},{1,97},{34,66... | collective-permute-start | bytes 393224 | tf_op jit(solution)/shard_map/ppermute | solution.py:408
  84.7 7.0 %collective-permute-start.17 = (f32[1,128]{1,0:T(1,128)S(1)}, f32[1,128]{1,0:T(1,128)S(1)}, u32[]{:S(2)}, u32[]{:S(2)}) collective-permute-start(f32[1,128]{1,0:T(1,128)S(1)} %get-tuple-element.39.curvature), channel_id=1, source_target_pairs={{0,1},{1,0},{2,3},{3,2},{4,5},{5,4},{6,7},{7,6},{8,9},{9,8},{10,11... | collective-permute-start | bytes 1544 | tf_op jit(solution)/shard_map/ppermute | solution.py:486

commit v15 on v14

--- a/solution.py
+++ b/solution.py
@@ -469,7 +469,7 @@
     one, two, three = (
         lax.ppermute(mine, "zh", [(i, (i + k) % 4) for i in range(4)]) for k in (1, 2, 3)
     )
-    mine = (mine + two) + (one + three)
+    mine = (one + three) + (mine + two)
     kept = same_parity(jnp.broadcast_to(mine[None], (GROUP, CHUNK, B)).reshape(KEPT, B))
     parts = call(cut_kernel, streams_of(BACK_STREAMS), [V], 6, "cut", moved=2_200_000)(kept)
     parts = to_neighbours(parts)

time: 94.3 us -> 95.5 us (1.013)
  transfers between devices with their start and end apart: 18 -> 18, of which waited for: 7 -> 6; matrix products, arithmetic and copies ran while one was open for 1% -> 1% of each run, Pallas kernels for 7% -> 7%
where the time goes in v15:
time: 95.5 us; the launch traced here: 95.3 us
  blocking collectives  41.2 us (43%)
  starting transfers between devices  28.5 us (30%)
  waiting for transfers between devices  12.1 us (13%)
  Pallas kernels  9.51 us (10%)
  other arithmetic  2.22 us (2%)
  between operations  1.65 us (2%)
    all_to_all x2, blocking collectives, same_parity(): lax.all_to_all(value, axes, 0, 0, axis_index_groups=parity_groups(), tile...  41.2 us
    ppermute x1, starting transfers between devices, body(): other = lax.ppermute(curvature, 'c', swap)  6.39 us
    ppermute x3, waiting for transfers between devices, body(): lax.ppermute(mine, 'zh', [(i, (i + k) % 4) for i in range(4)])  5.27 us
    ppermute x3, starting transfers between devices, body(): lax.ppermute(mine, 'zh', [(i, (i + k) % 4) for i in range(4)])  4.59 us
    ppermute x1, starting transfers between devices, body(): far_2 = lax.ppermute(sum_2, 'zh', HIGH)  4.29 us
    ppermute x1, waiting for transfers between devices, body(): row_two = lax.ppermute(row_sum, 'x', [(0, 2), (1, 3), (2, 0), (3, 1)])  3.46 us
    ppermute x1, starting transfers between devices, body(): oth_feat = lax.ppermute(feat.astype(F32), 'c', swap)  3.33 us
    ppermute x5, starting transfers between devices, to_neighbours(): lax.ppermute(part, axis, pairs)  2.96 us
  transfers between devices with their start and end apart: 18, of which 6 were waited for; matrix products, arithmetic and copies ran while one was open for 1% of the time, Pallas kernels for 7%

profile of v15, /device:TPU:1, one launch (start us, length us, event | category | flops | bytes accessed | tf_op | source)
XLA Modules:
  0.0 95.3 jit_solution(3453549902805369359)
XLA Ops:
  0.6 0.0 copy-start
  0.6 0.0 copy-start.1
  0.7 0.0 copy-start.2
  0.7 0.0 copy-start.3
  0.7 0.0 copy-start.5
  0.7 1.1 %bitcast_convert_fusion.1 = f32[512,256]{1,0:T(8,128)S(1)} fusion(bf16[1,16,32,256]{3,2,1,0:T(8,128)(2,1)} %param.8), kind=kLoop, calls=%fused_computation.2 | loop fusion | flops 131072 | bytes 786432 | tf_op jit(solution)/shard_map/convert_element_type | solution.py:421
  1.8 3.3 %collective-permute-start = (f32[512,256]{1,0:T(8,128)S(1)}, f32[512,256]{1,0:T(8,128)S(1)}, u32[]{:S(2)}, u32[]{:S(2)}) collective-permute-start(f32[512,256]{1,0:T(8,128)S(1)} %bitcast_convert_fusion.1), channel_id=1, source_target_pairs={{0,1},{1,0},{2,3},{3,2},{4,5},{5,4},{6,7},{7,6},{8,9},{9,8},{10,11... | collective-permute-start | bytes 1572872 | tf_op jit(solution)/shard_map/ppermute | solution.py:421
  5.1 1.0 %convert_element_type.10 = f32[2,512,128]{2,1,0:T(8,128)S(1)} convert(bf16[2,512,128]{2,1,0:T(8,128)(2,1)} %bitcast.17) | non-fusion elementwise | flops 131072 | bytes 786432 | tf_op jit(solution)/shard_map/convert_element_type | solution.py:422
  6.1 0.1 collective-permute-start.1
  6.2 0.0 copy-done.2
  6.2 0.1 bitcast_convert_fusion
  6.3 0.6 collective-permute-start.2
  6.8 0.0 copy-done.3
  6.9 1.3 %collective-permute-start.3 = (f32[1,16]{1,0:T(1,128)S(1)}, f32[1,16]{1,0:T(1,128)S(1)}, u32[]{:S(2)}, u32[]{:S(2)}) collective-permute-start(f32[1,16]{1,0:T(1,128)S(1)} %copy-done.3), channel_id=1, source_target_pairs={{0,8},{8,0},{16,24},{24,16},{1,9},{9,1},{17,25},{25,17},{2,10},{10... | collective-permute-start | bytes 200 | tf_op jit(solution)/shard_map/ppermute | solution.py:423
  8.8 0.0 collective-permute-done.oth_feat
  8.8 0.0 collective-permute-done.1.oth_pair
  8.8 0.0 copy-done
  8.8 0.0 copy-done.1
  8.8 0.0 copy-done.5
  8.8 1.4 %forward.1 = (bf16[2,1024,384]{2,1,0:T(8,128)(2,1)S(1)}, f32[2,1024,256]{2,1,0:T(8,128)S(1)}, bf16[2,32,256]{2,1,0:T(8,128)(2,1)S(1)}) custom-call(bf16[512,256]{1,0:T(8,128)(2,1)S(1)} %bitcast.16, bf16[2,512,128]{2,1,0:T(8,128)(2,1)S(1)} %bitcast.18, f32[512,256]{1,0:T(8,128)S(1)} %collective-permute-done.oth_feat, ...), custom_call_target="tpu_custom_call" | custom-call | flops 1000000000 | bytes 6000000 | tf_op jit(solution)/shard_map/forward/pallas_call | solution.py:426
  10.2 0.0 collective-permute-done.3.far
  10.2 4.3 %collective-permute-start.4 = (f32[1,16]{1,0:T(1,128)S(1)}, f32[1,16]{1,0:T(1,128)S(1)}, u32[]{:S(2)}, u32[]{:S(2)}) collective-permute-start(f32[1,16]{1,0:T(1,128)S(1)} %pair.1.near), channel_id=1, source_target_pairs={{8,16},{16,8},{24,0},{0,24},{9,17},{17,9},{25,1},{1,25},{10,18},{1... | collective-permute-start | bytes 200 | tf_op jit(solution)/shard_map/ppermute | solution.py:436
  14.5 0.0 collective-permute-done.2.oth_psi
  14.5 2.8 %factors.1 = (f32[2,896,128]{2,1,0:T(8,128)S(1)}, f32[2,384,128]{2,1,0:T(8,128)S(1)}, f32[128,128]{1,0:T(8,128)S(1)}) custom-call(bf16[2,1024,384]{2,1,0:T(8,128)(2,1)S(1)} %get-tuple-element.23.x_s, f32[2,1024,256]{2,1,0:T(8,128)S(1)} %get-tuple-element.24.d_s, bf16[2,32,256]{2,1,0:T(8,128)(2,1)S(1)} %get-tuple-element.25.m_s.after, ...), custom_call_target="tpu_custom_call" | custom-call | flops 2500000000 | bytes 8000000 | tf_op jit(solution)/shard_map/factors/pallas_call | solution.py:439
  17.3 0.0 collective-permute-done.4.far
  17.3 0.1 tie.1
  17.4 1.3 %collective-permute-start.5 = (f32[520,128]{1,0:T(8,128)S(1)}, f32[520,128]{1,0:T(8,128)S(1)}, u32[]{:S(2)}, u32[]{:S(2)}) collective-permute-start(f32[520,128]{1,0:T(8,128)S(1)} %get-tuple-element.29), channel_id=1, source_target_pairs={{0,2},{2,0},{4,6},{6,4},{1,3},{3,1},{5,7},{7,5},{8,10},{10,8},{12,... | collective-permute-start | bytes 798728 | tf_op jit(solution)/shard_map/ppermute | solution.py:461
  18.7 1.3 %collective-permute-start.7 = (f32[512,128]{1,0:T(8,128)S(1)}, f32[512,128]{1,0:T(8,128)S(1)}, u32[]{:S(2)}, u32[]{:S(2)}) collective-permute-start(f32[512,128]{1,0:T(8,128)S(1)} %get-tuple-element.31), channel_id=1, source_target_pairs={{0,32},{32,0},{64,96},{96,64},{1,33},{33,1},{65,97},{97,65},{2,34}... | collective-permute-start | bytes 786440 | tf_op jit(solution)/shard_map/ppermute | solution.py:462
  20.0 1.8 %collective-permute-start.6 = (f32[392,128]{1,0:T(8,128)S(1)}, f32[392,128]{1,0:T(8,128)S(1)}, u32[]{:S(2)}, u32[]{:S(2)}) collective-permute-start(f32[392,128]{1,0:T(8,128)S(1)} %get-tuple-element.30), channel_id=1, source_target_pairs={{2,4},{4,2},{6,0},{0,6},{3,5},{5,3},{7,1},{1,7},{10,12},{12,10},{1... | collective-permute-start | bytes 602120 | tf_op jit(solution)/shard_map/ppermute | solution.py:463
  21.8 0.6 collective-permute-start.8
  22.4 3.5 %collective-permute-done.8.row_two = f32[8,128]{1,0:T(8,128)S(1)} collective-permute-done((f32[8,128]{1,0:T(8,128)S(1)}, f32[8,128]{1,0:T(8,128)S(1)}, u32[]{:S(2)}, u32[]{:S(2)}) %collective-permute-start.8) | collective-permute-done | bytes 4128 | tf_op jit(solution)/shard_map/ppermute | solution.py:464
  25.9 0.0 collective-permute-done.6.from_1
  25.9 0.0 collective-permute-done.7.from_2
  25.9 0.0 collective-permute-done.5.from_0
  25.9 0.5 add.16
  26.4 21.0 %all_to_all.17 = f32[16,136,128]{2,1,0:T(8,128)S(1)} all-to-all(f32[16,136,128]{2,1,0:T(8,128)S(1)} %bitcast.15), channel_id=1, replica_groups={{0,4,34,38,64,68,98,102,130,134,160,164,194,198,224,228},{2,6,32,36,66,..., dimensions={0} | all-to-all | bytes 2228224 | tf_op jit(solution)/shard_map/all_to_all | solution.py:400
  47.5 0.1 reduce_sum.9
  47.5 1.8 %collective-permute-start.11 = (f32[136,128]{1,0:T(8,128)S(1)}, f32[136,128]{1,0:T(8,128)S(1)}, u32[]{:S(2)}, u32[]{:S(2)}) collective-permute-start(f32[136,128]{1,0:T(8,128)S(1)} %reduce_sum.9), channel_id=1, source_target_pairs={{0,16},{8,24},{16,0},{24,8},{1,17},{9,25},{17,1},{25,9},{2,18},{10... | collective-permute-start | bytes 208904 | tf_op jit(solution)/shard_map/ppermute | solution.py:470
  49.4 2.7 %collective-permute-start.10 = (f32[136,128]{1,0:T(8,128)S(1)}, f32[136,128]{1,0:T(8,128)S(1)}, u32[]{:S(2)}, u32[]{:S(2)}) collective-permute-start(f32[136,128]{1,0:T(8,128)S(1)} %reduce_sum.9), channel_id=1, source_target_pairs={{0,24},{8,0},{16,8},{24,16},{1,25},{9,1},{17,9},{25,17},{2,26},{10... | collective-permute-start | bytes 208904 | tf_op jit(solution)/shard_map/ppermute | solution.py:470
  52.1 0.0 collective-permute-start.9
  52.1 3.3 %collective-permute-done.11 = f32[136,128]{1,0:T(8,128)S(1)} collective-permute-done((f32[136,128]{1,0:T(8,128)S(1)}, f32[136,128]{1,0:T(8,128)S(1)}, u32[]{:S(2)}, u32[]{:S(2)}) %collective-permute-start.11) | collective-permute-done | bytes 69664 | tf_op jit(solution)/shard_map/ppermute | solution.py:470
  55.4 0.0 collective-permute-done.10
  55.4 2.0 %collective-permute-done.9 = f32[136,128]{1,0:T(8,128)S(1)} collective-permute-done((f32[136,128]{1,0:T(8,128)S(1)}, f32[136,128]{1,0:T(8,128)S(1)}, u32[]{:S(2)}, u32[]{:S(2)}) %collective-permute-start.9) | collective-permute-done | bytes 69664 | tf_op jit(solution)/shard_map/ppermute | solution.py:470
  57.4 0.0 copy-start.6
  57.4 0.1 broadcast_in_dim.15
  57.5 0.0 copy-start.4
  57.5 20.1 %all_to_all.18 = f32[16,136,128]{2,1,0:T(8,128)S(1)} all-to-all(f32[16,136,128]{2,1,0:T(8,128)S(1)} %broadcast_in_dim.15), channel_id=1, replica_groups={{0,4,34,38,64,68,98,102,130,134,160,164,194,198,224,228},{2,6,32,36,66,..., dimensions={0} | all-to-all | bytes 2228224 | tf_op jit(solution)/shard_map/all_to_all | solution.py:400
  77.7 0.1 cut.1
  77.7 0.3 collective-permute-start.15
  78.0 0.1 collective-permute-start.16
  78.1 0.9 collective-permute-start.12
  79.0 1.7 %collective-permute-start.13 = (f32[384,128]{1,0:T(8,128)S(1)}, f32[384,128]{1,0:T(8,128)S(1)}, u32[]{:S(2)}, u32[]{:S(2)}) collective-permute-start(f32[384,128]{1,0:T(8,128)S(1)} %get-tuple-element.34), channel_id=1, source_target_pairs={{2,4},{4,2},{6,0},{0,6},{3,5},{5,3},{7,1},{1,7},{10,12},{12,10},{1... | collective-permute-start | bytes 589832 | tf_op jit(solution)/shard_map/ppermute | solution.py:408
  80.7 0.0 collective-permute-start.14
  80.7 2.0 %collective-permute-done.16.from_1 = f32[384,128]{1,0:T(8,128)S(1)} collective-permute-done((f32[384,128]{1,0:T(8,128)S(1)}, f32[384,128]{1,0:T(8,128)S(1)}, u32[]{:S(2)}, u32[]{:S(2)}) %collective-permute-start.16) | collective-permute-done | bytes 196640 | tf_op jit(solution)/shard_map/ppermute | solution.py:408
  82.7 0.6 collective-permute-done.15.from_0
  83.2 0.0 copy-done.6
  83.2 0.0 copy-done.4
  83.2 2.4 %natural.1 = (f32[896,256]{1,0:T(8,128)S(1)}, f32[1,128]{1,0:T(1,128)S(1)}) custom-call(f32[2176,128]{1,0:T(8,128)S(1)} %bitcast.13, f32[512,128]{1,0:T(8,128)S(1)} %collective-permute-done.15.from_0, f32[384,128]{1,0:T(8,128)S(1)} %collective-permute-done.16.from_1, f32[896,896]{1,0:T(8,128)S(1)} %bitcast.20, f32[256,256]{1,0:T(8,128)S(1)} %bitcast.21), custom_call_target="tpu_custom_call" | custom-call | flops 1500000000 | bytes 5000000 | tf_op jit(solution)/shard_map/natural/pallas_call | solution.py:477
  85.6 6.4 %collective-permute-start.17 = (f32[1,128]{1,0:T(1,128)S(1)}, f32[1,128]{1,0:T(1,128)S(1)}, u32[]{:S(2)}, u32[]{:S(2)}) collective-permute-start(f32[1,128]{1,0:T(1,128)S(1)} %get-tuple-element.39.curvature), channel_id=1, source_target_pairs={{0,1},{1,0},{2,3},{3,2},{4,5},{5,4},{6,7},{7,6},{8,9},{9,8},{10,11... | collective-permute-start | bytes 1544 | tf_op jit(solution)/shard_map/ppermute | solution.py:486
  92.0 0.0 collective-permute-done.14.from_4
  92.0 0.0 collective-permute-done.13.from_3
  92.0 0.8 collective-permute-done.17.other
  92.8 0.0 collective-permute-done.12.from_2
  92.8 2.3 %finish.1 = (f32[896,896]{1,0:T(8,128)}, f32[256,256]{1,0:T(8,128)}, f32[896,256]{1,0:T(8,128)}) custom-call(f32[2176,128]{1,0:T(8,128)S(1)} %bitcast.14, f32[640,128]{1,0:T(8,128)S(1)} %collective-permute-done.12.from_2, f32[384,128]{1,0:T(8,128)S(1)} %collective-permute-done.13.from_3, f32[256,128]{1,0:T(8,128)S(1)} %collective-permute-done.14.from_4, ...), custom_call_target="tpu_custom_call" | custom-call | flops 10000000 | bytes 7000000 | tf_op jit(solution)/shard_map/finish/pallas_call | solution.py:487
  (2 shorter events, 0.0 us)
Async XLA Ops:
  0.6 8.2 %copy-start = (bf16[1,16,32,256]{3,2,1,0:T(8,128)(2,1)S(1)}, bf16[1,16,32,256]{3,2,1,0:T(8,128)(2,1)}, u32[]{:S(2)}) copy-start(bf16[1,16,32,256]{3,2,1,0:T(8,128)(2,1)} %param.8) | copy-start | bytes 786436
  0.6 8.2 %copy-start.1 = (bf16[1,2,16,32,128]{4,3,2,1,0:T(8,128)(2,1)S(1)}, bf16[1,2,16,32,128]{4,3,2,1,0:T(8,128)(2,1)}, u32[]{:S(2)}) copy-start(bf16[1,2,16,32,128]{4,3,2,1,0:T(8,128)(2,1)} %param.10) | copy-start | bytes 786436
  0.7 5.6 %copy-start.2 = (bf16[1,16,32,256]{3,2,1,0:T(8,128)(2,1)S(1)}, bf16[1,16,32,256]{3,2,1,0:T(8,128)(2,1)}, u32[]{:S(2)}) copy-start(bf16[1,16,32,256]{3,2,1,0:T(8,128)(2,1)} %param.9) | copy-start | bytes 786436
  0.7 6.2 %copy-start.3 = (f32[1,16]{1,0:T(1,128)S(1)}, f32[1,16]{1,0:T(1,128)}, u32[]{:S(2)}) copy-start(f32[1,16]{1,0:T(1,128)} %near.1) | copy-start | bytes 196
  0.7 8.2 %copy-start.5 = (bf16[2,896,256]{2,1,0:T(8,128)(2,1)S(1)}, bf16[2,896,256]{2,1,0:T(8,128)(2,1)}, u32[]{:S(2)}) copy-start(bf16[2,896,256]{2,1,0:T(8,128)(2,1)} %weights.3) | copy-start | bytes 2752516
  1.8 7.0 %collective-permute-start = (f32[512,256]{1,0:T(8,128)S(1)}, f32[512,256]{1,0:T(8,128)S(1)}, u32[]{:S(2)}, u32[]{:S(2)}) collective-permute-start(f32[512,256]{1,0:T(8,128)S(1)} %bitcast_convert_fusion.1), channel_id=1, source_target_pairs={{0,1},{1,0},{2,3},{3,2},{4,5},{5,4},{6,7},{7,6},{8,9},{9,8},{10,11... | collective-permute-start | bytes 1572872 | tf_op jit(solution)/shard_map/ppermute | solution.py:421
  6.1 2.7 %collective-permute-start.1 = (f32[2,512,128]{2,1,0:T(8,128)S(1)}, f32[2,512,128]{2,1,0:T(8,128)S(1)}, u32[]{:S(2)}, u32[]{:S(2)}) collective-permute-start(f32[2,512,128]{2,1,0:T(8,128)S(1)} %convert_element_type.10), channel_id=1, source_target_pairs={{0,1},{1,0},{2,3},{3,2},{4,5},{5,4},{6,7},{7,6},{8,9},{9,8},{10,11... | collective-permute-start | bytes 1572872 | tf_op jit(solution)/shard_map/ppermute | solution.py:422
  6.3 8.2 %collective-permute-start.2 = (f32[512,256]{1,0:T(8,128)S(1)}, f32[512,256]{1,0:T(8,128)S(1)}, u32[]{:S(2)}, u32[]{:S(2)}) collective-permute-start(f32[512,256]{1,0:T(8,128)S(1)} %bitcast_convert_fusion), channel_id=1, source_target_pairs={{0,1},{1,0},{2,3},{3,2},{4,5},{5,4},{6,7},{7,6},{8,9},{9,8},{10,11... | collective-permute-start | bytes 1572872 | tf_op jit(solution)/shard_map/ppermute | solution.py:424
  6.9 3.4 %collective-permute-start.3 = (f32[1,16]{1,0:T(1,128)S(1)}, f32[1,16]{1,0:T(1,128)S(1)}, u32[]{:S(2)}, u32[]{:S(2)}) collective-permute-start(f32[1,16]{1,0:T(1,128)S(1)} %copy-done.3), channel_id=1, source_target_pairs={{0,8},{8,0},{16,24},{24,16},{1,9},{9,1},{17,25},{25,17},{2,10},{10... | collective-permute-start | bytes 200 | tf_op jit(solution)/shard_map/ppermute | solution.py:423
  10.2 7.1 %collective-permute-start.4 = (f32[1,16]{1,0:T(1,128)S(1)}, f32[1,16]{1,0:T(1,128)S(1)}, u32[]{:S(2)}, u32[]{:S(2)}) collective-permute-start(f32[1,16]{1,0:T(1,128)S(1)} %pair.1.near), channel_id=1, source_target_pairs={{8,16},{16,8},{24,0},{0,24},{9,17},{17,9},{25,1},{1,25},{10,18},{1... | collective-permute-start | bytes 200 | tf_op jit(solution)/shard_map/ppermute | solution.py:436
  17.4 8.5 %collective-permute-start.5 = (f32[520,128]{1,0:T(8,128)S(1)}, f32[520,128]{1,0:T(8,128)S(1)}, u32[]{:S(2)}, u32[]{:S(2)}) collective-permute-start(f32[520,128]{1,0:T(8,128)S(1)} %get-tuple-element.29), channel_id=1, source_target_pairs={{0,2},{2,0},{4,6},{6,4},{1,3},{3,1},{5,7},{7,5},{8,10},{10,8},{12,... | collective-permute-start | bytes 798728 | tf_op jit(solution)/shard_map/ppermute | solution.py:461
  18.7 7.2 %collective-permute-start.7 = (f32[512,128]{1,0:T(8,128)S(1)}, f32[512,128]{1,0:T(8,128)S(1)}, u32[]{:S(2)}, u32[]{:S(2)}) collective-permute-start(f32[512,128]{1,0:T(8,128)S(1)} %get-tuple-element.31), channel_id=1, source_target_pairs={{0,32},{32,0},{64,96},{96,64},{1,33},{33,1},{65,97},{97,65},{2,34}... | collective-permute-start | bytes 786440 | tf_op jit(solution)/shard_map/ppermute | solution.py:462
  20.0 5.9 %collective-permute-start.6 = (f32[392,128]{1,0:T(8,128)S(1)}, f32[392,128]{1,0:T(8,128)S(1)}, u32[]{:S(2)}, u32[]{:S(2)}) collective-permute-start(f32[392,128]{1,0:T(8,128)S(1)} %get-tuple-element.30), channel_id=1, source_target_pairs={{2,4},{4,2},{6,0},{0,6},{3,5},{5,3},{7,1},{1,7},{10,12},{12,10},{1... | collective-permute-start | bytes 602120 | tf_op jit(solution)/shard_map/ppermute | solution.py:463
  21.8 4.1 %collective-permute-start.8 = (f32[8,128]{1,0:T(8,128)S(1)}, f32[8,128]{1,0:T(8,128)S(1)}, u32[]{:S(2)}, u32[]{:S(2)}) collective-permute-start(f32[8,128]{1,0:T(8,128)S(1)} %get-tuple-element.32.row_sum), channel_id=1, source_target_pairs={{0,4},{2,6},{4,0},{6,2},{1,5},{3,7},{5,1},{7,3},{8,12},{10,14},{12... | collective-permute-start | bytes 12296 | tf_op jit(solution)/shard_map/ppermute | solution.py:464
  47.5 7.9 %collective-permute-start.11 = (f32[136,128]{1,0:T(8,128)S(1)}, f32[136,128]{1,0:T(8,128)S(1)}, u32[]{:S(2)}, u32[]{:S(2)}) collective-permute-start(f32[136,128]{1,0:T(8,128)S(1)} %reduce_sum.9), channel_id=1, source_target_pairs={{0,16},{8,24},{16,0},{24,8},{1,17},{9,25},{17,1},{25,9},{2,18},{10... | collective-permute-start | bytes 208904 | tf_op jit(solution)/shard_map/ppermute | solution.py:470
  49.4 6.1 %collective-permute-start.10 = (f32[136,128]{1,0:T(8,128)S(1)}, f32[136,128]{1,0:T(8,128)S(1)}, u32[]{:S(2)}, u32[]{:S(2)}) collective-permute-start(f32[136,128]{1,0:T(8,128)S(1)} %reduce_sum.9), channel_id=1, source_target_pairs={{0,24},{8,0},{16,8},{24,16},{1,25},{9,1},{17,9},{25,17},{2,26},{10... | collective-permute-start | bytes 208904 | tf_op jit(solution)/shard_map/ppermute | solution.py:470
  52.1 5.3 %collective-permute-start.9 = (f32[136,128]{1,0:T(8,128)S(1)}, f32[136,128]{1,0:T(8,128)S(1)}, u32[]{:S(2)}, u32[]{:S(2)}) collective-permute-start(f32[136,128]{1,0:T(8,128)S(1)} %reduce_sum.9), channel_id=1, source_target_pairs={{0,8},{8,16},{16,24},{24,0},{1,9},{9,17},{17,25},{25,1},{2,10},{10... | collective-permute-start | bytes 208904 | tf_op jit(solution)/shard_map/ppermute | solution.py:470
  57.4 25.8 %copy-start.6 = (f32[1,256,256]{2,1,0:T(8,128)S(1)}, f32[1,256,256]{2,1,0:T(8,128)}, u32[]{:S(2)}) copy-start(f32[1,256,256]{2,1,0:T(8,128)} %param.15) | copy-start | bytes 786436
  57.5 25.7 %copy-start.4 = (f32[1,896,896]{2,1,0:T(8,128)S(1)}, f32[1,896,896]{2,1,0:T(8,128)}, u32[]{:S(2)}) copy-start(f32[1,896,896]{2,1,0:T(8,128)} %param.14) | copy-start | bytes 9633796
  77.7 5.5 %collective-permute-start.15 = (f32[512,128]{1,0:T(8,128)S(1)}, f32[512,128]{1,0:T(8,128)S(1)}, u32[]{:S(2)}, u32[]{:S(2)}) collective-permute-start(f32[512,128]{1,0:T(8,128)S(1)} %get-tuple-element.36), channel_id=1, source_target_pairs={{0,2},{2,0},{4,6},{6,4},{1,3},{3,1},{5,7},{7,5},{8,10},{10,8},{12,... | collective-permute-start | bytes 786440 | tf_op jit(solution)/shard_map/ppermute | solution.py:408
  78.0 4.7 %collective-permute-start.16 = (f32[384,128]{1,0:T(8,128)S(1)}, f32[384,128]{1,0:T(8,128)S(1)}, u32[]{:S(2)}, u32[]{:S(2)}) collective-permute-start(f32[384,128]{1,0:T(8,128)S(1)} %get-tuple-element.37), channel_id=1, source_target_pairs={{0,32},{32,0},{64,96},{96,64},{1,33},{33,1},{65,97},{97,65},{2,34}... | collective-permute-start | bytes 589832 | tf_op jit(solution)/shard_map/ppermute | solution.py:408
  78.1 14.7 %collective-permute-start.12 = (f32[640,128]{1,0:T(8,128)S(1)}, f32[640,128]{1,0:T(8,128)S(1)}, u32[]{:S(2)}, u32[]{:S(2)}) collective-permute-start(f32[640,128]{1,0:T(8,128)S(1)} %get-tuple-element.33), channel_id=1, source_target_pairs={{0,128},{128,0},{1,129},{129,1},{2,130},{130,2},{3,131},{131,3},{4... | collective-permute-start | bytes 983048 | tf_op jit(solution)/shard_map/ppermute | solution.py:408
  79.0 13.0 %collective-permute-start.13 = (f32[384,128]{1,0:T(8,128)S(1)}, f32[384,128]{1,0:T(8,128)S(1)}, u32[]{:S(2)}, u32[]{:S(2)}) collective-permute-start(f32[384,128]{1,0:T(8,128)S(1)} %get-tuple-element.34), channel_id=1, source_target_pairs={{2,4},{4,2},{6,0},{0,6},{3,5},{5,3},{7,1},{1,7},{10,12},{12,10},{1... | collective-permute-start | bytes 589832 | tf_op jit(solution)/shard_map/ppermute | solution.py:408
  80.7 11.3 %collective-permute-start.14 = (f32[256,128]{1,0:T(8,128)S(1)}, f32[256,128]{1,0:T(8,128)S(1)}, u32[]{:S(2)}, u32[]{:S(2)}) collective-permute-start(f32[256,128]{1,0:T(8,128)S(1)} %get-tuple-element.35), channel_id=1, source_target_pairs={{32,64},{64,32},{96,0},{0,96},{33,65},{65,33},{97,1},{1,97},{34,66... | collective-permute-start | bytes 393224 | tf_op jit(solution)/shard_map/ppermute | solution.py:408
  85.6 7.2 %collective-permute-start.17 = (f32[1,128]{1,0:T(1,128)S(1)}, f32[1,128]{1,0:T(1,128)S(1)}, u32[]{:S(2)}, u32[]{:S(2)}) collective-permute-start(f32[1,128]{1,0:T(1,128)S(1)} %get-tuple-element.39.curvature), channel_id=1, source_target_pairs={{0,1},{1,0},{2,3},{3,2},{4,5},{5,4},{6,7},{7,6},{8,9},{9,8},{10,11... | collective-permute-start | bytes 1544 | tf_op jit(solution)/shard_map/ppermute | solution.py:486

commit v16 on v14

--- a/solution.py
+++ b/solution.py
@@ -196,22 +196,22 @@
     row_sum[...] = jnp.broadcast_to(zh_sum, (8, B))
     grads = GRADS * B
     to_0[:B, :] = fac[...]
-    to_0[B : B + grads, :] = out_0[1]
-    to_0[B + grads :, :] = row_sum[...]
-    to_1[:grads, :] = out[1, :grads, :]
-    to_1[grads:, :] = row_sum[...]
-    to_2[...] = out[1, grads:, :]
+    to_0[B : 2 * B, :] = out_0[1, :B, :]
+    to_0[2 * B :, :] = row_sum[...]
+    to_1[: grads - B, :] = out_0[1, B:, :]
+    to_1[grads - B :, :] = row_sum[...]
+    to_2[...] = out[1]
 
 
 def add_kernel(out, out_0, fac, from_0, from_1, from_2, row_sum, row_two, multiplicity, total):
     parity = own_parity()
     grads = GRADS * B
-    energy = (row_sum[...] + row_two[...]) + (from_0[B + grads :, :] + from_1[grads:, :])
+    energy = (row_sum[...] + row_two[...]) + (from_0[2 * B :, :] + from_1[grads - B :, :])
     mean = energy[:1, :] * (1.0 / 256.0)
-    plain = out_0[0] + from_0[B : B + grads, :]
-    total[:grads, :] = (out[0, :grads, :] + from_1[:grads, :]) - (mean + SHIFT) * plain
+    plain = out_0[0] + jnp.concatenate([from_0[B : 2 * B, :], from_1[: grads - B, :]], 0)
+    total[:grads, :] = (out[0, :grads, :] + from_2[:grads, :]) - (mean + SHIFT) * plain
     first = DIRECT[GRADS] * B
-    total[first : first + FACTORS * B, :] = out[0, grads:, :] + from_2[...]
+    total[first : first + FACTORS * B, :] = out[0, grads:, :] + from_2[grads:, :]
 
     def part(j):
         rows = slice(j * WALK, (j + 1) * WALK)
@@ -452,14 +452,15 @@
 
     to_0, to_1, to_2, row_sum = call(
         tie_kernel,
-        [((B + grads + 8, B), F32), ((grads + 8, B), F32), ((FACTORS * B, B), F32), ((8, B), F32)],
+        [((2 * B + 8, B), F32), ((grads - B + 8, B), F32), ((len(DIRECT) * B, B), F32), ((8, B), F32)],
         [V] * 5,
         6,
         "tie",
         moved=2_000_000,
     )(out, out_0, fac, sum_2, far_2)
+    ways = [(2 * a, 2 * b) for a, b in LOW] + [(2 * a + 1, 2 * b + 1) for a, b in HIGH]
+    from_2 = lax.ppermute(to_2, ("y", "c"), ways)
     from_0 = lax.ppermute(to_0, "x", LOW)
-    from_2 = lax.ppermute(to_2, "y", LOW)
     from_1 = lax.ppermute(to_1, "x", HIGH)
     row_two = lax.ppermute(row_sum, "x", [(0, 2), (1, 3), (2, 0), (3, 1)])
     (total,) = call(

time: 94.3 us -> 96.6 us (1.024)
  starting transfers between devices: 28.1 us -> 31.9 us
  waiting for transfers between devices: 12 us -> 9.99 us
    ppermute x5, waiting for transfers between devices: 2.68 us -> 0.19 us  [to_neighbours(): lax.ppermute(part, axis, pairs)]
    ppermute x5, starting transfers between devices: 2.81 us -> 5.3 us  [to_neighbours(): lax.ppermute(part, axis, pairs)]
    ppermute x1, starting transfers between devices: 1.3 us -> 2.8 us  [body(): from_2 = lax.ppermute(to_2, ('y', 'c'), ways)]
  transfers between devices with their start and end apart: 18 -> 18, of which waited for: 7 -> 6; matrix products, arithmetic and copies ran while one was open for 1% -> 1% of each run, Pallas kernels for 7% -> 7%
where the time goes in v16:
time: 96.6 us; the launch traced here: 96.4 us
  blocking collectives  41.1 us (43%)
  starting transfers between devices  31.9 us (33%)
  waiting for transfers between devices  9.99 us (10%)
  Pallas kernels  9.51 us (10%)
  other arithmetic  2.22 us (2%)
  between operations  1.65 us (2%)
    all_to_all x2, blocking collectives, same_parity(): lax.all_to_all(value, axes, 0, 0, axis_index_groups=parity_groups(), tile...  41.1 us
    ppermute x1, starting transfers between devices, body(): other = lax.ppermute(curvature, 'c', swap)  5.94 us
    ppermute x3, waiting for transfers between devices, body(): lax.ppermute(mine, 'zh', [(i, (i + k) % 4) for i in range(4)])  5.53 us
    ppermute x5, starting transfers between devices, to_neighbours(): lax.ppermute(part, axis, pairs)  5.3 us
    ppermute x3, starting transfers between devices, body(): lax.ppermute(mine, 'zh', [(i, (i + k) % 4) for i in range(4)])  4.59 us
    ppermute x1, starting transfers between devices, body(): far_2 = lax.ppermute(sum_2, 'zh', HIGH)  4.29 us
    ppermute x1, waiting for transfers between devices, body(): row_two = lax.ppermute(row_sum, 'x', [(0, 2), (1, 3), (2, 0), (3, 1)])  3.44 us
    ppermute x1, starting transfers between devices, body(): oth_feat = lax.ppermute(feat.astype(F32), 'c', swap)  3.33 us
  transfers between devices with their start and end apart: 18, of which 6 were waited for; matrix products, arithmetic and copies ran while one was open for 1% of the time, Pallas kernels for 7%

profile of v16, /device:TPU:1, one launch (start us, length us, event | category | flops | bytes accessed | tf_op | source)
XLA Modules:
  0.0 96.4 jit_solution(6490303577642629232)
XLA Ops:
  0.6 0.0 copy-start
  0.6 0.0 copy-start.1
  0.7 0.0 copy-start.2
  0.7 0.0 copy-start.3
  0.7 0.0 copy-start.5
  0.7 1.1 %bitcast_convert_fusion.1 = f32[512,256]{1,0:T(8,128)S(1)} fusion(bf16[1,16,32,256]{3,2,1,0:T(8,128)(2,1)} %param.8), kind=kLoop, calls=%fused_computation.2 | loop fusion | flops 131072 | bytes 786432 | tf_op jit(solution)/shard_map/convert_element_type | solution.py:421
  1.8 3.3 %collective-permute-start = (f32[512,256]{1,0:T(8,128)S(1)}, f32[512,256]{1,0:T(8,128)S(1)}, u32[]{:S(2)}, u32[]{:S(2)}) collective-permute-start(f32[512,256]{1,0:T(8,128)S(1)} %bitcast_convert_fusion.1), channel_id=1, source_target_pairs={{0,1},{1,0},{2,3},{3,2},{4,5},{5,4},{6,7},{7,6},{8,9},{9,8},{10,11... | collective-permute-start | bytes 1572872 | tf_op jit(solution)/shard_map/ppermute | solution.py:421
  5.1 1.0 %convert_element_type.10 = f32[2,512,128]{2,1,0:T(8,128)S(1)} convert(bf16[2,512,128]{2,1,0:T(8,128)(2,1)} %bitcast.17) | non-fusion elementwise | flops 131072 | bytes 786432 | tf_op jit(solution)/shard_map/convert_element_type | solution.py:422
  6.1 0.1 collective-permute-start.1
  6.2 0.0 copy-done.2
  6.2 0.1 bitcast_convert_fusion
  6.3 0.6 collective-permute-start.2
  6.8 0.0 copy-done.3
  6.9 1.3 %collective-permute-start.3 = (f32[1,16]{1,0:T(1,128)S(1)}, f32[1,16]{1,0:T(1,128)S(1)}, u32[]{:S(2)}, u32[]{:S(2)}) collective-permute-start(f32[1,16]{1,0:T(1,128)S(1)} %copy-done.3), channel_id=1, source_target_pairs={{0,8},{8,0},{16,24},{24,16},{1,9},{9,1},{17,25},{25,17},{2,10},{10... | collective-permute-start | bytes 200 | tf_op jit(solution)/shard_map/ppermute | solution.py:423
  8.8 0.0 collective-permute-done.oth_feat
  8.8 0.0 collective-permute-done.1.oth_pair
  8.8 0.0 copy-done
  8.8 0.0 copy-done.1
  8.8 0.0 copy-done.5
  8.8 1.4 %forward.1 = (bf16[2,1024,384]{2,1,0:T(8,128)(2,1)S(1)}, f32[2,1024,256]{2,1,0:T(8,128)S(1)}, bf16[2,32,256]{2,1,0:T(8,128)(2,1)S(1)}) custom-call(bf16[512,256]{1,0:T(8,128)(2,1)S(1)} %bitcast.16, bf16[2,512,128]{2,1,0:T(8,128)(2,1)S(1)} %bitcast.18, f32[512,256]{1,0:T(8,128)S(1)} %collective-permute-done.oth_feat, ...), custom_call_target="tpu_custom_call" | custom-call | flops 1000000000 | bytes 6000000 | tf_op jit(solution)/shard_map/forward/pallas_call | solution.py:426
  10.2 0.0 collective-permute-done.3.far
  10.2 4.3 %collective-permute-start.4 = (f32[1,16]{1,0:T(1,128)S(1)}, f32[1,16]{1,0:T(1,128)S(1)}, u32[]{:S(2)}, u32[]{:S(2)}) collective-permute-start(f32[1,16]{1,0:T(1,128)S(1)} %pair.1.near), channel_id=1, source_target_pairs={{8,16},{16,8},{24,0},{0,24},{9,17},{17,9},{25,1},{1,25},{10,18},{1... | collective-permute-start | bytes 200 | tf_op jit(solution)/shard_map/ppermute | solution.py:436
  14.5 0.0 collective-permute-done.2.oth_psi
  14.5 2.8 %factors.1 = (f32[2,896,128]{2,1,0:T(8,128)S(1)}, f32[2,384,128]{2,1,0:T(8,128)S(1)}, f32[128,128]{1,0:T(8,128)S(1)}) custom-call(bf16[2,1024,384]{2,1,0:T(8,128)(2,1)S(1)} %get-tuple-element.23.x_s, f32[2,1024,256]{2,1,0:T(8,128)S(1)} %get-tuple-element.24.d_s, bf16[2,32,256]{2,1,0:T(8,128)(2,1)S(1)} %get-tuple-element.25.m_s.after, ...), custom_call_target="tpu_custom_call" | custom-call | flops 2500000000 | bytes 8000000 | tf_op jit(solution)/shard_map/factors/pallas_call | solution.py:439
  17.3 0.0 collective-permute-done.4.far
  17.3 0.1 tie.1
  17.4 2.8 %collective-permute-start.7 = (f32[896,128]{1,0:T(8,128)S(1)}, f32[896,128]{1,0:T(8,128)S(1)}, u32[]{:S(2)}, u32[]{:S(2)}) collective-permute-start(f32[896,128]{1,0:T(8,128)S(1)} %get-tuple-element.31), channel_id=1, source_target_pairs={{0,32},{32,0},{64,96},{96,64},{33,65},{65,33},{97,1},{1,97},{2,34}... | collective-permute-start | bytes 1376264 | tf_op jit(solution)/shard_map/ppermute | solution.py:462
  20.2 1.2 %collective-permute-start.5 = (f32[264,128]{1,0:T(8,128)S(1)}, f32[264,128]{1,0:T(8,128)S(1)}, u32[]{:S(2)}, u32[]{:S(2)}) collective-permute-start(f32[264,128]{1,0:T(8,128)S(1)} %get-tuple-element.29), channel_id=1, source_target_pairs={{0,2},{2,0},{4,6},{6,4},{1,3},{3,1},{5,7},{7,5},{8,10},{10,8},{12,... | collective-permute-start | bytes 405512 | tf_op jit(solution)/shard_map/ppermute | solution.py:463
  21.4 1.8 %collective-permute-start.6 = (f32[264,128]{1,0:T(8,128)S(1)}, f32[264,128]{1,0:T(8,128)S(1)}, u32[]{:S(2)}, u32[]{:S(2)}) collective-permute-start(f32[264,128]{1,0:T(8,128)S(1)} %get-tuple-element.30), channel_id=1, source_target_pairs={{2,4},{4,2},{6,0},{0,6},{3,5},{5,3},{7,1},{1,7},{10,12},{12,10},{1... | collective-permute-start | bytes 405512 | tf_op jit(solution)/shard_map/ppermute | solution.py:464
  23.2 0.6 collective-permute-start.8
  23.9 3.4 %collective-permute-done.8.row_two = f32[8,128]{1,0:T(8,128)S(1)} collective-permute-done((f32[8,128]{1,0:T(8,128)S(1)}, f32[8,128]{1,0:T(8,128)S(1)}, u32[]{:S(2)}, u32[]{:S(2)}) %collective-permute-start.8) | collective-permute-done | bytes 4128 | tf_op jit(solution)/shard_map/ppermute | solution.py:465
  27.3 0.0 collective-permute-done.5.from_0
  27.3 0.0 collective-permute-done.6.from_1
  27.3 0.0 collective-permute-done.7.from_2
  27.3 0.5 add.16
  27.8 22.3 %all_to_all.17 = f32[16,136,128]{2,1,0:T(8,128)S(1)} all-to-all(f32[16,136,128]{2,1,0:T(8,128)S(1)} %bitcast.15), channel_id=1, replica_groups={{0,4,34,38,64,68,98,102,130,134,160,164,194,198,224,228},{2,6,32,36,66,..., dimensions={0} | all-to-all | bytes 2228224 | tf_op jit(solution)/shard_map/all_to_all | solution.py:400
  50.2 0.1 reduce_sum.9
  50.2 1.1 %collective-permute-start.11 = (f32[136,128]{1,0:T(8,128)S(1)}, f32[136,128]{1,0:T(8,128)S(1)}, u32[]{:S(2)}, u32[]{:S(2)}) collective-permute-start(f32[136,128]{1,0:T(8,128)S(1)} %reduce_sum.9), channel_id=1, source_target_pairs={{0,24},{8,0},{16,8},{24,16},{1,25},{9,1},{17,9},{25,17},{2,26},{10... | collective-permute-start | bytes 208904 | tf_op jit(solution)/shard_map/ppermute | solution.py:471
  51.3 1.3 %collective-permute-start.10 = (f32[136,128]{1,0:T(8,128)S(1)}, f32[136,128]{1,0:T(8,128)S(1)}, u32[]{:S(2)}, u32[]{:S(2)}) collective-permute-start(f32[136,128]{1,0:T(8,128)S(1)} %reduce_sum.9), channel_id=1, source_target_pairs={{0,8},{8,16},{16,24},{24,0},{1,9},{9,17},{17,25},{25,1},{2,10},{10... | collective-permute-start | bytes 208904 | tf_op jit(solution)/shard_map/ppermute | solution.py:471
  52.7 2.1 %collective-permute-start.9 = (f32[136,128]{1,0:T(8,128)S(1)}, f32[136,128]{1,0:T(8,128)S(1)}, u32[]{:S(2)}, u32[]{:S(2)}) collective-permute-start(f32[136,128]{1,0:T(8,128)S(1)} %reduce_sum.9), channel_id=1, source_target_pairs={{0,16},{8,24},{16,0},{24,8},{1,17},{9,25},{17,1},{25,9},{2,18},{10... | collective-permute-start | bytes 208904 | tf_op jit(solution)/shard_map/ppermute | solution.py:471
  54.8 0.3 collective-permute-done.11
  55.1 1.6 %collective-permute-done.10 = f32[136,128]{1,0:T(8,128)S(1)} collective-permute-done((f32[136,128]{1,0:T(8,128)S(1)}, f32[136,128]{1,0:T(8,128)S(1)}, u32[]{:S(2)}, u32[]{:S(2)}) %collective-permute-start.10) | collective-permute-done | bytes 69664 | tf_op jit(solution)/shard_map/ppermute | solution.py:471
  56.7 3.6 %collective-permute-done.9 = f32[136,128]{1,0:T(8,128)S(1)} collective-permute-done((f32[136,128]{1,0:T(8,128)S(1)}, f32[136,128]{1,0:T(8,128)S(1)}, u32[]{:S(2)}, u32[]{:S(2)}) %collective-permute-start.9) | collective-permute-done | bytes 69664 | tf_op jit(solution)/shard_map/ppermute | solution.py:471
  60.4 0.0 copy-start.6
  60.4 0.1 broadcast_in_dim.15
  60.4 0.0 copy-start.4
  60.5 18.8 %all_to_all.18 = f32[16,136,128]{2,1,0:T(8,128)S(1)} all-to-all(f32[16,136,128]{2,1,0:T(8,128)S(1)} %broadcast_in_dim.15), channel_id=1, replica_groups={{0,4,34,38,64,68,98,102,130,134,160,164,194,198,224,228},{2,6,32,36,66,..., dimensions={0} | all-to-all | bytes 2228224 | tf_op jit(solution)/shard_map/all_to_all | solution.py:400
  79.2 0.1 cut.1
  79.3 0.3 collective-permute-start.15
  79.6 0.2 collective-permute-start.16
  79.8 2.0 %collective-permute-start.12 = (f32[640,128]{1,0:T(8,128)S(1)}, f32[640,128]{1,0:T(8,128)S(1)}, u32[]{:S(2)}, u32[]{:S(2)}) collective-permute-start(f32[640,128]{1,0:T(8,128)S(1)} %get-tuple-element.33), channel_id=1, source_target_pairs={{0,128},{128,0},{1,129},{129,1},{2,130},{130,2},{3,131},{131,3},{4... | collective-permute-start | bytes 983048 | tf_op jit(solution)/shard_map/ppermute | solution.py:408
  81.8 1.0 collective-permute-start.13
  82.8 1.9 %collective-permute-start.14 = (f32[256,128]{1,0:T(8,128)S(1)}, f32[256,128]{1,0:T(8,128)S(1)}, u32[]{:S(2)}, u32[]{:S(2)}) collective-permute-start(f32[256,128]{1,0:T(8,128)S(1)} %get-tuple-element.35), channel_id=1, source_target_pairs={{32,64},{64,32},{96,0},{0,96},{33,65},{65,33},{97,1},{1,97},{34,66... | collective-permute-start | bytes 393224 | tf_op jit(solution)/shard_map/ppermute | solution.py:408
  84.6 0.0 collective-permute-done.16.from_1
  84.6 0.2 collective-permute-done.15.from_0
  84.8 0.0 copy-done.6
  84.8 0.0 copy-done.4
  84.8 2.4 %natural.1 = (f32[896,256]{1,0:T(8,128)S(1)}, f32[1,128]{1,0:T(1,128)S(1)}) custom-call(f32[2176,128]{1,0:T(8,128)S(1)} %bitcast.13, f32[512,128]{1,0:T(8,128)S(1)} %collective-permute-done.15.from_0, f32[384,128]{1,0:T(8,128)S(1)} %collective-permute-done.16.from_1, f32[896,896]{1,0:T(8,128)S(1)} %bitcast.20, f32[256,256]{1,0:T(8,128)S(1)} %bitcast.21), custom_call_target="tpu_custom_call" | custom-call | flops 1500000000 | bytes 5000000 | tf_op jit(solution)/shard_map/natural/pallas_call | solution.py:478
  87.2 5.9 %collective-permute-start.17 = (f32[1,128]{1,0:T(1,128)S(1)}, f32[1,128]{1,0:T(1,128)S(1)}, u32[]{:S(2)}, u32[]{:S(2)}) collective-permute-start(f32[1,128]{1,0:T(1,128)S(1)} %get-tuple-element.39.curvature), channel_id=1, source_target_pairs={{0,1},{1,0},{2,3},{3,2},{4,5},{5,4},{6,7},{7,6},{8,9},{9,8},{10,11... | collective-permute-start | bytes 1544 | tf_op jit(solution)/shard_map/ppermute | solution.py:487
  93.1 0.0 collective-permute-done.14.from_4
  93.1 0.0 collective-permute-done.13.from_3
  93.1 0.8 collective-permute-done.17.other
  93.9 0.0 collective-permute-done.12.from_2
  93.9 2.3 %finish.1 = (f32[896,896]{1,0:T(8,128)}, f32[256,256]{1,0:T(8,128)}, f32[896,256]{1,0:T(8,128)}) custom-call(f32[2176,128]{1,0:T(8,128)S(1)} %bitcast.14, f32[640,128]{1,0:T(8,128)S(1)} %collective-permute-done.12.from_2, f32[384,128]{1,0:T(8,128)S(1)} %collective-permute-done.13.from_3, f32[256,128]{1,0:T(8,128)S(1)} %collective-permute-done.14.from_4, ...), custom_call_target="tpu_custom_call" | custom-call | flops 10000000 | bytes 7000000 | tf_op jit(solution)/shard_map/finish/pallas_call | solution.py:488
  (2 shorter events, 0.0 us)
Async XLA Ops:
  0.6 8.2 %copy-start = (bf16[1,16,32,256]{3,2,1,0:T(8,128)(2,1)S(1)}, bf16[1,16,32,256]{3,2,1,0:T(8,128)(2,1)}, u32[]{:S(2)}) copy-start(bf16[1,16,32,256]{3,2,1,0:T(8,128)(2,1)} %param.8) | copy-start | bytes 786436
  0.6 8.2 %copy-start.1 = (bf16[1,2,16,32,128]{4,3,2,1,0:T(8,128)(2,1)S(1)}, bf16[1,2,16,32,128]{4,3,2,1,0:T(8,128)(2,1)}, u32[]{:S(2)}) copy-start(bf16[1,2,16,32,128]{4,3,2,1,0:T(8,128)(2,1)} %param.10) | copy-start | bytes 786436
  0.7 5.6 %copy-start.2 = (bf16[1,16,32,256]{3,2,1,0:T(8,128)(2,1)S(1)}, bf16[1,16,32,256]{3,2,1,0:T(8,128)(2,1)}, u32[]{:S(2)}) copy-start(bf16[1,16,32,256]{3,2,1,0:T(8,128)(2,1)} %param.9) | copy-start | bytes 786436
  0.7 6.2 %copy-start.3 = (f32[1,16]{1,0:T(1,128)S(1)}, f32[1,16]{1,0:T(1,128)}, u32[]{:S(2)}) copy-start(f32[1,16]{1,0:T(1,128)} %near.1) | copy-start | bytes 196
  0.7 8.2 %copy-start.5 = (bf16[2,896,256]{2,1,0:T(8,128)(2,1)S(1)}, bf16[2,896,256]{2,1,0:T(8,128)(2,1)}, u32[]{:S(2)}) copy-start(bf16[2,896,256]{2,1,0:T(8,128)(2,1)} %weights.3) | copy-start | bytes 2752516
  1.8 7.0 %collective-permute-start = (f32[512,256]{1,0:T(8,128)S(1)}, f32[512,256]{1,0:T(8,128)S(1)}, u32[]{:S(2)}, u32[]{:S(2)}) collective-permute-start(f32[512,256]{1,0:T(8,128)S(1)} %bitcast_convert_fusion.1), channel_id=1, source_target_pairs={{0,1},{1,0},{2,3},{3,2},{4,5},{5,4},{6,7},{7,6},{8,9},{9,8},{10,11... | collective-permute-start | bytes 1572872 | tf_op jit(solution)/shard_map/ppermute | solution.py:421
  6.1 2.7 %collective-permute-start.1 = (f32[2,512,128]{2,1,0:T(8,128)S(1)}, f32[2,512,128]{2,1,0:T(8,128)S(1)}, u32[]{:S(2)}, u32[]{:S(2)}) collective-permute-start(f32[2,512,128]{2,1,0:T(8,128)S(1)} %convert_element_type.10), channel_id=1, source_target_pairs={{0,1},{1,0},{2,3},{3,2},{4,5},{5,4},{6,7},{7,6},{8,9},{9,8},{10,11... | collective-permute-start | bytes 1572872 | tf_op jit(solution)/shard_map/ppermute | solution.py:422
  6.3 8.2 %collective-permute-start.2 = (f32[512,256]{1,0:T(8,128)S(1)}, f32[512,256]{1,0:T(8,128)S(1)}, u32[]{:S(2)}, u32[]{:S(2)}) collective-permute-start(f32[512,256]{1,0:T(8,128)S(1)} %bitcast_convert_fusion), channel_id=1, source_target_pairs={{0,1},{1,0},{2,3},{3,2},{4,5},{5,4},{6,7},{7,6},{8,9},{9,8},{10,11... | collective-permute-start | bytes 1572872 | tf_op jit(solution)/shard_map/ppermute | solution.py:424
  6.9 3.4 %collective-permute-start.3 = (f32[1,16]{1,0:T(1,128)S(1)}, f32[1,16]{1,0:T(1,128)S(1)}, u32[]{:S(2)}, u32[]{:S(2)}) collective-permute-start(f32[1,16]{1,0:T(1,128)S(1)} %copy-done.3), channel_id=1, source_target_pairs={{0,8},{8,0},{16,24},{24,16},{1,9},{9,1},{17,25},{25,17},{2,10},{10... | collective-permute-start | bytes 200 | tf_op jit(solution)/shard_map/ppermute | solution.py:423
  10.2 7.1 %collective-permute-start.4 = (f32[1,16]{1,0:T(1,128)S(1)}, f32[1,16]{1,0:T(1,128)S(1)}, u32[]{:S(2)}, u32[]{:S(2)}) collective-permute-start(f32[1,16]{1,0:T(1,128)S(1)} %pair.1.near), channel_id=1, source_target_pairs={{8,16},{16,8},{24,0},{0,24},{9,17},{17,9},{25,1},{1,25},{10,18},{1... | collective-permute-start | bytes 200 | tf_op jit(solution)/shard_map/ppermute | solution.py:436
  17.4 9.9 %collective-permute-start.7 = (f32[896,128]{1,0:T(8,128)S(1)}, f32[896,128]{1,0:T(8,128)S(1)}, u32[]{:S(2)}, u32[]{:S(2)}) collective-permute-start(f32[896,128]{1,0:T(8,128)S(1)} %get-tuple-element.31), channel_id=1, source_target_pairs={{0,32},{32,0},{64,96},{96,64},{33,65},{65,33},{97,1},{1,97},{2,34}... | collective-permute-start | bytes 1376264 | tf_op jit(solution)/shard_map/ppermute | solution.py:462
  20.2 7.1 %collective-permute-start.5 = (f32[264,128]{1,0:T(8,128)S(1)}, f32[264,128]{1,0:T(8,128)S(1)}, u32[]{:S(2)}, u32[]{:S(2)}) collective-permute-start(f32[264,128]{1,0:T(8,128)S(1)} %get-tuple-element.29), channel_id=1, source_target_pairs={{0,2},{2,0},{4,6},{6,4},{1,3},{3,1},{5,7},{7,5},{8,10},{10,8},{12,... | collective-permute-start | bytes 405512 | tf_op jit(solution)/shard_map/ppermute | solution.py:463
  21.4 5.9 %collective-permute-start.6 = (f32[264,128]{1,0:T(8,128)S(1)}, f32[264,128]{1,0:T(8,128)S(1)}, u32[]{:S(2)}, u32[]{:S(2)}) collective-permute-start(f32[264,128]{1,0:T(8,128)S(1)} %get-tuple-element.30), channel_id=1, source_target_pairs={{2,4},{4,2},{6,0},{0,6},{3,5},{5,3},{7,1},{1,7},{10,12},{12,10},{1... | collective-permute-start | bytes 405512 | tf_op jit(solution)/shard_map/ppermute | solution.py:464
  23.2 4.1 %collective-permute-start.8 = (f32[8,128]{1,0:T(8,128)S(1)}, f32[8,128]{1,0:T(8,128)S(1)}, u32[]{:S(2)}, u32[]{:S(2)}) collective-permute-start(f32[8,128]{1,0:T(8,128)S(1)} %get-tuple-element.32.row_sum), channel_id=1, source_target_pairs={{0,4},{2,6},{4,0},{6,2},{1,5},{3,7},{5,1},{7,3},{8,12},{10,14},{12... | collective-permute-start | bytes 12296 | tf_op jit(solution)/shard_map/ppermute | solution.py:465
  50.2 4.9 %collective-permute-start.11 = (f32[136,128]{1,0:T(8,128)S(1)}, f32[136,128]{1,0:T(8,128)S(1)}, u32[]{:S(2)}, u32[]{:S(2)}) collective-permute-start(f32[136,128]{1,0:T(8,128)S(1)} %reduce_sum.9), channel_id=1, source_target_pairs={{0,24},{8,0},{16,8},{24,16},{1,25},{9,1},{17,9},{25,17},{2,26},{10... | collective-permute-start | bytes 208904 | tf_op jit(solution)/shard_map/ppermute | solution.py:471
  51.3 5.4 %collective-permute-start.10 = (f32[136,128]{1,0:T(8,128)S(1)}, f32[136,128]{1,0:T(8,128)S(1)}, u32[]{:S(2)}, u32[]{:S(2)}) collective-permute-start(f32[136,128]{1,0:T(8,128)S(1)} %reduce_sum.9), channel_id=1, source_target_pairs={{0,8},{8,16},{16,24},{24,0},{1,9},{9,17},{17,25},{25,1},{2,10},{10... | collective-permute-start | bytes 208904 | tf_op jit(solution)/shard_map/ppermute | solution.py:471
  52.7 7.7 %collective-permute-start.9 = (f32[136,128]{1,0:T(8,128)S(1)}, f32[136,128]{1,0:T(8,128)S(1)}, u32[]{:S(2)}, u32[]{:S(2)}) collective-permute-start(f32[136,128]{1,0:T(8,128)S(1)} %reduce_sum.9), channel_id=1, source_target_pairs={{0,16},{8,24},{16,0},{24,8},{1,17},{9,25},{17,1},{25,9},{2,18},{10... | collective-permute-start | bytes 208904 | tf_op jit(solution)/shard_map/ppermute | solution.py:471
  60.4 24.5 %copy-start.6 = (f32[1,256,256]{2,1,0:T(8,128)S(1)}, f32[1,256,256]{2,1,0:T(8,128)}, u32[]{:S(2)}) copy-start(f32[1,256,256]{2,1,0:T(8,128)} %param.15) | copy-start | bytes 786436
  60.4 24.4 %copy-start.4 = (f32[1,896,896]{2,1,0:T(8,128)S(1)}, f32[1,896,896]{2,1,0:T(8,128)}, u32[]{:S(2)}) copy-start(f32[1,896,896]{2,1,0:T(8,128)} %param.14) | copy-start | bytes 9633796
  79.3 5.5 %collective-permute-start.15 = (f32[512,128]{1,0:T(8,128)S(1)}, f32[512,128]{1,0:T(8,128)S(1)}, u32[]{:S(2)}, u32[]{:S(2)}) collective-permute-start(f32[512,128]{1,0:T(8,128)S(1)} %get-tuple-element.36), channel_id=1, source_target_pairs={{0,2},{2,0},{4,6},{6,4},{1,3},{3,1},{5,7},{7,5},{8,10},{10,8},{12,... | collective-permute-start | bytes 786440 | tf_op jit(solution)/shard_map/ppermute | solution.py:408
  79.6 5.0 %collective-permute-start.16 = (f32[384,128]{1,0:T(8,128)S(1)}, f32[384,128]{1,0:T(8,128)S(1)}, u32[]{:S(2)}, u32[]{:S(2)}) collective-permute-start(f32[384,128]{1,0:T(8,128)S(1)} %get-tuple-element.37), channel_id=1, source_target_pairs={{0,32},{32,0},{64,96},{96,64},{1,33},{33,1},{65,97},{97,65},{2,34}... | collective-permute-start | bytes 589832 | tf_op jit(solution)/shard_map/ppermute | solution.py:408
  79.8 14.1 %collective-permute-start.12 = (f32[640,128]{1,0:T(8,128)S(1)}, f32[640,128]{1,0:T(8,128)S(1)}, u32[]{:S(2)}, u32[]{:S(2)}) collective-permute-start(f32[640,128]{1,0:T(8,128)S(1)} %get-tuple-element.33), channel_id=1, source_target_pairs={{0,128},{128,0},{1,129},{129,1},{2,130},{130,2},{3,131},{131,3},{4... | collective-permute-start | bytes 983048 | tf_op jit(solution)/shard_map/ppermute | solution.py:408
  81.8 11.3 %collective-permute-start.13 = (f32[384,128]{1,0:T(8,128)S(1)}, f32[384,128]{1,0:T(8,128)S(1)}, u32[]{:S(2)}, u32[]{:S(2)}) collective-permute-start(f32[384,128]{1,0:T(8,128)S(1)} %get-tuple-element.34), channel_id=1, source_target_pairs={{2,4},{4,2},{6,0},{0,6},{3,5},{5,3},{7,1},{1,7},{10,12},{12,10},{1... | collective-permute-start | bytes 589832 | tf_op jit(solution)/shard_map/ppermute | solution.py:408
  82.8 10.3 %collective-permute-start.14 = (f32[256,128]{1,0:T(8,128)S(1)}, f32[256,128]{1,0:T(8,128)S(1)}, u32[]{:S(2)}, u32[]{:S(2)}) collective-permute-start(f32[256,128]{1,0:T(8,128)S(1)} %get-tuple-element.35), channel_id=1, source_target_pairs={{32,64},{64,32},{96,0},{0,96},{33,65},{65,33},{97,1},{1,97},{34,66... | collective-permute-start | bytes 393224 | tf_op jit(solution)/shard_map/ppermute | solution.py:408
  87.2 6.8 %collective-permute-start.17 = (f32[1,128]{1,0:T(1,128)S(1)}, f32[1,128]{1,0:T(1,128)S(1)}, u32[]{:S(2)}, u32[]{:S(2)}) collective-permute-start(f32[1,128]{1,0:T(1,128)S(1)} %get-tuple-element.39.curvature), channel_id=1, source_target_pairs={{0,1},{1,0},{2,3},{3,2},{4,5},{5,4},{6,7},{7,6},{8,9},{9,8},{10,11... | collective-permute-start | bytes 1544 | tf_op jit(solution)/shard_map/ppermute | solution.py:487
